TPU v7x, 32 devices: a whole 2x2x4 slice. The times are simulated.
32 devices in a mesh: dp: 8 (over z, y), owner: 4 (over x, core).
Axes of the slice: x: 2, y: 2, z: 4, core: 2. Of those that a mesh axis runs over, the one named last changes fastest.
Arguments:
- images: bfloat16 [768, 7, 7, 2048], P(('dp', 'owner')), may hold values from -6 to 6
- valid_count: int32 [32], P(('dp', 'owner')), may hold values from 1 to 24, as said below
- labels: int32 [768], P(('dp', 'owner')), may hold values from 0 to 999
- loss_weight: int32 [768], P(('dp', 'owner')), may hold values from 1 to 4
- w_reduce: float32 [2, 512, 2048], P(None, 'owner', 'dp'), may hold values from -0.125 to 0.125
- w_spatial: float32 [2, 512, 4608], P(None, 'owner', 'dp'), may hold values from -0.09375 to 0.09375
- w_expand: float32 [2, 512, 2048], P(None, 'owner', 'dp'), may hold values from -0.25 to 0.25
- mom_reduce: float32 [2, 512, 2048], P(None, 'owner', 'dp'), may hold values from -0.001953125 to 0.001953125
- mom_spatial: float32 [2, 512, 4608], P(None, 'owner', 'dp'), may hold values from -0.001953125 to 0.001953125
- mom_expand: float32 [2, 512, 2048], P(None, 'owner', 'dp'), may hold values from -0.001953125 to 0.001953125
- head: float32 [1000, 2048], P('owner', 'dp'), may hold values from -0.5 to 0.5
- head_m: float32 [1000, 2048], P('owner', 'dp'), may hold values from -0.00048828125 to 0.00048828125
- head_v: float32 [1000, 2048], P('owner', 'dp'), may hold values from 4.6875e-10 to 1.875e-09
- norm_params: float32 [2, 2, 3072], replicated, may hold values from -1.5 to 1.5
- norm_m: float32 [2, 2, 3072], replicated, may hold values from -0.0012207031 to 0.0012207031
- norm_v: float32 [2, 2, 3072], replicated, may hold values from 3.8146974e-09 to 1.5894573e-08
- head_bias: float32 [1000], replicated, may hold values from -1.75 to 1.75
- bias_m: float32 [1000], replicated, may hold values from -0.0009765625 to 0.0009765625
- bias_v: float32 [1000], replicated, may hold values from 2.2135416e-09 to 8.854166e-09
Outputs:
- loss_sum: float32 [], replicated
- weight_total: float32 [], replicated
- new_reduce: float32 [2, 512, 2048], P(None, 'owner', 'dp')
- new_spatial: float32 [2, 512, 4608], P(None, 'owner', 'dp')
- new_expand: float32 [2, 512, 2048], P(None, 'owner', 'dp')
- new_mom_reduce: float32 [2, 512, 2048], P(None, 'owner', 'dp')
- new_mom_spatial: float32 [2, 512, 4608], P(None, 'owner', 'dp')
- new_mom_expand: float32 [2, 512, 2048], P(None, 'owner', 'dp')
- new_head: float32 [1000, 2048], P('owner', 'dp')
- new_head_m: float32 [1000, 2048], P('owner', 'dp')
- new_head_v: float32 [1000, 2048], P('owner', 'dp')
- new_norm: float32 [2, 2, 3072], replicated
- new_norm_m: float32 [2, 2, 3072], replicated
- new_norm_v: float32 [2, 2, 3072], replicated
- new_bias: float32 [1000], replicated
- new_bias_m: float32 [1000], replicated
- new_bias_v: float32 [1000], replicated
Inputs may be any that keep to these rules, and one draw needn't show every extreme that they name: The first valid_count[d] of device block d's 24 image slots are real images, the others padding.
All inputs are finite; a program needn't handle non-finite values.
Results may differ from a plain program's by a relative error of at most 0.025.
Values may be sent and summed in bfloat16 or wider, within the bound.
No kernel may reach another device: no remote copies, remote signals or barrier semaphores. Data moves between devices by JAX's collectives and lax.ppermute only.
A program may use at most 256 MiB of HBM per device.

v0:
```python
import jax
import jax.numpy as jnp
from jax import lax
from jax.sharding import PartitionSpec as P

LAYERS = 2
NS_STEPS = 5
STEP = 10


EPS = 1e-05
NS_A = 3.4445
NS_B = -4.775
NS_C = 2.0315
MOMENTUM = 0.9
LR_MATRIX = 0.5
DECAY_MATRIX = 0.01
BETA_ONE = 0.9
BETA_TWO = 0.999
ADAM_EPS = 1e-08
LR_HEAD = 0.2
DECAY_HEAD = 0.01
LR_VECTOR = 0.4


def shortened(shard):
    return jax.tree.map(lambda a: a.astype(jnp.bfloat16) if a.dtype == jnp.float32 else a, shard)


def contract_rows(left, right):
    return lax.dot_general(
        left, right, (((0,), (0,)), ((), ())), preferred_element_type=jnp.float32
    )


def contract_cols(left, right):
    return lax.dot_general(
        left, right, (((1,), (1,)), ((), ())), preferred_element_type=jnp.float32
    )


def silu_slope(values):
    sigmoid_part = jax.nn.sigmoid(values)
    return sigmoid_part * (1.0 + values * (1.0 - sigmoid_part))


def columns(values, count_img, side):
    chans = values.shape[1]
    grid = values.reshape(count_img, side, side, chans)
    padded = jnp.pad(grid, ((0, 0), (1, 1), (1, 1), (0, 0)))
    pieces = [
        padded[:, offset // 3 : offset // 3 + side, offset % 3 : offset % 3 + side, :]
        for offset in range(9)
    ]
    return jnp.concatenate(pieces, axis=3).reshape(count_img * side * side, 9 * chans)


def columns_back(grad_patches, count_img, side, chans):
    grid = grad_patches.reshape(count_img, side, side, 9, chans)
    summed = jnp.zeros((count_img, side + 2, side + 2, chans), jnp.float32)
    for offset in range(9):
        row_shift = offset // 3
        col_shift = offset % 3
        summed = summed + jnp.pad(
            grid[:, :, :, offset, :],
            ((0, 0), (row_shift, 2 - row_shift), (col_shift, 2 - col_shift), (0, 0)),
        )
    return summed[:, 1 : side + 1, 1 : side + 1, :].reshape(count_img * side * side, chans)


def norm_forward(hidden, norm_gain, norm_bias, mask_pix):
    local_terms = (
        jnp.sum(hidden * mask_pix, axis=0),
        jnp.sum(hidden * hidden * mask_pix, axis=0),
        jnp.sum(mask_pix),
    )
    first_sum, square_sum, total_count = lax.psum(
        (local_terms[0], local_terms[1], local_terms[2]), ("dp", "owner")
    )
    centre = first_sum / total_count
    spread = square_sum / total_count - centre * centre
    inverse = lax.rsqrt(spread + EPS)
    normed = (hidden - centre) * inverse
    return (normed * norm_gain + norm_bias, normed, inverse, total_count)


def norm_backward(grad_out, normed, inverse, norm_gain, mask_pix, total_count):
    bias_grad, gain_grad = lax.psum(
        (jnp.sum(grad_out, axis=0), jnp.sum(grad_out * normed, axis=0)), ("dp", "owner")
    )
    grad_in = (
        norm_gain * inverse * (grad_out - mask_pix * (bias_grad + normed * gain_grad) / total_count)
    )
    return (grad_in, gain_grad, bias_grad)


def layer_forward(
    inputs, weight_one, weight_two, weight_three, norm_gain, norm_bias, mask_pix, count_img, side
):
    narrow = weight_one.shape[0]
    inputs_low = inputs.astype(jnp.bfloat16)
    reduced = contract_cols(inputs_low, weight_one)
    first_out, first_norm, first_inv, total_count = norm_forward(
        reduced, norm_gain[:narrow], norm_bias[:narrow], mask_pix
    )
    first_act = jax.nn.silu(first_out).astype(jnp.bfloat16)
    patches = columns(first_act, count_img, side)
    spatial = contract_cols(patches, weight_two)
    second_out, second_norm, second_inv, unused_one = norm_forward(
        spatial, norm_gain[narrow : 2 * narrow], norm_bias[narrow : 2 * narrow], mask_pix
    )
    second_act = jax.nn.silu(second_out).astype(jnp.bfloat16)
    expanded = jnp.dot(second_act, weight_three, preferred_element_type=jnp.float32)
    third_out, third_norm, third_inv, unused_two = norm_forward(
        expanded, norm_gain[2 * narrow :], norm_bias[2 * narrow :], mask_pix
    )
    summed = inputs + third_out
    kept = (
        inputs_low,
        first_out,
        first_norm,
        first_inv,
        patches,
        second_out,
        second_norm,
        second_inv,
        second_act,
        third_norm,
        third_inv,
        summed,
        total_count,
    )
    return (jax.nn.silu(summed), kept)


def layer_backward(
    grad_out, kept, weight_one, weight_two, weight_three, norm_gain, mask_pix, count_img, side
):
    (
        inputs_low,
        first_out,
        first_norm,
        first_inv,
        patches,
        second_out,
        second_norm,
        second_inv,
        second_act,
        third_norm,
        third_inv,
        summed,
        total_count,
    ) = kept
    narrow = weight_one.shape[0]
    grad_sum = grad_out * silu_slope(summed)
    grad_third, gain_three, bias_three = norm_backward(
        grad_sum, third_norm, third_inv, norm_gain[2 * narrow :], mask_pix, total_count
    )
    grad_third = grad_third.astype(jnp.bfloat16)
    grad_w_three = contract_rows(second_act, grad_third)
    grad_second = contract_cols(grad_third, weight_three) * silu_slope(second_out)
    grad_spatial, gain_two, bias_two = norm_backward(
        grad_second, second_norm, second_inv, norm_gain[narrow : 2 * narrow], mask_pix, total_count
    )
    grad_spatial = grad_spatial.astype(jnp.bfloat16)
    grad_w_two = contract_rows(grad_spatial, patches)
    grad_patches = jnp.dot(grad_spatial, weight_two, preferred_element_type=jnp.float32)
    grad_first = columns_back(grad_patches, count_img, side, narrow) * silu_slope(first_out)
    grad_reduced, gain_one, bias_one = norm_backward(
        grad_first, first_norm, first_inv, norm_gain[:narrow], mask_pix, total_count
    )
    grad_reduced = grad_reduced.astype(jnp.bfloat16)
    grad_w_one = contract_rows(grad_reduced, inputs_low)
    grad_in = jnp.dot(grad_reduced, weight_one, preferred_element_type=jnp.float32) + grad_sum
    gain_grads = jnp.concatenate([gain_one, gain_two, gain_three])
    bias_grads = jnp.concatenate([bias_one, bias_two, bias_three])
    return (grad_in, (grad_w_one, grad_w_two, grad_w_three), gain_grads, bias_grads)


def newton_schulz(moments):
    row_parts = moments
    for iteration in range(NS_STEPS):
        all_rows = jax.tree.map(
            lambda part, own: part.astype(own.dtype),
            lax.all_gather(shortened(row_parts), "owner", axis=1, tiled=True),
            row_parts,
        )
        partial_gram = tuple(
            (
                jnp.einsum("lrk,lnk->lrn", rows_here, rows_all, precision=lax.Precision.HIGHEST)
                for rows_here, rows_all in zip(row_parts, all_rows)
            )
        )
        gram_rows = lax.psum(partial_gram, "dp")
        gram_full = jax.tree.map(
            lambda part, own: part.astype(own.dtype),
            lax.all_gather(shortened(gram_rows), "owner", axis=1, tiled=True),
            gram_rows,
        )
        if iteration == 0:
            factors = tuple(
                (
                    (1.0 / (jnp.sqrt(jnp.trace(gram, axis1=1, axis2=2)) + 1e-07))[:, None, None]
                    for gram in gram_full
                )
            )
            row_parts = tuple((rows_here * factor for rows_here, factor in zip(row_parts, factors)))
            all_rows = tuple((rows_all * factor for rows_all, factor in zip(all_rows, factors)))
            gram_rows = tuple((gram * factor * factor for gram, factor in zip(gram_rows, factors)))
            gram_full = tuple((gram * factor * factor for gram, factor in zip(gram_full, factors)))
        mixed = tuple(
            (
                NS_B * rows_gram
                + NS_C
                * jnp.einsum("lrn,lnm->lrm", rows_gram, whole_gram, precision=lax.Precision.HIGHEST)
                for rows_gram, whole_gram in zip(gram_rows, gram_full)
            )
        )
        row_parts = tuple(
            (
                NS_A * rows_here
                + jnp.einsum("lrn,lnk->lrk", mixed_rows, rows_all, precision=lax.Precision.HIGHEST)
                for rows_here, mixed_rows, rows_all in zip(row_parts, mixed, all_rows)
            )
        )
    return row_parts


def adamw(weight, grad, first, second, rate, decay):
    first = BETA_ONE * first + (1.0 - BETA_ONE) * grad
    second = BETA_TWO * second + (1.0 - BETA_TWO) * grad * grad
    first_hat = first / (1.0 - BETA_ONE**STEP)
    second_hat = second / (1.0 - BETA_TWO**STEP)
    weight = weight - rate * (first_hat / (jnp.sqrt(second_hat) + ADAM_EPS) + decay * weight)
    return (weight, first, second)


def per_device(
    images,
    valid_count,
    labels,
    loss_weight,
    w_reduce,
    w_spatial,
    w_expand,
    mom_reduce,
    mom_spatial,
    mom_expand,
    head,
    head_m,
    head_v,
    norm_params,
    norm_m,
    norm_v,
    head_bias,
    bias_m,
    bias_v,
):
    count_img = images.shape[0]
    side = images.shape[1]
    wide = images.shape[3]
    pixels = side * side
    local_shards = (
        w_reduce.astype(jnp.bfloat16),
        w_spatial.astype(jnp.bfloat16),
        w_expand.astype(jnp.bfloat16),
        head[None].astype(jnp.bfloat16),
    )
    by_columns = (
        lax.all_gather(local_shards[0], "dp", axis=2, tiled=True),
        lax.all_gather(local_shards[1], "dp", axis=2, tiled=True),
        lax.all_gather(local_shards[2], "dp", axis=2, tiled=True),
        lax.all_gather(local_shards[3], "dp", axis=2, tiled=True),
    )
    weight_one, weight_two, weight_three, head_stack = (
        lax.all_gather(by_columns[0], "owner", axis=1, tiled=True),
        lax.all_gather(by_columns[1], "owner", axis=1, tiled=True),
        lax.all_gather(by_columns[2], "owner", axis=1, tiled=True),
        lax.all_gather(by_columns[3], "owner", axis=1, tiled=True),
    )
    head_full = head_stack[0]
    valid = (jnp.arange(count_img, dtype=jnp.int32) < valid_count[0]).astype(jnp.float32)
    mask_pix = jnp.repeat(valid, pixels)[:, None]
    current = images.reshape(count_img * pixels, wide).astype(jnp.float32)
    kept_layers = []
    for layer in range(LAYERS):
        current, kept = layer_forward(
            current,
            weight_one[layer],
            weight_two[layer],
            weight_three[layer],
            norm_params[0, layer],
            norm_params[1, layer],
            mask_pix,
            count_img,
            side,
        )
        kept_layers.append(kept)
    pooled = jnp.mean(current.reshape(count_img, pixels, wide), axis=1)
    pooled_low = pooled.astype(jnp.bfloat16)
    logits = contract_cols(pooled_low, head_full) + head_bias
    top_logit = jnp.max(logits, axis=1, keepdims=True)
    log_total = jnp.log(jnp.sum(jnp.exp(logits - top_logit), axis=1, keepdims=True)) + top_logit
    onehot = (labels[:, None] == jnp.arange(logits.shape[1], dtype=jnp.int32)[None, :]).astype(
        jnp.float32
    )
    weight_img = valid * loss_weight.astype(jnp.float32)
    local_loss = jnp.sum(weight_img * (log_total[:, 0] - jnp.sum(logits * onehot, axis=1)))
    residue = weight_img[:, None] * (jnp.exp(logits - log_total) - onehot)
    weight_total, loss_sum, bias_raw = lax.psum(
        (jnp.sum(weight_img), local_loss, jnp.sum(residue, axis=0)), ("dp", "owner")
    )
    grad_bias = bias_raw / weight_total
    grad_low = (residue / weight_total).astype(jnp.bfloat16)
    grad_head = contract_rows(grad_low, pooled_low)
    grad_pooled = jnp.dot(grad_low, head_full, preferred_element_type=jnp.float32)
    grad_current = jnp.repeat(grad_pooled / pixels, pixels, axis=0)
    grads_one, grads_two, grads_three, gain_rows, bias_rows = ([], [], [], [], [])
    for layer in reversed(range(LAYERS)):
        grad_current, weight_grads, gain_grads, bias_grads = layer_backward(
            grad_current,
            kept_layers[layer],
            weight_one[layer],
            weight_two[layer],
            weight_three[layer],
            norm_params[0, layer],
            mask_pix,
            count_img,
            side,
        )
        grads_one.insert(0, weight_grads[0])
        grads_two.insert(0, weight_grads[1])
        grads_three.insert(0, weight_grads[2])
        gain_rows.insert(0, gain_grads)
        bias_rows.insert(0, bias_grads)
    grad_stacks = (
        jnp.stack(grads_one),
        jnp.stack(grads_two),
        jnp.stack(grads_three),
        grad_head[None],
    )
    norm_grad = jnp.stack([jnp.stack(gain_rows), jnp.stack(bias_rows)])
    partial_sums = (
        lax.psum_scatter(grad_stacks[0], "dp", scatter_dimension=2, tiled=True),
        lax.psum_scatter(grad_stacks[1], "dp", scatter_dimension=2, tiled=True),
        lax.psum_scatter(grad_stacks[2], "dp", scatter_dimension=2, tiled=True),
        lax.psum_scatter(grad_stacks[3], "dp", scatter_dimension=2, tiled=True),
    )
    reduced = (
        lax.psum_scatter(
            partial_sums[0].astype(jnp.bfloat16), "owner", scatter_dimension=1, tiled=True
        ).astype(jnp.float32),
        lax.psum_scatter(
            partial_sums[1].astype(jnp.bfloat16), "owner", scatter_dimension=1, tiled=True
        ).astype(jnp.float32),
        lax.psum_scatter(
            partial_sums[2].astype(jnp.bfloat16), "owner", scatter_dimension=1, tiled=True
        ).astype(jnp.float32),
        lax.psum_scatter(
            partial_sums[3].astype(jnp.bfloat16), "owner", scatter_dimension=1, tiled=True
        ).astype(jnp.float32),
    )
    moments = (
        MOMENTUM * mom_reduce + reduced[0],
        MOMENTUM * mom_spatial + reduced[1],
        MOMENTUM * mom_expand + reduced[2],
    )
    directions = newton_schulz(moments)
    masters = (w_reduce, w_spatial, w_expand)
    updated = tuple(
        (
            master * (1.0 - LR_MATRIX * DECAY_MATRIX) - LR_MATRIX * direction
            for master, direction in zip(masters, directions)
        )
    )
    new_head, new_head_m, new_head_v = adamw(
        head, reduced[3][0], head_m, head_v, LR_HEAD, DECAY_HEAD
    )
    new_norm, new_norm_m, new_norm_v = adamw(norm_params, norm_grad, norm_m, norm_v, LR_VECTOR, 0.0)
    new_bias, new_bias_m, new_bias_v = adamw(head_bias, grad_bias, bias_m, bias_v, LR_VECTOR, 0.0)
    return (
        loss_sum,
        weight_total,
        updated[0],
        updated[1],
        updated[2],
        moments[0],
        moments[1],
        moments[2],
        new_head,
        new_head_m,
        new_head_v,
        new_norm,
        new_norm_m,
        new_norm_v,
        new_bias,
        new_bias_m,
        new_bias_v,
    )


def solution(mesh):
    return jax.shard_map(
        per_device,
        mesh=mesh,
        in_specs=(
            P(("dp", "owner"), None, None, None),
            P(("dp", "owner")),
            P(("dp", "owner")),
            P(("dp", "owner")),
            P(None, "owner", "dp"),
            P(None, "owner", "dp"),
            P(None, "owner", "dp"),
            P(None, "owner", "dp"),
            P(None, "owner", "dp"),
            P(None, "owner", "dp"),
            P("owner", "dp"),
            P("owner", "dp"),
            P("owner", "dp"),
            P(),
            P(),
            P(),
            P(),
            P(),
            P(),
        ),
        out_specs=(
            P(),
            P(),
            P(None, "owner", "dp"),
            P(None, "owner", "dp"),
            P(None, "owner", "dp"),
            P(None, "owner", "dp"),
            P(None, "owner", "dp"),
            P(None, "owner", "dp"),
            P("owner", "dp"),
            P("owner", "dp"),
            P("owner", "dp"),
            P(),
            P(),
            P(),
            P(),
            P(),
            P(),
        ),
        check_vma=False,
    )
```

profile of v0, /device:TPU:0, one launch (start us, length us, event | category | flops | bytes accessed | tf_op | source)
XLA Modules:
  0.0 3250.7 jit_solution(136949946555570657)
XLA Ops:
  12.6 37.8 %all-gather = bf16[250,2048]{1,0:T(8,128)(2,1)} all-gather(bf16[250,256]{1,0:T(8,128)(2,1)S(1)} %convert_element_type.263), channel_id=2, replica_groups=mesh['dp'=8,'owner'=4] {'dp'}, dimensions={1}, use_global_device_ids=true | all-gather | bytes 1152000 | tf_op jit(solution)/shard_map/all_gather | solution.py:273
  56.8 54.7 %all-gather.35.cloned.1.call-done = bf16[2,128,4608]{1,2,0:T(8,128)(2,1)} async-done(((bf16[2,128,576]{1,2,0:T(8,128)(2,1)}), bf16[2,128,4608]{1,2,0:T(8,128)(2,1)}) %all-gather.35.cloned.1.call-update) | async-done | bytes 2359312 | tf_op jit(solution)/shard_map/all_gather | solution.py:271
  129.5 22.7 all-gather.39.cloned.1.call-done
  152.3 34.7 %all-gather.83.cloned.1.call-done = bf16[4,250,2048]{2,1,0:T(8,128)(2,1)} async-done(((bf16[1,250,2048]{2,1,0:T(8,128)(2,1)}), bf16[4,250,2048]{2,1,0:T(8,128)(2,1)}) %all-gather.83.cloned.1.call-update) | async-done | bytes 4096016 | tf_op jit(solution)/shard_map/all_gather | solution.py:279
  192.2 30.7 all-gather.33.cloned.1.call-done
  228.4 40.5 %all-reduce.34 = (f32[512]{0:T(512)S(1)}, f32[]{:T(128)}, f32[512]{0:T(512)S(1)}) all-reduce(f32[512]{0:T(512)S(1)} %get-tuple-element.66, f32[]{:T(128)} %broadcast_reduce_fusion, f32[512]{0:T(512)S(1)} %get-tuple-element.65), channel_id=1, replica_groups=mesh['dp'=8,'owner'=4] {'dp','owner'}, use_global_device_ids=true, to_apply=%region_5.0 | all-reduce | flops 1025 | bytes 8200 | tf_op jit(solution)/shard_map/psum | solution.py:77
  331.9 41.1 %all-reduce.33 = (f32[512]{0:T(512)S(1)}, f32[512]{0:T(512)S(1)}) all-reduce(f32[512]{0:T(512)S(1)} %get-tuple-element.64, f32[512]{0:T(512)S(1)} %get-tuple-element.63), channel_id=1, replica_groups=mesh['dp'=8,'owner'=4] {'dp','owner'}, use_global_device_ids=true, to_apply=%region_9.10 | all-reduce | flops 1024 | bytes 8192 | tf_op jit(solution)/shard_map/psum | solution.py:77
  381.6 50.3 %all-reduce.32 = (f32[2048]{0:T(1024)S(1)}, f32[2048]{0:T(1024)S(1)}) all-reduce(f32[2048]{0:T(1024)S(1)} %get-tuple-element.54, f32[2048]{0:T(1024)S(1)} %get-tuple-element.53), channel_id=1, replica_groups=mesh['dp'=8,'owner'=4] {'dp','owner'}, use_global_device_ids=true, to_apply=%region_11.12 | all-reduce | flops 4096 | bytes 32768 | tf_op jit(solution)/shard_map/psum | solution.py:77
  444.8 40.9 %all-reduce.31 = (f32[512]{0:T(512)S(1)}, f32[512]{0:T(512)S(1)}) all-reduce(f32[512]{0:T(512)S(1)} %get-tuple-element.62, f32[512]{0:T(512)S(1)} %get-tuple-element.61), channel_id=1, replica_groups=mesh['dp'=8,'owner'=4] {'dp','owner'}, use_global_device_ids=true, to_apply=%region_17.18 | all-reduce | flops 1024 | bytes 8192 | tf_op jit(solution)/shard_map/psum | solution.py:77
  541.3 39.3 %all-reduce.30 = (f32[512]{0:T(512)S(1)}, f32[512]{0:T(512)S(1)}) all-reduce(f32[512]{0:T(512)S(1)} %get-tuple-element.60, f32[512]{0:T(512)S(1)} %get-tuple-element.59), channel_id=1, replica_groups=mesh['dp'=8,'owner'=4] {'dp','owner'}, use_global_device_ids=true, to_apply=%region_21.22 | all-reduce | flops 1024 | bytes 8192 | tf_op jit(solution)/shard_map/psum | solution.py:77
  590.5 41.1 %all-reduce.29 = (f32[2048]{0:T(1024)S(1)}, f32[2048]{0:T(1024)S(1)}) all-reduce(f32[2048]{0:T(1024)S(1)} %get-tuple-element.52, f32[2048]{0:T(1024)S(1)} %get-tuple-element.51), channel_id=1, replica_groups=mesh['dp'=8,'owner'=4] {'dp','owner'}, use_global_device_ids=true, to_apply=%region_23.24 | all-reduce | flops 4096 | bytes 32768 | tf_op jit(solution)/shard_map/psum | solution.py:77
  664.7 39.7 %psum.330 = f32[]{:T(128)} all-reduce(f32[]{:T(128)} %get-tuple-element.80), channel_id=1, replica_groups=mesh['dp'=8,'owner'=4] {'dp','owner'}, use_global_device_ids=true, to_apply=%region_33.34 | all-reduce | flops 1 | bytes 8 | tf_op jit(solution)/shard_map/psum | solution.py:310
  737.9 41.3 %all-reduce.28 = (f32[2048]{0:T(1024)S(1)}, f32[2048]{0:T(1024)S(1)}) all-reduce(f32[2048]{0:T(1024)S(1)} %get-tuple-element.58, f32[2048]{0:T(1024)S(1)} %get-tuple-element.57), channel_id=1, replica_groups=mesh['dp'=8,'owner'=4] {'dp','owner'}, use_global_device_ids=true, to_apply=%region_37.38 | all-reduce | flops 4096 | bytes 32768 | tf_op jit(solution)/shard_map/psum | solution.py:88
  793.7 39.3 %all-reduce.27 = (f32[512]{0:T(512)S(1)}, f32[512]{0:T(512)S(1)}) all-reduce(f32[512]{0:T(512)S(1)} %get-tuple-element.74, f32[512]{0:T(512)S(1)} %get-tuple-element.73), channel_id=1, replica_groups=mesh['dp'=8,'owner'=4] {'dp','owner'}, use_global_device_ids=true, to_apply=%region_41.42 | all-reduce | flops 1024 | bytes 8192 | tf_op jit(solution)/shard_map/psum | solution.py:88
  907.3 40.9 %all-reduce.26 = (f32[512]{0:T(512)S(1)}, f32[512]{0:T(512)S(1)}) all-reduce(f32[512]{0:T(512)S(1)} %get-tuple-element.72, f32[512]{0:T(512)S(1)} %get-tuple-element.71), channel_id=1, replica_groups=mesh['dp'=8,'owner'=4] {'dp','owner'}, use_global_device_ids=true, to_apply=%region_45.46 | all-reduce | flops 1024 | bytes 8192 | tf_op jit(solution)/shard_map/psum | solution.py:88
  966.2 39.6 %all-reduce.25 = (f32[2048]{0:T(1024)S(1)}, f32[2048]{0:T(1024)S(1)}) all-reduce(f32[2048]{0:T(1024)S(1)} %get-tuple-element.56, f32[2048]{0:T(1024)S(1)} %get-tuple-element.55), channel_id=1, replica_groups=mesh['dp'=8,'owner'=4] {'dp','owner'}, use_global_device_ids=true, to_apply=%region_49.50 | all-reduce | flops 4096 | bytes 32768 | tf_op jit(solution)/shard_map/psum | solution.py:88
  1020.6 41.0 %all-reduce.24 = (f32[512]{0:T(512)S(1)}, f32[512]{0:T(512)S(1)}) all-reduce(f32[512]{0:T(512)S(1)} %get-tuple-element.70, f32[512]{0:T(512)S(1)} %get-tuple-element.69), channel_id=1, replica_groups=mesh['dp'=8,'owner'=4] {'dp','owner'}, use_global_device_ids=true, to_apply=%region_53.54 | all-reduce | flops 1024 | bytes 8192 | tf_op jit(solution)/shard_map/psum | solution.py:88
  1081.8 28.0 copy.193
  1109.7 722.8 %all-reduce.56 = bf16[2,512,4608]{1,0,2:T(2,128)(2,1)} all-reduce(f32[2,512,4608]{1,0,2:T(2,128)} %copy.193), channel_id=6, replica_groups=mesh['dp'=8,'owner'=4] {'dp'}, use_global_device_ids=true, to_apply=%region_66.67.clone | all-reduce | flops 4718592 | bytes 28311552
  1905.7 41.6 %all-reduce.23 = (f32[]{:T(128)}, f32[512]{0:T(512)S(1)}, f32[512]{0:T(512)S(1)}, f32[1000]{0:T(1024)S(1)}) all-reduce(f32[]{:T(128)} %get-tuple-element.81, f32[512]{0:T(512)S(1)} %get-tuple-element.68, f32[512]{0:T(512)S(1)} %get-tuple-element.67, f32[1000]{0:T(1024)S(1)} %copy-done.99), channel_id=1, replica_groups=mesh['dp'=8,'owner'=4] {'dp','owner'}, use_global_device_ids=true, to_apply=%region_31.32 | all-reduce | flops 2025 | bytes 16200 | tf_op jit(solution)/shard_map/psum | solution.py:310
  1966.6 55.6 %reduce-scatter.16.cloned.1.call-done = f32[2,512,256]{2,1,0:T(8,128)} async-done(((f32[2,512,2048]{2,1,0:T(8,128)}), f32[2,512,256]{2,1,0:T(8,128)}) %reduce-scatter.16.cloned.1.call-update) | async-done | bytes 1048592 | tf_op jit(solution)/shard_map/reduce_scatter | solution.py:346
  2024.3 149.8 %reduce-scatter.12.cloned.1.call-done = f32[2,512,256]{2,1,0:T(8,128)} async-done(((f32[2,512,2048]{2,1,0:T(8,128)}), f32[2,512,256]{2,1,0:T(8,128)}) %reduce-scatter.12.cloned.1.call-update) | async-done | bytes 1048592 | tf_op jit(solution)/shard_map/reduce_scatter | solution.py:344
  2195.3 21.3 reduce-scatter.18.cloned.1.call-done
  2224.2 17.0 reduce-scatter.14.cloned.1.call-done
  2251.9 90.2 %all-reduce.55.cloned.1.call-done = (f32[2,128,512]{2,1,0:T(8,128)}, f32[2,128,512]{2,1,0:T(8,128)}, f32[2,128,512]{2,1,0:T(8,128)}) async-done(((f32[2,128,512]{2,1,0:T(8,128)}, f32[2,128,512]{2,1,0:T(8,128)}, f32[2,128,512]{2,1,0:T(8,128)}), (f32[2,128,512]{2,1,0:T(8,128)}, f32[2,128,512]{2,1,0:T(8,128)}, f32[2,128,512]{2,1,0:T(8,128)})) %all-reduce.55.cloned.1.call-update) | async-done | bytes 1572880 | tf_op jit(solution)/shard_map/psum | solution.py:194
  2360.3 18.8 all-gather.73.cloned.1.call-done
  2379.2 18.8 all-gather.55.cloned.1.call-done
  2434.1 89.7 %all-reduce.53.cloned.1.call-done = (f32[2,128,512]{2,1,0:T(8,128)}, f32[2,128,512]{2,1,0:T(8,128)}, f32[2,128,512]{2,1,0:T(8,128)}) async-done(((f32[2,128,512]{2,1,0:T(8,128)}, f32[2,128,512]{2,1,0:T(8,128)}, f32[2,128,512]{2,1,0:T(8,128)}), (f32[2,128,512]{2,1,0:T(8,128)}, f32[2,128,512]{2,1,0:T(8,128)}, f32[2,128,512]{2,1,0:T(8,128)})) %all-reduce.53.cloned.1.call-update) | async-done | bytes 1572880 | tf_op jit(solution)/shard_map/psum | solution.py:194
  2602.2 91.5 %all-reduce.51.cloned.1.call-done = (f32[2,128,512]{2,1,0:T(8,128)}, f32[2,128,512]{2,1,0:T(8,128)}, f32[2,128,512]{2,1,0:T(8,128)}) async-done(((f32[2,128,512]{2,1,0:T(8,128)}, f32[2,128,512]{2,1,0:T(8,128)}, f32[2,128,512]{2,1,0:T(8,128)}), (f32[2,128,512]{2,1,0:T(8,128)}, f32[2,128,512]{2,1,0:T(8,128)}, f32[2,128,512]{2,1,0:T(8,128)})) %all-reduce.51.cloned.1.call-update) | async-done | bytes 1572880 | tf_op jit(solution)/shard_map/psum | solution.py:194
  2772.0 91.7 %all-reduce.49.cloned.1.call-done = (f32[2,128,512]{2,1,0:T(8,128)}, f32[2,128,512]{2,1,0:T(8,128)}, f32[2,128,512]{2,1,0:T(8,128)}) async-done(((f32[2,128,512]{2,1,0:T(8,128)}, f32[2,128,512]{2,1,0:T(8,128)}, f32[2,128,512]{2,1,0:T(8,128)}), (f32[2,128,512]{2,1,0:T(8,128)}, f32[2,128,512]{2,1,0:T(8,128)}, f32[2,128,512]{2,1,0:T(8,128)})) %all-reduce.49.cloned.1.call-update) | async-done | bytes 1572880 | tf_op jit(solution)/shard_map/psum | solution.py:194
  2947.5 86.1 %all-reduce.47.cloned.1.call-done = (f32[2,128,512]{2,1,0:T(8,128)}, f32[2,128,512]{2,1,0:T(8,128)}, f32[2,128,512]{2,1,0:T(8,128)}) async-done(((f32[2,128,512]{2,1,0:T(8,128)}, f32[2,128,512]{2,1,0:T(8,128)}, f32[2,128,512]{2,1,0:T(8,128)}), (f32[2,128,512]{2,1,0:T(8,128)}, f32[2,128,512]{2,1,0:T(8,128)}, f32[2,128,512]{2,1,0:T(8,128)})) %all-reduce.47.cloned.1.call-update) | async-done | bytes 1572880 | tf_op jit(solution)/shard_map/psum | solution.py:194
  3039.8 144.6 %reduce-scatter.20.cloned.1.call-done = f32[1,1000,256]{2,1,0:T(8,128)} async-done(((f32[1,1000,2048]{2,1,0:T(8,128)}), f32[1,1000,256]{2,1,0:T(8,128)}) %reduce-scatter.20.cloned.1.call-update) | async-done | bytes 1024016 | tf_op jit(solution)/shard_map/reduce_scatter | solution.py:347
  (605 shorter events, 888.9 us)
Async XLA Ops:
  8.9 102.6 %all-gather.35.cloned.1.call-start = ((), (), s32[]{:S(2)}) async-start(), calls=%async_computation.8 | async-start | bytes 2654208 | tf_op jit(solution)/shard_map/all_gather | solution.py:271
  10.8 141.4 %all-gather.39.cloned.1.call-start = ((), (), s32[]{:S(2)}) async-start(), calls=%async_computation.10 | async-start | bytes 1179648 | tf_op jit(solution)/shard_map/all_gather | solution.py:272
  12.5 174.5 %all-gather.83.cloned.1.call-start = ((), (), s32[]{:S(2)}) async-start(), calls=%async_computation.37 | async-start | bytes 5242880 | tf_op jit(solution)/shard_map/all_gather | solution.py:279
  50.4 172.5 %all-gather.33.cloned.1.call-start = ((), (), s32[]{:S(2)}) async-start(), calls=%async_computation.7 | async-start | bytes 5242880 | tf_op jit(solution)/shard_map/all_gather | solution.py:276
  56.8 265.0 %all-gather.37.cloned.1.call-start = ((), (), s32[]{:S(2)}) async-start(), calls=%async_computation.9 | async-start | bytes 11796480 | tf_op jit(solution)/shard_map/all_gather | solution.py:277
  111.5 262.7 %all-gather.41.cloned.1.call-start = ((), (), s32[]{:S(2)}) async-start(), calls=%async_computation.11 | async-start | bytes 5242880 | tf_op jit(solution)/shard_map/all_gather | solution.py:278
  152.2 1811.3 %reduce-scatter.22.cloned.1.call-start = ((), (), s32[]{:S(2)}) async-start(), calls=%async_computation.38 | async-start | bytes 1474560
  1842.5 179.6 %reduce-scatter.16.cloned.1.call-start = ((), (), s32[]{:S(2)}) async-start(), calls=%async_computation.29 | async-start | bytes 9437184 | tf_op jit(solution)/shard_map/reduce_scatter | solution.py:346
  1857.8 316.3 %reduce-scatter.12.cloned.1.call-start = ((), (), s32[]{:S(2)}) async-start(), calls=%async_computation.12 | async-start | bytes 9437184 | tf_op jit(solution)/shard_map/reduce_scatter | solution.py:344
  1963.5 228.8 %all-gather.53.cloned.1.call-start = ((), (), s32[]{:S(2)}) async-start(), calls=%async_computation.19 | async-start | bytes 1474560 | tf_op jit(solution)/shard_map/all_gather | solution.py:185
  1966.5 250.0 %reduce-scatter.18.cloned.1.call-start = ((), (), s32[]{:S(2)}) async-start(), calls=%async_computation.30 | async-start | bytes 655360 | tf_op jit(solution)/shard_map/reduce_scatter | solution.py:356
  2024.3 217.0 %reduce-scatter.14.cloned.1.call-start = ((), (), s32[]{:S(2)}) async-start(), calls=%async_computation.13 | async-start | bytes 655360 | tf_op jit(solution)/shard_map/reduce_scatter | solution.py:350
  2176.2 166.0 %all-reduce.55.cloned.1.call-start = ((), (), s32[]{:S(2)}) async-start(), calls=%async_computation.43 | async-start | bytes 3145728 | tf_op jit(solution)/shard_map/psum | solution.py:194
  2251.9 108.4 %all-gather.43.cloned.1.call-start = ((), (), s32[]{:S(2)}) async-start(), calls=%async_computation.14 | async-start | bytes 1310720 | tf_op jit(solution)/shard_map/all_gather | solution.py:197
  2346.7 84.2 %all-gather.57.cloned.1.call-start = ((), (), s32[]{:S(2)}) async-start(), calls=%async_computation.21 | async-start | bytes 1474560 | tf_op jit(solution)/shard_map/all_gather | solution.py:185
  2405.5 118.3 %all-reduce.53.cloned.1.call-start = ((), (), s32[]{:S(2)}) async-start(), calls=%async_computation.42 | async-start | bytes 3145728 | tf_op jit(solution)/shard_map/psum | solution.py:194
  2433.8 108.1 %all-gather.59.cloned.1.call-start = ((), (), s32[]{:S(2)}) async-start(), calls=%async_computation.22 | async-start | bytes 1310720 | tf_op jit(solution)/shard_map/all_gather | solution.py:197
  2527.5 52.4 %all-gather.45.cloned.1.call-start = ((), (), s32[]{:S(2)}) async-start(), calls=%async_computation.15 | async-start | bytes 1310720 | tf_op jit(solution)/shard_map/all_gather | solution.py:197
  2528.4 70.8 %all-gather.61.cloned.1.call-start = ((), (), s32[]{:S(2)}) async-start(), calls=%async_computation.23 | async-start | bytes 1474560 | tf_op jit(solution)/shard_map/all_gather | solution.py:185
  2545.9 147.8 %all-reduce.51.cloned.1.call-start = ((), (), s32[]{:S(2)}) async-start(), calls=%async_computation.41 | async-start | bytes 3145728 | tf_op jit(solution)/shard_map/psum | solution.py:194
  2602.1 109.9 %all-gather.63.cloned.1.call-start = ((), (), s32[]{:S(2)}) async-start(), calls=%async_computation.24 | async-start | bytes 1310720 | tf_op jit(solution)/shard_map/all_gather | solution.py:197
  2697.5 52.2 %all-gather.47.cloned.1.call-start = ((), (), s32[]{:S(2)}) async-start(), calls=%async_computation.16 | async-start | bytes 1310720 | tf_op jit(solution)/shard_map/all_gather | solution.py:197
  2698.3 70.6 %all-gather.65.cloned.1.call-start = ((), (), s32[]{:S(2)}) async-start(), calls=%async_computation.25 | async-start | bytes 1474560 | tf_op jit(solution)/shard_map/all_gather | solution.py:185
  2716.0 147.6 %all-reduce.49.cloned.1.call-start = ((), (), s32[]{:S(2)}) async-start(), calls=%async_computation.40 | async-start | bytes 3145728 | tf_op jit(solution)/shard_map/psum | solution.py:194
  2772.0 109.9 %all-gather.67.cloned.1.call-start = ((), (), s32[]{:S(2)}) async-start(), calls=%async_computation.26 | async-start | bytes 1310720 | tf_op jit(solution)/shard_map/all_gather | solution.py:197
  2867.5 52.4 %all-gather.49.cloned.1.call-start = ((), (), s32[]{:S(2)}) async-start(), calls=%async_computation.17 | async-start | bytes 1310720 | tf_op jit(solution)/shard_map/all_gather | solution.py:197
  2868.3 70.7 %all-gather.69.cloned.1.call-start = ((), (), s32[]{:S(2)}) async-start(), calls=%async_computation.27 | async-start | bytes 1474560 | tf_op jit(solution)/shard_map/all_gather | solution.py:185
  2885.8 147.8 %all-reduce.47.cloned.1.call-start = ((), (), s32[]{:S(2)}) async-start(), calls=%async_computation.39 | async-start | bytes 3145728 | tf_op jit(solution)/shard_map/psum | solution.py:194
  2941.9 242.4 %reduce-scatter.20.cloned.1.call-start = ((), (), s32[]{:S(2)}) async-start(), calls=%async_computation.36 | async-start | bytes 9216000 | tf_op jit(solution)/shard_map/reduce_scatter | solution.py:347
  2947.5 257.6 %all-gather.51.cloned.1.call-start = ((), (), s32[]{:S(2)}) async-start(), calls=%async_computation.18 | async-start | bytes 1310720 | tf_op jit(solution)/shard_map/all_gather | solution.py:197
  3035.5 185.3 %all-gather.81.cloned.1.call-start = ((), (), s32[]{:S(2)}) async-start(), calls=%async_computation.35 | async-start | bytes 1310720 | tf_op jit(solution)/shard_map/all_gather | solution.py:197
  3038.8 201.0 %all-gather.71.cloned.1.call-start = ((), (), s32[]{:S(2)}) async-start(), calls=%async_computation.28 | async-start | bytes 1310720 | tf_op jit(solution)/shard_map/all_gather | solution.py:197
  (152 other events, 6714.7 us)
Sparse Core Ops, SparseCore 0:
  10.7 46.0 all-gather.30
  59.5 51.9 all-gather.34
  114.1 38.0 all-gather.38
  153.6 33.3 all-gather.82
  188.4 34.4 all-gather.32
  224.3 66.7 all-gather.36
  292.7 34.2 all-gather.40
  1842.7 24.6 reduce-scatter.21
  1871.5 150.6 reduce-scatter.15
  2025.6 148.3 reduce-scatter.11
  2194.8 21.6 reduce-scatter.17
  2219.6 21.6 reduce-scatter.13
  2252.0 90.0 all-reduce.54
  2362.4 16.7 all-gather.72
  2381.2 16.7 all-gather.54
  2405.6 18.3 all-gather.56
  2434.0 89.7 all-reduce.52
  2544.2 16.7 all-gather.74
  2563.1 16.7 all-gather.44
  2581.5 17.5 all-gather.60
  2603.9 89.7 all-reduce.50
  2714.1 16.7 all-gather.76
  2733.0 16.7 all-gather.46
  2751.3 17.5 all-gather.64
  2773.9 89.7 all-reduce.48
  2884.1 16.7 all-gather.78
  2903.1 16.7 all-gather.48
  2921.3 17.5 all-gather.68
  2943.9 89.7 all-reduce.46
  3037.8 146.4 reduce-scatter.19
  3186.4 16.9 all-gather.50
  3223.0 16.7 all-gather.70
  (6 shorter events, 96.5 us)
where the time goes:
time: 3260 us; the launch traced here: 3250 us
  blocking collectives  1380 us (42%)
  waiting for transfers between devices  1220 us (37%)
  local copies, waits for them, and re-layouts  234 us (7%)
  matrix products  225 us (7%)
  other arithmetic  170 us (5%)
    unnamed x2, blocking collectives  736 us
    psum x5, waiting for transfers between devices, newton_schulz(): gram_rows = lax.psum(partial_gram, 'dp')  449 us
    psum x6, blocking collectives, norm_forward(): lax.psum((local_terms[0], local_terms[1], local_terms[2]), ('dp', 'owner'))  253 us
    psum x5, blocking collectives, norm_backward(): lax.psum((jnp.sum(grad_out, axis=0), jnp.sum(grad_out * normed, axis=0)),...  202 us
    all_gather x15, waiting for transfers between devices, newton_schulz(): lax.all_gather(shortened(gram_rows), 'owner', axis=1, tiled=True)  192 us
    reduce_scatter x1, waiting for transfers between devices, per_device(): lax.psum_scatter(grad_stacks[0], 'dp', scatter_dimension=2, tiled=True)  150 us
    reduce_scatter x1, waiting for transfers between devices, per_device(): lax.psum_scatter(grad_stacks[3], 'dp', scatter_dimension=2, tiled=True)  145 us
    psum x2, blocking collectives, per_device(): lax.psum((jnp.sum(weight_img), local_loss, jnp.sum(residue, axis=0)), ('d...  81.4 us
  transfers between devices with their start and end apart: 39, of which 33 were waited for; matrix products, arithmetic and copies ran while one was open for 8% of the time, Pallas kernels for 0%

commit v1 on v0

v1 whole, which is shorter than its diff:
```python
import math

import jax
import jax.numpy as jnp
from jax import lax
from jax.sharding import PartitionSpec as P

LAYERS = 2
NS_STEPS = 5
STEP = 10


AXES = ("dp", "owner")
EPS = 1e-05
NS_A = 3.4445
NS_B = -4.775
NS_C = 2.0315
MOMENTUM = 0.9
LR_MATRIX = 0.5
DECAY_MATRIX = 0.01
BETA_ONE = 0.9
BETA_TWO = 0.999
ADAM_EPS = 1e-08
LR_HEAD = 0.2
DECAY_HEAD = 0.01
LR_VECTOR = 0.4


def contract_rows(left, right):
    return lax.dot_general(
        left, right, (((0,), (0,)), ((), ())), preferred_element_type=jnp.float32
    )


def contract_cols(left, right):
    return lax.dot_general(
        left, right, (((1,), (1,)), ((), ())), preferred_element_type=jnp.float32
    )


def silu_slope(values):
    sigmoid_part = jax.nn.sigmoid(values)
    return sigmoid_part * (1.0 + values * (1.0 - sigmoid_part))


def columns(values, count_img, side):
    chans = values.shape[1]
    grid = values.reshape(count_img, side, side, chans)
    padded = jnp.pad(grid, ((0, 0), (1, 1), (1, 1), (0, 0)))
    pieces = [
        padded[:, offset // 3 : offset // 3 + side, offset % 3 : offset % 3 + side, :]
        for offset in range(9)
    ]
    return jnp.concatenate(pieces, axis=3).reshape(count_img * side * side, 9 * chans)


def columns_back(grad_patches, count_img, side, chans):
    grid = grad_patches.reshape(count_img, side, side, 9, chans)
    summed = jnp.zeros((count_img, side + 2, side + 2, chans), jnp.float32)
    for offset in range(9):
        row_shift = offset // 3
        col_shift = offset % 3
        summed = summed + jnp.pad(
            grid[:, :, :, offset, :],
            ((0, 0), (row_shift, 2 - row_shift), (col_shift, 2 - col_shift), (0, 0)),
        )
    return summed[:, 1 : side + 1, 1 : side + 1, :].reshape(count_img * side * side, chans)


def norm_forward(hidden, norm_gain, norm_bias, mask_pix):
    local_terms = (
        jnp.sum(hidden * mask_pix, axis=0),
        jnp.sum(hidden * hidden * mask_pix, axis=0),
        jnp.sum(mask_pix),
    )
    first_sum, square_sum, total_count = all_sum(local_terms)
    centre = first_sum / total_count
    spread = square_sum / total_count - centre * centre
    inverse = lax.rsqrt(spread + EPS)
    normed = (hidden - centre) * inverse
    return (normed * norm_gain + norm_bias, normed, inverse, total_count)


def norm_backward(grad_out, normed, inverse, norm_gain, mask_pix, total_count):
    bias_grad, gain_grad = all_sum(
        (jnp.sum(grad_out, axis=0), jnp.sum(grad_out * normed, axis=0))
    )
    grad_in = (
        norm_gain * inverse * (grad_out - mask_pix * (bias_grad + normed * gain_grad) / total_count)
    )
    return (grad_in, gain_grad, bias_grad)


def layer_forward(
    inputs, weight_one, weight_two, weight_three, norm_gain, norm_bias, mask_pix, count_img, side
):
    narrow = weight_one.shape[1]
    inputs_low = inputs.astype(jnp.bfloat16)
    reduced = jnp.dot(inputs_low, weight_one, preferred_element_type=jnp.float32)
    first_out, first_norm, first_inv, total_count = norm_forward(
        reduced, norm_gain[:narrow], norm_bias[:narrow], mask_pix
    )
    first_act = jax.nn.silu(first_out).astype(jnp.bfloat16)
    patches = columns(first_act, count_img, side)
    spatial = jnp.dot(patches, weight_two, preferred_element_type=jnp.float32)
    second_out, second_norm, second_inv, unused_one = norm_forward(
        spatial, norm_gain[narrow : 2 * narrow], norm_bias[narrow : 2 * narrow], mask_pix
    )
    second_act = jax.nn.silu(second_out).astype(jnp.bfloat16)
    expanded = contract_cols(second_act, weight_three)
    third_out, third_norm, third_inv, unused_two = norm_forward(
        expanded, norm_gain[2 * narrow :], norm_bias[2 * narrow :], mask_pix
    )
    summed = inputs + third_out
    kept = (
        inputs_low,
        first_out,
        first_norm,
        first_inv,
        patches,
        second_out,
        second_norm,
        second_inv,
        second_act,
        third_norm,
        third_inv,
        summed,
        total_count,
    )
    return (jax.nn.silu(summed), kept)


def layer_backward(
    grad_out, kept, weight_one, weight_two, weight_three, norm_gain, mask_pix, count_img, side
):
    (
        inputs_low,
        first_out,
        first_norm,
        first_inv,
        patches,
        second_out,
        second_norm,
        second_inv,
        second_act,
        third_norm,
        third_inv,
        summed,
        total_count,
    ) = kept
    narrow = weight_one.shape[1]
    grad_sum = grad_out * silu_slope(summed)
    grad_third, gain_three, bias_three = norm_backward(
        grad_sum, third_norm, third_inv, norm_gain[2 * narrow :], mask_pix, total_count
    )
    grad_third = grad_third.astype(jnp.bfloat16)
    grad_w_three = contract_rows(grad_third, second_act)
    grad_second = jnp.dot(grad_third, weight_three, preferred_element_type=jnp.float32) * silu_slope(second_out)
    grad_spatial, gain_two, bias_two = norm_backward(
        grad_second, second_norm, second_inv, norm_gain[narrow : 2 * narrow], mask_pix, total_count
    )
    grad_spatial = grad_spatial.astype(jnp.bfloat16)
    grad_w_two = contract_rows(patches, grad_spatial)
    grad_patches = contract_cols(grad_spatial, weight_two)
    grad_first = columns_back(grad_patches, count_img, side, narrow) * silu_slope(first_out)
    grad_reduced, gain_one, bias_one = norm_backward(
        grad_first, first_norm, first_inv, norm_gain[:narrow], mask_pix, total_count
    )
    grad_reduced = grad_reduced.astype(jnp.bfloat16)
    grad_w_one = contract_rows(inputs_low, grad_reduced)
    grad_in = contract_cols(grad_reduced, weight_one) + grad_sum
    gain_grads = jnp.concatenate([gain_one, gain_two, gain_three])
    bias_grads = jnp.concatenate([bias_one, bias_two, bias_three])
    return (grad_in, (grad_w_one, grad_w_two, grad_w_three), gain_grads, bias_grads)


def all_sum(parts):
    shapes = [part.shape for part in parts]
    sizes = [math.prod(shape) for shape in shapes]
    flat = jnp.concatenate([part.reshape(-1) for part in parts])
    total = flat.shape[0]
    rows = -(-total // 1024) * 8
    flat = jnp.pad(flat, (0, rows * 128 - total)).reshape(rows, 128)
    copies = jnp.broadcast_to(flat[None], (device_count(), rows, 128))
    summed = jnp.sum(lax.all_to_all(copies, AXES, 0, 0, tiled=True), axis=0).reshape(-1)
    out, start = [], 0
    for shape, size in zip(shapes, sizes):
        out.append(summed[start : start + size].reshape(shape))
        start += size
    return out


def device_count():
    return lax.axis_size("dp") * lax.axis_size("owner")


def my_index():
    return lax.axis_index("dp") * lax.axis_size("owner") + lax.axis_index("owner")


def swap(values, bit):
    count = device_count()
    return lax.ppermute(values, AXES, [(src, src ^ (1 << bit)) for src in range(count)])


def halving_sum(blocks, order):
    count, rows, lanes = blocks.shape
    left = list(range(count.bit_length() - 2, -1, -1))
    values = blocks
    for bit in order:
        place = left.index(bit)
        values = values.reshape(2**place, 2, -1, rows, lanes)
        own = (my_index() >> bit) & 1
        kept = lax.dynamic_index_in_dim(values, own, 1, keepdims=False)
        sent = lax.dynamic_index_in_dim(values, 1 - own, 1, keepdims=False)
        values = kept + swap(sent, bit)
        left.pop(place)
    return values.reshape(rows, lanes)


def rotated_halving(blocks, cuts):
    count = blocks.shape[0]
    bits = list(range(1, count.bit_length() - 1))
    out, start = [], 0
    for number, rows in enumerate(cuts):
        turn = number % len(bits)
        order = [0] + bits[turn:] + bits[:turn]
        out.append(halving_sum(blocks[:, start : start + rows], order))
        start += rows
    return jnp.concatenate(out, axis=0)


def pack(parts):
    return jnp.concatenate([part.T.astype(jnp.bfloat16) for part in parts], axis=0)


def spread(gathered, start, rows):
    piece = gathered[:, :, start : start + rows]
    return piece.transpose(0, 2, 1, 3).reshape(piece.shape[0] * rows, -1)


def unspread(grad, dp_size, owner_size):
    rows, lanes = grad.shape[0] // dp_size, grad.shape[1] // owner_size
    grad = grad.astype(jnp.bfloat16).reshape(dp_size, rows, owner_size, lanes)
    return grad.transpose(0, 2, 1, 3).reshape(dp_size * owner_size, rows, lanes)


def newton_schulz(moments):
    dp_size, owner_size = lax.axis_size("dp"), lax.axis_size("owner")
    owner = lax.axis_index("owner")
    cols = [moment.shape[0] for moment in moments]
    lanes = moments[0].shape[1]
    low = jnp.concatenate([moment.astype(jnp.bfloat16) for moment in moments], axis=0)
    all_rows = lax.all_gather(low, "owner")
    all_rows = all_rows.transpose(1, 0, 2).reshape(low.shape[0], owner_size * lanes)
    pieces, start = [], 0
    for size in cols:
        pieces.append(all_rows[start : start + size])
        start += size
    side = owner_size * lanes
    pairs = [(i, j) for i in range(owner_size) for j in range(i, owner_size)]
    packed = []
    for piece in pieces:
        gram = contract_rows(piece, piece)
        blocks = [gram[i * lanes : (i + 1) * lanes, j * lanes : (j + 1) * lanes] for i, j in pairs]
        packed.append(jnp.concatenate(blocks, axis=0))
    rows = packed[0].shape[0] // owner_size
    stack = jnp.stack(packed + [jnp.zeros_like(packed[0])] * (dp_size - len(packed)))
    mine = lax.dynamic_slice_in_dim(stack, owner * rows, rows, axis=1)
    bits = [bit for bit in range(device_count().bit_length() - 1) if (1 << bit) >= owner_size]
    values = mine
    for bit in bits:
        place = dp_size.bit_length() - 1 - (len(bits) - bits.index(bit))
        own = (my_index() >> bit) & 1
        values = values.reshape(-1, 2, rows, lanes)
        kept = lax.dynamic_index_in_dim(values, own, 1, keepdims=False)
        sent = lax.dynamic_index_in_dim(values, 1 - own, 1, keepdims=False)
        values = kept + swap(sent, bit)
    whole = lax.all_gather(values[0], "owner", tiled=True)
    blocks = {}
    for number, (i, j) in enumerate(pairs):
        block = whole[number * lanes : (number + 1) * lanes]
        blocks[i, j] = block
        if i != j:
            blocks[j, i] = block.T
    gram = jnp.concatenate(
        [jnp.concatenate([blocks[i, j] for j in range(owner_size)], axis=1) for i in range(owner_size)],
        axis=0,
    )
    dot = lambda left, right: jnp.dot(left, right, precision=lax.Precision.HIGHEST)
    eye = jnp.eye(side, dtype=jnp.float32)
    factor = 1.0 / (jnp.sqrt(jnp.trace(gram)) + 1e-07)
    gram = gram * (factor * factor)
    product = None
    for iteration in range(NS_STEPS):
        square = dot(gram, gram)
        poly = NS_A * eye + NS_B * gram + NS_C * square
        if iteration < NS_STEPS - 1:
            gram = dot(dot(gram, poly), poly)
        product = poly if product is None else dot(product, poly)
    product = (product * factor).astype(jnp.bfloat16)
    own_rows = lax.dynamic_slice_in_dim(product, owner * lanes, lanes, axis=0)
    copies = jnp.broadcast_to(own_rows[None], (dp_size,) + own_rows.shape)
    products = lax.all_to_all(copies, "dp", 0, 0, tiled=True)
    return [contract_cols(piece, products[number]) for number, piece in enumerate(pieces)]


def adamw(weight, grad, first, second, rate, decay):
    first = BETA_ONE * first + (1.0 - BETA_ONE) * grad
    second = BETA_TWO * second + (1.0 - BETA_TWO) * grad * grad
    first_hat = first / (1.0 - BETA_ONE**STEP)
    second_hat = second / (1.0 - BETA_TWO**STEP)
    weight = weight - rate * (first_hat / (jnp.sqrt(second_hat) + ADAM_EPS) + decay * weight)
    return (weight, first, second)


def per_device(
    images,
    valid_count,
    labels,
    loss_weight,
    w_reduce,
    w_spatial,
    w_expand,
    mom_reduce,
    mom_spatial,
    mom_expand,
    head,
    head_m,
    head_v,
    norm_params,
    norm_m,
    norm_v,
    head_bias,
    bias_m,
    bias_v,
):
    count_img = images.shape[0]
    side = images.shape[1]
    wide = images.shape[3]
    pixels = side * side
    dp_size, owner_size = lax.axis_size("dp"), lax.axis_size("owner")
    rows_of = (w_reduce.shape[2], w_spatial.shape[2], w_expand.shape[2])
    starts = (0, rows_of[0], rows_of[0] + rows_of[1])
    weight_one, weight_two, weight_three = ([], [], [])
    for layer in range(LAYERS):
        gathered = lax.all_gather(pack((w_reduce[layer], w_spatial[layer], w_expand[layer])), AXES)
        gathered = gathered.reshape((dp_size, owner_size) + gathered.shape[1:])
        for kind, stack in enumerate((weight_one, weight_two, weight_three)):
            stack.append(spread(gathered, starts[kind], rows_of[kind]))
    classes = head.shape[0]
    class_slots = -(-classes // 16) * 16
    slack = class_slots - classes
    head_low = jnp.pad(head.astype(jnp.bfloat16), ((0, slack), (0, 0)))
    head_all = lax.all_gather(head_low, AXES)
    head_all = head_all.reshape(dp_size, owner_size * class_slots, head.shape[1])
    head_full = head_all.transpose(1, 0, 2).reshape(owner_size * class_slots, wide)
    slot_bias = jnp.pad(
        head_bias.reshape(owner_size, classes), ((0, 0), (0, slack)), constant_values=-1e30
    ).reshape(-1)
    slot_labels = (labels // classes) * class_slots + labels % classes
    valid = (jnp.arange(count_img, dtype=jnp.int32) < valid_count[0]).astype(jnp.float32)
    mask_pix = jnp.repeat(valid, pixels)[:, None]
    current = images.reshape(count_img * pixels, wide).astype(jnp.float32)
    kept_layers = []
    for layer in range(LAYERS):
        current, kept = layer_forward(
            current,
            weight_one[layer],
            weight_two[layer],
            weight_three[layer],
            norm_params[0, layer],
            norm_params[1, layer],
            mask_pix,
            count_img,
            side,
        )
        kept_layers.append(kept)
    pooled = jnp.mean(current.reshape(count_img, pixels, wide), axis=1)
    pooled_low = pooled.astype(jnp.bfloat16)
    logits = contract_cols(pooled_low, head_full) + slot_bias
    top_logit = jnp.max(logits, axis=1, keepdims=True)
    log_total = jnp.log(jnp.sum(jnp.exp(logits - top_logit), axis=1, keepdims=True)) + top_logit
    onehot = (slot_labels[:, None] == jnp.arange(logits.shape[1], dtype=jnp.int32)[None, :]).astype(
        jnp.float32
    )
    weight_img = valid * loss_weight.astype(jnp.float32)
    local_loss = jnp.sum(weight_img * (log_total[:, 0] - jnp.sum(logits * onehot, axis=1)))
    residue = weight_img[:, None] * (jnp.exp(logits - log_total) - onehot)
    weight_total, loss_sum, bias_raw = all_sum(
        (jnp.sum(weight_img), local_loss, jnp.sum(residue, axis=0))
    )
    grad_bias = bias_raw.reshape(owner_size, class_slots)[:, :classes].reshape(-1) / weight_total
    grad_low = (residue / weight_total).astype(jnp.bfloat16)
    grad_head = contract_rows(grad_low, pooled_low)
    grad_pooled = jnp.dot(grad_low, head_full, preferred_element_type=jnp.float32)
    grad_current = jnp.repeat(grad_pooled / pixels, pixels, axis=0)
    grads_one, grads_two, grads_three, gain_rows, bias_rows = ([], [], [], [], [])
    for layer in reversed(range(LAYERS)):
        grad_current, weight_grads, gain_grads, bias_grads = layer_backward(
            grad_current,
            kept_layers[layer],
            weight_one[layer],
            weight_two[layer],
            weight_three[layer],
            norm_params[0, layer],
            mask_pix,
            count_img,
            side,
        )
        grads_one.insert(0, weight_grads[0])
        grads_two.insert(0, weight_grads[1])
        grads_three.insert(0, weight_grads[2])
        gain_rows.insert(0, gain_grads)
        bias_rows.insert(0, bias_grads)
    norm_grad = jnp.stack([jnp.stack(gain_rows), jnp.stack(bias_rows)])
    head_blocks = grad_head.astype(jnp.bfloat16).reshape(
        owner_size, class_slots, dp_size, head.shape[1]
    )
    head_blocks = head_blocks.transpose(2, 0, 1, 3).reshape(
        dp_size * owner_size, class_slots, head.shape[1]
    )
    lanes = w_reduce.shape[1]
    halves = head.shape[1] // lanes if head.shape[1] % lanes == 0 else 0
    sums = []
    for layer in range(LAYERS):
        blocks = jnp.concatenate(
            [
                unspread(grad, dp_size, owner_size)
                for grad in (grads_one[layer], grads_two[layer], grads_three[layer])
            ],
            axis=1,
        )
        if layer == 0:
            third = blocks.shape[1] // 48 * 16
            cuts = (third, third, blocks.shape[1] - 2 * third)
            sums.append(rotated_halving(blocks, cuts).astype(jnp.float32))
        elif halves:
            extra = [head_blocks[:, :, i * lanes : (i + 1) * lanes] for i in range(halves)]
            blocks = jnp.concatenate([blocks] + extra, axis=1)
            total = lax.psum_scatter(blocks, AXES, scatter_dimension=0).astype(jnp.float32)
            height = sum(rows_of)
            sums.append(total[:height])
            head_sum = jnp.concatenate(
                [
                    total[height + i * class_slots : height + i * class_slots + classes]
                    for i in range(halves)
                ],
                axis=1,
            )
        else:
            sums.append(lax.psum_scatter(blocks, AXES, scatter_dimension=0).astype(jnp.float32))
            head_sum = lax.psum_scatter(head_blocks, AXES, scatter_dimension=0)
            head_sum = head_sum.astype(jnp.float32)[:classes]
    olds = (mom_reduce, mom_spatial, mom_expand)
    moments_t = [
        MOMENTUM * olds[kind][layer].T + sums[layer][starts[kind] : starts[kind] + rows_of[kind]]
        for layer in range(LAYERS)
        for kind in range(3)
    ]
    directions_t = newton_schulz(moments_t)
    moments, directions = (
        [
            jnp.stack([values[layer * 3 + kind].T for layer in range(LAYERS)])
            for kind in range(3)
        ]
        for values in (moments_t, directions_t)
    )
    masters = (w_reduce, w_spatial, w_expand)
    updated = tuple(
        (
            master * (1.0 - LR_MATRIX * DECAY_MATRIX) - LR_MATRIX * direction
            for master, direction in zip(masters, directions)
        )
    )
    new_head, new_head_m, new_head_v = adamw(
        head, head_sum, head_m, head_v, LR_HEAD, DECAY_HEAD
    )
    new_norm, new_norm_m, new_norm_v = adamw(norm_params, norm_grad, norm_m, norm_v, LR_VECTOR, 0.0)
    new_bias, new_bias_m, new_bias_v = adamw(head_bias, grad_bias, bias_m, bias_v, LR_VECTOR, 0.0)
    return (
        loss_sum,
        weight_total,
        updated[0],
        updated[1],
        updated[2],
        moments[0],
        moments[1],
        moments[2],
        new_head,
        new_head_m,
        new_head_v,
        new_norm,
        new_norm_m,
        new_norm_v,
        new_bias,
        new_bias_m,
        new_bias_v,
    )


def solution(mesh):
    return jax.shard_map(
        per_device,
        mesh=mesh,
        in_specs=(
            P(("dp", "owner"), None, None, None),
            P(("dp", "owner")),
            P(("dp", "owner")),
            P(("dp", "owner")),
            P(None, "owner", "dp"),
            P(None, "owner", "dp"),
            P(None, "owner", "dp"),
            P(None, "owner", "dp"),
            P(None, "owner", "dp"),
            P(None, "owner", "dp"),
            P("owner", "dp"),
            P("owner", "dp"),
            P("owner", "dp"),
            P(),
            P(),
            P(),
            P(),
            P(),
            P(),
        ),
        out_specs=(
            P(),
            P(),
            P(None, "owner", "dp"),
            P(None, "owner", "dp"),
            P(None, "owner", "dp"),
            P(None, "owner", "dp"),
            P(None, "owner", "dp"),
            P(None, "owner", "dp"),
            P("owner", "dp"),
            P("owner", "dp"),
            P("owner", "dp"),
            P(),
            P(),
            P(),
            P(),
            P(),
            P(),
        ),
        check_vma=False,
    )
```

time: 3260 us -> 1040 us (0.32)
  blocking collectives: 1380 us -> 21.4 us
  waiting for transfers between devices: 1220 us -> 213 us
  local copies, waits for them, and re-layouts: 234 us -> 353 us
  starting transfers between devices: 3.75 us -> 76.6 us
  matrix products: 225 us -> 191 us
    unnamed x2 -> x0, blocking collectives: 736 us -> none
    psum x13 -> x0, blocking collectives: 537 us -> none  [the longest x6 253 us: norm_forward(): lax.psum((local_terms[0], local_terms[1], local_terms[2]), ('dp', 'owner'))]
    psum x5 -> x0, waiting for transfers between devices: 449 us -> none  [newton_schulz(): gram_rows = lax.psum(partial_gram, 'dp')]
    reduce_scatter x5 -> x1, waiting for transfers between devices: 388 us -> 0.02 us  [per_device(): lax.psum_scatter(blocks, AXES, scatter_dimension=0).astype(jnp.float32)]
    all_gather x27 -> x4, waiting for transfers between devices: 378 us -> 85.2 us  [the longest x2 64.8 us: per_device(): lax.all_gather(pack((w_reduce[layer], w_spatial[layer], w_expand[layer]))...]
    all_gather x11 -> x1, blocking collectives: 110 us -> 7.28 us  [newton_schulz(): whole = lax.all_gather(values[0], 'owner', tiled=True)]
    ppermute x0 -> x18, waiting for transfers between devices: none -> 69.3 us  [swap(): lax.ppermute(values, AXES, [(src, src ^ 1 << bit) for src in range(count)])]
    dot_general x50 -> x23, matrix products: 131 us -> 68.3 us  [the longest x17 34.7 us: newton_schulz(): jnp.dot(left, right, precision=lax.Precision.HIGHEST)]
  transfers between devices with their start and end apart: 39 -> 36, of which waited for: 33 -> 22; matrix products, arithmetic and copies ran while one was open for 8% -> 43% of each run, Pallas kernels for 0% -> 0%
where the time goes in v1:
time: 1040 us; the launch traced here: 1030 us
  local copies, waits for them, and re-layouts  353 us (34%)
  waiting for transfers between devices  213 us (20%)
  matrix products  191 us (18%)
  other arithmetic  156 us (15%)
  starting transfers between devices  76.6 us (7%)
  blocking collectives  21.4 us (2%)
  between operations  18.7 us (2%)
    unnamed x362, local copies, waits for them, and re-layouts  71.9 us
    ppermute x18, waiting for transfers between devices, swap(): lax.ppermute(values, AXES, [(src, src ^ 1 << bit) for src in range(count)])  69.3 us
    all_gather x2, waiting for transfers between devices, per_device(): lax.all_gather(pack((w_reduce[layer], w_spatial[layer], w_expand[layer]))...  64.8 us
    dot_general x12, matrix products, contract_cols(): lax.dot_general(left, right, (((1,), (1,)), ((), ())), preferred_element_...  62 us
    dot_general x13, matrix products, contract_rows(): lax.dot_general(left, right, (((0,), (0,)), ((), ())), preferred_element_...  56.3 us
    all_to_all x12, starting transfers between devices, all_sum(): lax.all_to_all(copies, AXES, 0, 0, tiled=True)  52.1 us
    concatenate x18, local copies, waits for them, and re-layouts, columns(): jnp.concatenate(pieces, axis=3).reshape(count_img * side * side, 9 * chans)  51.3 us
    all_to_all x12, waiting for transfers between devices, all_sum(): lax.all_to_all(copies, AXES, 0, 0, tiled=True)  45.8 us
  transfers between devices with their start and end apart: 36, of which 22 were waited for; matrix products, arithmetic and copies ran while one was open for 43% of the time, Pallas kernels for 0%

profile of v1, /device:TPU:0, one launch (start us, length us, event | category | flops | bytes accessed | tf_op | source)
XLA Modules:
  0.0 1029.9 jit_solution(976411005618749786)
XLA Ops:
  20.5 7.9 reshape.653
  29.0 64.7 %all-gather.10.cloned.1.call-done = bf16[34816,128]{1,0:T(8,128)(2,1)} async-done(((bf16[1088,128]{1,0:T(8,128)(2,1)}), bf16[34816,128]{1,0:T(8,128)(2,1)}) %all-gather.10.cloned.1.call-update) | async-done | bytes 8912912 | tf_op jit(solution)/shard_map/all_gather | solution.py:347
  130.4 9.3 pad_slice_fusion.8
  198.6 9.3 multiply_reduce_fusion.5
  222.3 7.8 all-to-all-done.2
  266.6 9.0 pad_slice_fusion
  334.4 9.3 multiply_reduce_fusion.3
  355.5 11.2 %all-to-all-done.5 = f32[32,40,128]{2,1,0:T(8,128)S(1)} async-done(((f32[32,40,128]{2,1,0:T(8,128)}), f32[32,40,128]{2,1,0:T(8,128)S(1)}, u32[]{:S(2)}, u32[]{:S(2)}) %all-to-all-start.5) | async-done | bytes 655392 | tf_op jit(solution)/shard_map/all_to_all | solution.py:185
  368.6 12.2 %fusion = f32[1176,2048]{1,0:T(8,128)} fusion(f32[1176,2048]{1,0:T(8,128)} %copy-done, f32[2048]{0:T(1024)S(1)} %bitcast.809, f32[2048]{0:T(1024)S(1)} %bitcast.805, f32[2048]{0:T(1024)S(1)} %get-tuple-element.251, f32[1176,2048]{1,0:T(8,128)} %get-tuple-element.271, f32[2048]{0:T(1024)S(1)} %fusion.76), kind=kLoop, calls=%fused_computation.7 | loop fusion | flops 21676032 | bytes 28934144 | tf_op jit(solution)/shard_map/jit(silu)/mul | solution.py:130
  380.7 8.9 reshape.677
  400.8 14.1 %all_to_all.70 = f32[32,16,128]{2,1,0:T(8,128)S(1)} all-to-all(f32[32,16,128]{2,1,0:T(8,128)S(1)} %broadcast_in_dim.61), channel_id=1, replica_groups=mesh['dp'=8,'owner'=4] {'dp','owner'}, dimensions={0} | all-to-all | bytes 524288 | tf_op jit(solution)/shard_map/all_to_all | solution.py:185
  425.0 9.1 reshape.685
  434.1 15.4 %fusion.102 = (f32[2048]{0:T(1024)S(1)}, f32[2048]{0:T(1024)S(1)}, f32[1176,2048]{1,0:T(8,128)}) fusion(f32[2048]{0:T(1024)S(1)} %get-tuple-element.251, f32[1176,2048]{1,0:T(8,128)} %get-tuple-element.271, f32[2048]{0:T(1024)S(1)} %fusion.76, f32[1176,2048]{1,0:T(8,128)} %reshape.685, f32[1176,2048]{1,0:T(8,128)} %copy-done, f32[2048]{0:T(1024)S(1)} %bitcast.810, ...), kind=kLoop, calls=%fused_computation.486 | loop fusion | flops 38531072 | bytes 38584320 | tf_op jit(solution)/shard_map/reduce_sum | solution.py:86
  452.9 8.1 reshape.737
  468.6 9.3 multiply_convert_fusion.1
  512.4 12.7 %fusion.10 = f32[24,7,7,9,512]{4,0,3,2,1:T(8,128)} fusion(bf16[9,512,512,1,1]{2,1,0,3,4:T(8,128)(2,1)} %reshape.737, bf16[24,7,7,512,1]{3,2,1,0,4:T(8,128)(2,1)} %bitcast.794), kind=kOutput, calls=%fused_computation.44 | convolution fusion | flops 5549064192 | bytes 27598848 | tf_op jit(solution)/shard_map/dot_general | solution.py:36
  525.1 13.4 %slice_bitcast_fusion.17 = (f32[24,7,7,512]{3,0,2,1:T(8,128)}, f32[24,7,7,512]{3,0,2,1:T(8,128)S(1)}, f32[24,7,7,512]{3,0,2,1:T(8,128)S(1)}, f32[24,7,7,512]{3,0...) fusion(f32[24,7,7,9,512]{4,0,3,2,1:T(8,128)} %fusion.10), kind=kLoop, calls=%fused_computation.87 | loop fusion | bytes 43352064 | tf_op jit(solution)/shard_map/squeeze | solution.py:64
  567.8 11.1 %convolution_convert_fusion = bf16[4608,512]{1,0:T(8,128)(2,1)} fusion(bf16[1176,4608]{1,0:T(8,128)(2,1)} %copy-done.67, bf16[1176,512]{1,0:T(8,128)(2,1)} %multiply_convert_fusion.4), kind=kOutput, calls=%fused_computation.34 | convolution fusion | flops 5551423488 | bytes 16760832 | tf_op jit(solution)/shard_map/dot_general | solution.py:30
  596.6 8.2 convolution_convert_fusion.4
  621.7 15.7 %fusion.101 = (f32[2048]{0:T(1024)S(1)}, f32[2048]{0:T(1024)S(1)}, f32[1176,2048]{1,0:T(8,128)}) fusion(f32[2048]{0:T(1024)S(1)} %copy-done.72, f32[1176,2048]{1,0:T(8,128)} %get-tuple-element.268, f32[2048]{0:T(1024)S(1)} %copy-done.70, f32[2048]{0:T(1024)S(1)} %bitcast.835, f32[2048]{0:T(1024)S(1)} %bitcast.813, bf16[1176,2048]{1,0:T(8,128)(2,1)} %reshape.653, ...), kind=kOutput, calls=%fused_computation.485 | convolution fusion | flops 2509598720 | bytes 37068800 | tf_op jit(solution)/shard_map/dot_general | solution.py:36
  644.6 8.1 reshape.739
  652.7 12.4 %all-to-all-done.10 = f32[32,32,128]{2,1,0:T(8,128)S(1)} async-done(((f32[32,32,128]{2,1,0:T(8,128)}), f32[32,32,128]{2,1,0:T(8,128)S(1)}, u32[]{:S(2)}, u32[]{:S(2)}) %all-to-all-start.10) | async-done | bytes 524320 | tf_op jit(solution)/shard_map/all_to_all | solution.py:185
  665.2 9.5 multiply_convert_fusion
  700.6 10.3 %convolution_convert_fusion.1 = bf16[4608,512]{1,0:T(8,128)(2,1)} fusion(bf16[1176,4608]{1,0:T(8,128)(2,1)} %copy-done.66, bf16[1176,512]{1,0:T(8,128)(2,1)S(1)} %multiply_convert_fusion.2), kind=kOutput, calls=%fused_computation.35 | convolution fusion | flops 5551423488 | bytes 16760832 | tf_op jit(solution)/shard_map/dot_general | solution.py:30
  711.0 7.8 reshape.690
  724.7 10.8 %fusion.8 = f32[24,7,7,9,512]{4,0,3,2,1:T(8,128)} fusion(bf16[9,512,512,1,1]{2,1,0,3,4:T(8,128)(2,1)S(1)} %bitcast.763, bf16[24,7,7,512,1]{3,2,1,0,4:T(8,128)(2,1)S(1)} %bitcast.793), kind=kOutput, calls=%fused_computation.42 | convolution fusion | flops 5549064192 | bytes 27598848 | tf_op jit(solution)/shard_map/dot_general | solution.py:36
  735.4 12.7 %slice_bitcast_fusion.8 = (f32[24,7,7,512]{3,0,2,1:T(8,128)}, f32[24,7,7,512]{3,0,2,1:T(8,128)S(1)}, f32[24,7,7,512]{3,0,2,1:T(8,128)S(1)}, f32[24,7,7,512]{3,0,...) fusion(f32[24,7,7,9,512]{4,0,3,2,1:T(8,128)} %fusion.8), kind=kLoop, calls=%fused_computation.72 | loop fusion | bytes 43352064 | tf_op jit(solution)/shard_map/squeeze | solution.py:64
  813.8 14.0 %collective-permute-done.11 = bf16[2,4,384,128]{3,2,1,0:T(8,128)(2,1)S(1)} collective-permute-done((bf16[2,4,384,128]{3,2,1,0:T(8,128)(2,1)S(1)}, bf16[2,4,384,128]{3,2,1,0:T(8,128)(2,1)S(1)}, u32[]{:S(2)}, u32[]{:S(2)}) %collective-permute-start.11) | collective-permute-done | bytes 786464 | tf_op jit(solution)/shard_map/ppermute | solution.py:203
  831.8 16.1 %collective-permute-done.12 = bf16[1,4,384,128]{3,2,1,0:T(8,128)(2,1)S(1)} collective-permute-done((bf16[1,4,384,128]{3,2,1,0:T(8,128)(2,1)S(1)}, bf16[1,4,384,128]{3,2,1,0:T(8,128)(2,1)S(1)}, u32[]{:S(2)}, u32[]{:S(2)}) %collective-permute-start.12) | collective-permute-done | bytes 393248 | tf_op jit(solution)/shard_map/ppermute | solution.py:203
  871.5 20.4 %all-gather.16.cloned.1.call-done = bf16[8704,128]{1,0:T(8,128)(2,1)} async-done(((bf16[2176,128]{1,0:T(8,128)(2,1)}), bf16[8704,128]{1,0:T(8,128)(2,1)}) %all-gather.16.cloned.1.call-update) | async-done | bytes 2228240 | tf_op jit(solution)/shard_map/all_gather | solution.py:254
  903.0 14.6 %collective-permute-done.15 = f32[4,320,128]{2,1,0:T(8,128)S(1)} collective-permute-done((f32[4,320,128]{2,1,0:T(8,128)S(1)}, f32[4,320,128]{2,1,0:T(8,128)S(1)}, u32[]{:S(2)}, u32[]{:S(2)}) %collective-permute-start.15) | collective-permute-done | bytes 655392 | tf_op jit(solution)/shard_map/ppermute | solution.py:203
  1004.5 12.9 %all-to-all-done.13 = bf16[8,128,512]{2,1,0:T(8,128)(2,1)S(1)} async-done(((bf16[8,128,512]{2,1,0:T(8,128)(2,1)}), bf16[8,128,512]{2,1,0:T(8,128)(2,1)S(1)}, u32[]{:S(2)}, u32[]{:S(2)}) %all-to-all-start.13) | async-done | bytes 1048608 | tf_op jit(solution)/shard_map/all_to_all | solution.py:304
  (725 shorter events, 595.2 us)
Async XLA Ops:
  7.2 86.6 %all-gather.10.cloned.1.call-start = ((), (), s32[]{:S(2)}) async-start(), calls=%async_computation.16 | async-start | bytes 9191424 | tf_op jit(solution)/shard_map/all_gather | solution.py:347
  11.3 200.9 %all-gather.12.cloned.1.call-start = ((), (), s32[]{:S(2)}) async-start(), calls=%async_computation.17 | async-start | bytes 9191424 | tf_op jit(solution)/shard_map/all_gather | solution.py:347
  109.1 13.9 %all-to-all-start = ((f32[32,16,128]{2,1,0:T(8,128)}), f32[32,16,128]{2,1,0:T(8,128)S(1)}, u32[]{:S(2)}, u32[]{:S(2)}) async-start(f32[32,16,128]{2,1,0:T(8,128)} %broadcast_in_dim.49), calls=%async_computation | async-start | bytes 524288 | tf_op jit(solution)/shard_map/all_to_all | solution.py:185
  181.6 14.5 %all-to-all-start.1 = ((f32[32,16,128]{2,1,0:T(8,128)}), f32[32,16,128]{2,1,0:T(8,128)S(1)}, u32[]{:S(2)}, u32[]{:S(2)}) async-start(f32[32,16,128]{2,1,0:T(8,128)} %broadcast_in_dim.51), calls=%async_computation.1 | async-start | bytes 524288 | tf_op jit(solution)/shard_map/all_to_all | solution.py:185
  209.4 20.7 %all-to-all-start.2 = ((f32[32,40,128]{2,1,0:T(8,128)}), f32[32,40,128]{2,1,0:T(8,128)S(1)}, u32[]{:S(2)}, u32[]{:S(2)}) async-start(f32[32,40,128]{2,1,0:T(8,128)} %broadcast_in_dim.53), calls=%async_computation.2 | async-start | bytes 1310720 | tf_op jit(solution)/shard_map/all_to_all | solution.py:185
  244.9 14.0 %all-to-all-start.3 = ((f32[32,16,128]{2,1,0:T(8,128)}), f32[32,16,128]{2,1,0:T(8,128)S(1)}, u32[]{:S(2)}, u32[]{:S(2)}) async-start(f32[32,16,128]{2,1,0:T(8,128)} %broadcast_in_dim.55), calls=%async_computation.3 | async-start | bytes 524288 | tf_op jit(solution)/shard_map/all_to_all | solution.py:185
  248.4 100.6 %all-gather.14.cloned.1.call-start = ((), (), s32[]{:S(2)}) async-start(), calls=%async_computation.18 | async-start | bytes 4325376 | tf_op jit(solution)/shard_map/all_gather | solution.py:355
  316.8 15.6 %all-to-all-start.4 = ((f32[32,16,128]{2,1,0:T(8,128)}), f32[32,16,128]{2,1,0:T(8,128)S(1)}, u32[]{:S(2)}, u32[]{:S(2)}) async-start(f32[32,16,128]{2,1,0:T(8,128)} %broadcast_in_dim.57), calls=%async_computation.4 | async-start | bytes 524288 | tf_op jit(solution)/shard_map/all_to_all | solution.py:185
  345.2 21.4 %all-to-all-start.5 = ((f32[32,40,128]{2,1,0:T(8,128)}), f32[32,40,128]{2,1,0:T(8,128)S(1)}, u32[]{:S(2)}, u32[]{:S(2)}) async-start(f32[32,40,128]{2,1,0:T(8,128)} %broadcast_in_dim.59), calls=%async_computation.5 | async-start | bytes 1310720 | tf_op jit(solution)/shard_map/all_to_all | solution.py:185
  450.3 18.2 %all-to-all-start.7 = ((f32[32,32,128]{2,1,0:T(8,128)}), f32[32,32,128]{2,1,0:T(8,128)S(1)}, u32[]{:S(2)}, u32[]{:S(2)}) async-start(f32[32,32,128]{2,1,0:T(8,128)} %broadcast_in_dim.63), calls=%async_computation.7 | async-start | bytes 1048576 | tf_op jit(solution)/shard_map/all_to_all | solution.py:185
  483.9 20.6 %all-to-all-start.8 = ((f32[32,8,128]{2,1,0:T(8,128)}), f32[32,8,128]{2,1,0:T(8,128)S(1)}, u32[]{:S(2)}, u32[]{:S(2)}) async-start(f32[32,8,128]{2,1,0:T(8,128)} %broadcast_in_dim.64), calls=%async_computation.8 | async-start | bytes 262144 | tf_op jit(solution)/shard_map/all_to_all | solution.py:185
  561.8 30.5 %all-to-all-start.9 = ((f32[32,8,128]{2,1,0:T(8,128)}), f32[32,8,128]{2,1,0:T(8,128)S(1)}, u32[]{:S(2)}, u32[]{:S(2)}) async-start(f32[32,8,128]{2,1,0:T(8,128)} %broadcast_in_dim.65), calls=%async_computation.9 | async-start | bytes 262144 | tf_op jit(solution)/shard_map/all_to_all | solution.py:185
  567.8 300.8 %reduce-scatter.2.cloned.1.call-start = ((), (), s32[]{:S(2)}) async-start(), calls=%async_computation.15 | async-start | bytes 13516800 | tf_op jit(solution)/shard_map/reduce_scatter | solution.py:441
  638.2 26.8 %all-to-all-start.10 = ((f32[32,32,128]{2,1,0:T(8,128)}), f32[32,32,128]{2,1,0:T(8,128)S(1)}, u32[]{:S(2)}, u32[]{:S(2)}) async-start(f32[32,32,128]{2,1,0:T(8,128)} %broadcast_in_dim.66), calls=%async_computation.10 | async-start | bytes 1048576 | tf_op jit(solution)/shard_map/all_to_all | solution.py:185
  680.7 15.7 %all-to-all-start.11 = ((f32[32,8,128]{2,1,0:T(8,128)}), f32[32,8,128]{2,1,0:T(8,128)S(1)}, u32[]{:S(2)}, u32[]{:S(2)}) async-start(f32[32,8,128]{2,1,0:T(8,128)} %broadcast_in_dim.67), calls=%async_computation.11 | async-start | bytes 262144 | tf_op jit(solution)/shard_map/all_to_all | solution.py:185
  770.6 14.1 %all-to-all-start.12 = ((f32[32,8,128]{2,1,0:T(8,128)}), f32[32,8,128]{2,1,0:T(8,128)S(1)}, u32[]{:S(2)}, u32[]{:S(2)}) async-start(f32[32,8,128]{2,1,0:T(8,128)} %broadcast_in_dim.68), calls=%async_computation.12 | async-start | bytes 262144 | tf_op jit(solution)/shard_map/all_to_all | solution.py:185
  776.5 115.4 %all-gather.16.cloned.1.call-start = ((), (), s32[]{:S(2)}) async-start(), calls=%async_computation.19 | async-start | bytes 2785280 | tf_op jit(solution)/shard_map/all_gather | solution.py:254
  781.7 24.6 %collective-permute-start.10 = (bf16[16,1,384,128]{3,2,0,1:T(8,128)(2,1)}, bf16[16,1,384,128]{3,2,0,1:T(8,128)(2,1)}, u32[]{:S(2)}, u32[]{:S(2)}) collective-permute-start(bf16[16,1,384,128]{3,2,0,1:T(8,128)(2,1)} %dynamic-slice_bitcast_fusion), channel_id=1, source_target_pairs={{0,1},{1,0},{2,3},{3,2},{4,5},{5,4},{6,7},{7,6},{8,9},{9,8},{10,11... | collective-permute-start | bytes 4718600 | tf_op jit(solution)/shard_map/ppermute | solution.py:203
  802.2 8.8 collective-permute-start.5
  808.1 19.7 %collective-permute-start.11 = (bf16[2,4,384,128]{3,2,1,0:T(8,128)(2,1)S(1)}, bf16[2,4,384,128]{3,2,1,0:T(8,128)(2,1)S(1)}, u32[]{:S(2)}, u32[]{:S(2)}) collective-permute-start(bf16[2,4,384,128]{3,2,1,0:T(8,128)(2,1)S(1)} %dynamic-slice_bitcast_fusion.3), channel_id=1, source_target_pairs={{0,8},{1,9},{2,10},{3,11},{4,12},{5,13},{6,14},{7,15},{8,0},{9,1},... | collective-permute-start | bytes 2359304 | tf_op jit(solution)/shard_map/ppermute | solution.py:203
  810.6 18.3 %collective-permute-start.1 = (bf16[8,1,352,128]{3,2,0,1:T(8,128)(2,1)S(1)}, bf16[8,1,352,128]{3,2,0,1:T(8,128)(2,1)S(1)}, u32[]{:S(2)}, u32[]{:S(2)}) collective-permute-start(bf16[8,1,352,128]{3,2,0,1:T(8,128)(2,1)S(1)} %dynamic-slice_bitcast_fusion.5), channel_id=1, source_target_pairs={{0,2},{1,3},{2,0},{3,1},{4,6},{5,7},{6,4},{7,5},{8,10},{9,11},{10,... | collective-permute-start | bytes 2162696 | tf_op jit(solution)/shard_map/ppermute | solution.py:203
  812.7 17.8 %collective-permute-start.6 = (bf16[4,2,352,128]{3,2,1,0:T(8,128)(2,1)S(1)}, bf16[4,2,352,128]{3,2,1,0:T(8,128)(2,1)S(1)}, u32[]{:S(2)}, u32[]{:S(2)}) collective-permute-start(bf16[4,2,352,128]{3,2,1,0:T(8,128)(2,1)S(1)} %dynamic-slice_bitcast_fusion.4), channel_id=1, source_target_pairs={{0,4},{1,5},{2,6},{3,7},{4,0},{5,1},{6,2},{7,3},{8,12},{9,13},{10,... | collective-permute-start | bytes 2162696 | tf_op jit(solution)/shard_map/ppermute | solution.py:203
  828.0 19.9 %collective-permute-start.12 = (bf16[1,4,384,128]{3,2,1,0:T(8,128)(2,1)S(1)}, bf16[1,4,384,128]{3,2,1,0:T(8,128)(2,1)S(1)}, u32[]{:S(2)}, u32[]{:S(2)}) collective-permute-start(bf16[1,4,384,128]{3,2,1,0:T(8,128)(2,1)S(1)} %constant_dynamic-slice_fusion.3), channel_id=1, source_target_pairs={{0,16},{1,17},{2,18},{3,19},{4,20},{5,21},{6,22},{7,23},{8,24},{9,... | collective-permute-start | bytes 1179656 | tf_op jit(solution)/shard_map/ppermute | solution.py:203
  829.0 19.4 %collective-permute-start.2 = (bf16[4,1,352,128]{3,2,0,1:T(8,128)(2,1)S(1)}, bf16[4,1,352,128]{3,2,0,1:T(8,128)(2,1)S(1)}, u32[]{:S(2)}, u32[]{:S(2)}) collective-permute-start(bf16[4,1,352,128]{3,2,0,1:T(8,128)(2,1)S(1)} %dynamic-slice_bitcast_fusion.8), channel_id=1, source_target_pairs={{0,4},{1,5},{2,6},{3,7},{4,0},{5,1},{6,2},{7,3},{8,12},{9,13},{10,... | collective-permute-start | bytes 1081352 | tf_op jit(solution)/shard_map/ppermute | solution.py:203
  830.7 17.9 %collective-permute-start.7 = (bf16[2,2,352,128]{3,2,1,0:T(8,128)(2,1)S(1)}, bf16[2,2,352,128]{3,2,1,0:T(8,128)(2,1)S(1)}, u32[]{:S(2)}, u32[]{:S(2)}) collective-permute-start(bf16[2,2,352,128]{3,2,1,0:T(8,128)(2,1)S(1)} %dynamic-slice_bitcast_fusion.7), channel_id=1, source_target_pairs={{0,8},{1,9},{2,10},{3,11},{4,12},{5,13},{6,14},{7,15},{8,0},{9,1},... | collective-permute-start | bytes 1081352 | tf_op jit(solution)/shard_map/ppermute | solution.py:203
  848.5 9.2 collective-permute-start.3
  848.7 11.9 %collective-permute-start.8 = (bf16[1,2,352,128]{3,2,1,0:T(8,128)(2,1)S(1)}, bf16[1,2,352,128]{3,2,1,0:T(8,128)(2,1)S(1)}, u32[]{:S(2)}, u32[]{:S(2)}) collective-permute-start(bf16[1,2,352,128]{3,2,1,0:T(8,128)(2,1)S(1)} %constant_dynamic-slice_fusion.5), channel_id=1, source_target_pairs={{0,16},{1,17},{2,18},{3,19},{4,20},{5,21},{6,22},{7,23},{8,24},{9,... | collective-permute-start | bytes 540680 | tf_op jit(solution)/shard_map/ppermute | solution.py:203
  854.7 12.0 %collective-permute-start.14 = (bf16[1,1,384,128]{3,2,1,0:T(8,128)(2,1)S(1)}, bf16[1,1,384,128]{3,2,1,0:T(8,128)(2,1)S(1)}, u32[]{:S(2)}, u32[]{:S(2)}) collective-permute-start(bf16[1,1,384,128]{3,2,1,0:T(8,128)(2,1)S(1)} %constant_dynamic-slice_fusion.2), channel_id=1, source_target_pairs={{0,4},{1,5},{2,6},{3,7},{4,0},{5,1},{6,2},{7,3},{8,12},{9,13},{10,... | collective-permute-start | bytes 294920 | tf_op jit(solution)/shard_map/ppermute | solution.py:203
  900.7 16.9 %collective-permute-start.15 = (f32[4,320,128]{2,1,0:T(8,128)S(1)}, f32[4,320,128]{2,1,0:T(8,128)S(1)}, u32[]{:S(2)}, u32[]{:S(2)}) collective-permute-start(f32[4,320,128]{2,1,0:T(8,128)S(1)} %dynamic-slice_bitcast_fusion.6), channel_id=1, source_target_pairs={{0,4},{1,5},{2,6},{3,7},{4,0},{5,1},{6,2},{7,3},{8,12},{9,13},{10,... | collective-permute-start | bytes 1966088 | tf_op jit(solution)/shard_map/ppermute | solution.py:203
  917.7 9.1 collective-permute-start.16
  926.9 9.1 collective-permute-start.17
  985.5 31.9 %all-to-all-start.13 = ((bf16[8,128,512]{2,1,0:T(8,128)(2,1)}), bf16[8,128,512]{2,1,0:T(8,128)(2,1)S(1)}, u32[]{:S(2)}, u32[]{:S(2)}) async-start(bf16[8,128,512]{2,1,0:T(8,128)(2,1)} %broadcast_in_dim.69), calls=%async_computation.14 | async-start | bytes 2097152 | tf_op jit(solution)/shard_map/all_to_all | solution.py:304
  (137 other events, 1162.5 us)
Sparse Core Ops, SparseCore 0:
  11.5 82.2 all-gather.9
  97.1 80.8 all-gather.11
  252.6 63.2 all-gather.13
  619.9 163.5 reduce-scatter.1
  870.8 21.1 all-gather.15

commit v2 on v1

v2 whole, which is shorter than its diff:
```python
import functools
import math

import jax
import jax.numpy as jnp
from jax import lax
from jax.experimental import pallas as pl
from jax.experimental.pallas import tpu as pltpu
from jax.sharding import PartitionSpec as P

LAYERS = 2
NS_STEPS = 5
STEP = 10

AXES = ("dp", "owner")
EPS = 1e-05
NS_A = 3.4445
NS_B = -4.775
NS_C = 2.0315
MOMENTUM = 0.9
LR_MATRIX = 0.5
DECAY_MATRIX = 0.01
BETA_ONE = 0.9
BETA_TWO = 0.999
ADAM_EPS = 1e-08
LR_HEAD = 0.2
DECAY_HEAD = 0.01
LR_VECTOR = 0.4
LANES = 128
SLOT = 8
F32 = jnp.float32
BF16 = jnp.bfloat16


def device_count():
    return lax.axis_size("dp") * lax.axis_size("owner")


def my_index():
    return lax.axis_index("dp") * lax.axis_size("owner") + lax.axis_index("owner")


def exchange(copies):
    return lax.all_to_all(copies, AXES, 0, 0, tiled=True)


def swap(values, bit):
    count = device_count()
    return lax.ppermute(values, AXES, [(src, src ^ (1 << bit)) for src in range(count)])


def halving_sum(blocks, left, order):
    count, rows, lanes = blocks.shape
    left = list(left)
    values = blocks
    for bit in order:
        place = left.index(bit)
        values = values.reshape(2**place, 2, -1, rows, lanes)
        own = (my_index() >> bit) & 1
        kept = lax.dynamic_index_in_dim(values, own, 1, keepdims=False)
        sent = lax.dynamic_index_in_dim(values, 1 - own, 1, keepdims=False)
        values = kept + swap(sent, bit)
        left.pop(place)
    return values.reshape(rows, lanes)


def bits_of(dp_size, owner_size):
    low = owner_size.bit_length() - 1
    high = dp_size.bit_length() - 1
    return list(range(low - 1, -1, -1)) + list(range(low + high - 1, low - 1, -1))


def sigmoid(values):
    return 1.0 / (1.0 + jnp.exp(-values))


def silu(values):
    return values * sigmoid(values)


def silu_slope(values):
    part = sigmoid(values)
    return part * (1.0 + values * (1.0 - part))


def total_of(parts_ref):
    return jnp.sum(parts_ref[...], axis=0)


def row_of(table, start, width):
    count = width // LANES
    return jnp.concatenate([table[start + i : start + i + 1, :] for i in range(count)], axis=1)


def send_rows(out_ref, rows):
    place = 0
    for row in rows:
        for i in range(row.shape[1] // LANES):
            piece = row[:, i * LANES : (i + 1) * LANES]
            out_ref[:, place, :] = jnp.broadcast_to(piece, (out_ref.shape[0], LANES))
            place += 1


def fold_rows(values):
    return jnp.sum(values.reshape(values.shape[0] // 8, 8, values.shape[1]), axis=0)


def norm_of(parts_ref, count, width):
    table = total_of(parts_ref)
    centre = row_of(table, 0, width) / count
    spread = row_of(table, width // LANES, width) / count - centre * centre
    return centre, lax.rsqrt(spread + EPS)


def keep_norm(stat_ref, centre, inverse):
    stat_ref[0:1, :] = centre
    stat_ref[1:2, :] = inverse


class Weights:
    def __init__(self, array, start, rows):
        self.array, self.start, self.rows = array, start, rows
        self.blocks, self.owners = array.shape[0], array.shape[1]
        self.depth = self.blocks * rows
        self.width = self.owners * LANES

    def scratch(self):
        return [
            pltpu.VMEM((self.depth, self.width), BF16),
            pltpu.SemaphoreType.DMA((self.blocks * self.owners,)),
        ]

    def copies(self, ref, buffer, sems):
        return [
            pltpu.make_async_copy(
                ref.at[d, o, pl.ds(self.start, self.rows)],
                buffer.at[pl.ds(d * self.rows, self.rows), pl.ds(o * LANES, LANES)],
                sems.at[d * self.owners + o],
            )
            for d in range(self.blocks)
            for o in range(self.owners)
        ]


def whole(shape):
    return pl.BlockSpec(shape, lambda *ids: (0,) * len(shape), pipeline_mode=pl.Buffered(1))


def strip(rows, width):
    return pl.BlockSpec((rows, width), lambda i: (i, 0))


ANYWHERE = pl.BlockSpec(memory_space=pl.ANY)
SCALAR = pl.BlockSpec(memory_space=pltpu.SMEM)


def launch(kernel, name, grid, operands, specs, outs, out_specs, scratch, flops):
    moved = sum(math.prod(a.shape) * a.dtype.itemsize for a in jax.tree.leaves((operands, outs)))
    return pl.pallas_call(
        kernel,
        name=name,
        grid=grid,
        in_specs=specs,
        out_specs=out_specs,
        out_shape=outs,
        scratch_shapes=scratch,
        cost_estimate=pl.CostEstimate(flops=flops, bytes_accessed=min(moved, 2**25), transcendentals=0),
        compiler_params=pltpu.CompilerParams(
            vmem_limit_bytes=60 * 2**20, dimension_semantics=("arbitrary",) * len(grid)
        ),
    )(*operands)


def out_of(shape, dtype):
    return jax.ShapeDtypeStruct(shape, dtype)


def block_rows(rows, parts):
    for count in range(parts, rows):
        if rows % count == 0 and (rows // count) % 16 == 0:
            return rows // count
    return rows


def dot_nn(left, right):
    return jnp.dot(left, right, preferred_element_type=F32)


def dot_nt(left, right):
    return lax.dot_general(left, right, (((1,), (1,)), ((), ())), preferred_element_type=F32)


def dot_tn(left, right):
    return lax.dot_general(left, right, (((0,), (0,)), ((), ())), preferred_element_type=F32)


def first_reduce(images, masks, weights, devices):
    rows, wide = images.shape
    narrow = weights.width
    strip_rows = block_rows(rows, 3)
    steps = rows // strip_rows

    def kernel(x_ref, mask_ref, w_ref, h_ref, send_ref, buffer, sems, sums):
        step = pl.program_id(0)

        @pl.when(step == 0)
        def _():
            copies = weights.copies(w_ref, buffer, sems)
            for copy in copies:
                copy.start()
            sums[...] = jnp.zeros_like(sums)
            for copy in copies:
                copy.wait()

        hidden = dot_nn(x_ref[...], buffer[...])
        h_ref[...] = hidden
        kept = hidden * mask_ref[:, 0:1]
        sums[0:8] += fold_rows(kept)
        sums[8:16] += fold_rows(kept * hidden)

        @pl.when(step == steps - 1)
        def _():
            send_rows(send_ref, [jnp.sum(sums[i * 8 : i * 8 + 8], axis=0, keepdims=True) for i in range(2)])

    send = (devices, 2 * narrow // LANES, LANES)
    return launch(
        kernel, "reduce_first", (steps,),
        (images, masks, weights.array),
        [strip(strip_rows, wide), strip(strip_rows, 2), ANYWHERE],
        (out_of((rows, narrow), F32), out_of(send, F32)),
        (strip(strip_rows, narrow), whole(send)),
        weights.scratch() + [pltpu.VMEM((16, narrow), F32)],
        2 * rows * wide * narrow,
    )


def store_shifted(shifted, place, values, zone, narrow):
    for offset in range(3):
        moved = values if offset == 1 else pltpu.roll(values, 1 if offset == 0 else zone - 1, 0)
        shifted[pl.ds(place, zone), offset * narrow : (offset + 1) * narrow] = moved.astype(BF16)


def clear_edges(shifted, rows, zone):
    edge = jnp.zeros((zone, shifted.shape[1]), BF16)
    shifted[0:zone] = edge
    shifted[zone + rows : 2 * zone + rows] = edge


def spatial_conv(hidden, parts, counts, norms, masks, weights, layer, zone, devices):
    rows, narrow = hidden.shape
    strip_rows = block_rows(rows, 3)
    steps = rows // strip_rows

    def kernel(
        h_ref, parts_ref, count_ref, norm_ref, mask_ref, w_ref,
        a_ref, out_ref, stat_ref, send_ref, buffer, sems, sums, shifted,
    ):
        step = pl.program_id(0)

        @pl.when(step == 0)
        def _():
            copies = weights.copies(w_ref, buffer, sems)
            for copy in copies:
                copy.start()
            sums[...] = jnp.zeros_like(sums)
            centre, inverse = norm_of(parts_ref, count_ref[0:1, 0:1], narrow)
            keep_norm(stat_ref, centre, inverse)
            gain = norm_ref[0, layer : layer + 1, 0:narrow]
            bias = norm_ref[1, layer : layer + 1, 0:narrow]
            clear_edges(shifted, rows, zone)

            def body(index, carry):
                start = pl.multiple_of(index * zone, zone)
                place = pl.ds(start, zone)
                value = silu((h_ref[place, :] - centre) * inverse * gain + bias) * mask_ref[place, 1:2]
                a_ref[place, :] = value.astype(BF16)
                store_shifted(shifted, pl.multiple_of(start + zone, zone), value, zone, narrow)
                return carry

            lax.fori_loop(0, rows // zone, body, 0)
            for copy in copies:
                copy.wait()

        base = step * strip_rows
        total = None
        for tap in range(3):
            piece = shifted[pl.ds(pl.multiple_of(base + tap * zone, 16), strip_rows), :]
            part = dot_nn(piece, buffer[tap * 3 * narrow : (tap + 1) * 3 * narrow])
            total = part if total is None else total + part
        out_ref[...] = total
        kept = total * mask_ref[pl.ds(pl.multiple_of(base, 16), strip_rows), 0:1]
        sums[0:8] += fold_rows(kept)
        sums[8:16] += fold_rows(kept * total)

        @pl.when(step == steps - 1)
        def _():
            send_rows(send_ref, [jnp.sum(sums[i * 8 : i * 8 + 8], axis=0, keepdims=True) for i in range(2)])

    send = (devices, 2 * narrow // LANES, LANES)
    return launch(
        kernel, "spatial_conv", (steps,),
        (hidden, parts, counts, norms, masks, weights.array),
        [whole(hidden.shape), whole(parts.shape), whole(counts.shape), whole(norms.shape), whole(masks.shape), ANYWHERE],
        (out_of((rows, narrow), BF16), out_of((rows, narrow), F32), out_of((8, narrow), F32), out_of(send, F32)),
        (whole((rows, narrow)), strip(strip_rows, narrow), whole((8, narrow)), whole(send)),
        weights.scratch() + [pltpu.VMEM((16, narrow), F32), pltpu.VMEM((rows + 2 * zone, 3 * narrow), BF16)],
        2 * rows * 9 * narrow * narrow,
    )


def expand(hidden, parts, counts, norms, masks, weights, layer, devices):
    rows, narrow = hidden.shape
    wide = weights.depth
    strip_rows = block_rows(rows, 4)
    steps = rows // strip_rows

    def kernel(
        h_ref, parts_ref, count_ref, norm_ref, mask_ref, w_ref,
        a_ref, out_ref, stat_ref, send_ref, buffer, sems, sums,
    ):
        step = pl.program_id(0)

        @pl.when(step == 0)
        def _():
            copies = weights.copies(w_ref, buffer, sems)
            for copy in copies:
                copy.start()
            sums[...] = jnp.zeros_like(sums)
            centre, inverse = norm_of(parts_ref, count_ref[0:1, 0:1], narrow)
            stat_ref[...] = jnp.zeros_like(stat_ref)
            keep_norm(stat_ref, centre, inverse)
            for copy in copies:
                copy.wait()

        gain = norm_ref[0, layer : layer + 1, narrow : 2 * narrow]
        bias = norm_ref[1, layer : layer + 1, narrow : 2 * narrow]
        value = silu((h_ref[...] - stat_ref[0:1]) * stat_ref[1:2] * gain + bias).astype(BF16)
        a_ref[...] = value
        total = dot_nt(value, buffer[...])
        out_ref[...] = total
        kept = total * mask_ref[:, 0:1]
        sums[0:8] += fold_rows(kept)
        sums[8:16] += fold_rows(kept * total)

        @pl.when(step == steps - 1)
        def _():
            send_rows(send_ref, [jnp.sum(sums[i * 8 : i * 8 + 8], axis=0, keepdims=True) for i in range(2)])

    send = (devices, 2 * wide // LANES, LANES)
    return launch(
        kernel, "expand", (steps,),
        (hidden, parts, counts, norms, masks, weights.array),
        [strip(strip_rows, narrow), whole(parts.shape), whole(counts.shape), whole(norms.shape), strip(strip_rows, 2), ANYWHERE],
        (out_of((rows, narrow), BF16), out_of((rows, wide), F32), out_of((8, narrow), F32), out_of(send, F32)),
        (strip(strip_rows, narrow), strip(strip_rows, wide), whole((8, narrow)), whole(send)),
        weights.scratch() + [pltpu.VMEM((16, wide), F32)],
        2 * rows * wide * narrow,
    )


def close_and_reduce(hidden, inputs, parts, counts, norms, masks, weights, layer, devices):
    rows, wide = hidden.shape
    narrow = weights.width
    strip_rows = block_rows(rows, 6)
    steps = rows // strip_rows

    def kernel(
        h_ref, x_ref, parts_ref, count_ref, norm_ref, mask_ref, w_ref,
        next_ref, low_ref, out_ref, stat_ref, send_ref, buffer, sems, sums,
    ):
        step = pl.program_id(0)

        @pl.when(step == 0)
        def _():
            copies = weights.copies(w_ref, buffer, sems)
            for copy in copies:
                copy.start()
            sums[...] = jnp.zeros_like(sums)
            centre, inverse = norm_of(parts_ref, count_ref[0:1, 0:1], wide)
            stat_ref[...] = jnp.zeros_like(stat_ref)
            keep_norm(stat_ref, centre, inverse)
            for copy in copies:
                copy.wait()

        gain = norm_ref[0, layer : layer + 1, 2 * narrow :]
        bias = norm_ref[1, layer : layer + 1, 2 * narrow :]
        normed = (h_ref[...] - stat_ref[0:1]) * stat_ref[1:2] * gain + bias
        value = silu(x_ref[...].astype(F32) + normed)
        next_ref[...] = value
        low = value.astype(BF16)
        low_ref[...] = low
        total = dot_nn(low, buffer[...])
        out_ref[...] = total
        kept = total * mask_ref[:, 0:1]
        sums[0:8] += fold_rows(kept)
        sums[8:16] += fold_rows(kept * total)

        @pl.when(step == steps - 1)
        def _():
            send_rows(send_ref, [jnp.sum(sums[i * 8 : i * 8 + 8], axis=0, keepdims=True) for i in range(2)])

    send = (devices, 2 * narrow // LANES, LANES)
    return launch(
        kernel, "close_and_reduce", (steps,),
        (hidden, inputs, parts, counts, norms, masks, weights.array),
        [strip(strip_rows, wide), strip(strip_rows, wide), whole(parts.shape), whole(counts.shape), whole(norms.shape), strip(strip_rows, 2), ANYWHERE],
        (out_of((rows, wide), F32), out_of((rows, wide), BF16), out_of((rows, narrow), F32), out_of((8, wide), F32), out_of(send, F32)),
        (strip(strip_rows, wide), strip(strip_rows, wide), strip(strip_rows, narrow), whole((8, wide)), whole(send)),
        weights.scratch() + [pltpu.VMEM((16, narrow), F32)],
        2 * rows * wide * narrow,
    )


def head_step(hidden, inputs, parts, counts, norms, masks, head_all, slot_bias, image_cols, layer, pixels, zone, devices):
    rows, wide = hidden.shape
    images = zone // SLOT
    dp_size, owners, slots, cols = head_all.shape
    classes = owners * slots
    steps = rows // zone
    count_rows = classes // LANES + 8
    tile = LANES

    def kernel(
        h_ref, x_ref, parts_ref, count_ref, norm_ref, mask_ref, head_ref, bias_ref, image_ref,
        ds_ref, stat_ref, send_ref, extra_ref, grad_ref, summed, pooled, sums,
    ):
        step = pl.program_id(0)
        gain = norm_ref[0, layer : layer + 1, norm_ref.shape[2] - wide :]
        bias = norm_ref[1, layer : layer + 1, norm_ref.shape[2] - wide :]

        @pl.when(step == 0)
        def _():
            sums[...] = jnp.zeros_like(sums)
            pooled[...] = jnp.zeros_like(pooled)
            centre, inverse = norm_of(parts_ref, count_ref[0:1, 0:1], wide)
            stat_ref[...] = jnp.zeros_like(stat_ref)
            keep_norm(stat_ref, centre, inverse)

        @pl.when(step < steps)
        def _():
            place = pl.ds(pl.multiple_of(step * zone, zone), zone)
            value = x_ref[...] + ((h_ref[...] - stat_ref[0:1]) * stat_ref[1:2] * gain + bias)
            summed[place, :] = value
            out = silu(value) * mask_ref[:, 1:2]
            pooled[...] += jnp.sum(out.reshape(images, SLOT, wide), axis=1)

        @pl.when(step == steps - 1)
        def _():
            low = (pooled[...] * (1.0 / pixels)).astype(BF16)
            columns = []
            for o in range(owners):
                logit = None
                for d in range(dp_size):
                    part = dot_nt(low[:, d * cols : (d + 1) * cols], head_ref[d, o])
                    logit = part if logit is None else logit + part
                columns.append(logit)
            logits = jnp.concatenate(columns, axis=1) + bias_ref[0:1, :]
            top = jnp.max(logits, axis=1, keepdims=True)
            shifted = jnp.exp(logits - top)
            mass = jnp.sum(shifted, axis=1, keepdims=True)
            log_total = jnp.log(mass) + top
            spots = lax.broadcasted_iota(jnp.int32, logits.shape, 1)
            onehot = (spots == image_ref[:, 0:1]).astype(F32)
            weight = image_ref[:, 1:2].astype(F32)
            picked = jnp.sum(logits * onehot, axis=1, keepdims=True)
            loss = jnp.sum(weight * (log_total - picked), axis=0, keepdims=True)
            residue = weight * (jnp.exp(logits - log_total) - onehot)
            send_rows(
                extra_ref,
                [jnp.sum(residue, axis=0, keepdims=True), jnp.broadcast_to(loss, (1, 8 * LANES))],
            )
            grad = (residue / count_ref[1:2, 0:1]).astype(BF16)
            for d in range(dp_size):
                back = None
                for o in range(owners):
                    mine = grad[:, o * slots : (o + 1) * slots]
                    part = dot_nn(mine, head_ref[d, o])
                    back = part if back is None else back + part
                    weight_part = dot_tn(mine, low[:, d * cols : (d + 1) * cols]).astype(BF16)
                    for i in range(grad_ref.shape[2]):
                        grad_ref[o, d, i] = weight_part[:, i * tile : (i + 1) * tile]
                pooled[:, d * cols : (d + 1) * cols] = back * (1.0 / pixels)

        @pl.when(step >= steps)
        def _():
            place = pl.ds(pl.multiple_of((step - steps) * zone, zone), zone)
            spread = jnp.broadcast_to(pooled[...][:, None, :], (images, SLOT, wide)).reshape(zone, wide)
            ds = spread * silu_slope(summed[place, :]) * mask_ref[:, 1:2]
            ds_ref[...] = ds
            normed = (h_ref[...] - stat_ref[0:1]) * stat_ref[1:2]
            sums[0:8] += fold_rows(ds)
            sums[8:16] += fold_rows(ds * normed)

        @pl.when(step == 2 * steps - 1)
        def _():
            send_rows(send_ref, [jnp.sum(sums[i * 8 : i * 8 + 8], axis=0, keepdims=True) for i in range(2)])

    send = (devices, 2 * wide // LANES, LANES)
    extra = (devices, count_rows, LANES)
    grads = (owners, dp_size, cols // tile, slots, tile)
    again = pl.BlockSpec((zone, wide), lambda i: (lax.rem(i, steps), 0))
    once = pl.BlockSpec((zone, wide), lambda i: (jnp.minimum(i, steps - 1), 0))
    later = pl.BlockSpec((zone, wide), lambda i: (jnp.maximum(i - steps, 0), 0))
    return launch(
        kernel, "head_step", (2 * steps,),
        (hidden, inputs, parts, counts, norms, masks, head_all, slot_bias, image_cols),
        [
            again, once, whole(parts.shape), whole(counts.shape), whole(norms.shape),
            pl.BlockSpec((zone, 2), lambda i: (lax.rem(i, steps), 0)),
            whole(head_all.shape), whole(slot_bias.shape), whole(image_cols.shape),
        ],
        (out_of((rows, wide), F32), out_of((8, wide), F32), out_of(send, F32), out_of(extra, F32), out_of(grads, BF16)),
        (later, whole((8, wide)), whole(send), whole(extra), whole(grads)),
        [pltpu.VMEM((rows, wide), F32), pltpu.VMEM((images, wide), F32), pltpu.VMEM((16, wide), F32)],
        6 * images * classes * wide,
    )


def back_norm(grad, normed, gain, inverse, mask, bias_sum, gain_sum, count):
    return gain * inverse * (grad - mask * (bias_sum + normed * gain_sum) / count)


def back_expand(ds, hidden, parts, stat_wide, counts, norms, masks, narrow_hidden, stat_narrow, weights, layer, devices):
    rows, wide = ds.shape
    narrow = weights.width
    strip_rows = block_rows(rows, 4)
    steps = rows // strip_rows

    def kernel(
        ds_ref, h_ref, parts_ref, stat_ref, count_ref, norm_ref, mask_ref, narrow_ref, narrow_stat, w_ref,
        low_ref, out_ref, send_ref, buffer, sems, sums, terms,
    ):
        step = pl.program_id(0)

        @pl.when(step == 0)
        def _():
            copies = weights.copies(w_ref, buffer, sems)
            for copy in copies:
                copy.start()
            sums[...] = jnp.zeros_like(sums)
            table = total_of(parts_ref)
            terms[0:1] = row_of(table, 0, wide)
            terms[1:2] = row_of(table, wide // LANES, wide)
            for copy in copies:
                copy.wait()

        gain = norm_ref[0, layer : layer + 1, 2 * narrow :]
        normed = (h_ref[...] - stat_ref[0:1]) * stat_ref[1:2]
        low = back_norm(
            ds_ref[...], normed, gain, stat_ref[1:2], mask_ref[:, 0:1], terms[0:1], terms[1:2], count_ref[0:1, 0:1]
        ).astype(BF16)
        low_ref[...] = low
        back = dot_nn(low, buffer[...])
        inner = (narrow_ref[...] - narrow_stat[0:1]) * narrow_stat[1:2]
        value = inner * norm_ref[0, layer : layer + 1, narrow : 2 * narrow] + norm_ref[1, layer : layer + 1, narrow : 2 * narrow]
        total = back * silu_slope(value)
        out_ref[...] = total
        sums[0:8] += fold_rows(total)
        sums[8:16] += fold_rows(total * inner)

        @pl.when(step == steps - 1)
        def _():
            send_rows(send_ref, [jnp.sum(sums[i * 8 : i * 8 + 8], axis=0, keepdims=True) for i in range(2)])

    send = (devices, 2 * narrow // LANES, LANES)
    return launch(
        kernel, "back_expand", (steps,),
        (ds, hidden, parts, stat_wide, counts, norms, masks, narrow_hidden, stat_narrow, weights.array),
        [
            strip(strip_rows, wide), strip(strip_rows, wide), whole(parts.shape), whole(stat_wide.shape), whole(counts.shape),
            whole(norms.shape), strip(strip_rows, 2), strip(strip_rows, narrow), whole(stat_narrow.shape), ANYWHERE,
        ],
        (out_of((rows, wide), BF16), out_of((rows, narrow), F32), out_of(send, F32)),
        (strip(strip_rows, wide), strip(strip_rows, narrow), whole(send)),
        weights.scratch() + [pltpu.VMEM((16, narrow), F32), pltpu.VMEM((8, wide), F32)],
        2 * rows * wide * narrow,
    )


def back_conv(dz, hidden, parts, stat_two, counts, norms, masks, first_hidden, stat_one, weights, layer, zone, devices):
    rows, narrow = dz.shape
    strip_rows = block_rows(rows, 3)
    steps = rows // strip_rows

    def kernel(
        dz_ref, h_ref, parts_ref, stat_ref, count_ref, norm_ref, mask_ref, first_ref, first_stat, w_ref,
        low_ref, out_ref, send_ref, buffer, sems, sums, shifted,
    ):
        step = pl.program_id(0)

        @pl.when(step == 0)
        def _():
            copies = weights.copies(w_ref, buffer, sems)
            for copy in copies:
                copy.start()
            sums[...] = jnp.zeros_like(sums)
            table = total_of(parts_ref)
            bias_sum = row_of(table, 0, narrow)
            gain_sum = row_of(table, narrow // LANES, narrow)
            centre, inverse = stat_ref[0:1], stat_ref[1:2]
            gain = norm_ref[0, layer : layer + 1, narrow : 2 * narrow]
            count = count_ref[0:1, 0:1]
            clear_edges(shifted, rows, zone)

            def body(index, carry):
                start = pl.multiple_of(index * zone, zone)
                place = pl.ds(start, zone)
                normed = (h_ref[place, :] - centre) * inverse
                value = back_norm(dz_ref[place, :], normed, gain, inverse, mask_ref[place, 0:1], bias_sum, gain_sum, count)
                low_ref[place, :] = value.astype(BF16)
                store_shifted(shifted, pl.multiple_of(start + zone, zone), value, zone, narrow)
                return carry

            lax.fori_loop(0, rows // zone, body, 0)
            for copy in copies:
                copy.wait()

        base = step * strip_rows
        total = None
        for tap_row in range(3):
            here = pl.ds(pl.multiple_of(base + (2 - tap_row) * zone, 16), strip_rows)
            for tap_col in range(3):
                tap = tap_row * 3 + tap_col
                piece = shifted[here, (2 - tap_col) * narrow : (3 - tap_col) * narrow]
                part = dot_nt(piece, buffer[tap * narrow : (tap + 1) * narrow])
                total = part if total is None else total + part
        place = pl.ds(pl.multiple_of(base, 16), strip_rows)
        inner = (first_ref[...] - first_stat[0:1]) * first_stat[1:2]
        value = inner * norm_ref[0, layer : layer + 1, 0:narrow] + norm_ref[1, layer : layer + 1, 0:narrow]
        total = total * silu_slope(value) * mask_ref[place, 1:2]
        out_ref[...] = total
        sums[0:8] += fold_rows(total)
        sums[8:16] += fold_rows(total * inner)

        @pl.when(step == steps - 1)
        def _():
            send_rows(send_ref, [jnp.sum(sums[i * 8 : i * 8 + 8], axis=0, keepdims=True) for i in range(2)])

    send = (devices, 2 * narrow // LANES, LANES)
    return launch(
        kernel, "back_conv", (steps,),
        (dz, hidden, parts, stat_two, counts, norms, masks, first_hidden, stat_one, weights.array),
        [
            whole(dz.shape), whole(hidden.shape), whole(parts.shape), whole(stat_two.shape), whole(counts.shape),
            whole(norms.shape), whole(masks.shape), strip(strip_rows, narrow), whole(stat_one.shape), ANYWHERE,
        ],
        (out_of((rows, narrow), BF16), out_of((rows, narrow), F32), out_of(send, F32)),
        (whole((rows, narrow)), strip(strip_rows, narrow), whole(send)),
        weights.scratch() + [pltpu.VMEM((16, narrow), F32), pltpu.VMEM((rows + 2 * zone, 3 * narrow), BF16)],
        2 * rows * 9 * narrow * narrow,
    )


def back_reduce(dz, first_hidden, parts, stat_one, counts, norms, masks, ds, hidden, inputs, stat_wide, weights, layer, devices):
    rows, narrow = dz.shape
    wide = ds.shape[1]
    strip_rows = block_rows(rows, 6)
    steps = rows // strip_rows
    below = layer - 1

    def kernel(
        dz_ref, first_ref, parts_ref, first_stat, count_ref, norm_ref, mask_ref, ds_ref, h_ref, x_ref, stat_ref, w_ref,
        low_ref, out_ref, send_ref, buffer, sems, sums, terms,
    ):
        step = pl.program_id(0)

        @pl.when(step == 0)
        def _():
            copies = weights.copies(w_ref, buffer, sems)
            for copy in copies:
                copy.start()
            sums[...] = jnp.zeros_like(sums)
            table = total_of(parts_ref)
            terms[0:1] = row_of(table, 0, narrow)
            terms[1:2] = row_of(table, narrow // LANES, narrow)
            for copy in copies:
                copy.wait()

        normed = (first_ref[...] - first_stat[0:1]) * first_stat[1:2]
        low = back_norm(
            dz_ref[...], normed, norm_ref[0, layer : layer + 1, 0:narrow], first_stat[1:2], mask_ref[:, 0:1],
            terms[0:1], terms[1:2], count_ref[0:1, 0:1],
        ).astype(BF16)
        low_ref[...] = low
        grad = dot_nt(low, buffer[...]) + ds_ref[...]
        inner = (h_ref[...] - stat_ref[0:1]) * stat_ref[1:2]
        value = inner * norm_ref[0, below : below + 1, 2 * narrow :] + norm_ref[1, below : below + 1, 2 * narrow :]
        total = grad * silu_slope(x_ref[...].astype(F32) + value)
        out_ref[...] = total
        sums[0:8] += fold_rows(total)
        sums[8:16] += fold_rows(total * inner)

        @pl.when(step == steps - 1)
        def _():
            send_rows(send_ref, [jnp.sum(sums[i * 8 : i * 8 + 8], axis=0, keepdims=True) for i in range(2)])

    send = (devices, 2 * wide // LANES, LANES)
    return launch(
        kernel, "back_reduce", (steps,),
        (dz, first_hidden, parts, stat_one, counts, norms, masks, ds, hidden, inputs, stat_wide, weights.array),
        [
            strip(strip_rows, narrow), strip(strip_rows, narrow), whole(parts.shape), whole(stat_one.shape), whole(counts.shape),
            whole(norms.shape), strip(strip_rows, 2), strip(strip_rows, wide), strip(strip_rows, wide), strip(strip_rows, wide),
            whole(stat_wide.shape), ANYWHERE,
        ],
        (out_of((rows, narrow), BF16), out_of((rows, wide), F32), out_of(send, F32)),
        (strip(strip_rows, narrow), strip(strip_rows, wide), whole(send)),
        weights.scratch() + [pltpu.VMEM((16, wide), F32), pltpu.VMEM((8, narrow), F32)],
        2 * rows * wide * narrow,
    )


def last_back(dz, first_hidden, parts, stat_one, counts, norms, masks, layer):
    rows, narrow = dz.shape
    strip_rows = block_rows(rows, 3)

    def kernel(dz_ref, first_ref, parts_ref, first_stat, count_ref, norm_ref, mask_ref, low_ref):
        table = total_of(parts_ref)
        normed = (first_ref[...] - first_stat[0:1]) * first_stat[1:2]
        low_ref[...] = back_norm(
            dz_ref[...], normed, norm_ref[0, layer : layer + 1, 0:narrow], first_stat[1:2], mask_ref[:, 0:1],
            row_of(table, 0, narrow), row_of(table, narrow // LANES, narrow), count_ref[0:1, 0:1],
        ).astype(BF16)

    return launch(
        kernel, "last_back", (rows // strip_rows,),
        (dz, first_hidden, parts, stat_one, counts, norms, masks),
        [
            strip(strip_rows, narrow), strip(strip_rows, narrow), whole(parts.shape), whole(stat_one.shape), whole(counts.shape),
            whole(norms.shape), strip(strip_rows, 2),
        ],
        out_of((rows, narrow), BF16),
        strip(strip_rows, narrow),
        [],
        rows * narrow,
    )


def weight_grad(left, right, owners):
    rows, depth = left.shape
    narrow = right.shape[1]
    tile = min(depth, 512)

    def kernel(left_ref, right_ref, out_ref):
        total = dot_tn(left_ref[...], right_ref[...]).astype(BF16)
        for o in range(owners):
            out_ref[o] = total[:, o * LANES : (o + 1) * LANES]

    return launch(
        kernel, "weight_grad", (depth // tile,),
        (left, right),
        [pl.BlockSpec((rows, tile), lambda i: (0, i)), whole(right.shape)],
        out_of((owners, depth, LANES), BF16),
        pl.BlockSpec((owners, tile, LANES), lambda i: (0, i, 0)),
        [],
        2 * rows * depth * narrow,
    )


def spatial_grad(act, right, owners, zone):
    rows, narrow = act.shape

    def kernel(act_ref, right_ref, out_ref, shifted):
        tap = pl.program_id(0)

        @pl.when(tap == 0)
        def _():
            clear_edges(shifted, rows, zone)

            def body(index, carry):
                start = pl.multiple_of(index * zone, zone)
                value = act_ref[pl.ds(start, zone), :].astype(F32)
                store_shifted(shifted, pl.multiple_of(start + zone, zone), value, zone, narrow)
                return carry

            lax.fori_loop(0, rows // zone, body, 0)

        for tap_col in range(3):
            piece = shifted[pl.ds(pl.multiple_of(tap * zone, zone), rows), tap_col * narrow : (tap_col + 1) * narrow]
            total = dot_tn(piece, right_ref[...]).astype(BF16)
            for o in range(owners):
                out_ref[o, tap_col * narrow : (tap_col + 1) * narrow] = total[:, o * LANES : (o + 1) * LANES]

    return launch(
        kernel, "spatial_grad", (3,),
        (act, right),
        [whole(act.shape), whole(right.shape)],
        out_of((owners, 9 * narrow, LANES), BF16),
        pl.BlockSpec((owners, 3 * narrow, LANES), lambda i: (0, i, 0)),
        [pltpu.VMEM((rows + 2 * zone, 3 * narrow), BF16)],
        2 * rows * 9 * narrow * narrow,
    )


def newton_schulz(moments):
    dp_size, owner_size = lax.axis_size("dp"), lax.axis_size("owner")
    owner = lax.axis_index("owner")
    cols = [moment.shape[0] for moment in moments]
    lanes = moments[0].shape[1]
    low = jnp.concatenate([moment.astype(jnp.bfloat16) for moment in moments], axis=0)
    all_rows = lax.all_gather(low, "owner")
    all_rows = all_rows.transpose(1, 0, 2).reshape(low.shape[0], owner_size * lanes)
    pieces, start = [], 0
    for size in cols:
        pieces.append(all_rows[start : start + size])
        start += size
    side = owner_size * lanes
    pairs = [(i, j) for i in range(owner_size) for j in range(i, owner_size)]
    packed = []
    for piece in pieces:
        gram = dot_tn(piece, piece)
        blocks = [gram[i * lanes : (i + 1) * lanes, j * lanes : (j + 1) * lanes] for i, j in pairs]
        packed.append(jnp.concatenate(blocks, axis=0))
    rows = packed[0].shape[0] // owner_size
    stack = jnp.stack(packed + [jnp.zeros_like(packed[0])] * (dp_size - len(packed)))
    mine = lax.dynamic_slice_in_dim(stack, owner * rows, rows, axis=1)
    bits = [bit for bit in range(device_count().bit_length() - 1) if (1 << bit) >= owner_size]
    values = mine
    for bit in bits:
        place = dp_size.bit_length() - 1 - (len(bits) - bits.index(bit))
        own = (my_index() >> bit) & 1
        values = values.reshape(-1, 2, rows, lanes)
        kept = lax.dynamic_index_in_dim(values, own, 1, keepdims=False)
        sent = lax.dynamic_index_in_dim(values, 1 - own, 1, keepdims=False)
        values = kept + swap(sent, bit)
    whole = lax.all_gather(values[0], "owner", tiled=True)
    blocks = {}
    for number, (i, j) in enumerate(pairs):
        block = whole[number * lanes : (number + 1) * lanes]
        blocks[i, j] = block
        if i != j:
            blocks[j, i] = block.T
    gram = jnp.concatenate(
        [jnp.concatenate([blocks[i, j] for j in range(owner_size)], axis=1) for i in range(owner_size)],
        axis=0,
    )
    dot = lambda left, right: jnp.dot(left, right, precision=lax.Precision.HIGHEST)
    eye = jnp.eye(side, dtype=jnp.float32)
    factor = 1.0 / (jnp.sqrt(jnp.trace(gram)) + 1e-07)
    gram = gram * (factor * factor)
    product = None
    for iteration in range(NS_STEPS):
        square = dot(gram, gram)
        poly = NS_A * eye + NS_B * gram + NS_C * square
        if iteration < NS_STEPS - 1:
            gram = dot(dot(gram, poly), poly)
        product = poly if product is None else dot(product, poly)
    product = (product * factor).astype(jnp.bfloat16)
    own_rows = lax.dynamic_slice_in_dim(product, owner * lanes, lanes, axis=0)
    copies = jnp.broadcast_to(own_rows[None], (dp_size,) + own_rows.shape)
    products = lax.all_to_all(copies, "dp", 0, 0, tiled=True)
    return [dot_nt(piece, products[number]) for number, piece in enumerate(pieces)]


def adamw(weight, grad, first, second, rate, decay):
    first = BETA_ONE * first + (1.0 - BETA_ONE) * grad
    second = BETA_TWO * second + (1.0 - BETA_TWO) * grad * grad
    first_hat = first / (1.0 - BETA_ONE**STEP)
    second_hat = second / (1.0 - BETA_TWO**STEP)
    weight = weight - rate * (first_hat / (jnp.sqrt(second_hat) + ADAM_EPS) + decay * weight)
    return (weight, first, second)


def per_device(
    images, valid_count, labels, loss_weight, w_reduce, w_spatial, w_expand, mom_reduce, mom_spatial, mom_expand,
    head, head_m, head_v, norm_params, norm_m, norm_v, head_bias, bias_m, bias_v,
):
    dp_size, owner_size = lax.axis_size("dp"), lax.axis_size("owner")
    devices = dp_size * owner_size
    count_img, side, _, wide = images.shape
    pixels = side * side
    narrow = w_reduce.shape[1] * owner_size
    zone = count_img * SLOT
    rows = side * zone

    valid = (jnp.arange(count_img, dtype=jnp.int32) < valid_count[0]).astype(jnp.int32)
    weight_img = valid * loss_weight
    tallies = jnp.stack([valid_count[0] * pixels, jnp.sum(weight_img)]).astype(F32)
    tallies = jnp.pad(tallies, (0, 6))[:, None]
    counts = jnp.sum(exchange(jnp.broadcast_to(tallies[None], (devices, 8, LANES))), axis=0)
    weight_total = counts[1, 0]

    rows_of = (w_reduce.shape[2], w_spatial.shape[2], w_expand.shape[2])
    starts = (0, rows_of[0], rows_of[0] + rows_of[1])
    mats = []
    for layer in range(LAYERS):
        parts = (w_reduce[layer], w_spatial[layer], w_expand[layer])
        packed = jnp.concatenate([part.T.astype(BF16) for part in parts], axis=0)
        gathered = lax.all_gather(packed, AXES).reshape(dp_size, owner_size, packed.shape[0], LANES)
        for kind in range(3):
            if dp_size <= 8:
                mats.append(Weights(gathered, starts[kind], rows_of[kind]))
            else:
                piece = gathered[:, :, starts[kind] : starts[kind] + rows_of[kind]]
                piece = piece.transpose(1, 0, 2, 3).reshape(1, owner_size, -1, LANES)
                mats.append(Weights(piece, 0, piece.shape[2]))
    classes = head.shape[0]
    slots = -(-classes // LANES) * LANES
    slack = slots - classes
    head_low = jnp.pad(head.astype(BF16), ((0, slack), (0, 0)))
    head_all = lax.all_gather(head_low, AXES).reshape(dp_size, owner_size, slots, head.shape[1])
    aligned = head.shape[1] % LANES == 0
    if not aligned:
        head_all = head_all.transpose(1, 2, 0, 3).reshape(1, owner_size, slots, wide)
    slot_bias = jnp.pad(head_bias.reshape(owner_size, classes), ((0, 0), (0, slack)), constant_values=-1e30)
    slot_bias = jnp.broadcast_to(slot_bias.reshape(1, -1), (8, owner_size * slots))
    slot_labels = (labels // classes) * slots + labels % classes
    image_cols = jnp.stack([slot_labels, weight_img], axis=1)

    in_map = (jnp.arange(SLOT) < side).astype(F32)
    pad_mask = jnp.broadcast_to(in_map, (side, count_img, SLOT))
    masks = jnp.stack([pad_mask * valid.astype(F32)[:, None], pad_mask], axis=-1).reshape(rows, 2)
    pixels_in = jnp.pad(images, ((0, 0), (0, 0), (0, SLOT - side), (0, 0))).transpose(1, 0, 2, 3).reshape(rows, wide)

    norms = norm_params
    h1, h2, h3, a1, a2, stat1, stat2, stat3 = ([None] * LAYERS for _ in range(8))
    inputs, inputs_low = [pixels_in] + [None] * (LAYERS - 1), [pixels_in] + [None] * (LAYERS - 1)
    h1[0], sums = first_reduce(pixels_in, masks, mats[0], devices)
    for layer in range(LAYERS):
        a1[layer], h2[layer], stat1[layer], sums = spatial_conv(
            h1[layer], exchange(sums), counts, norms, masks, mats[3 * layer + 1], layer, zone, devices
        )
        a2[layer], h3[layer], stat2[layer], sums = expand(
            h2[layer], exchange(sums), counts, norms, masks, mats[3 * layer + 2], layer, devices
        )
        if layer < LAYERS - 1:
            inputs[layer + 1], inputs_low[layer + 1], h1[layer + 1], stat3[layer], sums = close_and_reduce(
                h3[layer], inputs[layer], exchange(sums), counts, norms, masks, mats[3 * layer + 3], layer, devices
            )
    last = LAYERS - 1
    ds, stat3[last], sums, extra, grad_head = head_step(
        h3[last], inputs[last], exchange(sums), counts, norms, masks, head_all, slot_bias, image_cols, last, pixels, zone, devices
    )
    extra = jnp.sum(exchange(extra), axis=0)
    class_rows = owner_size * slots // LANES
    bias_raw = extra[:class_rows].reshape(owner_size, slots)[:, :classes].reshape(-1)
    loss_sum = extra[class_rows, 0]
    grad_bias = bias_raw / weight_total

    norm_sums, grads = ([], [])
    for layer in reversed(range(LAYERS)):
        parts3 = exchange(sums)
        dh3, dz2, sums = back_expand(
            ds, h3[layer], parts3, stat3[layer], counts, norms, masks, h2[layer], stat2[layer], mats[3 * layer + 2], layer, devices
        )
        grad_three = weight_grad(dh3, a2[layer], owner_size)
        parts2 = exchange(sums)
        dh2, dz1, sums = back_conv(
            dz2, h2[layer], parts2, stat2[layer], counts, norms, masks, h1[layer], stat1[layer], mats[3 * layer + 1], layer, zone, devices
        )
        grad_two = spatial_grad(a1[layer], dh2, owner_size, zone)
        parts1 = exchange(sums)
        if layer > 0:
            dh1, ds, sums = back_reduce(
                dz1, h1[layer], parts1, stat1[layer], counts, norms, masks, ds, h3[layer - 1], inputs[layer - 1], stat3[layer - 1],
                mats[3 * layer], layer, devices,
            )
        else:
            dh1 = last_back(dz1, h1[layer], parts1, stat1[layer], counts, norms, masks, layer)
        grad_one = weight_grad(inputs_low[layer], dh1, owner_size)
        grads.insert(0, (grad_one, grad_two, grad_three))
        norm_sums.insert(0, [jnp.sum(part, axis=0).reshape(2, -1) for part in (parts1, parts2, parts3)])
    norm_grad = jnp.stack(
        [jnp.stack([jnp.concatenate([part[kind] for part in norm_sums[layer]]) for layer in range(LAYERS)]) for kind in (1, 0)]
    )

    left = bits_of(dp_size, owner_size)
    sums_of = []
    for layer in range(LAYERS):
        blocks = [grad.reshape(devices, -1, LANES) for grad in grads[layer]]
        if layer == 0:
            bits = list(range(1, len(left)))
            pieces = []
            for number, block in enumerate(blocks):
                turn = number % len(bits)
                pieces.append(halving_sum(block, left, [0] + bits[turn:] + bits[:turn]))
            sums_of.append([piece.astype(F32) for piece in pieces])
            continue
        if aligned:
            head_blocks = grad_head.reshape(devices, -1, LANES)
        else:
            head_blocks = grad_head.reshape(owner_size, wide // LANES, slots, LANES // head.shape[1], head.shape[1])
            head_blocks = head_blocks.transpose(0, 1, 3, 2, 4).reshape(devices, slots, head.shape[1])
        height = sum(rows_of)
        if aligned:
            total = lax.psum_scatter(jnp.concatenate(blocks + [head_blocks], axis=1), ("owner", "dp"), scatter_dimension=0).astype(F32)
            head_sum = total[height:]
        else:
            total = lax.psum_scatter(jnp.concatenate(blocks, axis=1), ("owner", "dp"), scatter_dimension=0).astype(F32)
            head_sum = lax.psum_scatter(head_blocks, ("owner", "dp"), scatter_dimension=0).astype(F32)
        sums_of.append([total[starts[kind] : starts[kind] + rows_of[kind]] for kind in range(3)])
        head_sum = head_sum.reshape(-1, slots, head_sum.shape[-1])[:, :classes].transpose(1, 0, 2).reshape(classes, -1)

    olds = (mom_reduce, mom_spatial, mom_expand)
    moments_t = [MOMENTUM * olds[kind][layer].T + sums_of[layer][kind] for layer in range(LAYERS) for kind in range(3)]
    directions_t = newton_schulz(moments_t)
    moments, directions = (
        [jnp.stack([values[layer * 3 + kind].T for layer in range(LAYERS)]) for kind in range(3)]
        for values in (moments_t, directions_t)
    )
    masters = (w_reduce, w_spatial, w_expand)
    updated = tuple(
        (
            master * (1.0 - LR_MATRIX * DECAY_MATRIX) - LR_MATRIX * direction
            for master, direction in zip(masters, directions)
        )
    )
    new_head, new_head_m, new_head_v = adamw(head, head_sum, head_m, head_v, LR_HEAD, DECAY_HEAD)
    new_norm, new_norm_m, new_norm_v = adamw(norm_params, norm_grad, norm_m, norm_v, LR_VECTOR, 0.0)
    new_bias, new_bias_m, new_bias_v = adamw(head_bias, grad_bias, bias_m, bias_v, LR_VECTOR, 0.0)
    return (
        loss_sum,
        weight_total,
        updated[0],
        updated[1],
        updated[2],
        moments[0],
        moments[1],
        moments[2],
        new_head,
        new_head_m,
        new_head_v,
        new_norm,
        new_norm_m,
        new_norm_v,
        new_bias,
        new_bias_m,
        new_bias_v,
    )


def solution(mesh):
    return jax.shard_map(
        per_device,
        mesh=mesh,
        in_specs=(
            P(("dp", "owner"), None, None, None),
            P(("dp", "owner")),
            P(("dp", "owner")),
            P(("dp", "owner")),
            P(None, "owner", "dp"),
            P(None, "owner", "dp"),
            P(None, "owner", "dp"),
            P(None, "owner", "dp"),
            P(None, "owner", "dp"),
            P(None, "owner", "dp"),
            P("owner", "dp"),
            P("owner", "dp"),
            P("owner", "dp"),
            P(),
            P(),
            P(),
            P(),
            P(),
            P(),
        ),
        out_specs=(
            P(),
            P(),
            P(None, "owner", "dp"),
            P(None, "owner", "dp"),
            P(None, "owner", "dp"),
            P(None, "owner", "dp"),
            P(None, "owner", "dp"),
            P(None, "owner", "dp"),
            P("owner", "dp"),
            P("owner", "dp"),
            P("owner", "dp"),
            P(),
            P(),
            P(),
            P(),
            P(),
            P(),
        ),
        check_vma=False,
    )
```

time: 1040 us -> 942 us (0.906)
  local copies, waits for them, and re-layouts: 353 us -> 57.6 us
  Pallas kernels: 0 us -> 252 us
  waiting for transfers between devices: 213 us -> 368 us
  matrix products: 191 us -> 40.4 us
  other arithmetic: 156 us -> 46.9 us
  blocking collectives: 21.4 us -> 65.5 us
    pallas_call x0 -> x19, Pallas kernels: none -> 252 us  [launch(): pl.pallas_call(kernel, name=name, grid=grid, in_specs=specs, out_specs=ou...]
    dot_general x32 -> x12, matrix products: 156 us -> 5.99 us  [the longest x6 3.5 us: dot_nt(): lax.dot_general(left, right, (((1,), (1,)), ((), ())), preferred_element_...]
    ppermute x18, waiting for transfers between devices: 69.3 us -> 149 us  [swap(): lax.ppermute(values, AXES, [(src, src ^ 1 << bit) for src in range(count)])]
    reshape x16 -> x1, local copies, waits for them, and re-layouts: 75 us -> 0.01 us  [per_device(): extra[:class_rows].reshape(owner_size, slots)[:, :classes].reshape(-1)]
    concatenate x20 -> x0, local copies, waits for them, and re-layouts: 54.5 us -> none  [the longest x18 51.3 us: columns(): jnp.concatenate(pieces, axis=3).reshape(count_img * side * side, 9 * chans)]
    unnamed x362 -> x205, local copies, waits for them, and re-layouts: 71.9 us -> 23.8 us
    reduce_scatter x1, waiting for transfers between devices: 0.02 us -> 46.5 us  [per_device(): lax.psum_scatter(jnp.concatenate(blocks + [head_blocks], axis=1), ('owner...]
    all_to_all x1 -> x4, blocking collectives: 14.1 us -> 58.2 us  [exchange(): return lax.all_to_all(copies, AXES, 0, 0, tiled=True)]
  transfers between devices with their start and end apart: 36 -> 34, of which waited for: 22 -> 23; matrix products, arithmetic and copies ran while one was open for 43% -> 6% of each run, Pallas kernels for 0% -> 17%
where the time goes in v2:
time: 942 us; the launch traced here: 930 us
  waiting for transfers between devices  368 us (39%)
  Pallas kernels  252 us (27%)
  starting transfers between devices  82 us (9%)
  blocking collectives  65.5 us (7%)
  local copies, waits for them, and re-layouts  57.6 us (6%)
  other arithmetic  46.9 us (5%)
  matrix products  40.4 us (4%)
  between operations  17.4 us (2%)
    pallas_call x19, Pallas kernels, launch(): pl.pallas_call(kernel, name=name, grid=grid, in_specs=specs, out_specs=ou...  252 us
    ppermute x18, waiting for transfers between devices, swap(): lax.ppermute(values, AXES, [(src, src ^ 1 << bit) for src in range(count)])  149 us
    all_gather x2, waiting for transfers between devices, per_device(): lax.all_gather(packed, AXES)  93.7 us
    all_to_all x4, blocking collectives, exchange(): return lax.all_to_all(copies, AXES, 0, 0, tiled=True)  58.2 us
    all_to_all x10, waiting for transfers between devices, exchange(): return lax.all_to_all(copies, AXES, 0, 0, tiled=True)  58 us
    all_to_all x10, starting transfers between devices, exchange(): return lax.all_to_all(copies, AXES, 0, 0, tiled=True)  47.4 us
    reduce_scatter x1, waiting for transfers between devices, per_device(): lax.psum_scatter(jnp.concatenate(blocks + [head_blocks], axis=1), ('owner...  46.5 us
    dot_general x17, matrix products, newton_schulz(): jnp.dot(left, right, precision=lax.Precision.HIGHEST)  34.4 us
  transfers between devices with their start and end apart: 34, of which 23 were waited for; matrix products, arithmetic and copies ran while one was open for 6% of the time, Pallas kernels for 17%

profile of v2, /device:TPU:0, one launch (start us, length us, event | category | flops | bytes accessed | tf_op | source)
XLA Modules:
  0.0 930.1 jit_solution(1939009434379683333)
XLA Ops:
  33.2 62.2 %all-gather.10.cloned.1.call-done = bf16[34816,128]{1,0:T(8,128)(2,1)} async-done(((bf16[1088,128]{1,0:T(8,128)(2,1)}), bf16[34816,128]{1,0:T(8,128)(2,1)}) %all-gather.10.cloned.1.call-update) | async-done | bytes 8912912 | tf_op jit(solution)/shard_map/all_gather | solution.py:889
  107.9 8.8 all-to-all-done.parts_ref
  117.3 13.2 %spatial_conv.2 = (bf16[1344,512]{1,0:T(8,128)(2,1)}, f32[1344,512]{1,0:T(8,128)}, f32[8,512]{1,0:T(8,128)}, f32[32,8,128]{2,1,0:T(8,128)}) custom-call(f32[1344,512]{1,0:T(8,128)} %get-tuple-element.60.h_ref.first_ref, f32[32,8,128]{2,1,0:T(8,128)} %copy-done.55, f32[8,128]{1,0:T(8,128)} %reduce_sum.92.count_ref, f32[2,2,3072]{2,1,0:T(2,128)} %norm_ref.23, ...), custom_call_target="tpu_custom_call" | custom-call | flops 6341787648 | bytes 16136704 | tf_op jit(solution)/shard_map/spatial_conv/pallas_call | solution.py:159
  130.5 13.5 %all_to_all.75.parts_ref = f32[32,8,128]{2,1,0:T(8,128)} all-to-all(f32[32,8,128]{2,1,0:T(8,128)} %get-tuple-element.63), channel_id=1, replica_groups=mesh['dp'=8,'owner'=4] {'dp','owner'}, dimensions={0} | all-to-all | bytes 262144 | tf_op jit(solution)/shard_map/all_to_all | solution.py:44
  144.0 10.8 %expand.2 = (bf16[1344,512]{1,0:T(8,128)(2,1)}, f32[1344,2048]{1,0:T(8,128)}, f32[8,512]{1,0:T(8,128)}, f32[32,32,128]{2,1,0:T(8,128)}) custom-call(f32[1344,512]{1,0:T(8,128)} %get-tuple-element.62.h_ref.narrow_ref, f32[32,8,128]{2,1,0:T(8,128)} %all_to_all.75.parts_ref, f32[8,128]{1,0:T(8,128)} %reduce_sum.92.count_ref, f32[2,2,3072]{2,1,0:T(2,128)} %norm_ref.23, ...), custom_call_target="tpu_custom_call" | custom-call | flops 2818572288 | bytes 24787456 | tf_op jit(solution)/shard_map/expand/pallas_call | solution.py:159
  158.2 31.5 %all-gather.12.cloned.1.call-done = bf16[34816,128]{1,0:T(8,128)(2,1)} async-done(((bf16[1088,128]{1,0:T(8,128)(2,1)}), bf16[34816,128]{1,0:T(8,128)(2,1)}) %all-gather.12.cloned.1.call-update) | async-done | bytes 8912912 | tf_op jit(solution)/shard_map/all_gather | solution.py:889
  190.5 17.7 %close_and_reduce.1 = (f32[1344,2048]{1,0:T(8,128)}, bf16[1344,2048]{1,0:T(8,128)(2,1)}, f32[1344,512]{1,0:T(8,128)}, f32[8,2048]{1,0:T(8,128)}, f32[32,8,128]{2,1,0:T(8,128)}) custom-call(f32[1344,2048]{1,0:T(8,128)} %get-tuple-element.64.h_ref, bf16[1344,2048]{1,0:T(8,128)(2,1)} %bitcast.411, f32[32,32,128]{2,1,0:T(8,128)} %copy-done.9, ...), custom_call_target="tpu_custom_call" | custom-call | flops 2818572288 | bytes 33554432 | tf_op jit(solution)/shard_map/close_and_reduce/pallas_call | solution.py:159
  208.2 12.2 %all_to_all.76.parts_ref = f32[32,8,128]{2,1,0:T(8,128)} all-to-all(f32[32,8,128]{2,1,0:T(8,128)} %get-tuple-element.67), channel_id=1, replica_groups=mesh['dp'=8,'owner'=4] {'dp','owner'}, dimensions={0} | all-to-all | bytes 262144 | tf_op jit(solution)/shard_map/all_to_all | solution.py:44
  220.4 13.2 %spatial_conv.3 = (bf16[1344,512]{1,0:T(8,128)(2,1)}, f32[1344,512]{1,0:T(8,128)}, f32[8,512]{1,0:T(8,128)}, f32[32,8,128]{2,1,0:T(8,128)}) custom-call(f32[1344,512]{1,0:T(8,128)} %get-tuple-element.66.h_ref.first_ref, f32[32,8,128]{2,1,0:T(8,128)} %all_to_all.76.parts_ref, f32[8,128]{1,0:T(8,128)} %reduce_sum.92.count_ref, f32[2,2,3072]{2,1,0:T(2,128)} %norm_ref.23, ...), custom_call_target="tpu_custom_call" | custom-call | flops 6341787648 | bytes 16136704 | tf_op jit(solution)/shard_map/spatial_conv/pallas_call | solution.py:159
  233.6 13.6 %all_to_all.77.parts_ref = f32[32,8,128]{2,1,0:T(8,128)} all-to-all(f32[32,8,128]{2,1,0:T(8,128)} %get-tuple-element.69), channel_id=1, replica_groups=mesh['dp'=8,'owner'=4] {'dp','owner'}, dimensions={0} | all-to-all | bytes 262144 | tf_op jit(solution)/shard_map/all_to_all | solution.py:44
  247.2 10.7 %expand.3 = (bf16[1344,512]{1,0:T(8,128)(2,1)}, f32[1344,2048]{1,0:T(8,128)}, f32[8,512]{1,0:T(8,128)}, f32[32,32,128]{2,1,0:T(8,128)}) custom-call(f32[1344,512]{1,0:T(8,128)} %get-tuple-element.68.h_ref.narrow_ref, f32[32,8,128]{2,1,0:T(8,128)} %all_to_all.77.parts_ref, f32[8,128]{1,0:T(8,128)} %reduce_sum.92.count_ref, f32[2,2,3072]{2,1,0:T(2,128)} %norm_ref.23, ...), custom_call_target="tpu_custom_call" | custom-call | flops 2818572288 | bytes 24787456 | tf_op jit(solution)/shard_map/expand/pallas_call | solution.py:159
  262.4 14.7 %all-to-all-done.6.parts_ref = f32[32,32,128]{2,1,0:T(8,128)S(1)} async-done(((f32[32,32,128]{2,1,0:T(8,128)}), f32[32,32,128]{2,1,0:T(8,128)S(1)}, u32[]{:S(2)}, u32[]{:S(2)}) %all-to-all-start.6) | async-done | bytes 524320 | tf_op jit(solution)/shard_map/all_to_all | solution.py:44
  277.9 35.4 %head_step.1 = (f32[1344,2048]{1,0:T(8,128)}, f32[8,2048]{1,0:T(8,128)}, f32[32,32,128]{2,1,0:T(8,128)}, f32[32,16,128]{2,1,0:T(8,128)}, bf16[4,8,2,256,128]{4,3,2,1,0:T(8,128)(2,1)}) custom-call(f32[1344,2048]{1,0:T(8,128)} %get-tuple-element.70.h_ref, f32[1344,2048]{1,0:T(8,128)} %get-tuple-element.71.x_ref, f32[32,32,128]{2,1,0:T(8,128)} %copy-done.12, ...), custom_call_target="tpu_custom_call" | custom-call | flops 301989888 | bytes 33554432 | tf_op jit(solution)/shard_map/head_step/pallas_call | solution.py:159
  313.3 18.9 %all_to_all.78.parts_ref = f32[32,32,128]{2,1,0:T(8,128)} all-to-all(f32[32,32,128]{2,1,0:T(8,128)} %get-tuple-element.75), channel_id=1, replica_groups=mesh['dp'=8,'owner'=4] {'dp','owner'}, dimensions={0} | all-to-all | bytes 1048576 | tf_op jit(solution)/shard_map/all_to_all | solution.py:44
  332.2 16.1 %back_expand.2 = (bf16[1344,2048]{1,0:T(8,128)(2,1)}, f32[1344,512]{1,0:T(8,128)}, f32[32,8,128]{2,1,0:T(8,128)}) custom-call(f32[1344,2048]{1,0:T(8,128)} %get-tuple-element.74.ds_ref, f32[1344,2048]{1,0:T(8,128)} %get-tuple-element.70.h_ref, f32[32,32,128]{2,1,0:T(8,128)} %all_to_all.78.parts_ref, f32[8,2048]{1,0:T(8,128)} %get-tuple-element.76.stat_ref, ...), custom_call_target="tpu_custom_call" | custom-call | flops 2818572288 | bytes 33554432 | tf_op jit(solution)/shard_map/back_expand/pallas_call | solution.py:159
  360.6 15.3 %back_conv.2 = (bf16[1344,512]{1,0:T(8,128)(2,1)}, f32[1344,512]{1,0:T(8,128)}, f32[32,8,128]{2,1,0:T(8,128)}) custom-call(f32[1344,512]{1,0:T(8,128)} %get-tuple-element.78.dz_ref, f32[1344,512]{1,0:T(8,128)} %get-tuple-element.68.h_ref.narrow_ref, f32[32,8,128]{2,1,0:T(8,128)} %copy-done.36, f32[8,512]{1,0:T(8,128)} %get-tuple-element.77.narrow_stat.stat_ref, ...), custom_call_target="tpu_custom_call" | custom-call | flops 6341787648 | bytes 21658112 | tf_op jit(solution)/shard_map/back_conv/pallas_call | solution.py:159
  380.9 11.6 %spatial_grad.3 = bf16[4,4608,128]{2,1,0:T(8,128)(2,1)} custom-call(bf16[1344,512]{1,0:T(8,128)(2,1)} %get-tuple-element.98.act_ref, bf16[1344,512]{1,0:T(8,128)(2,1)} %get-tuple-element.99.right_ref), custom_call_target="tpu_custom_call" | custom-call | flops 6341787648 | bytes 7471104 | tf_op jit(solution)/shard_map/spatial_grad/pallas_call | solution.py:159
  393.2 22.0 %back_reduce.1 = (bf16[1344,512]{1,0:T(8,128)(2,1)}, f32[1344,2048]{1,0:T(8,128)}, f32[32,32,128]{2,1,0:T(8,128)}) custom-call(f32[1344,512]{1,0:T(8,128)} %get-tuple-element.81.dz_ref, f32[1344,512]{1,0:T(8,128)} %get-tuple-element.66.h_ref.first_ref, f32[32,8,128]{2,1,0:T(8,128)} %copy-done.14, f32[8,512]{1,0:T(8,128)} %get-tuple-element.80.first_stat, ...), custom_call_target="tpu_custom_call" | custom-call | flops 2818572288 | bytes 33554432 | tf_op jit(solution)/shard_map/back_reduce/pallas_call | solution.py:159
  422.7 10.7 %pad_maximum_fusion = bf16[32,1600,128]{2,1,0:T(8,128)(2,1)} fusion(bf16[32,512,128]{2,1,0:T(8,128)(2,1)} %bitcast.428, bf16[32,256,128]{2,1,0:T(8,128)(2,1)S(1)} %bitcast.446, bf16[32,576,128]{2,1,0:T(8,128)(2,1)} %bitcast.423, bf16[32,256,128]{2,1,0:T(8,128)(2,1)} %bitcast.447), kind=kLoop, calls=%fused_computation | loop fusion | flops 52428800 | bytes 26214400 | tf_op jit(solution)/shard_map/concatenate | solution.py:986
  439.3 22.2 %all-to-all-done.11.parts_ref = f32[32,32,128]{2,1,0:T(8,128)S(1)} async-done(((f32[32,32,128]{2,1,0:T(8,128)}), f32[32,32,128]{2,1,0:T(8,128)S(1)}, u32[]{:S(2)}, u32[]{:S(2)}) %all-to-all-start.11) | async-done | bytes 524320 | tf_op jit(solution)/shard_map/all_to_all | solution.py:44
  462.3 16.2 %back_expand.3 = (bf16[1344,2048]{1,0:T(8,128)(2,1)}, f32[1344,512]{1,0:T(8,128)}, f32[32,8,128]{2,1,0:T(8,128)}) custom-call(f32[1344,2048]{1,0:T(8,128)} %get-tuple-element.84.ds_ref, f32[1344,2048]{1,0:T(8,128)} %get-tuple-element.64.h_ref, f32[32,32,128]{2,1,0:T(8,128)} %copy-done.1, f32[8,2048]{1,0:T(8,128)} %get-tuple-element.83.stat_ref, ...), custom_call_target="tpu_custom_call" | custom-call | flops 2818572288 | bytes 33554432 | tf_op jit(solution)/shard_map/back_expand/pallas_call | solution.py:159
  494.1 15.3 %back_conv.3 = (bf16[1344,512]{1,0:T(8,128)(2,1)}, f32[1344,512]{1,0:T(8,128)}, f32[32,8,128]{2,1,0:T(8,128)}) custom-call(f32[1344,512]{1,0:T(8,128)} %get-tuple-element.87.dz_ref, f32[1344,512]{1,0:T(8,128)} %get-tuple-element.62.h_ref.narrow_ref, f32[32,8,128]{2,1,0:T(8,128)} %copy-done.37, f32[8,512]{1,0:T(8,128)} %get-tuple-element.86.narrow_stat.stat_ref, ...), custom_call_target="tpu_custom_call" | custom-call | flops 6341787648 | bytes 21658112 | tf_op jit(solution)/shard_map/back_conv/pallas_call | solution.py:159
  513.6 11.7 %spatial_grad.2 = bf16[4,4608,128]{2,1,0:T(8,128)(2,1)} custom-call(bf16[1344,512]{1,0:T(8,128)(2,1)} %get-tuple-element.92.act_ref, bf16[1344,512]{1,0:T(8,128)(2,1)} %get-tuple-element.93.right_ref), custom_call_target="tpu_custom_call" | custom-call | flops 6341787648 | bytes 7471104 | tf_op jit(solution)/shard_map/spatial_grad/pallas_call | solution.py:159
  550.5 19.6 %collective-permute-done.11 = bf16[4,2,256,128]{3,2,1,0:T(8,128)(2,1)S(1)} collective-permute-done((bf16[4,2,256,128]{3,2,1,0:T(8,128)(2,1)S(1)}, bf16[4,2,256,128]{3,2,1,0:T(8,128)(2,1)S(1)}, u32[]{:S(2)}, u32[]{:S(2)}) %collective-permute-start.11) | collective-permute-done | bytes 524320 | tf_op jit(solution)/shard_map/ppermute | solution.py:49
  587.9 9.6 %collective-permute-done.12 = bf16[2,2,256,128]{3,2,1,0:T(8,128)(2,1)} collective-permute-done((bf16[2,2,256,128]{3,2,1,0:T(8,128)(2,1)}, bf16[2,2,256,128]{3,2,1,0:T(8,128)(2,1)}, u32[]{:S(2)}, u32[]{:S(2)}) %collective-permute-start.12) | collective-permute-done | bytes 262176 | tf_op jit(solution)/shard_map/ppermute | solution.py:49
  601.0 53.3 %collective-permute-done.6 = bf16[8,1,576,128]{3,2,0,1:T(8,128)(2,1)} collective-permute-done((bf16[8,1,576,128]{3,2,0,1:T(8,128)(2,1)}, bf16[8,1,576,128]{3,2,0,1:T(8,128)(2,1)}, u32[]{:S(2)}, u32[]{:S(2)}) %collective-permute-start.6) | collective-permute-done | bytes 1179680 | tf_op jit(solution)/shard_map/ppermute | solution.py:49
  660.5 10.5 %collective-permute-done.2 = bf16[4,1,256,128]{3,2,0,1:T(8,128)(2,1)S(1)} collective-permute-done((bf16[4,1,256,128]{3,2,0,1:T(8,128)(2,1)S(1)}, bf16[4,1,256,128]{3,2,0,1:T(8,128)(2,1)S(1)}, u32[]{:S(2)}, u32[]{:S(2)}) %collective-permute-start.2) | collective-permute-done | bytes 262176 | tf_op jit(solution)/shard_map/ppermute | solution.py:49
  688.6 14.8 %collective-permute-done.8 = bf16[2,1,576,128]{3,2,1,0:T(8,128)(2,1)S(1)} collective-permute-done((bf16[2,1,576,128]{3,2,1,0:T(8,128)(2,1)S(1)}, bf16[2,1,576,128]{3,2,1,0:T(8,128)(2,1)S(1)}, u32[]{:S(2)}, u32[]{:S(2)}) %collective-permute-start.8) | collective-permute-done | bytes 294944 | tf_op jit(solution)/shard_map/ppermute | solution.py:49
  710.7 46.5 %reduce-scatter.2.cloned.1.call-done = bf16[1,1600,128]{2,1,0:T(8,128)(2,1)} async-done(((bf16[32,1600,128]{2,1,0:T(8,128)(2,1)}), bf16[1,1600,128]{2,1,0:T(8,128)(2,1)}) %reduce-scatter.2.cloned.1.call-update) | async-done | bytes 409616 | tf_op jit(solution)/shard_map/reduce_scatter | solution.py:986
  768.5 9.4 %all-to-all-done.7 = f32[32,16,128]{2,1,0:T(8,128)S(1)} async-done(((f32[32,16,128]{2,1,0:T(8,128)}), f32[32,16,128]{2,1,0:T(8,128)S(1)}, u32[]{:S(2)}, u32[]{:S(2)}) %all-to-all-start.7) | async-done | bytes 262176 | tf_op jit(solution)/shard_map/all_to_all | solution.py:44
  805.9 15.4 %collective-permute-done.15 = f32[4,320,128]{2,1,0:T(8,128)S(1)} collective-permute-done((f32[4,320,128]{2,1,0:T(8,128)S(1)}, f32[4,320,128]{2,1,0:T(8,128)S(1)}, u32[]{:S(2)}, u32[]{:S(2)}) %collective-permute-start.15) | collective-permute-done | bytes 655392 | tf_op jit(solution)/shard_map/ppermute | solution.py:49
  901.3 16.7 %all-to-all-done.14 = bf16[8,128,512]{2,1,0:T(8,128)(2,1)S(1)} async-done(((bf16[8,128,512]{2,1,0:T(8,128)(2,1)}), bf16[8,128,512]{2,1,0:T(8,128)(2,1)S(1)}, u32[]{:S(2)}, u32[]{:S(2)}) %all-to-all-start.14) | async-done | bytes 1048608 | tf_op jit(solution)/shard_map/all_to_all | solution.py:851
  (434 shorter events, 299.2 us)
Async XLA Ops:
  7.2 88.3 %all-gather.10.cloned.1.call-start = ((), (), s32[]{:S(2)}) async-start(), calls=%async_computation.17 | async-start | bytes 9191424 | tf_op jit(solution)/shard_map/all_gather | solution.py:889
  11.4 178.3 %all-gather.12.cloned.1.call-start = ((), (), s32[]{:S(2)}) async-start(), calls=%async_computation.18 | async-start | bytes 9191424 | tf_op jit(solution)/shard_map/all_gather | solution.py:889
  12.3 250.1 %all-gather.14.cloned.1.call-start = ((), (), s32[]{:S(2)}) async-start(), calls=%async_computation.19 | async-start | bytes 4325376 | tf_op jit(solution)/shard_map/all_gather | solution.py:901
  15.8 88.2 %all-to-all-start.1 = ((f32[32,8,128]{2,1,0:T(8,128)}), f32[32,8,128]{2,1,0:T(8,128)S(1)}, u32[]{:S(2)}, u32[]{:S(2)}) async-start(f32[32,8,128]{2,1,0:T(8,128)} %broadcast_in_dim.31), calls=%async_computation.1 | async-start | bytes 262144 | tf_op jit(solution)/shard_map/all_to_all | solution.py:44
  104.0 12.6 %all-to-all-start = ((f32[32,8,128]{2,1,0:T(8,128)}), f32[32,8,128]{2,1,0:T(8,128)S(1)}, u32[]{:S(2)}, u32[]{:S(2)}) async-start(f32[32,8,128]{2,1,0:T(8,128)} %get-tuple-element.61), calls=%async_computation | async-start | bytes 262144 | tf_op jit(solution)/shard_map/all_to_all | solution.py:44
  154.8 34.9 %all-to-all-start.3 = ((f32[32,32,128]{2,1,0:T(8,128)}), f32[32,32,128]{2,1,0:T(8,128)S(1)}, u32[]{:S(2)}, u32[]{:S(2)}) async-start(f32[32,32,128]{2,1,0:T(8,128)} %get-tuple-element.65), calls=%async_computation.3 | async-start | bytes 1048576 | tf_op jit(solution)/shard_map/all_to_all | solution.py:44
  258.0 19.1 %all-to-all-start.6 = ((f32[32,32,128]{2,1,0:T(8,128)}), f32[32,32,128]{2,1,0:T(8,128)S(1)}, u32[]{:S(2)}, u32[]{:S(2)}) async-start(f32[32,32,128]{2,1,0:T(8,128)} %get-tuple-element.72), calls=%async_computation.6 | async-start | bytes 1048576 | tf_op jit(solution)/shard_map/all_to_all | solution.py:44
  348.3 11.6 %all-to-all-start.9 = ((f32[32,8,128]{2,1,0:T(8,128)}), f32[32,8,128]{2,1,0:T(8,128)S(1)}, u32[]{:S(2)}, u32[]{:S(2)}) async-start(f32[32,8,128]{2,1,0:T(8,128)} %get-tuple-element.79), calls=%async_computation.9 | async-start | bytes 262144 | tf_op jit(solution)/shard_map/all_to_all | solution.py:44
  375.9 16.7 %all-to-all-start.10 = ((f32[32,8,128]{2,1,0:T(8,128)}), f32[32,8,128]{2,1,0:T(8,128)S(1)}, u32[]{:S(2)}, u32[]{:S(2)}) async-start(f32[32,8,128]{2,1,0:T(8,128)} %get-tuple-element.82), calls=%async_computation.10 | async-start | bytes 262144 | tf_op jit(solution)/shard_map/all_to_all | solution.py:44
  380.9 376.3 %reduce-scatter.2.cloned.1.call-start = ((), (), s32[]{:S(2)}) async-start(), calls=%async_computation.16 | async-start | bytes 13516800 | tf_op jit(solution)/shard_map/reduce_scatter | solution.py:986
  433.4 28.0 %all-to-all-start.11 = ((f32[32,32,128]{2,1,0:T(8,128)}), f32[32,32,128]{2,1,0:T(8,128)S(1)}, u32[]{:S(2)}, u32[]{:S(2)}) async-start(f32[32,32,128]{2,1,0:T(8,128)} %get-tuple-element.85), calls=%async_computation.11 | async-start | bytes 1048576 | tf_op jit(solution)/shard_map/all_to_all | solution.py:44
  478.5 15.0 %all-to-all-start.12 = ((f32[32,8,128]{2,1,0:T(8,128)}), f32[32,8,128]{2,1,0:T(8,128)S(1)}, u32[]{:S(2)}, u32[]{:S(2)}) async-start(f32[32,8,128]{2,1,0:T(8,128)} %get-tuple-element.88), calls=%async_computation.12 | async-start | bytes 262144 | tf_op jit(solution)/shard_map/all_to_all | solution.py:44
  509.5 19.8 %all-to-all-start.13 = ((f32[32,8,128]{2,1,0:T(8,128)}), f32[32,8,128]{2,1,0:T(8,128)S(1)}, u32[]{:S(2)}, u32[]{:S(2)}) async-start(f32[32,8,128]{2,1,0:T(8,128)} %get-tuple-element.91), calls=%async_computation.13 | async-start | bytes 262144 | tf_op jit(solution)/shard_map/all_to_all | solution.py:44
  513.5 273.9 %all-gather.16.cloned.1.call-start = ((), (), s32[]{:S(2)}) async-start(), calls=%async_computation.20 | async-start | bytes 2785280 | tf_op jit(solution)/shard_map/all_gather | solution.py:801
  528.6 41.5 %collective-permute-start.5 = (bf16[2,8,576,128]{3,2,1,0:T(8,128)(2,1)}, bf16[2,8,576,128]{3,2,1,0:T(8,128)(2,1)}, u32[]{:S(2)}, u32[]{:S(2)}) collective-permute-start(bf16[2,8,576,128]{3,2,1,0:T(8,128)(2,1)} %dynamic-slice_bitcast_fusion), channel_id=1, source_target_pairs={{0,1},{1,0},{2,3},{3,2},{4,5},{5,4},{6,7},{7,6},{8,9},{9,8},{10,11... | collective-permute-start | bytes 7077896 | tf_op jit(solution)/shard_map/ppermute | solution.py:49
  529.0 16.0 %collective-permute-start.10 = (bf16[2,8,256,128]{3,2,1,0:T(8,128)(2,1)S(1)}, bf16[2,8,256,128]{3,2,1,0:T(8,128)(2,1)}, u32[]{:S(2)}, u32[]{:S(2)}) collective-permute-start(bf16[2,8,256,128]{3,2,1,0:T(8,128)(2,1)S(1)} %dynamic-slice_bitcast_fusion.2), channel_id=1, source_target_pairs={{0,1},{1,0},{2,3},{3,2},{4,5},{5,4},{6,7},{7,6},{8,9},{9,8},{10,11... | collective-permute-start | bytes 3145736 | tf_op jit(solution)/shard_map/ppermute | solution.py:49
  546.4 23.7 %collective-permute-start.11 = (bf16[4,2,256,128]{3,2,1,0:T(8,128)(2,1)S(1)}, bf16[4,2,256,128]{3,2,1,0:T(8,128)(2,1)S(1)}, u32[]{:S(2)}, u32[]{:S(2)}) collective-permute-start(bf16[4,2,256,128]{3,2,1,0:T(8,128)(2,1)S(1)} %dynamic-slice_bitcast_fusion.6), channel_id=1, source_target_pairs={{0,8},{1,9},{2,10},{3,11},{4,12},{5,13},{6,14},{7,15},{8,0},{9,1},... | collective-permute-start | bytes 1572872 | tf_op jit(solution)/shard_map/ppermute | solution.py:49
  574.2 80.2 %collective-permute-start.6 = (bf16[8,1,576,128]{3,2,0,1:T(8,128)(2,1)}, bf16[8,1,576,128]{3,2,0,1:T(8,128)(2,1)}, u32[]{:S(2)}, u32[]{:S(2)}) collective-permute-start(bf16[8,1,576,128]{3,2,0,1:T(8,128)(2,1)} %dynamic-slice_bitcast_fusion.1), channel_id=1, source_target_pairs={{0,4},{1,5},{2,6},{3,7},{4,0},{5,1},{6,2},{7,3},{8,12},{9,13},{10,... | collective-permute-start | bytes 3538952 | tf_op jit(solution)/shard_map/ppermute | solution.py:49
  578.0 19.6 %collective-permute-start.12 = (bf16[2,2,256,128]{3,2,1,0:T(8,128)(2,1)}, bf16[2,2,256,128]{3,2,1,0:T(8,128)(2,1)}, u32[]{:S(2)}, u32[]{:S(2)}) collective-permute-start(bf16[2,2,256,128]{3,2,1,0:T(8,128)(2,1)} %dynamic-slice_bitcast_fusion.9), channel_id=1, source_target_pairs={{0,16},{1,17},{2,18},{3,19},{4,20},{5,21},{6,22},{7,23},{8,24},{9,... | collective-permute-start | bytes 786440 | tf_op jit(solution)/shard_map/ppermute | solution.py:49
  581.2 18.6 %collective-permute-start.1 = (bf16[1,8,256,128]{3,2,1,0:T(8,128)(2,1)}, bf16[1,8,256,128]{3,2,1,0:T(8,128)(2,1)}, u32[]{:S(2)}, u32[]{:S(2)}) collective-permute-start(bf16[1,8,256,128]{3,2,1,0:T(8,128)(2,1)} %constant_dynamic-slice_fusion.6), channel_id=1, source_target_pairs={{0,2},{1,3},{2,0},{3,1},{4,6},{5,7},{6,4},{7,5},{8,10},{9,11},{10,... | collective-permute-start | bytes 1572872 | tf_op jit(solution)/shard_map/ppermute | solution.py:49
  598.7 59.8 %collective-permute-start.13 = (bf16[1,2,256,128]{3,2,1,0:T(8,128)(2,1)S(1)}, bf16[1,2,256,128]{3,2,1,0:T(8,128)(2,1)S(1)}, u32[]{:S(2)}, u32[]{:S(2)}) collective-permute-start(bf16[1,2,256,128]{3,2,1,0:T(8,128)(2,1)S(1)} %constant_dynamic-slice_fusion.3), channel_id=1, source_target_pairs={{0,2},{1,3},{2,0},{3,1},{4,6},{5,7},{6,4},{7,5},{8,10},{9,11},{10,... | collective-permute-start | bytes 393224 | tf_op jit(solution)/shard_map/ppermute | solution.py:49
  600.9 70.0 %collective-permute-start.2 = (bf16[4,1,256,128]{3,2,0,1:T(8,128)(2,1)S(1)}, bf16[4,1,256,128]{3,2,0,1:T(8,128)(2,1)S(1)}, u32[]{:S(2)}, u32[]{:S(2)}) collective-permute-start(bf16[4,1,256,128]{3,2,0,1:T(8,128)(2,1)S(1)} %dynamic-slice_bitcast_fusion.10), channel_id=1, source_target_pairs={{0,4},{1,5},{2,6},{3,7},{4,0},{5,1},{6,2},{7,3},{8,12},{9,13},{10,... | collective-permute-start | bytes 786440 | tf_op jit(solution)/shard_map/ppermute | solution.py:49
  655.8 23.1 %collective-permute-start.7 = (bf16[4,1,576,128]{3,2,0,1:T(8,128)(2,1)S(1)}, bf16[4,1,576,128]{3,2,0,1:T(8,128)(2,1)S(1)}, u32[]{:S(2)}, u32[]{:S(2)}) collective-permute-start(bf16[4,1,576,128]{3,2,0,1:T(8,128)(2,1)S(1)} %dynamic-slice_bitcast_fusion.5), channel_id=1, source_target_pairs={{0,8},{1,9},{2,10},{3,11},{4,12},{5,13},{6,14},{7,15},{8,0},{9,1},... | collective-permute-start | bytes 1769480 | tf_op jit(solution)/shard_map/ppermute | solution.py:49
  658.6 51.4 %collective-permute-start.14 = (bf16[1,1,256,128]{3,2,1,0:T(8,128)(2,1)S(1)}, bf16[1,1,256,128]{3,2,1,0:T(8,128)(2,1)S(1)}, u32[]{:S(2)}, u32[]{:S(2)}) collective-permute-start(bf16[1,1,256,128]{3,2,1,0:T(8,128)(2,1)S(1)} %constant_dynamic-slice_fusion.2), channel_id=1, source_target_pairs={{0,4},{1,5},{2,6},{3,7},{4,0},{5,1},{6,2},{7,3},{8,12},{9,13},{10,... | collective-permute-start | bytes 196616 | tf_op jit(solution)/shard_map/ppermute | solution.py:49
  671.1 14.6 %collective-permute-start.3 = (bf16[2,1,256,128]{3,2,0,1:T(8,128)(2,1)S(1)}, bf16[2,1,256,128]{3,2,0,1:T(8,128)(2,1)S(1)}, u32[]{:S(2)}, u32[]{:S(2)}) collective-permute-start(bf16[2,1,256,128]{3,2,0,1:T(8,128)(2,1)S(1)} %dynamic-slice_bitcast_fusion.11), channel_id=1, source_target_pairs={{0,8},{1,9},{2,10},{3,11},{4,12},{5,13},{6,14},{7,15},{8,0},{9,1},... | collective-permute-start | bytes 393224 | tf_op jit(solution)/shard_map/ppermute | solution.py:49
  679.0 24.3 %collective-permute-start.8 = (bf16[2,1,576,128]{3,2,1,0:T(8,128)(2,1)S(1)}, bf16[2,1,576,128]{3,2,1,0:T(8,128)(2,1)S(1)}, u32[]{:S(2)}, u32[]{:S(2)}) collective-permute-start(bf16[2,1,576,128]{3,2,1,0:T(8,128)(2,1)S(1)} %dynamic-slice_bitcast_fusion.8), channel_id=1, source_target_pairs={{0,16},{1,17},{2,18},{3,19},{4,20},{5,21},{6,22},{7,23},{8,24},{9,... | collective-permute-start | bytes 884744 | tf_op jit(solution)/shard_map/ppermute | solution.py:49
  685.7 19.8 %collective-permute-start.4 = (bf16[1,1,256,128]{3,2,0,1:T(8,128)(2,1)S(1)}, bf16[1,1,256,128]{3,2,0,1:T(8,128)(2,1)S(1)}, u32[]{:S(2)}, u32[]{:S(2)}) collective-permute-start(bf16[1,1,256,128]{3,2,0,1:T(8,128)(2,1)S(1)} %constant_dynamic-slice_fusion.5), channel_id=1, source_target_pairs={{0,16},{1,17},{2,18},{3,19},{4,20},{5,21},{6,22},{7,23},{8,24},{9,... | collective-permute-start | bytes 196616 | tf_op jit(solution)/shard_map/ppermute | solution.py:49
  761.2 16.7 %all-to-all-start.7 = ((f32[32,16,128]{2,1,0:T(8,128)}), f32[32,16,128]{2,1,0:T(8,128)S(1)}, u32[]{:S(2)}, u32[]{:S(2)}) async-start(f32[32,16,128]{2,1,0:T(8,128)} %get-tuple-element.73), calls=%async_computation.7 | async-start | bytes 524288 | tf_op jit(solution)/shard_map/all_to_all | solution.py:44
  804.3 17.0 %collective-permute-start.15 = (f32[4,320,128]{2,1,0:T(8,128)S(1)}, f32[4,320,128]{2,1,0:T(8,128)S(1)}, u32[]{:S(2)}, u32[]{:S(2)}) collective-permute-start(f32[4,320,128]{2,1,0:T(8,128)S(1)} %dynamic-slice_bitcast_fusion.4), channel_id=1, source_target_pairs={{0,4},{1,5},{2,6},{3,7},{4,0},{5,1},{6,2},{7,3},{8,12},{9,13},{10,... | collective-permute-start | bytes 1966088 | tf_op jit(solution)/shard_map/ppermute | solution.py:49
  821.4 9.1 collective-permute-start.16
  830.6 9.1 collective-permute-start.17
  886.7 31.3 %all-to-all-start.14 = ((bf16[8,128,512]{2,1,0:T(8,128)(2,1)}), bf16[8,128,512]{2,1,0:T(8,128)(2,1)S(1)}, u32[]{:S(2)}, u32[]{:S(2)}) async-start(bf16[8,128,512]{2,1,0:T(8,128)(2,1)} %broadcast_in_dim.34), calls=%async_computation.15 | async-start | bytes 2097152 | tf_op jit(solution)/shard_map/all_to_all | solution.py:851
  (70 other events, 1604.2 us)
Sparse Core Ops, SparseCore 0:
  11.5 83.9 all-gather.9
  98.9 90.7 all-gather.11
  193.1 62.3 all-gather.13
  433.6 323.6 reduce-scatter.1
  761.3 26.0 all-gather.15

commit v3 on v2

--- a/solution.py
+++ b/solution.py
@@ -49,19 +49,67 @@
     return lax.ppermute(values, AXES, [(src, src ^ (1 << bit)) for src in range(count)])
 
 
-def halving_sum(blocks, left, order):
-    count, rows, lanes = blocks.shape
-    left = list(left)
-    values = blocks
-    for bit in order:
-        place = left.index(bit)
-        values = values.reshape(2**place, 2, -1, rows, lanes)
-        own = (my_index() >> bit) & 1
-        kept = lax.dynamic_index_in_dim(values, own, 1, keepdims=False)
-        sent = lax.dynamic_index_in_dim(values, 1 - own, 1, keepdims=False)
-        values = kept + swap(sent, bit)
-        left.pop(place)
-    return values.reshape(rows, lanes)
+def half_of(values, place, side):
+    split = values.reshape((2**place, 2, -1) + values.shape[1:])
+    picked = lax.dynamic_index_in_dim(split, side, 1, keepdims=False)
+    return picked.reshape((-1,) + values.shape[1:])
+
+
+class Flow:
+    def __init__(self, pairs, left, order):
+        self.left, self.order = [bit for bit in left if bit != order[0]], list(order[1:])
+        self.kept = [kept for kept, _ in pairs]
+        self.sent = [sent for _, sent in pairs]
+        self.bit = order[0]
+        self.values = self.got = None
+
+    def send(self):
+        self.got = [swap(sent, self.bit) for sent in self.sent]
+        self.sent = None
+
+    def add(self):
+        if self.values is None:
+            parts = [kept + got for kept, got in zip(self.kept, self.got)]
+            self.values = parts[0] if len(parts) == 1 else jnp.concatenate(parts, axis=1)
+        else:
+            self.values = half_of(self.values, self.place, self.own) + self.got[0]
+        self.got = None
+
+    def split(self):
+        if self.order:
+            self.bit = self.order.pop(0)
+            self.place = self.left.index(self.bit)
+            self.left.pop(self.place)
+            self.own = (my_index() >> self.bit) & 1
+            self.sent = [half_of(self.values, self.place, 1 - self.own)]
+
+    def turn(self):
+        if self.got is not None:
+            self.add()
+            self.split()
+        if self.sent is not None:
+            self.send()
+
+    def result(self):
+        while self.got is not None or self.sent is not None:
+            self.turn()
+        return self.values[0] if self.values.shape[0] == 1 else self.values
+
+
+def advance(ahead, flows):
+    got = [flow.got for flow in flows]
+    ahead, got = lax.optimization_barrier((ahead, got))
+    for flow, values in zip(flows, got):
+        flow.got = values
+        if values is not None:
+            flow.add()
+            flow.split()
+    ahead, sent = lax.optimization_barrier((ahead, [flow.sent for flow in flows]))
+    for flow, values in zip(flows, sent):
+        flow.sent = values
+        if values is not None:
+            flow.send()
+    return ahead
 
 
 def bits_of(dp_size, owner_size):
@@ -92,8 +140,7 @@
     return jnp.concatenate([table[start + i : start + i + 1, :] for i in range(count)], axis=1)
 
 
-def send_rows(out_ref, rows):
-    place = 0
+def send_rows(out_ref, rows, place=0):
     for row in rows:
         for i in range(row.shape[1] // LANES):
             piece = row[:, i * LANES : (i + 1) * LANES]
@@ -118,28 +165,70 @@
 
 
 class Weights:
-    def __init__(self, array, start, rows):
-        self.array, self.start, self.rows = array, start, rows
-        self.blocks, self.owners = array.shape[0], array.shape[1]
-        self.depth = self.blocks * rows
-        self.width = self.owners * LANES
+    def __init__(self, operands, blocks, rows, dp_size, owners, masked):
+        self.operands, self.blocks, self.rows, self.masked = operands, blocks, rows, masked
+        self.owners = owners
+        self.depth, self.width = dp_size * rows, owners * LANES
 
     def scratch(self):
-        return [
-            pltpu.VMEM((self.depth, self.width), BF16),
-            pltpu.SemaphoreType.DMA((self.blocks * self.owners,)),
-        ]
-
-    def copies(self, ref, buffer, sems):
-        return [
-            pltpu.make_async_copy(
-                ref.at[d, o, pl.ds(self.start, self.rows)],
-                buffer.at[pl.ds(d * self.rows, self.rows), pl.ds(o * LANES, LANES)],
-                sems.at[d * self.owners + o],
+        return [pltpu.VMEM((self.depth, self.width), BF16), pltpu.SemaphoreType.DMA((len(self.blocks),))]
+
+    def copies(self, refs, buffer, sems):
+        shift = self.owners.bit_length() - 1
+        me = (lax.axis_index("dp") << shift) | lax.axis_index("owner") if self.masked else 0
+        out = []
+        for number, (operand, index, start, rows, device, offset) in enumerate(self.blocks):
+            device = me ^ device
+            base, lane = (device >> shift) * self.rows + offset, (device & (self.owners - 1)) * LANES
+            if self.masked:
+                base, lane = pl.multiple_of(base, 16), pl.multiple_of(lane, LANES)
+            out.append(
+                pltpu.make_async_copy(
+                    refs[operand].at[index + (pl.ds(start, rows),)],
+                    buffer.at[pl.ds(base, rows), pl.ds(lane, LANES)],
+                    sems.at[number],
+                )
             )
-            for d in range(self.blocks)
-            for o in range(self.owners)
-        ]
+        return out
+
+
+def gathered_weights(array, start, rows):
+    dp_size, owners = array.shape[:2]
+    blocks = [(0, (d, o), start, rows, d * owners + o, 0) for d in range(dp_size) for o in range(owners)]
+    return Weights([array], blocks, rows, dp_size, owners, False)
+
+
+def relative_weights(pieces, rows, dp_size, owners):
+    operands, blocks = [], []
+    for arrays, masks, start, height, offset in pieces:
+        for array, names in zip(arrays, masks):
+            for index, mask in enumerate(names):
+                blocks.append((len(operands), (index,), start, height, mask, offset))
+            operands.append(array)
+    return Weights(operands, blocks, rows, dp_size, owners, True)
+
+
+class Gather:
+    def __init__(self, block, order):
+        self.values, self.masks, self.order = block[None], [0], list(order)
+
+    def send(self):
+        self.bit = self.order.pop(0)
+        self.got = swap(self.values, self.bit)
+
+    def join(self):
+        more = [mask ^ (1 << self.bit) for mask in self.masks]
+        if self.order:
+            self.values, self.masks = jnp.concatenate([self.values, self.got], axis=0), self.masks + more
+        else:
+            self.values, self.masks = [self.values, self.got], [self.masks, more]
+
+
+def meet(flows):
+    got = lax.optimization_barrier([flow.got for flow in flows])
+    for flow, values in zip(flows, got):
+        flow.got = values
+        flow.join()
 
 
 def whole(shape):
@@ -155,12 +244,29 @@
 
 
 def launch(kernel, name, grid, operands, specs, outs, out_specs, scratch, flops):
-    moved = sum(math.prod(a.shape) * a.dtype.itemsize for a in jax.tree.leaves((operands, outs)))
+    arrays, flat_specs, groups = [], [], []
+    for operand, spec in zip(operands, specs):
+        group = operand.operands if isinstance(operand, Weights) else [operand]
+        groups.append(len(group) if isinstance(operand, Weights) else 0)
+        arrays += group
+        flat_specs += [spec] * len(group)
+
+    def grouped(*refs):
+        refs, firsts = list(refs), []
+        for count in groups:
+            if count:
+                firsts.append(tuple(refs[:count]))
+                refs = refs[count:]
+            else:
+                firsts.append(refs.pop(0))
+        kernel(*firsts, *refs)
+
+    moved = sum(math.prod(a.shape) * a.dtype.itemsize for a in jax.tree.leaves((arrays, outs)))
     return pl.pallas_call(
-        kernel,
+        grouped,
         name=name,
         grid=grid,
-        in_specs=specs,
+        in_specs=flat_specs,
         out_specs=out_specs,
         out_shape=outs,
         scratch_shapes=scratch,
@@ -168,7 +274,7 @@
         compiler_params=pltpu.CompilerParams(
             vmem_limit_bytes=60 * 2**20, dimension_semantics=("arbitrary",) * len(grid)
         ),
-    )(*operands)
+    )(*arrays)
 
 
 def out_of(shape, dtype):
@@ -192,6 +298,14 @@
 
 def dot_tn(left, right):
     return lax.dot_general(left, right, (((0,), (0,)), ((), ())), preferred_element_type=F32)
+
+
+def store_halves(kept_ref, sent_ref, place, values):
+    even = (lax.axis_index("owner") & 1) == 0
+    for pair in range(len(values) // 2):
+        first, second = values[2 * pair], values[2 * pair + 1]
+        kept_ref[(pair,) + place] = jnp.where(even, first, second).astype(BF16)
+        sent_ref[(pair,) + place] = jnp.where(even, second, first).astype(BF16)
 
 
 def first_reduce(images, masks, weights, devices):
@@ -225,7 +339,7 @@
     send = (devices, 2 * narrow // LANES, LANES)
     return launch(
         kernel, "reduce_first", (steps,),
-        (images, masks, weights.array),
+        (images, masks, weights),
         [strip(strip_rows, wide), strip(strip_rows, 2), ANYWHERE],
         (out_of((rows, narrow), F32), out_of(send, F32)),
         (strip(strip_rows, narrow), whole(send)),
@@ -299,7 +413,7 @@
     send = (devices, 2 * narrow // LANES, LANES)
     return launch(
         kernel, "spatial_conv", (steps,),
-        (hidden, parts, counts, norms, masks, weights.array),
+        (hidden, parts, counts, norms, masks, weights),
         [whole(hidden.shape), whole(parts.shape), whole(counts.shape), whole(norms.shape), whole(masks.shape), ANYWHERE],
         (out_of((rows, narrow), BF16), out_of((rows, narrow), F32), out_of((8, narrow), F32), out_of(send, F32)),
         (whole((rows, narrow)), strip(strip_rows, narrow), whole((8, narrow)), whole(send)),
@@ -349,7 +463,7 @@
     send = (devices, 2 * wide // LANES, LANES)
     return launch(
         kernel, "expand", (steps,),
-        (hidden, parts, counts, norms, masks, weights.array),
+        (hidden, parts, counts, norms, masks, weights),
         [strip(strip_rows, narrow), whole(parts.shape), whole(counts.shape), whole(norms.shape), strip(strip_rows, 2), ANYWHERE],
         (out_of((rows, narrow), BF16), out_of((rows, wide), F32), out_of((8, narrow), F32), out_of(send, F32)),
         (strip(strip_rows, narrow), strip(strip_rows, wide), whole((8, narrow)), whole(send)),
@@ -402,7 +516,7 @@
     send = (devices, 2 * narrow // LANES, LANES)
     return launch(
         kernel, "close_and_reduce", (steps,),
-        (hidden, inputs, parts, counts, norms, masks, weights.array),
+        (hidden, inputs, parts, counts, norms, masks, weights),
         [strip(strip_rows, wide), strip(strip_rows, wide), whole(parts.shape), whole(counts.shape), whole(norms.shape), strip(strip_rows, 2), ANYWHERE],
         (out_of((rows, wide), F32), out_of((rows, wide), BF16), out_of((rows, narrow), F32), out_of((8, wide), F32), out_of(send, F32)),
         (strip(strip_rows, wide), strip(strip_rows, wide), strip(strip_rows, narrow), whole((8, wide)), whole(send)),
@@ -422,7 +536,7 @@
 
     def kernel(
         h_ref, x_ref, parts_ref, count_ref, norm_ref, mask_ref, head_ref, bias_ref, image_ref,
-        ds_ref, stat_ref, send_ref, extra_ref, grad_ref, summed, pooled, sums,
+        ds_ref, stat_ref, send_ref, kept_ref, sent_ref, summed, pooled, sums,
     ):
         step = pl.program_id(0)
         gain = norm_ref[0, layer : layer + 1, norm_ref.shape[2] - wide :]
@@ -466,19 +580,20 @@
             loss = jnp.sum(weight * (log_total - picked), axis=0, keepdims=True)
             residue = weight * (jnp.exp(logits - log_total) - onehot)
             send_rows(
-                extra_ref,
+                send_ref,
                 [jnp.sum(residue, axis=0, keepdims=True), jnp.broadcast_to(loss, (1, 8 * LANES))],
+                2 * wide // LANES,
             )
             grad = (residue / count_ref[1:2, 0:1]).astype(BF16)
             for d in range(dp_size):
-                back = None
+                back, weight_parts = None, []
                 for o in range(owners):
                     mine = grad[:, o * slots : (o + 1) * slots]
                     part = dot_nn(mine, head_ref[d, o])
                     back = part if back is None else back + part
-                    weight_part = dot_tn(mine, low[:, d * cols : (d + 1) * cols]).astype(BF16)
-                    for i in range(grad_ref.shape[2]):
-                        grad_ref[o, d, i] = weight_part[:, i * tile : (i + 1) * tile]
+                    weight_parts.append(dot_tn(mine, low[:, d * cols : (d + 1) * cols]))
+                for i in range(kept_ref.shape[2]):
+                    store_halves(kept_ref, sent_ref, (d, i), [part[:, i * tile : (i + 1) * tile] for part in weight_parts])
                 pooled[:, d * cols : (d + 1) * cols] = back * (1.0 / pixels)
 
         @pl.when(step >= steps)
@@ -495,9 +610,8 @@
         def _():
             send_rows(send_ref, [jnp.sum(sums[i * 8 : i * 8 + 8], axis=0, keepdims=True) for i in range(2)])
 
-    send = (devices, 2 * wide // LANES, LANES)
-    extra = (devices, count_rows, LANES)
-    grads = (owners, dp_size, cols // tile, slots, tile)
+    send = (devices, 2 * wide // LANES + count_rows, LANES)
+    grads = (owners // 2, dp_size, cols // tile, slots, tile)
     again = pl.BlockSpec((zone, wide), lambda i: (lax.rem(i, steps), 0))
     once = pl.BlockSpec((zone, wide), lambda i: (jnp.minimum(i, steps - 1), 0))
     later = pl.BlockSpec((zone, wide), lambda i: (jnp.maximum(i - steps, 0), 0))
@@ -509,8 +623,8 @@
             pl.BlockSpec((zone, 2), lambda i: (lax.rem(i, steps), 0)),
             whole(head_all.shape), whole(slot_bias.shape), whole(image_cols.shape),
         ],
-        (out_of((rows, wide), F32), out_of((8, wide), F32), out_of(send, F32), out_of(extra, F32), out_of(grads, BF16)),
-        (later, whole((8, wide)), whole(send), whole(extra), whole(grads)),
+        (out_of((rows, wide), F32), out_of((8, wide), F32), out_of(send, F32), out_of(grads, BF16), out_of(grads, BF16)),
+        (later, whole((8, wide)), whole(send), whole(grads), whole(grads)),
         [pltpu.VMEM((rows, wide), F32), pltpu.VMEM((images, wide), F32), pltpu.VMEM((16, wide), F32)],
         6 * images * classes * wide,
     )
@@ -565,7 +679,7 @@
     send = (devices, 2 * narrow // LANES, LANES)
     return launch(
         kernel, "back_expand", (steps,),
-        (ds, hidden, parts, stat_wide, counts, norms, masks, narrow_hidden, stat_narrow, weights.array),
+        (ds, hidden, parts, stat_wide, counts, norms, masks, narrow_hidden, stat_narrow, weights),
         [
             strip(strip_rows, wide), strip(strip_rows, wide), whole(parts.shape), whole(stat_wide.shape), whole(counts.shape),
             whole(norms.shape), strip(strip_rows, 2), strip(strip_rows, narrow), whole(stat_narrow.shape), ANYWHERE,
@@ -639,7 +753,7 @@
     send = (devices, 2 * narrow // LANES, LANES)
     return launch(
         kernel, "back_conv", (steps,),
-        (dz, hidden, parts, stat_two, counts, norms, masks, first_hidden, stat_one, weights.array),
+        (dz, hidden, parts, stat_two, counts, norms, masks, first_hidden, stat_one, weights),
         [
             whole(dz.shape), whole(hidden.shape), whole(parts.shape), whole(stat_two.shape), whole(counts.shape),
             whole(norms.shape), whole(masks.shape), strip(strip_rows, narrow), whole(stat_one.shape), ANYWHERE,
@@ -697,7 +811,7 @@
     send = (devices, 2 * wide // LANES, LANES)
     return launch(
         kernel, "back_reduce", (steps,),
-        (dz, first_hidden, parts, stat_one, counts, norms, masks, ds, hidden, inputs, stat_wide, weights.array),
+        (dz, first_hidden, parts, stat_one, counts, norms, masks, ds, hidden, inputs, stat_wide, weights),
         [
             strip(strip_rows, narrow), strip(strip_rows, narrow), whole(parts.shape), whole(stat_one.shape), whole(counts.shape),
             whole(norms.shape), strip(strip_rows, 2), strip(strip_rows, wide), strip(strip_rows, wide), strip(strip_rows, wide),
@@ -741,17 +855,19 @@
     narrow = right.shape[1]
     tile = min(depth, 512)
 
-    def kernel(left_ref, right_ref, out_ref):
-        total = dot_tn(left_ref[...], right_ref[...]).astype(BF16)
-        for o in range(owners):
-            out_ref[o] = total[:, o * LANES : (o + 1) * LANES]
+    def kernel(left_ref, right_ref, kept_ref, sent_ref):
+        total = dot_tn(left_ref[...], right_ref[...])
+        store_halves(kept_ref, sent_ref, (), [total[:, o * LANES : (o + 1) * LANES] for o in range(owners)])
+
+    half = out_of((owners // 2, depth, LANES), BF16)
+    half_spec = pl.BlockSpec((owners // 2, tile, LANES), lambda i: (0, i, 0))
 
     return launch(
         kernel, "weight_grad", (depth // tile,),
         (left, right),
         [pl.BlockSpec((rows, tile), lambda i: (0, i)), whole(right.shape)],
-        out_of((owners, depth, LANES), BF16),
-        pl.BlockSpec((owners, tile, LANES), lambda i: (0, i, 0)),
+        (half, half),
+        (half_spec, half_spec),
         [],
         2 * rows * depth * narrow,
     )
@@ -760,7 +876,7 @@
 def spatial_grad(act, right, owners, zone):
     rows, narrow = act.shape
 
-    def kernel(act_ref, right_ref, out_ref, shifted):
+    def kernel(act_ref, right_ref, kept_ref, sent_ref, shifted):
         tap = pl.program_id(0)
 
         @pl.when(tap == 0)
@@ -777,79 +893,194 @@
 
         for tap_col in range(3):
             piece = shifted[pl.ds(pl.multiple_of(tap * zone, zone), rows), tap_col * narrow : (tap_col + 1) * narrow]
-            total = dot_tn(piece, right_ref[...]).astype(BF16)
-            for o in range(owners):
-                out_ref[o, tap_col * narrow : (tap_col + 1) * narrow] = total[:, o * LANES : (o + 1) * LANES]
+            total = dot_tn(piece, right_ref[...])
+            place = (slice(tap_col * narrow, (tap_col + 1) * narrow),)
+            store_halves(kept_ref, sent_ref, place, [total[:, o * LANES : (o + 1) * LANES] for o in range(owners)])
+
+    half = out_of((owners // 2, 9 * narrow, LANES), BF16)
+    half_spec = pl.BlockSpec((owners // 2, 3 * narrow, LANES), lambda i: (0, i, 0))
 
     return launch(
         kernel, "spatial_grad", (3,),
         (act, right),
         [whole(act.shape), whole(right.shape)],
-        out_of((owners, 9 * narrow, LANES), BF16),
-        pl.BlockSpec((owners, 3 * narrow, LANES), lambda i: (0, i, 0)),
+        (half, half),
+        (half_spec, half_spec),
         [pltpu.VMEM((rows + 2 * zone, 3 * narrow), BF16)],
         2 * rows * 9 * narrow * narrow,
     )
 
 
-def newton_schulz(moments):
-    dp_size, owner_size = lax.axis_size("dp"), lax.axis_size("owner")
-    owner = lax.axis_index("owner")
-    cols = [moment.shape[0] for moment in moments]
-    lanes = moments[0].shape[1]
-    low = jnp.concatenate([moment.astype(jnp.bfloat16) for moment in moments], axis=0)
-    all_rows = lax.all_gather(low, "owner")
-    all_rows = all_rows.transpose(1, 0, 2).reshape(low.shape[0], owner_size * lanes)
-    pieces, start = [], 0
-    for size in cols:
-        pieces.append(all_rows[start : start + size])
-        start += size
-    side = owner_size * lanes
-    pairs = [(i, j) for i in range(owner_size) for j in range(i, owner_size)]
-    packed = []
-    for piece in pieces:
-        gram = dot_tn(piece, piece)
-        blocks = [gram[i * lanes : (i + 1) * lanes, j * lanes : (j + 1) * lanes] for i, j in pairs]
-        packed.append(jnp.concatenate(blocks, axis=0))
-    rows = packed[0].shape[0] // owner_size
-    stack = jnp.stack(packed + [jnp.zeros_like(packed[0])] * (dp_size - len(packed)))
-    mine = lax.dynamic_slice_in_dim(stack, owner * rows, rows, axis=1)
-    bits = [bit for bit in range(device_count().bit_length() - 1) if (1 << bit) >= owner_size]
-    values = mine
-    for bit in bits:
-        place = dp_size.bit_length() - 1 - (len(bits) - bits.index(bit))
-        own = (my_index() >> bit) & 1
-        values = values.reshape(-1, 2, rows, lanes)
-        kept = lax.dynamic_index_in_dim(values, own, 1, keepdims=False)
-        sent = lax.dynamic_index_in_dim(values, 1 - own, 1, keepdims=False)
-        values = kept + swap(sent, bit)
-    whole = lax.all_gather(values[0], "owner", tiled=True)
-    blocks = {}
-    for number, (i, j) in enumerate(pairs):
-        block = whole[number * lanes : (number + 1) * lanes]
-        blocks[i, j] = block
-        if i != j:
-            blocks[j, i] = block.T
-    gram = jnp.concatenate(
-        [jnp.concatenate([blocks[i, j] for j in range(owner_size)], axis=1) for i in range(owner_size)],
-        axis=0,
-    )
-    dot = lambda left, right: jnp.dot(left, right, precision=lax.Precision.HIGHEST)
-    eye = jnp.eye(side, dtype=jnp.float32)
-    factor = 1.0 / (jnp.sqrt(jnp.trace(gram)) + 1e-07)
-    gram = gram * (factor * factor)
-    product = None
-    for iteration in range(NS_STEPS):
-        square = dot(gram, gram)
-        poly = NS_A * eye + NS_B * gram + NS_C * square
-        if iteration < NS_STEPS - 1:
-            gram = dot(dot(gram, poly), poly)
-        product = poly if product is None else dot(product, poly)
-    product = (product * factor).astype(jnp.bfloat16)
-    own_rows = lax.dynamic_slice_in_dim(product, owner * lanes, lanes, axis=0)
-    copies = jnp.broadcast_to(own_rows[None], (dp_size,) + own_rows.shape)
-    products = lax.all_to_all(copies, "dp", 0, 0, tiled=True)
-    return [dot_nt(piece, products[number]) for number, piece in enumerate(pieces)]
+def padded(values):
+    return jnp.pad(values, ((0, -values.shape[0] % 16), (0, 0)))
+
+
+def gather_rows(moments_t):
+    low = [padded(moment.astype(BF16)) for moment in moments_t]
+    starts = [sum(part.shape[0] for part in low[:i]) for i in range(len(low))]
+    return lax.all_gather(jnp.concatenate(low, axis=0), "owner"), starts
+
+
+def upper_pairs(owners):
+    return [(i, j) for i in range(owners) for j in range(i, owners)]
+
+
+def own_grams(gathered, starts, sizes):
+    owners = gathered.shape[0]
+    pairs = upper_pairs(owners)
+    share = len(pairs) * LANES // owners
+
+    def kernel(all_ref, out_ref, packed):
+        for number, (start, size) in enumerate(zip(starts, sizes)):
+            for place, (i, j) in enumerate(pairs):
+                packed[place * LANES : (place + 1) * LANES] = dot_tn(
+                    all_ref[i, start : start + size, :], all_ref[j, start : start + size, :]
+                )
+            own = pl.multiple_of(lax.axis_index("owner") * share, 8)
+            out_ref[number] = packed[pl.ds(own, share), :]
+
+    shape = (len(sizes), share, LANES)
+    return launch(
+        kernel, "own_grams", (1,), (gathered,), [whole(gathered.shape)], out_of(shape, F32), whole(shape),
+        [pltpu.VMEM((len(pairs) * LANES, LANES), F32)], 2 * sum(sizes) * len(pairs) * LANES * LANES,
+    )
+
+
+def dp_bits():
+    low = lax.axis_size("owner").bit_length() - 1
+    return list(range(low, low + lax.axis_size("dp").bit_length() - 1))
+
+
+def bit_of(bit):
+    return (my_index() >> bit) & 1
+
+
+def keep_half(values, bit):
+    own = bit_of(bit)
+    half = values.shape[0] // 2
+    values = values.reshape((2, half) + values.shape[1:])
+    kept = lax.dynamic_index_in_dim(values, own, 0, keepdims=False)
+    sent = lax.dynamic_index_in_dim(values, 1 - own, 0, keepdims=False)
+    return kept + swap(sent, bit)
+
+
+def split_two(values):
+    high = values.astype(BF16)
+    return high, (values - high.astype(F32)).astype(BF16)
+
+
+def dot_fine(left, right):
+    return jnp.dot(left, right, precision=lax.Precision.HIGHEST, preferred_element_type=F32)
+
+
+def dot_split(left, right):
+    left_high, left_low = split_two(left)
+    right_high, right_low = split_two(right)
+    return dot_nn(left_high, right_high) + (dot_nn(left_high, right_low) + dot_nn(left_low, right_high))
+
+
+def polynomial(packed, owners):
+    side = owners * LANES
+    pairs = upper_pairs(owners)
+
+    def kernel(packed_ref, out_ref, gram, product):
+        for place, (i, j) in enumerate(pairs):
+            block = packed_ref[place * LANES : (place + 1) * LANES, :]
+            gram[i * LANES : (i + 1) * LANES, j * LANES : (j + 1) * LANES] = block
+            if i != j:
+                gram[j * LANES : (j + 1) * LANES, i * LANES : (i + 1) * LANES] = block.T
+        eye = (
+            lax.broadcasted_iota(jnp.int32, (side, side), 0) == lax.broadcasted_iota(jnp.int32, (side, side), 1)
+        ).astype(F32)
+        trace = jnp.sum(jnp.sum(gram[...] * eye, axis=0, keepdims=True), axis=1, keepdims=True)
+        factor = 1.0 / (jnp.sqrt(trace) + 1e-07)
+        first = gram[...] * (factor * factor)
+        poly = NS_A * eye + NS_B * first + NS_C * dot_fine(first, first)
+        gram[...] = dot_fine(dot_fine(first, poly), poly)
+        product[...] = poly * factor
+
+        def body(index, carry):
+            now = gram[...]
+            poly = NS_A * eye + NS_B * now + NS_C * dot_split(now, now)
+            gram[...] = dot_split(dot_split(now, poly), poly)
+            product[...] = dot_split(product[...], poly)
+            return carry
+
+        lax.fori_loop(0, NS_STEPS - 2, body, 0)
+        now = gram[...]
+        poly = NS_A * eye + NS_B * now + NS_C * dot_split(now, now)
+        own = pl.ds(pl.multiple_of(lax.axis_index("owner") * LANES, LANES), LANES)
+        out_ref[...] = dot_split(product[own, :], poly).astype(BF16)
+
+    return launch(
+        kernel, "polynomial", (1,), (packed,), [whole(packed.shape)], out_of((LANES, side), BF16), whole((LANES, side)),
+        [pltpu.VMEM((side, side), F32), pltpu.VMEM((side, side), F32)], 60 * 2 * side**3,
+    )
+
+
+def apply_polynomials(early, late, gathered, starts, products, masters):
+    owners = gathered[0].shape[0]
+    y_bit, z_bit = dp_bits()[:2]
+    shift = lax.axis_size("owner").bit_length() - 1
+    q_own, q_other, q_late = products
+    kinds = len(masters)
+
+    def kernel(own_ref, other_ref, late_ref, early_all, late_all, *refs):
+        sources, outs = refs[:kinds], refs[kinds:]
+        place = lax.axis_index("dp")
+        my_y = (place >> (y_bit - shift)) & 1
+        my_z = (place >> (z_bit - shift)) & 1
+
+        def finish(layer, kind, poly, all_ref, start):
+            size = sources[kind].shape[2]
+            total = None
+            for o in range(owners):
+                part = dot_nt(poly[:, o * LANES : (o + 1) * LANES], all_ref[o, start : start + size, :])
+                total = part if total is None else total + part
+            outs[kind][layer] = sources[kind][layer] * (1.0 - LR_MATRIX * DECAY_MATRIX) - LR_MATRIX * total
+
+        for number, (layer, kind) in enumerate(early):
+            y, z = number // 2, number % 2
+            turn = y ^ my_y
+            poly = jnp.where(my_z == z, own_ref[turn].astype(F32), other_ref[turn].astype(F32)).astype(BF16)
+            finish(layer, kind, poly, early_all, starts[0][number])
+        for number, (layer, kind) in enumerate(late):
+            finish(layer, kind, late_ref[number ^ my_y], late_all, starts[1][number])
+
+    operands = (q_own, q_other, q_late, gathered[0], gathered[1]) + masters
+    outs = tuple(out_of(master.shape, F32) for master in masters)
+    return launch(
+        kernel, "apply_polynomials", (1,), operands, [whole(a.shape) for a in operands], outs,
+        tuple(whole(master.shape) for master in masters), [], 2**31,
+    )
+
+
+def newton_schulz(early, late, moments_t, masters):
+    y_bit, z_bit, turn_bit = dp_bits()[:3]
+    gathered, starts, grams = [], [], []
+    for names in (early, late):
+        both, begin = gather_rows([moments_t[name] for name in names])
+        gathered.append(both)
+        starts.append(begin)
+        values = own_grams(both, begin, [moments_t[name].shape[0] for name in names])
+        for bit in dp_bits():
+            if values.shape[0] > 1:
+                values = keep_half(values, bit)
+            else:
+                values = values + swap(values, bit)
+        grams.append(values[0])
+    on_late = bit_of(turn_bit) == 1
+    mine = jnp.where(on_late, grams[1], grams[0])
+    packed = lax.all_gather(mine, "owner", tiled=True)
+    own = polynomial(packed, gathered[0].shape[0])
+    other = swap(own, turn_bit)
+    q_early = jnp.where(on_late, other, own)
+    q_late = jnp.where(on_late, own, other)
+    both = jnp.stack([q_early, q_late])
+    pair = jnp.stack([both, swap(both, y_bit)])
+    q_own, q_late = pair[:, 0], pair[:, 1]
+    q_other = swap(q_own, z_bit)
+    return apply_polynomials(early, late, gathered, starts, (q_own, q_other, q_late), masters)
 
 
 def adamw(weight, grad, first, second, rate, decay):
@@ -878,22 +1109,71 @@
     tallies = jnp.stack([valid_count[0] * pixels, jnp.sum(weight_img)]).astype(F32)
     tallies = jnp.pad(tallies, (0, 6))[:, None]
     counts = jnp.sum(exchange(jnp.broadcast_to(tallies[None], (devices, 8, LANES))), axis=0)
-    weight_total = counts[1, 0]
+
+    in_map = (jnp.arange(SLOT) < side).astype(F32)
+    pad_mask = jnp.broadcast_to(in_map, (side, count_img, SLOT))
+    masks = jnp.stack([pad_mask * valid.astype(F32)[:, None], pad_mask], axis=-1).reshape(rows, 2)
+    pixels_in = jnp.pad(images, ((0, 0), (0, 0), (0, SLOT - side), (0, 0))).transpose(1, 0, 2, 3).reshape(rows, wide)
 
     rows_of = (w_reduce.shape[2], w_spatial.shape[2], w_expand.shape[2])
     starts = (0, rows_of[0], rows_of[0] + rows_of[1])
+    packs = [
+        [part.T.astype(BF16) for part in (w_reduce[layer], w_spatial[layer], w_expand[layer])] for layer in range(LAYERS)
+    ]
     mats = []
-    for layer in range(LAYERS):
-        parts = (w_reduce[layer], w_spatial[layer], w_expand[layer])
-        packed = jnp.concatenate([part.T.astype(BF16) for part in parts], axis=0)
+    if dp_size == 8 and owner_size == 4:
+        first = Gather(packs[0][0], (4, 3, 2, 1, 0))
+        first.send()
+        first.join()
+        first.send()
+        halves = [[part[: part.shape[0] // 2], part[part.shape[0] // 2 :]] for part in packs[0][1:]]
+        sets = [jnp.concatenate([part[i] for part in halves], axis=0) for i in range(2)]
+        first.got, sets = lax.optimization_barrier((first.got, sets))
+        others = [Gather(sets[0], (4, 3, 1, 2, 0)), Gather(sets[1], (4, 2, 3, 1, 0))]
+        first.join()
+        first.send()
+        for flow in others:
+            flow.send()
+        meet([first] + others)
+        first.send()
+        for flow in others:
+            flow.send()
+        meet([first] + others)
+        first.values, pixels_in, masks, counts, packs[1] = lax.optimization_barrier(
+            (first.values, pixels_in, masks, counts, packs[1])
+        )
+        first.send()
+        for flow in others:
+            flow.send()
+        first.join()
+        mats.append(relative_weights([(first.values, first.masks, 0, rows_of[0], 0)], rows_of[0], dp_size, owner_size))
+        h1_first, sums = first_reduce(pixels_in, masks, mats[0], devices)
+        got, h1_first = lax.optimization_barrier(([flow.got for flow in others], h1_first))
+        for flow, values in zip(others, got):
+            flow.got = values
+            flow.join()
+        for _ in range(2):
+            for flow in others:
+                flow.send()
+            meet(others)
+        tops = (rows_of[1] // 2, rows_of[2] // 2)
+        for kind in (1, 2):
+            pieces = [
+                (others[i].values, others[i].masks, 0 if kind == 1 else tops[0], tops[kind - 1], i * tops[kind - 1])
+                for i in range(2)
+            ]
+            mats.append(relative_weights(pieces, rows_of[kind], dp_size, owner_size))
+    layers_done = len(mats) // 3
+    for layer in range(layers_done, LAYERS):
+        packed = jnp.concatenate(packs[layer], axis=0)
         gathered = lax.all_gather(packed, AXES).reshape(dp_size, owner_size, packed.shape[0], LANES)
         for kind in range(3):
             if dp_size <= 8:
-                mats.append(Weights(gathered, starts[kind], rows_of[kind]))
+                mats.append(gathered_weights(gathered, starts[kind], rows_of[kind]))
             else:
                 piece = gathered[:, :, starts[kind] : starts[kind] + rows_of[kind]]
                 piece = piece.transpose(1, 0, 2, 3).reshape(1, owner_size, -1, LANES)
-                mats.append(Weights(piece, 0, piece.shape[2]))
+                mats.append(gathered_weights(piece, 0, piece.shape[2]))
     classes = head.shape[0]
     slots = -(-classes // LANES) * LANES
     slack = slots - classes
@@ -907,15 +1187,14 @@
     slot_labels = (labels // classes) * slots + labels % classes
     image_cols = jnp.stack([slot_labels, weight_img], axis=1)
 
-    in_map = (jnp.arange(SLOT) < side).astype(F32)
-    pad_mask = jnp.broadcast_to(in_map, (side, count_img, SLOT))
-    masks = jnp.stack([pad_mask * valid.astype(F32)[:, None], pad_mask], axis=-1).reshape(rows, 2)
-    pixels_in = jnp.pad(images, ((0, 0), (0, 0), (0, SLOT - side), (0, 0))).transpose(1, 0, 2, 3).reshape(rows, wide)
-
+    weight_total = counts[1, 0]
     norms = norm_params
     h1, h2, h3, a1, a2, stat1, stat2, stat3 = ([None] * LAYERS for _ in range(8))
     inputs, inputs_low = [pixels_in] + [None] * (LAYERS - 1), [pixels_in] + [None] * (LAYERS - 1)
-    h1[0], sums = first_reduce(pixels_in, masks, mats[0], devices)
+    if layers_done:
+        h1[0] = h1_first
+    else:
+        h1[0], sums = first_reduce(pixels_in, masks, mats[0], devices)
     for layer in range(LAYERS):
         a1[layer], h2[layer], stat1[layer], sums = spatial_conv(
             h1[layer], exchange(sums), counts, norms, masks, mats[3 * layer + 1], layer, zone, devices
@@ -928,28 +1207,52 @@
                 h3[layer], inputs[layer], exchange(sums), counts, norms, masks, mats[3 * layer + 3], layer, devices
             )
     last = LAYERS - 1
-    ds, stat3[last], sums, extra, grad_head = head_step(
+    ds, stat3[last], sums, *head_halves = head_step(
         h3[last], inputs[last], exchange(sums), counts, norms, masks, head_all, slot_bias, image_cols, last, pixels, zone, devices
     )
-    extra = jnp.sum(exchange(extra), axis=0)
-    class_rows = owner_size * slots // LANES
-    bias_raw = extra[:class_rows].reshape(owner_size, slots)[:, :classes].reshape(-1)
-    loss_sum = extra[class_rows, 0]
-    grad_bias = bias_raw / weight_total
-
-    norm_sums, grads = ([], [])
+    left = bits_of(dp_size, owner_size)
+    rest = list(range(1, len(left)))
+    turned = [[0] + rest[turn:] + rest[:turn] for turn in range(3)]
+    if not aligned:
+        width = head.shape[1]
+        head_halves = [
+            jnp.pad(
+                half.reshape(owner_size // 2, wide // LANES, slots, LANES // width, width).transpose(0, 1, 3, 2, 4),
+                ((0, 0),) * 4 + ((0, LANES - width),),
+            )
+            for half in head_halves
+        ]
+    blocked = lambda halves: tuple(half.reshape(devices // 2, -1, LANES) for half in halves)
+    head_flow = Flow([blocked(head_halves)], left, turned[0])
+    flows = [head_flow]
+    norm_sums = []
+    wide_rows = 2 * wide // LANES
     for layer in reversed(range(LAYERS)):
         parts3 = exchange(sums)
+        if layer == last:
+            extra = parts3
+        parts3 = advance(parts3, flows)
         dh3, dz2, sums = back_expand(
             ds, h3[layer], parts3, stat3[layer], counts, norms, masks, h2[layer], stat2[layer], mats[3 * layer + 2], layer, devices
         )
-        grad_three = weight_grad(dh3, a2[layer], owner_size)
+        grad_three = blocked(weight_grad(dh3, a2[layer], owner_size))
+        if layer == 0:
+            three_flow = Flow([grad_three], left, turned[0])
+            flows.append(three_flow)
         parts2 = exchange(sums)
+        parts2 = advance(parts2, flows)
         dh2, dz1, sums = back_conv(
             dz2, h2[layer], parts2, stat2[layer], counts, norms, masks, h1[layer], stat1[layer], mats[3 * layer + 1], layer, zone, devices
         )
-        grad_two = spatial_grad(a1[layer], dh2, owner_size, zone)
+        grad_two = blocked(spatial_grad(a1[layer], dh2, owner_size, zone))
+        if layer > 0:
+            high_flow = Flow([grad_three, grad_two], left, turned[1])
+            flows.append(high_flow)
+        else:
+            two_flow = Flow([grad_two], left, [0])
+            flows.append(two_flow)
         parts1 = exchange(sums)
+        parts1 = advance(parts1, flows)
         if layer > 0:
             dh1, ds, sums = back_reduce(
                 dz1, h1[layer], parts1, stat1[layer], counts, norms, masks, ds, h3[layer - 1], inputs[layer - 1], stat3[layer - 1],
@@ -957,54 +1260,49 @@
             )
         else:
             dh1 = last_back(dz1, h1[layer], parts1, stat1[layer], counts, norms, masks, layer)
-        grad_one = weight_grad(inputs_low[layer], dh1, owner_size)
-        grads.insert(0, (grad_one, grad_two, grad_three))
-        norm_sums.insert(0, [jnp.sum(part, axis=0).reshape(2, -1) for part in (parts1, parts2, parts3)])
+        grad_one = blocked(weight_grad(inputs_low[layer], dh1, owner_size))
+        if layer > 0:
+            one_flow = Flow([grad_one], left, turned[2])
+            flows.append(one_flow)
+        norm_sums.insert(0, [jnp.sum(part, axis=0).reshape(2, -1) for part in (parts1, parts2, parts3[:, :wide_rows])])
     norm_grad = jnp.stack(
         [jnp.stack([jnp.concatenate([part[kind] for part in norm_sums[layer]]) for layer in range(LAYERS)]) for kind in (1, 0)]
     )
-
-    left = bits_of(dp_size, owner_size)
-    sums_of = []
-    for layer in range(LAYERS):
-        blocks = [grad.reshape(devices, -1, LANES) for grad in grads[layer]]
-        if layer == 0:
-            bits = list(range(1, len(left)))
-            pieces = []
-            for number, block in enumerate(blocks):
-                turn = number % len(bits)
-                pieces.append(halving_sum(block, left, [0] + bits[turn:] + bits[:turn]))
-            sums_of.append([piece.astype(F32) for piece in pieces])
-            continue
-        if aligned:
-            head_blocks = grad_head.reshape(devices, -1, LANES)
-        else:
-            head_blocks = grad_head.reshape(owner_size, wide // LANES, slots, LANES // head.shape[1], head.shape[1])
-            head_blocks = head_blocks.transpose(0, 1, 3, 2, 4).reshape(devices, slots, head.shape[1])
-        height = sum(rows_of)
-        if aligned:
-            total = lax.psum_scatter(jnp.concatenate(blocks + [head_blocks], axis=1), ("owner", "dp"), scatter_dimension=0).astype(F32)
-            head_sum = total[height:]
-        else:
-            total = lax.psum_scatter(jnp.concatenate(blocks, axis=1), ("owner", "dp"), scatter_dimension=0).astype(F32)
-            head_sum = lax.psum_scatter(head_blocks, ("owner", "dp"), scatter_dimension=0).astype(F32)
-        sums_of.append([total[starts[kind] : starts[kind] + rows_of[kind]] for kind in range(3)])
-        head_sum = head_sum.reshape(-1, slots, head_sum.shape[-1])[:, :classes].transpose(1, 0, 2).reshape(classes, -1)
+    extra = jnp.sum(extra[:, wide_rows:], axis=0)
+    class_rows = owner_size * slots // LANES
+    bias_raw = extra[:class_rows].reshape(owner_size, slots)[:, :classes].reshape(-1)
+    loss_sum = extra[class_rows, 0]
+    grad_bias = bias_raw / weight_total
+    last_flow = Flow([grad_one], left, [0])
+    low_sums = jnp.concatenate([two_flow.result(), last_flow.result()], axis=1)
+    remaining = [bit for bit in left if bit != 0]
+    height = low_sums.shape[1]
+    third = height // 3 // 16 * 16
+    cuts = [0, third, 2 * third, height]
+    thirds = []
+    for i in range(3):
+        order = turned[i][1:]
+        piece = low_sums[:, cuts[i] : cuts[i + 1]]
+        place = remaining.index(order[0])
+        own = (my_index() >> order[0]) & 1
+        thirds.append(Flow([(half_of(piece, place, own), half_of(piece, place, 1 - own))], remaining, order))
+    high, low = LAYERS - 1, 0
+    low_sums = jnp.concatenate([flow.result() for flow in thirds], axis=0)
+    two_low, one_low = low_sums[: rows_of[1]], low_sums[rows_of[1] :]
+    three_low, one_high = three_flow.result(), one_flow.result()
+    three_high, two_high = jnp.split(high_flow.result(), [rows_of[2]])
+    head_sum = head_flow.result().astype(F32).reshape(-1, slots, LANES)[:, :classes]
+    head_sum = head_sum.transpose(1, 0, 2).reshape(classes, -1)[:, : head.shape[1]]
 
     olds = (mom_reduce, mom_spatial, mom_expand)
-    moments_t = [MOMENTUM * olds[kind][layer].T + sums_of[layer][kind] for layer in range(LAYERS) for kind in range(3)]
-    directions_t = newton_schulz(moments_t)
-    moments, directions = (
-        [jnp.stack([values[layer * 3 + kind].T for layer in range(LAYERS)]) for kind in range(3)]
-        for values in (moments_t, directions_t)
-    )
-    masters = (w_reduce, w_spatial, w_expand)
-    updated = tuple(
-        (
-            master * (1.0 - LR_MATRIX * DECAY_MATRIX) - LR_MATRIX * direction
-            for master, direction in zip(masters, directions)
-        )
-    )
+    moment = lambda layer, kind, total: MOMENTUM * olds[kind][layer].T + total.astype(F32)
+    early = [(high, 2, three_high), (high, 1, two_high), (high, 0, one_high), (low, 2, three_low)]
+    late = [(low, 1, two_low), (low, 0, one_low)]
+    moments_t = {(layer, kind): moment(layer, kind, total) for layer, kind, total in early + late}
+    updated = newton_schulz(
+        [item[:2] for item in early], [item[:2] for item in late], moments_t, (w_reduce, w_spatial, w_expand)
+    )
+    moments = [jnp.stack([moments_t[layer, kind].T for layer in range(LAYERS)]) for kind in range(3)]
     new_head, new_head_m, new_head_v = adamw(head, head_sum, head_m, head_v, LR_HEAD, DECAY_HEAD)
     new_norm, new_norm_m, new_norm_v = adamw(norm_params, norm_grad, norm_m, norm_v, LR_VECTOR, 0.0)
     new_bias, new_bias_m, new_bias_v = adamw(head_bias, grad_bias, bias_m, bias_v, LR_VECTOR, 0.0)

time: 942 us -> 805 us (0.85)
  waiting for transfers between devices: 368 us -> 178 us
  matrix products: 40.4 us -> 0 us
  blocking collectives: 65.5 us -> 102 us
  Pallas kernels: 252 us -> 283 us
  starting transfers between devices: 82 us -> 101 us
  local copies, waits for them, and re-layouts: 57.6 us -> 69.8 us
    all_gather x2 -> x1, waiting for transfers between devices: 93.7 us -> 0.01 us  [per_device(): lax.all_gather(packed, AXES)]
    reduce_scatter x1 -> x0, waiting for transfers between devices: 46.5 us -> none  [per_device(): lax.psum_scatter(jnp.concatenate(blocks + [head_blocks], axis=1), ('owner...]
    dot_general x29 -> x0, matrix products: 40.4 us -> none  [the longest x17 34.4 us: newton_schulz(): jnp.dot(left, right, precision=lax.Precision.HIGHEST)]
    all_to_all x10 -> x8, waiting for transfers between devices: 58 us -> 23.8 us  [exchange(): return lax.all_to_all(copies, AXES, 0, 0, tiled=True)]
    ppermute x18 -> x59, starting transfers between devices: 29.3 us -> 62.5 us  [swap(): lax.ppermute(values, AXES, [(src, src ^ 1 << bit) for src in range(count)])]
    pallas_call x19 -> x23, Pallas kernels: 252 us -> 283 us  [launch(): pl.pallas_call(grouped, name=name, grid=grid, in_specs=flat_specs, out_sp...]
    all_to_all x4 -> x5, blocking collectives: 58.2 us -> 84.5 us  [exchange(): return lax.all_to_all(copies, AXES, 0, 0, tiled=True)]
    all_to_all x1 -> x0, waiting for transfers between devices: 16.7 us -> none  [newton_schulz(): products = lax.all_to_all(copies, 'dp', 0, 0, tiled=True)]
  transfers between devices with their start and end apart: 34 -> 70, of which waited for: 23 -> 38; matrix products, arithmetic and copies ran while one was open for 6% -> 9% of each run, Pallas kernels for 17% -> 28%
where the time goes in v3:
time: 805 us; the launch traced here: 793 us
  Pallas kernels  283 us (35%)
  waiting for transfers between devices  178 us (22%)
  blocking collectives  102 us (13%)
  starting transfers between devices  101 us (13%)
  local copies, waits for them, and re-layouts  69.8 us (9%)
  other arithmetic  43.6 us (5%)
  between operations  16.4 us (2%)
    pallas_call x23, Pallas kernels, launch(): pl.pallas_call(grouped, name=name, grid=grid, in_specs=flat_specs, out_sp...  283 us
    ppermute x59, waiting for transfers between devices, swap(): lax.ppermute(values, AXES, [(src, src ^ 1 << bit) for src in range(count)])  151 us
    all_to_all x5, blocking collectives, exchange(): return lax.all_to_all(copies, AXES, 0, 0, tiled=True)  84.5 us
    ppermute x59, starting transfers between devices, swap(): lax.ppermute(values, AXES, [(src, src ^ 1 << bit) for src in range(count)])  62.5 us
    all_to_all x8, starting transfers between devices, exchange(): return lax.all_to_all(copies, AXES, 0, 0, tiled=True)  37.7 us
    unnamed x168, local copies, waits for them, and re-layouts  34.4 us
    all_to_all x8, waiting for transfers between devices, exchange(): return lax.all_to_all(copies, AXES, 0, 0, tiled=True)  23.8 us
  transfers between devices with their start and end apart: 70, of which 38 were waited for; matrix products, arithmetic and copies ran while one was open for 9% of the time, Pallas kernels for 28%

profile of v3, /device:TPU:0, one launch (start us, length us, event | category | flops | bytes accessed | tf_op | source)
XLA Modules:
  0.0 793.3 jit_solution(8609992869420125133)
XLA Ops:
  38.7 8.4 %copy.180 = bf16[7,24,8,2048]{3,2,1,0:T(8,128)(2,1)} copy(bf16[7,24,8,2048]{3,1,2,0:T(8,128)(2,1)} %pad_bitcast_fusion) | data formatting | bytes 11010048 | tf_op jit(solution)/shard_map/transpose | solution.py:1116
  68.6 8.6 %reduce_first.1 = (f32[1344,512]{1,0:T(8,128)}, f32[32,8,128]{2,1,0:T(8,128)}) custom-call(bf16[1344,2048]{1,0:T(8,128)(2,1)} %bitcast.358, f32[1344,2]{1,0:T(8,128)} %copy.181.refs_1_.refs_4_.refs_5_.refs_6_, bf16[16,256,128]{2,1,0:T(8,128)(2,1)} %constant_dynamic-update-slice_fusion.refs_2_, bf16[16,256,128]{2,1,0:T(8,128)(2,1)} %collective-permute-done.10.refs_3_), custom_call_target="tpu_custom_call" | custom-call | flops 2818572288 | bytes 10496512 | tf_op jit(solution)/shard_map/reduce_first/pallas_call | solution.py:265
  84.6 23.7 %collective-permute-done.12 = bf16[8,416,128]{2,1,0:T(8,128)(2,1)S(1)} collective-permute-done((bf16[8,416,128]{2,1,0:T(8,128)(2,1)S(1)}, bf16[8,416,128]{2,1,0:T(8,128)(2,1)S(1)}, u32[]{:S(2)}, u32[]{:S(2)}) %collective-permute-start.12) | collective-permute-done | bytes 852000 | tf_op jit(solution)/shard_map/ppermute | solution.py:49
  114.7 8.1 %all-to-all-done.1.refs_1_ = f32[32,8,128]{2,1,0:T(8,128)S(1)} async-done(((f32[32,8,128]{2,1,0:T(8,128)}), f32[32,8,128]{2,1,0:T(8,128)S(1)}, u32[]{:S(2)}, u32[]{:S(2)}) %all-to-all-start.1) | async-done | bytes 131104 | tf_op jit(solution)/shard_map/all_to_all | solution.py:44
  123.5 13.6 %spatial_conv.2 = (bf16[1344,512]{1,0:T(8,128)(2,1)}, f32[1344,512]{1,0:T(8,128)}, f32[8,512]{1,0:T(8,128)}, f32[32,8,128]{2,1,0:T(8,128)}) custom-call(f32[1344,512]{1,0:T(8,128)} %get-tuple-element.150.refs_0_.refs_7_.refs_1_, f32[32,8,128]{2,1,0:T(8,128)} %copy-done.56, f32[8,128]{1,0:T(8,128)} %reduce_sum.82.refs_2_.refs_3_.refs_4_, ...), custom_call_target="tpu_custom_call" | custom-call | flops 6341787648 | bytes 14039552 | tf_op jit(solution)/shard_map/spatial_conv/pallas_call | solution.py:265
  137.1 13.9 %all_to_all.65.refs_1_ = f32[32,8,128]{2,1,0:T(8,128)} all-to-all(f32[32,8,128]{2,1,0:T(8,128)} %get-tuple-element.160), channel_id=1, replica_groups=mesh['dp'=8,'owner'=4] {'dp','owner'}, dimensions={0} | all-to-all | bytes 262144 | tf_op jit(solution)/shard_map/all_to_all | solution.py:44
  151.1 11.1 %expand.2 = (bf16[1344,512]{1,0:T(8,128)(2,1)}, f32[1344,2048]{1,0:T(8,128)}, f32[8,512]{1,0:T(8,128)}, f32[32,32,128]{2,1,0:T(8,128)}) custom-call(f32[1344,512]{1,0:T(8,128)} %get-tuple-element.159.refs_0_.refs_7_.refs_1_, f32[32,8,128]{2,1,0:T(8,128)} %all_to_all.65.refs_1_, f32[8,128]{1,0:T(8,128)} %reduce_sum.82.refs_2_.refs_3_.refs_4_, ...), custom_call_target="tpu_custom_call" | custom-call | flops 2818572288 | bytes 22690304 | tf_op jit(solution)/shard_map/expand/pallas_call | solution.py:265
  162.2 21.2 %all_to_all.66.refs_2_ = f32[32,32,128]{2,1,0:T(8,128)} all-to-all(f32[32,32,128]{2,1,0:T(8,128)} %get-tuple-element.162), channel_id=1, replica_groups=mesh['dp'=8,'owner'=4] {'dp','owner'}, dimensions={0} | all-to-all | bytes 1048576 | tf_op jit(solution)/shard_map/all_to_all | solution.py:44
  183.4 17.8 %close_and_reduce.1 = (f32[1344,2048]{1,0:T(8,128)}, bf16[1344,2048]{1,0:T(8,128)(2,1)}, f32[1344,512]{1,0:T(8,128)}, f32[8,2048]{1,0:T(8,128)}, f32[32,8,128]{2,1,0:T(8,128)}) custom-call(f32[1344,2048]{1,0:T(8,128)} %get-tuple-element.161.refs_0_.refs_8_.refs_1_, bf16[1344,2048]{1,0:T(8,128)(2,1)} %bitcast.359, f32[32,32,128]{2,1,0:T(8,128)} %all_to_all.66.refs_2_, ...), custom_call_target="tpu_custom_call" | custom-call | flops 2818572288 | bytes 33554432 | tf_op jit(solution)/shard_map/close_and_reduce/pallas_call | solution.py:265
  201.2 13.6 %all_to_all.67.refs_1_ = f32[32,8,128]{2,1,0:T(8,128)} all-to-all(f32[32,8,128]{2,1,0:T(8,128)} %get-tuple-element.167), channel_id=1, replica_groups=mesh['dp'=8,'owner'=4] {'dp','owner'}, dimensions={0} | all-to-all | bytes 262144 | tf_op jit(solution)/shard_map/all_to_all | solution.py:44
  214.9 13.3 %spatial_conv.3 = (bf16[1344,512]{1,0:T(8,128)(2,1)}, f32[1344,512]{1,0:T(8,128)}, f32[8,512]{1,0:T(8,128)}, f32[32,8,128]{2,1,0:T(8,128)}) custom-call(f32[1344,512]{1,0:T(8,128)} %get-tuple-element.166.refs_0_.refs_7_.refs_1_, f32[32,8,128]{2,1,0:T(8,128)} %all_to_all.67.refs_1_, f32[8,128]{1,0:T(8,128)} %reduce_sum.82.refs_2_.refs_3_.refs_4_, ...), custom_call_target="tpu_custom_call" | custom-call | flops 6341787648 | bytes 16136704 | tf_op jit(solution)/shard_map/spatial_conv/pallas_call | solution.py:265
  228.1 11.8 %all_to_all.68.refs_1_ = f32[32,8,128]{2,1,0:T(8,128)} all-to-all(f32[32,8,128]{2,1,0:T(8,128)} %get-tuple-element.169), channel_id=1, replica_groups=mesh['dp'=8,'owner'=4] {'dp','owner'}, dimensions={0} | all-to-all | bytes 262144 | tf_op jit(solution)/shard_map/all_to_all | solution.py:44
  239.9 10.8 %expand.3 = (bf16[1344,512]{1,0:T(8,128)(2,1)}, f32[1344,2048]{1,0:T(8,128)}, f32[8,512]{1,0:T(8,128)}, f32[32,32,128]{2,1,0:T(8,128)}) custom-call(f32[1344,512]{1,0:T(8,128)} %get-tuple-element.168.refs_0_.refs_7_.refs_1_, f32[32,8,128]{2,1,0:T(8,128)} %all_to_all.68.refs_1_, f32[8,128]{1,0:T(8,128)} %reduce_sum.82.refs_2_.refs_3_.refs_4_, ...), custom_call_target="tpu_custom_call" | custom-call | flops 2818572288 | bytes 24787456 | tf_op jit(solution)/shard_map/expand/pallas_call | solution.py:265
  254.5 14.7 %all-to-all-done.6.refs_2_ = f32[32,32,128]{2,1,0:T(8,128)S(1)} async-done(((f32[32,32,128]{2,1,0:T(8,128)}), f32[32,32,128]{2,1,0:T(8,128)S(1)}, u32[]{:S(2)}, u32[]{:S(2)}) %all-to-all-start.6) | async-done | bytes 524320 | tf_op jit(solution)/shard_map/all_to_all | solution.py:44
  269.9 35.3 %head_step.1 = (f32[1344,2048]{1,0:T(8,128)}, f32[8,2048]{1,0:T(8,128)}, f32[32,48,128]{2,1,0:T(8,128)}, bf16[2,8,2,256,128]{4,3,2,1,0:T(8,128)(2,1)}, bf16[2,8,2,256,128]{4,3,2,1,0:T(8,128)(2,1)}) custom-call(f32[1344,2048]{1,0:T(8,128)} %get-tuple-element.170.refs_0_.refs_1_, f32[1344,2048]{1,0:T(8,128)} %get-tuple-element.171.refs_1_, ...), custom_call_target="tpu_custom_call" | custom-call | flops 301989888 | bytes 33554432 | tf_op jit(solution)/shard_map/head_step/pallas_call | solution.py:265
  305.2 23.9 %all_to_all.69.refs_2_ = f32[32,48,128]{2,1,0:T(8,128)} all-to-all(f32[32,48,128]{2,1,0:T(8,128)} %get-tuple-element.173), channel_id=1, replica_groups=mesh['dp'=8,'owner'=4] {'dp','owner'}, dimensions={0} | all-to-all | bytes 1572864 | tf_op jit(solution)/shard_map/all_to_all | solution.py:44
  329.2 16.2 %back_expand.2 = (bf16[1344,2048]{1,0:T(8,128)(2,1)}, f32[1344,512]{1,0:T(8,128)}, f32[32,8,128]{2,1,0:T(8,128)}) custom-call(f32[1344,2048]{1,0:T(8,128)} %get-tuple-element.175.refs_0_.refs_7_, f32[1344,2048]{1,0:T(8,128)} %get-tuple-element.170.refs_0_.refs_1_, f32[32,48,128]{2,1,0:T(8,128)} %all_to_all.69.refs_2_, f32[8,2048]{1,0:T(8,128)} %get-tuple-element.178.refs_3_, ...), custom_call_target="tpu_custom_call" | custom-call | flops 2818572288 | bytes 33554432 | tf_op jit(solution)/shard_map/back_expand/pallas_call | solution.py:265
  363.0 15.3 %back_conv.2 = (bf16[1344,512]{1,0:T(8,128)(2,1)}, f32[1344,512]{1,0:T(8,128)}, f32[32,8,128]{2,1,0:T(8,128)}) custom-call(f32[1344,512]{1,0:T(8,128)} %get-tuple-element.180.refs_0_, f32[1344,512]{1,0:T(8,128)} %get-tuple-element.168.refs_0_.refs_7_.refs_1_, f32[32,8,128]{2,1,0:T(8,128)} %copy-done.45, f32[8,512]{1,0:T(8,128)} %get-tuple-element.179.refs_8_.refs_3_, ...), custom_call_target="tpu_custom_call" | custom-call | flops 6341787648 | bytes 21658112 | tf_op jit(solution)/shard_map/back_conv/pallas_call | solution.py:265
  383.0 11.7 %spatial_grad.2 = (bf16[2,4608,128]{2,1,0:T(8,128)(2,1)}, bf16[2,4608,128]{2,1,0:T(8,128)(2,1)}) custom-call(bf16[1344,512]{1,0:T(8,128)(2,1)} %get-tuple-element.196.refs_0_, bf16[1344,512]{1,0:T(8,128)(2,1)} %get-tuple-element.197.refs_1_), custom_call_target="tpu_custom_call" | custom-call | flops 6341787648 | bytes 7471104 | tf_op jit(solution)/shard_map/spatial_grad/pallas_call | solution.py:265
  398.4 22.0 %back_reduce.1 = (bf16[1344,512]{1,0:T(8,128)(2,1)}, f32[1344,2048]{1,0:T(8,128)}, f32[32,32,128]{2,1,0:T(8,128)}) custom-call(f32[1344,512]{1,0:T(8,128)} %get-tuple-element.188.refs_0_, f32[1344,512]{1,0:T(8,128)} %get-tuple-element.166.refs_0_.refs_7_.refs_1_, f32[32,8,128]{2,1,0:T(8,128)} %copy-done.28, f32[8,512]{1,0:T(8,128)} %get-tuple-element.187.refs_8_.refs_3_, ...), custom_call_target="tpu_custom_call" | custom-call | flops 2818572288 | bytes 33554432 | tf_op jit(solution)/shard_map/back_reduce/pallas_call | solution.py:265
  436.4 9.8 %collective-permute-done.17 = bf16[4,512,128]{2,1,0:T(8,128)(2,1)S(1)} collective-permute-done((bf16[4,512,128]{2,1,0:T(8,128)(2,1)}, bf16[4,512,128]{2,1,0:T(8,128)(2,1)S(1)}, u32[]{:S(2)}, u32[]{:S(2)}) %collective-permute-start.17) | collective-permute-done | bytes 524320 | tf_op jit(solution)/shard_map/ppermute | solution.py:49
  481.4 16.4 %back_expand.3 = (bf16[1344,2048]{1,0:T(8,128)(2,1)}, f32[1344,512]{1,0:T(8,128)}, f32[32,8,128]{2,1,0:T(8,128)}) custom-call(f32[1344,2048]{1,0:T(8,128)} %get-tuple-element.201.refs_0_, f32[1344,2048]{1,0:T(8,128)} %get-tuple-element.161.refs_0_.refs_8_.refs_1_, f32[32,32,128]{2,1,0:T(8,128)} %copy-done.4, f32[8,2048]{1,0:T(8,128)} %get-tuple-element.200.refs_10_.refs_3_, ...), custom_call_target="tpu_custom_call" | custom-call | flops 2818572288 | bytes 33554432 | tf_op jit(solution)/shard_map/back_expand/pallas_call | solution.py:265
  504.9 7.3 weight_grad.6
  521.6 15.6 %back_conv.3 = (bf16[1344,512]{1,0:T(8,128)(2,1)}, f32[1344,512]{1,0:T(8,128)}, f32[32,8,128]{2,1,0:T(8,128)}) custom-call(f32[1344,512]{1,0:T(8,128)} %get-tuple-element.217.refs_0_, f32[1344,512]{1,0:T(8,128)} %get-tuple-element.159.refs_0_.refs_7_.refs_1_, f32[32,8,128]{2,1,0:T(8,128)} %copy-done.43, f32[8,512]{1,0:T(8,128)} %get-tuple-element.216.refs_8_.refs_3_, ...), custom_call_target="tpu_custom_call" | custom-call | flops 6341787648 | bytes 19560960 | tf_op jit(solution)/shard_map/back_conv/pallas_call | solution.py:265
  547.5 11.8 %spatial_grad.3 = (bf16[2,4608,128]{2,1,0:T(8,128)(2,1)}, bf16[2,4608,128]{2,1,0:T(8,128)(2,1)}) custom-call(bf16[1344,512]{1,0:T(8,128)(2,1)} %get-tuple-element.174.refs_0_, bf16[1344,512]{1,0:T(8,128)(2,1)} %get-tuple-element.232.refs_1_), custom_call_target="tpu_custom_call" | custom-call | flops 6341787648 | bytes 7471104 | tf_op jit(solution)/shard_map/spatial_grad/pallas_call | solution.py:265
  579.0 14.2 %collective-permute-done.46 = bf16[4,256,128]{2,1,0:T(8,128)(2,1)S(1)} collective-permute-done((bf16[4,256,128]{2,1,0:T(8,128)(2,1)S(1)}, bf16[4,256,128]{2,1,0:T(8,128)(2,1)S(1)}, u32[]{:S(2)}, u32[]{:S(2)}) %collective-permute-start.46) | collective-permute-done | bytes 262176 | tf_op jit(solution)/shard_map/ppermute | solution.py:49
  626.3 7.7 collective-permute-done.28
  651.5 9.0 %collective-permute-done.38 = bf16[4,288,128]{2,1,0:T(8,128)(2,1)S(1)} collective-permute-done((bf16[4,288,128]{2,1,0:T(8,128)(2,1)S(1)}, bf16[4,288,128]{2,1,0:T(8,128)(2,1)S(1)}, u32[]{:S(2)}, u32[]{:S(2)}) %collective-permute-start.38) | collective-permute-done | bytes 294944 | tf_op jit(solution)/shard_map/ppermute | solution.py:49
  671.6 9.4 %all-gather.2 = bf16[3328,128]{1,0:T(8,128)(2,1)} all-gather(bf16[832,128]{1,0:T(8,128)(2,1)S(1)} %pad_maximum_fusion.17), channel_id=4, replica_groups=mesh['dp'=8,'owner'=4] {'owner'}, dimensions={0}, use_global_device_ids=true | all-gather | bytes 1064960 | tf_op jit(solution)/shard_map/all_gather | solution.py:921
  723.7 7.7 all-gather.4
  731.4 19.3 %polynomial.1 = bf16[128,512]{1,0:T(8,128)(2,1)} custom-call(f32[1280,128]{1,0:T(8,128)} %bitcast.422), custom_call_target="tpu_custom_call" | custom-call | flops 16106127360 | bytes 786432 | tf_op jit(solution)/shard_map/polynomial/pallas_call | solution.py:265
  750.8 9.3 %collective-permute-done.56 = bf16[128,512]{1,0:T(8,128)(2,1)S(1)} collective-permute-done((bf16[128,512]{1,0:T(8,128)(2,1)}, bf16[128,512]{1,0:T(8,128)(2,1)S(1)}, u32[]{:S(2)}, u32[]{:S(2)}) %collective-permute-start.56) | collective-permute-done | bytes 131104 | tf_op jit(solution)/shard_map/ppermute | solution.py:49
  (469 shorter events, 324.3 us)
Async XLA Ops:
  8.3 19.5 %collective-permute-start = (bf16[1,256,128]{2,1,0:T(8,128)(2,1)S(1)}, bf16[1,256,128]{2,1,0:T(8,128)(2,1)S(1)}, u32[]{:S(2)}, u32[]{:S(2)}) collective-permute-start(bf16[1,256,128]{2,1,0:T(8,128)(2,1)S(1)} %get-tuple-element.409), channel_id=1, source_target_pairs={{0,16},{1,17},{2,18},{3,19},{4,20},{5,21},{6,22},{7,23},{8,24},{9,... | collective-permute-start | bytes 196616 | tf_op jit(solution)/shard_map/ppermute | solution.py:49
  15.8 37.0 %all-to-all-start = ((f32[32,8,128]{2,1,0:T(8,128)}), f32[32,8,128]{2,1,0:T(8,128)S(1)}, u32[]{:S(2)}, u32[]{:S(2)}) async-start(f32[32,8,128]{2,1,0:T(8,128)} %broadcast_in_dim.35), calls=%async_computation | async-start | bytes 262144 | tf_op jit(solution)/shard_map/all_to_all | solution.py:44
  19.7 163.7 %all-gather.9.cloned.1.call-start = ((), (), s32[]{:S(2)}) async-start(), calls=%async_computation.13 | async-start | bytes 9191424 | tf_op jit(solution)/shard_map/all_gather | solution.py:1169
  62.0 192.5 %all-gather.11.cloned.1.call-start = ((), (), s32[]{:S(2)}) async-start(), calls=%async_computation.14 | async-start | bytes 4325376 | tf_op jit(solution)/shard_map/all_gather | solution.py:1181
  80.2 28.2 %collective-permute-start.12 = (bf16[8,416,128]{2,1,0:T(8,128)(2,1)S(1)}, bf16[8,416,128]{2,1,0:T(8,128)(2,1)S(1)}, u32[]{:S(2)}, u32[]{:S(2)}) collective-permute-start(bf16[8,416,128]{2,1,0:T(8,128)(2,1)S(1)} %pad_maximum_fusion.3), channel_id=1, source_target_pairs={{0,2},{1,3},{2,0},{3,1},{4,6},{5,7},{6,4},{7,5},{8,10},{9,11},{10,... | collective-permute-start | bytes 2555912 | tf_op jit(solution)/shard_map/ppermute | solution.py:49
  81.8 26.5 %collective-permute-start.11 = (bf16[8,416,128]{2,1,0:T(8,128)(2,1)S(1)}, bf16[8,416,128]{2,1,0:T(8,128)(2,1)S(1)}, u32[]{:S(2)}, u32[]{:S(2)}) collective-permute-start(bf16[8,416,128]{2,1,0:T(8,128)(2,1)S(1)} %pad_maximum_fusion.2), channel_id=1, source_target_pairs={{0,4},{1,5},{2,6},{3,7},{4,0},{5,1},{6,2},{7,3},{8,12},{9,13},{10,... | collective-permute-start | bytes 2555912 | tf_op jit(solution)/shard_map/ppermute | solution.py:49
  250.7 18.4 %all-to-all-start.6 = ((f32[32,32,128]{2,1,0:T(8,128)}), f32[32,32,128]{2,1,0:T(8,128)S(1)}, u32[]{:S(2)}, u32[]{:S(2)}) async-start(f32[32,32,128]{2,1,0:T(8,128)} %get-tuple-element.172), calls=%async_computation.6 | async-start | bytes 1048576 | tf_op jit(solution)/shard_map/all_to_all | solution.py:44
  329.2 28.6 %collective-permute-start.15 = (bf16[16,512,128]{2,1,0:T(8,128)(2,1)}, bf16[16,512,128]{2,1,0:T(8,128)(2,1)S(1)}, u32[]{:S(2)}, u32[]{:S(2)}) collective-permute-start(bf16[16,512,128]{2,1,0:T(8,128)(2,1)} %bitcast.433), channel_id=1, source_target_pairs={{0,1},{1,0},{2,3},{3,2},{4,5},{5,4},{6,7},{7,6},{8,9},{9,8},{10,11... | collective-permute-start | bytes 6291464 | tf_op jit(solution)/shard_map/ppermute | solution.py:49
  362.0 32.7 %collective-permute-start.16 = (bf16[8,512,128]{2,1,0:T(8,128)(2,1)S(1)}, bf16[8,512,128]{2,1,0:T(8,128)(2,1)}, u32[]{:S(2)}, u32[]{:S(2)}) collective-permute-start(bf16[8,512,128]{2,1,0:T(8,128)(2,1)S(1)} %dynamic-slice_bitcast_fusion.1), channel_id=1, source_target_pairs={{0,2},{1,3},{2,0},{3,1},{4,6},{5,7},{6,4},{7,5},{8,10},{9,11},{10,... | collective-permute-start | bytes 3145736 | tf_op jit(solution)/shard_map/ppermute | solution.py:49
  378.3 16.4 %all-to-all-start.9 = ((f32[32,8,128]{2,1,0:T(8,128)}), f32[32,8,128]{2,1,0:T(8,128)S(1)}, u32[]{:S(2)}, u32[]{:S(2)}) async-start(f32[32,8,128]{2,1,0:T(8,128)} %get-tuple-element.189), calls=%async_computation.9 | async-start | bytes 262144 | tf_op jit(solution)/shard_map/all_to_all | solution.py:44
  397.9 48.3 %collective-permute-start.19 = (bf16[16,576,128]{2,1,0:T(8,128)(2,1)}, bf16[16,576,128]{2,1,0:T(8,128)(2,1)}, u32[]{:S(2)}, u32[]{:S(2)}) collective-permute-start(bf16[16,576,128]{2,1,0:T(8,128)(2,1)} %bitcast.40), channel_id=1, source_target_pairs={{0,1},{1,0},{2,3},{3,2},{4,5},{5,4},{6,7},{7,6},{8,9},{9,8},{10,11... | collective-permute-start | bytes 7077896 | tf_op jit(solution)/shard_map/ppermute | solution.py:49
  398.1 48.1 %collective-permute-start.18 = (bf16[16,256,128]{2,1,0:T(8,128)(2,1)}, bf16[16,256,128]{2,1,0:T(8,128)(2,1)}, u32[]{:S(2)}, u32[]{:S(2)}) collective-permute-start(bf16[16,256,128]{2,1,0:T(8,128)(2,1)} %bitcast.39), channel_id=1, source_target_pairs={{0,1},{1,0},{2,3},{3,2},{4,5},{5,4},{6,7},{7,6},{8,9},{9,8},{10,11... | collective-permute-start | bytes 3145736 | tf_op jit(solution)/shard_map/ppermute | solution.py:49
  420.4 25.8 %all-to-all-start.10 = ((f32[32,32,128]{2,1,0:T(8,128)}), f32[32,32,128]{2,1,0:T(8,128)S(1)}, u32[]{:S(2)}, u32[]{:S(2)}) async-start(f32[32,32,128]{2,1,0:T(8,128)} %get-tuple-element.202), calls=%async_computation.10 | async-start | bytes 1048576 | tf_op jit(solution)/shard_map/all_to_all | solution.py:44
  426.4 19.8 %collective-permute-start.17 = (bf16[4,512,128]{2,1,0:T(8,128)(2,1)}, bf16[4,512,128]{2,1,0:T(8,128)(2,1)S(1)}, u32[]{:S(2)}, u32[]{:S(2)}) collective-permute-start(bf16[4,512,128]{2,1,0:T(8,128)(2,1)} %dynamic-slice_bitcast_fusion.6), channel_id=1, source_target_pairs={{0,4},{1,5},{2,6},{3,7},{4,0},{5,1},{6,2},{7,3},{8,12},{9,13},{10,... | collective-permute-start | bytes 1572872 | tf_op jit(solution)/shard_map/ppermute | solution.py:49
  454.5 59.2 %collective-permute-start.21 = (bf16[8,832,128]{2,1,0:T(8,128)(2,1)}, bf16[8,832,128]{2,1,0:T(8,128)(2,1)}, u32[]{:S(2)}, u32[]{:S(2)}) collective-permute-start(bf16[8,832,128]{2,1,0:T(8,128)(2,1)} %dynamic-slice_bitcast_fusion), channel_id=1, source_target_pairs={{0,4},{1,5},{2,6},{3,7},{4,0},{5,1},{6,2},{7,3},{8,12},{9,13},{10,... | collective-permute-start | bytes 5111816 | tf_op jit(solution)/shard_map/ppermute | solution.py:49
  475.4 38.3 %collective-permute-start.22 = (bf16[16,256,128]{2,1,0:T(8,128)(2,1)}, bf16[16,256,128]{2,1,0:T(8,128)(2,1)}, u32[]{:S(2)}, u32[]{:S(2)}) collective-permute-start(bf16[16,256,128]{2,1,0:T(8,128)(2,1)} %bitcast.434), channel_id=1, source_target_pairs={{0,1},{1,0},{2,3},{3,2},{4,5},{5,4},{6,7},{7,6},{8,9},{9,8},{10,11... | collective-permute-start | bytes 3145736 | tf_op jit(solution)/shard_map/ppermute | solution.py:49
  521.1 41.2 %collective-permute-start.26 = (bf16[16,256,128]{2,1,0:T(8,128)(2,1)}, bf16[16,256,128]{2,1,0:T(8,128)(2,1)S(1)}, u32[]{:S(2)}, u32[]{:S(2)}) collective-permute-start(bf16[16,256,128]{2,1,0:T(8,128)(2,1)} %bitcast.56), channel_id=1, source_target_pairs={{0,1},{1,0},{2,3},{3,2},{4,5},{5,4},{6,7},{7,6},{8,9},{9,8},{10,11... | collective-permute-start | bytes 3145736 | tf_op jit(solution)/shard_map/ppermute | solution.py:49
  521.2 41.1 %collective-permute-start.24 = (bf16[4,832,128]{2,1,0:T(8,128)(2,1)}, bf16[4,832,128]{2,1,0:T(8,128)(2,1)}, u32[]{:S(2)}, u32[]{:S(2)}) collective-permute-start(bf16[4,832,128]{2,1,0:T(8,128)(2,1)} %dynamic-slice_bitcast_fusion.2), channel_id=1, source_target_pairs={{0,8},{1,9},{2,10},{3,11},{4,12},{5,13},{6,14},{7,15},{8,0},{9,1},... | collective-permute-start | bytes 2555912 | tf_op jit(solution)/shard_map/ppermute | solution.py:49
  537.2 22.6 %all-to-all-start.12 = ((f32[32,8,128]{2,1,0:T(8,128)}), f32[32,8,128]{2,1,0:T(8,128)S(1)}, u32[]{:S(2)}, u32[]{:S(2)}) async-start(f32[32,8,128]{2,1,0:T(8,128)} %get-tuple-element.234), calls=%async_computation.12 | async-start | bytes 262144 | tf_op jit(solution)/shard_map/all_to_all | solution.py:44
  543.0 145.9 %all-gather.13.cloned.1.call-start = ((), (), s32[]{:S(2)}) async-start(), calls=%async_computation.15 | async-start | bytes 1720320 | tf_op jit(solution)/shard_map/all_gather | solution.py:921
  543.2 19.0 %collective-permute-start.25 = (bf16[8,256,128]{2,1,0:T(8,128)(2,1)}, bf16[8,256,128]{2,1,0:T(8,128)(2,1)}, u32[]{:S(2)}, u32[]{:S(2)}) collective-permute-start(bf16[8,256,128]{2,1,0:T(8,128)(2,1)} %bitcast.55), channel_id=1, source_target_pairs={{0,8},{1,9},{2,10},{3,11},{4,12},{5,13},{6,14},{7,15},{8,0},{9,1},... | collective-permute-start | bytes 1572872 | tf_op jit(solution)/shard_map/ppermute | solution.py:49
  545.1 14.8 %collective-permute-start.23 = (bf16[1,512,128]{2,1,0:T(8,128)(2,1)S(1)}, bf16[1,512,128]{2,1,0:T(8,128)(2,1)S(1)}, u32[]{:S(2)}, u32[]{:S(2)}) collective-permute-start(bf16[1,512,128]{2,1,0:T(8,128)(2,1)S(1)} %constant_dynamic-slice_fusion.16), channel_id=1, source_target_pairs={{0,16},{1,17},{2,18},{3,19},{4,20},{5,21},{6,22},{7,23},{8,24},{9,... | collective-permute-start | bytes 393224 | tf_op jit(solution)/shard_map/ppermute | solution.py:49
  568.3 24.9 %collective-permute-start.46 = (bf16[4,256,128]{2,1,0:T(8,128)(2,1)S(1)}, bf16[4,256,128]{2,1,0:T(8,128)(2,1)S(1)}, u32[]{:S(2)}, u32[]{:S(2)}) collective-permute-start(bf16[4,256,128]{2,1,0:T(8,128)(2,1)S(1)} %bitcast.427), channel_id=1, source_target_pairs={{0,16},{1,17},{2,18},{3,19},{4,20},{5,21},{6,22},{7,23},{8,24},{9,... | collective-permute-start | bytes 786440 | tf_op jit(solution)/shard_map/ppermute | solution.py:49
  570.6 33.1 %collective-permute-start.44 = (bf16[2,832,128]{2,1,0:T(8,128)(2,1)}, bf16[2,832,128]{2,1,0:T(8,128)(2,1)}, u32[]{:S(2)}, u32[]{:S(2)}) collective-permute-start(bf16[2,832,128]{2,1,0:T(8,128)(2,1)} %dynamic-slice_bitcast_fusion.7), channel_id=1, source_target_pairs={{0,16},{1,17},{2,18},{3,19},{4,20},{5,21},{6,22},{7,23},{8,24},{9,... | collective-permute-start | bytes 1277960 | tf_op jit(solution)/shard_map/ppermute | solution.py:49
  572.5 32.9 %collective-permute-start.49 = (bf16[8,256,128]{2,1,0:T(8,128)(2,1)S(1)}, bf16[8,256,128]{2,1,0:T(8,128)(2,1)S(1)}, u32[]{:S(2)}, u32[]{:S(2)}) collective-permute-start(bf16[8,256,128]{2,1,0:T(8,128)(2,1)S(1)} %dynamic-slice_bitcast_fusion.5), channel_id=1, source_target_pairs={{0,2},{1,3},{2,0},{3,1},{4,6},{5,7},{6,4},{7,5},{8,10},{9,11},{10,... | collective-permute-start | bytes 1572872 | tf_op jit(solution)/shard_map/ppermute | solution.py:49
  573.9 45.0 %collective-permute-start.27 = (bf16[16,576,128]{2,1,0:T(8,128)(2,1)}, bf16[16,576,128]{2,1,0:T(8,128)(2,1)}, u32[]{:S(2)}, u32[]{:S(2)}) collective-permute-start(bf16[16,576,128]{2,1,0:T(8,128)(2,1)} %bitcast.67), channel_id=1, source_target_pairs={{0,1},{1,0},{2,3},{3,2},{4,5},{5,4},{6,7},{7,6},{8,9},{9,8},{10,11... | collective-permute-start | bytes 7077896 | tf_op jit(solution)/shard_map/ppermute | solution.py:49
  602.1 22.9 %collective-permute-start.36 = (bf16[16,256,128]{2,1,0:T(8,128)(2,1)}, bf16[16,256,128]{2,1,0:T(8,128)(2,1)S(1)}, u32[]{:S(2)}, u32[]{:S(2)}) collective-permute-start(bf16[16,256,128]{2,1,0:T(8,128)(2,1)} %bitcast.435), channel_id=1, source_target_pairs={{0,1},{1,0},{2,3},{3,2},{4,5},{5,4},{6,7},{7,6},{8,9},{9,8},{10,11... | collective-permute-start | bytes 3145736 | tf_op jit(solution)/shard_map/ppermute | solution.py:49
  625.3 14.6 %collective-permute-start.32 = (bf16[8,272,128]{2,1,0:T(8,128)(2,1)S(1)}, bf16[8,272,128]{2,1,0:T(8,128)(2,1)S(1)}, u32[]{:S(2)}, u32[]{:S(2)}) collective-permute-start(bf16[8,272,128]{2,1,0:T(8,128)(2,1)S(1)} %dynamic-slice_bitcast_fusion.3), channel_id=1, source_target_pairs={{0,4},{1,5},{2,6},{3,7},{4,0},{5,1},{6,2},{7,3},{8,12},{9,13},{10,... | collective-permute-start | bytes 1671176 | tf_op jit(solution)/shard_map/ppermute | solution.py:49
  626.0 17.5 %collective-permute-start.37 = (bf16[8,288,128]{2,1,0:T(8,128)(2,1)S(1)}, bf16[8,288,128]{2,1,0:T(8,128)(2,1)S(1)}, u32[]{:S(2)}, u32[]{:S(2)}) collective-permute-start(bf16[8,288,128]{2,1,0:T(8,128)(2,1)S(1)} %bitcast.424), channel_id=1, source_target_pairs={{0,8},{1,9},{2,10},{3,11},{4,12},{5,13},{6,14},{7,15},{8,0},{9,1},... | collective-permute-start | bytes 1769480 | tf_op jit(solution)/shard_map/ppermute | solution.py:49
  643.7 16.9 %collective-permute-start.38 = (bf16[4,288,128]{2,1,0:T(8,128)(2,1)S(1)}, bf16[4,288,128]{2,1,0:T(8,128)(2,1)S(1)}, u32[]{:S(2)}, u32[]{:S(2)}) collective-permute-start(bf16[4,288,128]{2,1,0:T(8,128)(2,1)S(1)} %bitcast.426), channel_id=1, source_target_pairs={{0,16},{1,17},{2,18},{3,19},{4,20},{5,21},{6,22},{7,23},{8,24},{9,... | collective-permute-start | bytes 884744 | tf_op jit(solution)/shard_map/ppermute | solution.py:49
  643.9 18.3 %collective-permute-start.30 = (bf16[2,272,128]{2,1,0:T(8,128)(2,1)S(1)}, bf16[2,272,128]{2,1,0:T(8,128)(2,1)S(1)}, u32[]{:S(2)}, u32[]{:S(2)}) collective-permute-start(bf16[2,272,128]{2,1,0:T(8,128)(2,1)S(1)} %dynamic-slice_bitcast_fusion.15), channel_id=1, source_target_pairs={{0,8},{1,9},{2,10},{3,11},{4,12},{5,13},{6,14},{7,15},{8,0},{9,1},... | collective-permute-start | bytes 417800 | tf_op jit(solution)/shard_map/ppermute | solution.py:49
  706.9 14.6 %collective-permute-start.43 = (f32[1,320,128]{2,1,0:T(8,128)S(1)}, f32[1,320,128]{2,1,0:T(8,128)S(1)}, u32[]{:S(2)}, u32[]{:S(2)}) collective-permute-start(f32[1,320,128]{2,1,0:T(8,128)S(1)} %add.385), channel_id=1, source_target_pairs={{0,16},{1,17},{2,18},{3,19},{4,20},{5,21},{6,22},{7,23},{8,24},{9,... | collective-permute-start | bytes 491528 | tf_op jit(solution)/shard_map/ppermute | solution.py:49
  (107 other events, 897.3 us)
Sparse Core Ops, SparseCore 0:
  62.1 92.6 all-gather.8
  158.2 64.8 all-gather.10
  671.4 17.4 all-gather.12

commit v4 on v3

--- a/solution.py
+++ b/solution.py
@@ -28,6 +28,7 @@
 LR_VECTOR = 0.4
 LANES = 128
 SLOT = 8
+PATIENT = 280000
 F32 = jnp.float32
 BF16 = jnp.bfloat16
 
@@ -62,9 +63,11 @@
         self.sent = [sent for _, sent in pairs]
         self.bit = order[0]
         self.values = self.got = None
+        self.wait = 1
 
     def send(self):
         self.got = [swap(sent, self.bit) for sent in self.sent]
+        self.wait = 2 if self.order is not None and self.values is not None and self.sent[0].size > PATIENT else 1
         self.sent = None
 
     def add(self):
@@ -96,19 +99,76 @@
         return self.values[0] if self.values.shape[0] == 1 else self.values
 
 
-def advance(ahead, flows):
-    got = [flow.got for flow in flows]
-    ahead, got = lax.optimization_barrier((ahead, got))
-    for flow, values in zip(flows, got):
+class Fork:
+    def __init__(self, pair, left, first, orders):
+        self.trunk, self.orders, self.branches = Flow([pair], left, [first]), orders, []
+        self.wait = 1
+
+    @property
+    def parts(self):
+        return self.branches or [self.trunk]
+
+    def add(self):
+        for part in self.parts:
+            part.add()
+
+    def split(self):
+        if self.branches:
+            for part in self.branches:
+                part.split()
+            return
+        values, left, count = self.trunk.values, self.trunk.left, len(self.orders)
+        step = values.shape[1] // count // 16 * 16
+        for number, order in enumerate(self.orders):
+            piece = values[:, number * step : (number + 1) * step if number < count - 1 else values.shape[1]]
+            place = left.index(order[0])
+            own = (my_index() >> order[0]) & 1
+            self.branches.append(Flow([(half_of(piece, place, own), half_of(piece, place, 1 - own))], left, order))
+
+    def send(self):
+        for part in self.parts:
+            if part.sent is not None:
+                part.send()
+        self.wait = max(part.wait for part in self.parts)
+
+    @property
+    def got(self):
+        got = [part.got for part in self.parts]
+        return None if all(values is None for values in got) else got
+
+    @got.setter
+    def got(self, values):
+        for part, value in zip(self.parts, values or [None] * len(self.parts)):
+            part.got = value
+
+    @property
+    def sent(self):
+        sent = [part.sent for part in self.parts]
+        return None if all(values is None for values in sent) else sent
+
+    @sent.setter
+    def sent(self, values):
+        for part, value in zip(self.parts, values or [None] * len(self.parts)):
+            part.sent = value
+
+    def result(self):
+        return jnp.concatenate([part.result() for part in self.branches], axis=0)
+
+
+def advance(ahead, flows, eager=False):
+    for flow in flows:
+        flow.wait -= flow.got is not None
+    moving = [flow for flow in flows if flow.got is not None and (eager or flow.wait <= 0)]
+    ahead, got = lax.optimization_barrier((ahead, [flow.got for flow in moving]))
+    for flow, values in zip(moving, got):
         flow.got = values
-        if values is not None:
-            flow.add()
-            flow.split()
-    ahead, sent = lax.optimization_barrier((ahead, [flow.sent for flow in flows]))
-    for flow, values in zip(flows, sent):
+        flow.add()
+        flow.split()
+    moving = [flow for flow in flows if flow.sent is not None]
+    ahead, sent = lax.optimization_barrier((ahead, [flow.sent for flow in moving]))
+    for flow, values in zip(moving, sent):
         flow.sent = values
-        if values is not None:
-            flow.send()
+        flow.send()
     return ahead
 
 
@@ -118,17 +178,15 @@
     return list(range(low - 1, -1, -1)) + list(range(low + high - 1, low - 1, -1))
 
 
-def sigmoid(values):
-    return 1.0 / (1.0 + jnp.exp(-values))
-
-
 def silu(values):
-    return values * sigmoid(values)
+    half = 0.5 * values
+    return half * jnp.tanh(half) + half
 
 
 def silu_slope(values):
-    part = sigmoid(values)
-    return part * (1.0 + values * (1.0 - part))
+    half = 0.5 * values
+    bend = jnp.tanh(half)
+    return 0.5 * (1.0 + bend + half * (1.0 - bend * bend))
 
 
 def total_of(parts_ref):
@@ -159,9 +217,31 @@
     return centre, lax.rsqrt(spread + EPS)
 
 
-def keep_norm(stat_ref, centre, inverse):
-    stat_ref[0:1, :] = centre
-    stat_ref[1:2, :] = inverse
+def keep_norm(stat_ref, centre, inverse, gain, bias):
+    scale = inverse * gain
+    rows = [centre, inverse, scale, bias - centre * scale]
+    stat_ref[...] = jnp.concatenate(rows + [jnp.zeros_like(centre)] * 4, axis=0)
+
+
+def normed_of(values, stat_ref):
+    return values * stat_ref[2:3] + stat_ref[3:4]
+
+
+def back_terms(terms, table, stat_ref, count, width):
+    bias_sum, gain_sum = row_of(table, 0, width), row_of(table, width // LANES, width)
+    centre, inverse, scale = stat_ref[0:1], stat_ref[1:2], stat_ref[2:3]
+    terms[0:1] = scale * (bias_sum - centre * inverse * gain_sum) / count
+    terms[1:2] = scale * inverse * gain_sum / count
+
+
+def back_norm(grad, hidden, stat_ref, terms, mask):
+    return grad * stat_ref[2:3] - mask * (terms[0:1] + hidden * terms[1:2])
+
+
+def send_back_sums(send_ref, sums, stat_ref):
+    bias_sum = jnp.sum(sums[0:8], axis=0, keepdims=True)
+    cross = jnp.sum(sums[8:16], axis=0, keepdims=True)
+    send_rows(send_ref, [bias_sum, (cross - stat_ref[0:1] * bias_sum) * stat_ref[1:2]])
 
 
 class Weights:
@@ -308,13 +388,13 @@
         sent_ref[(pair,) + place] = jnp.where(even, second, first).astype(BF16)
 
 
-def first_reduce(images, masks, weights, devices):
+def first_reduce(images, masks, tallies, weights, devices):
     rows, wide = images.shape
     narrow = weights.width
     strip_rows = block_rows(rows, 3)
     steps = rows // strip_rows
 
-    def kernel(x_ref, mask_ref, w_ref, h_ref, send_ref, buffer, sems, sums):
+    def kernel(x_ref, mask_ref, tally_ref, w_ref, h_ref, send_ref, buffer, sems, sums):
         step = pl.program_id(0)
 
         @pl.when(step == 0)
@@ -335,12 +415,13 @@
         @pl.when(step == steps - 1)
         def _():
             send_rows(send_ref, [jnp.sum(sums[i * 8 : i * 8 + 8], axis=0, keepdims=True) for i in range(2)])
-
-    send = (devices, 2 * narrow // LANES, LANES)
+            send_ref[:, send_ref.shape[1] - 8 :, :] = jnp.broadcast_to(tally_ref[...][None], (devices, 8, LANES))
+
+    send = (devices, 2 * narrow // LANES + 8, LANES)
     return launch(
         kernel, "reduce_first", (steps,),
-        (images, masks, weights),
-        [strip(strip_rows, wide), strip(strip_rows, 2), ANYWHERE],
+        (images, masks, tallies, weights),
+        [strip(strip_rows, wide), strip(strip_rows, 2), whole(tallies.shape), ANYWHERE],
         (out_of((rows, narrow), F32), out_of(send, F32)),
         (strip(strip_rows, narrow), whole(send)),
         weights.scratch() + [pltpu.VMEM((16, narrow), F32)],
@@ -378,15 +459,13 @@
                 copy.start()
             sums[...] = jnp.zeros_like(sums)
             centre, inverse = norm_of(parts_ref, count_ref[0:1, 0:1], narrow)
-            keep_norm(stat_ref, centre, inverse)
-            gain = norm_ref[0, layer : layer + 1, 0:narrow]
-            bias = norm_ref[1, layer : layer + 1, 0:narrow]
+            keep_norm(stat_ref, centre, inverse, norm_ref[0, layer : layer + 1, 0:narrow], norm_ref[1, layer : layer + 1, 0:narrow])
             clear_edges(shifted, rows, zone)
 
             def body(index, carry):
                 start = pl.multiple_of(index * zone, zone)
                 place = pl.ds(start, zone)
-                value = silu((h_ref[place, :] - centre) * inverse * gain + bias) * mask_ref[place, 1:2]
+                value = silu(normed_of(h_ref[place, :], stat_ref)) * mask_ref[place, 1:2]
                 a_ref[place, :] = value.astype(BF16)
                 store_shifted(shifted, pl.multiple_of(start + zone, zone), value, zone, narrow)
                 return carry
@@ -441,17 +520,15 @@
                 copy.start()
             sums[...] = jnp.zeros_like(sums)
             centre, inverse = norm_of(parts_ref, count_ref[0:1, 0:1], narrow)
-            stat_ref[...] = jnp.zeros_like(stat_ref)
-            keep_norm(stat_ref, centre, inverse)
+            span = slice(narrow, 2 * narrow)
+            keep_norm(stat_ref, centre, inverse, norm_ref[0, layer : layer + 1, span], norm_ref[1, layer : layer + 1, span])
             for copy in copies:
                 copy.wait()
 
-        gain = norm_ref[0, layer : layer + 1, narrow : 2 * narrow]
-        bias = norm_ref[1, layer : layer + 1, narrow : 2 * narrow]
-        value = silu((h_ref[...] - stat_ref[0:1]) * stat_ref[1:2] * gain + bias).astype(BF16)
+        value = silu(normed_of(h_ref[...], stat_ref)).astype(BF16)
         a_ref[...] = value
         total = dot_nt(value, buffer[...])
-        out_ref[...] = total
+        out_ref[...] = total.astype(BF16)
         kept = total * mask_ref[:, 0:1]
         sums[0:8] += fold_rows(kept)
         sums[8:16] += fold_rows(kept * total)
@@ -465,7 +542,7 @@
         kernel, "expand", (steps,),
         (hidden, parts, counts, norms, masks, weights),
         [strip(strip_rows, narrow), whole(parts.shape), whole(counts.shape), whole(norms.shape), strip(strip_rows, 2), ANYWHERE],
-        (out_of((rows, narrow), BF16), out_of((rows, wide), F32), out_of((8, narrow), F32), out_of(send, F32)),
+        (out_of((rows, narrow), BF16), out_of((rows, wide), BF16), out_of((8, narrow), F32), out_of(send, F32)),
         (strip(strip_rows, narrow), strip(strip_rows, wide), whole((8, narrow)), whole(send)),
         weights.scratch() + [pltpu.VMEM((16, wide), F32)],
         2 * rows * wide * narrow,
@@ -480,7 +557,7 @@
 
     def kernel(
         h_ref, x_ref, parts_ref, count_ref, norm_ref, mask_ref, w_ref,
-        next_ref, low_ref, out_ref, stat_ref, send_ref, buffer, sems, sums,
+        low_ref, out_ref, stat_ref, send_ref, buffer, sems, sums,
     ):
         step = pl.program_id(0)
 
@@ -491,16 +568,12 @@
                 copy.start()
             sums[...] = jnp.zeros_like(sums)
             centre, inverse = norm_of(parts_ref, count_ref[0:1, 0:1], wide)
-            stat_ref[...] = jnp.zeros_like(stat_ref)
-            keep_norm(stat_ref, centre, inverse)
+            span = slice(2 * narrow, None)
+            keep_norm(stat_ref, centre, inverse, norm_ref[0, layer : layer + 1, span], norm_ref[1, layer : layer + 1, span])
             for copy in copies:
                 copy.wait()
 
-        gain = norm_ref[0, layer : layer + 1, 2 * narrow :]
-        bias = norm_ref[1, layer : layer + 1, 2 * narrow :]
-        normed = (h_ref[...] - stat_ref[0:1]) * stat_ref[1:2] * gain + bias
-        value = silu(x_ref[...].astype(F32) + normed)
-        next_ref[...] = value
+        value = silu(x_ref[...].astype(F32) + normed_of(h_ref[...].astype(F32), stat_ref))
         low = value.astype(BF16)
         low_ref[...] = low
         total = dot_nn(low, buffer[...])
@@ -518,8 +591,8 @@
         kernel, "close_and_reduce", (steps,),
         (hidden, inputs, parts, counts, norms, masks, weights),
         [strip(strip_rows, wide), strip(strip_rows, wide), whole(parts.shape), whole(counts.shape), whole(norms.shape), strip(strip_rows, 2), ANYWHERE],
-        (out_of((rows, wide), F32), out_of((rows, wide), BF16), out_of((rows, narrow), F32), out_of((8, wide), F32), out_of(send, F32)),
-        (strip(strip_rows, wide), strip(strip_rows, wide), strip(strip_rows, narrow), whole((8, wide)), whole(send)),
+        (out_of((rows, wide), BF16), out_of((rows, narrow), F32), out_of((8, wide), F32), out_of(send, F32)),
+        (strip(strip_rows, wide), strip(strip_rows, narrow), whole((8, wide)), whole(send)),
         weights.scratch() + [pltpu.VMEM((16, narrow), F32)],
         2 * rows * wide * narrow,
     )
@@ -536,39 +609,35 @@
 
     def kernel(
         h_ref, x_ref, parts_ref, count_ref, norm_ref, mask_ref, head_ref, bias_ref, image_ref,
-        ds_ref, stat_ref, send_ref, kept_ref, sent_ref, summed, pooled, sums,
+        ds_ref, stat_ref, send_ref, kept_ref, sent_ref, summed, kept, piled, pooled, sums,
     ):
         step = pl.program_id(0)
-        gain = norm_ref[0, layer : layer + 1, norm_ref.shape[2] - wide :]
-        bias = norm_ref[1, layer : layer + 1, norm_ref.shape[2] - wide :]
-
         @pl.when(step == 0)
         def _():
             sums[...] = jnp.zeros_like(sums)
-            pooled[...] = jnp.zeros_like(pooled)
+            piled[...] = jnp.zeros_like(piled)
             centre, inverse = norm_of(parts_ref, count_ref[0:1, 0:1], wide)
-            stat_ref[...] = jnp.zeros_like(stat_ref)
-            keep_norm(stat_ref, centre, inverse)
+            span = slice(norm_ref.shape[2] - wide, None)
+            keep_norm(stat_ref, centre, inverse, norm_ref[0, layer : layer + 1, span], norm_ref[1, layer : layer + 1, span])
 
         @pl.when(step < steps)
         def _():
             place = pl.ds(pl.multiple_of(step * zone, zone), zone)
-            value = x_ref[...] + ((h_ref[...] - stat_ref[0:1]) * stat_ref[1:2] * gain + bias)
+            hidden_here = h_ref[...]
+            kept[place, :] = hidden_here
+            value = x_ref[...].astype(F32) + normed_of(hidden_here.astype(F32), stat_ref)
             summed[place, :] = value
             out = silu(value) * mask_ref[:, 1:2]
-            pooled[...] += jnp.sum(out.reshape(images, SLOT, wide), axis=1)
+            piled[...] += out
 
         @pl.when(step == steps - 1)
         def _():
-            low = (pooled[...] * (1.0 / pixels)).astype(BF16)
-            columns = []
-            for o in range(owners):
-                logit = None
-                for d in range(dp_size):
-                    part = dot_nt(low[:, d * cols : (d + 1) * cols], head_ref[d, o])
-                    logit = part if logit is None else logit + part
-                columns.append(logit)
-            logits = jnp.concatenate(columns, axis=1) + bias_ref[0:1, :]
+            low = (jnp.sum(piled[...].reshape(images, SLOT, wide), axis=1) * (1.0 / pixels)).astype(BF16)
+            flipped = None
+            for d in range(dp_size):
+                part = dot_nt(head_ref[d].reshape(classes, cols), low[:, d * cols : (d + 1) * cols])
+                flipped = part if flipped is None else flipped + part
+            logits = flipped.T + bias_ref[0:1, :]
             top = jnp.max(logits, axis=1, keepdims=True)
             shifted = jnp.exp(logits - top)
             mass = jnp.sum(shifted, axis=1, keepdims=True)
@@ -584,16 +653,14 @@
                 [jnp.sum(residue, axis=0, keepdims=True), jnp.broadcast_to(loss, (1, 8 * LANES))],
                 2 * wide // LANES,
             )
-            grad = (residue / count_ref[1:2, 0:1]).astype(BF16)
+            exact = residue / count_ref[1:2, 0:1]
+            grad, grad_flipped = exact.astype(BF16), exact.T.astype(BF16)
             for d in range(dp_size):
-                back, weight_parts = None, []
-                for o in range(owners):
-                    mine = grad[:, o * slots : (o + 1) * slots]
-                    part = dot_nn(mine, head_ref[d, o])
-                    back = part if back is None else back + part
-                    weight_parts.append(dot_tn(mine, low[:, d * cols : (d + 1) * cols]))
+                back = dot_nn(grad, head_ref[d].reshape(classes, cols))
+                weight_part = dot_nn(grad_flipped, low[:, d * cols : (d + 1) * cols])
                 for i in range(kept_ref.shape[2]):
-                    store_halves(kept_ref, sent_ref, (d, i), [part[:, i * tile : (i + 1) * tile] for part in weight_parts])
+                    parts = [weight_part[o * slots : (o + 1) * slots, i * tile : (i + 1) * tile] for o in range(owners)]
+                    store_halves(kept_ref, sent_ref, (d, i), parts)
                 pooled[:, d * cols : (d + 1) * cols] = back * (1.0 / pixels)
 
         @pl.when(step >= steps)
@@ -601,37 +668,31 @@
             place = pl.ds(pl.multiple_of((step - steps) * zone, zone), zone)
             spread = jnp.broadcast_to(pooled[...][:, None, :], (images, SLOT, wide)).reshape(zone, wide)
             ds = spread * silu_slope(summed[place, :]) * mask_ref[:, 1:2]
-            ds_ref[...] = ds
-            normed = (h_ref[...] - stat_ref[0:1]) * stat_ref[1:2]
+            ds_ref[...] = ds.astype(BF16)
             sums[0:8] += fold_rows(ds)
-            sums[8:16] += fold_rows(ds * normed)
+            sums[8:16] += fold_rows(ds * kept[place, :].astype(F32))
 
         @pl.when(step == 2 * steps - 1)
         def _():
-            send_rows(send_ref, [jnp.sum(sums[i * 8 : i * 8 + 8], axis=0, keepdims=True) for i in range(2)])
+            send_back_sums(send_ref, sums, stat_ref)
 
     send = (devices, 2 * wide // LANES + count_rows, LANES)
     grads = (owners // 2, dp_size, cols // tile, slots, tile)
-    again = pl.BlockSpec((zone, wide), lambda i: (lax.rem(i, steps), 0))
     once = pl.BlockSpec((zone, wide), lambda i: (jnp.minimum(i, steps - 1), 0))
     later = pl.BlockSpec((zone, wide), lambda i: (jnp.maximum(i - steps, 0), 0))
     return launch(
         kernel, "head_step", (2 * steps,),
         (hidden, inputs, parts, counts, norms, masks, head_all, slot_bias, image_cols),
         [
-            again, once, whole(parts.shape), whole(counts.shape), whole(norms.shape),
+            once, once, whole(parts.shape), whole(counts.shape), whole(norms.shape),
             pl.BlockSpec((zone, 2), lambda i: (lax.rem(i, steps), 0)),
             whole(head_all.shape), whole(slot_bias.shape), whole(image_cols.shape),
         ],
-        (out_of((rows, wide), F32), out_of((8, wide), F32), out_of(send, F32), out_of(grads, BF16), out_of(grads, BF16)),
+        (out_of((rows, wide), BF16), out_of((8, wide), F32), out_of(send, F32), out_of(grads, BF16), out_of(grads, BF16)),
         (later, whole((8, wide)), whole(send), whole(grads), whole(grads)),
-        [pltpu.VMEM((rows, wide), F32), pltpu.VMEM((images, wide), F32), pltpu.VMEM((16, wide), F32)],
+        [pltpu.VMEM((rows, wide), F32), pltpu.VMEM((rows, wide), BF16), pltpu.VMEM((zone, wide), F32), pltpu.VMEM((images, wide), F32), pltpu.VMEM((16, wide), F32)],
         6 * images * classes * wide,
     )
-
-
-def back_norm(grad, normed, gain, inverse, mask, bias_sum, gain_sum, count):
-    return gain * inverse * (grad - mask * (bias_sum + normed * gain_sum) / count)
 
 
 def back_expand(ds, hidden, parts, stat_wide, counts, norms, masks, narrow_hidden, stat_narrow, weights, layer, devices):
@@ -652,29 +713,20 @@
             for copy in copies:
                 copy.start()
             sums[...] = jnp.zeros_like(sums)
-            table = total_of(parts_ref)
-            terms[0:1] = row_of(table, 0, wide)
-            terms[1:2] = row_of(table, wide // LANES, wide)
+            back_terms(terms, total_of(parts_ref), stat_ref, count_ref[0:1, 0:1], wide)
             for copy in copies:
                 copy.wait()
 
-        gain = norm_ref[0, layer : layer + 1, 2 * narrow :]
-        normed = (h_ref[...] - stat_ref[0:1]) * stat_ref[1:2]
-        low = back_norm(
-            ds_ref[...], normed, gain, stat_ref[1:2], mask_ref[:, 0:1], terms[0:1], terms[1:2], count_ref[0:1, 0:1]
-        ).astype(BF16)
+        low = back_norm(ds_ref[...].astype(F32), h_ref[...].astype(F32), stat_ref, terms, mask_ref[:, 0:1]).astype(BF16)
         low_ref[...] = low
-        back = dot_nn(low, buffer[...])
-        inner = (narrow_ref[...] - narrow_stat[0:1]) * narrow_stat[1:2]
-        value = inner * norm_ref[0, layer : layer + 1, narrow : 2 * narrow] + norm_ref[1, layer : layer + 1, narrow : 2 * narrow]
-        total = back * silu_slope(value)
+        total = dot_nn(low, buffer[...]) * silu_slope(normed_of(narrow_ref[...], narrow_stat))
         out_ref[...] = total
         sums[0:8] += fold_rows(total)
-        sums[8:16] += fold_rows(total * inner)
+        sums[8:16] += fold_rows(total * narrow_ref[...])
 
         @pl.when(step == steps - 1)
         def _():
-            send_rows(send_ref, [jnp.sum(sums[i * 8 : i * 8 + 8], axis=0, keepdims=True) for i in range(2)])
+            send_back_sums(send_ref, sums, narrow_stat)
 
     send = (devices, 2 * narrow // LANES, LANES)
     return launch(
@@ -698,7 +750,7 @@
 
     def kernel(
         dz_ref, h_ref, parts_ref, stat_ref, count_ref, norm_ref, mask_ref, first_ref, first_stat, w_ref,
-        low_ref, out_ref, send_ref, buffer, sems, sums, shifted,
+        low_ref, out_ref, send_ref, buffer, sems, sums, terms, shifted,
     ):
         step = pl.program_id(0)
 
@@ -708,19 +760,13 @@
             for copy in copies:
                 copy.start()
             sums[...] = jnp.zeros_like(sums)
-            table = total_of(parts_ref)
-            bias_sum = row_of(table, 0, narrow)
-            gain_sum = row_of(table, narrow // LANES, narrow)
-            centre, inverse = stat_ref[0:1], stat_ref[1:2]
-            gain = norm_ref[0, layer : layer + 1, narrow : 2 * narrow]
-            count = count_ref[0:1, 0:1]
+            back_terms(terms, total_of(parts_ref), stat_ref, count_ref[0:1, 0:1], narrow)
             clear_edges(shifted, rows, zone)
 
             def body(index, carry):
                 start = pl.multiple_of(index * zone, zone)
                 place = pl.ds(start, zone)
-                normed = (h_ref[place, :] - centre) * inverse
-                value = back_norm(dz_ref[place, :], normed, gain, inverse, mask_ref[place, 0:1], bias_sum, gain_sum, count)
+                value = back_norm(dz_ref[place, :], h_ref[place, :], stat_ref, terms, mask_ref[place, 0:1])
                 low_ref[place, :] = value.astype(BF16)
                 store_shifted(shifted, pl.multiple_of(start + zone, zone), value, zone, narrow)
                 return carry
@@ -739,16 +785,14 @@
                 part = dot_nt(piece, buffer[tap * narrow : (tap + 1) * narrow])
                 total = part if total is None else total + part
         place = pl.ds(pl.multiple_of(base, 16), strip_rows)
-        inner = (first_ref[...] - first_stat[0:1]) * first_stat[1:2]
-        value = inner * norm_ref[0, layer : layer + 1, 0:narrow] + norm_ref[1, layer : layer + 1, 0:narrow]
-        total = total * silu_slope(value) * mask_ref[place, 1:2]
+        total = total * silu_slope(normed_of(first_ref[...], first_stat)) * mask_ref[place, 1:2]
         out_ref[...] = total
         sums[0:8] += fold_rows(total)
-        sums[8:16] += fold_rows(total * inner)
+        sums[8:16] += fold_rows(total * first_ref[...])
 
         @pl.when(step == steps - 1)
         def _():
-            send_rows(send_ref, [jnp.sum(sums[i * 8 : i * 8 + 8], axis=0, keepdims=True) for i in range(2)])
+            send_back_sums(send_ref, sums, first_stat)
 
     send = (devices, 2 * narrow // LANES, LANES)
     return launch(
@@ -760,7 +804,7 @@
         ],
         (out_of((rows, narrow), BF16), out_of((rows, narrow), F32), out_of(send, F32)),
         (whole((rows, narrow)), strip(strip_rows, narrow), whole(send)),
-        weights.scratch() + [pltpu.VMEM((16, narrow), F32), pltpu.VMEM((rows + 2 * zone, 3 * narrow), BF16)],
+        weights.scratch() + [pltpu.VMEM((16, narrow), F32), pltpu.VMEM((8, narrow), F32), pltpu.VMEM((rows + 2 * zone, 3 * narrow), BF16)],
         2 * rows * 9 * narrow * narrow,
     )
 
@@ -770,7 +814,6 @@
     wide = ds.shape[1]
     strip_rows = block_rows(rows, 6)
     steps = rows // strip_rows
-    below = layer - 1
 
     def kernel(
         dz_ref, first_ref, parts_ref, first_stat, count_ref, norm_ref, mask_ref, ds_ref, h_ref, x_ref, stat_ref, w_ref,
@@ -784,29 +827,22 @@
             for copy in copies:
                 copy.start()
             sums[...] = jnp.zeros_like(sums)
-            table = total_of(parts_ref)
-            terms[0:1] = row_of(table, 0, narrow)
-            terms[1:2] = row_of(table, narrow // LANES, narrow)
+            back_terms(terms, total_of(parts_ref), first_stat, count_ref[0:1, 0:1], narrow)
             for copy in copies:
                 copy.wait()
 
-        normed = (first_ref[...] - first_stat[0:1]) * first_stat[1:2]
-        low = back_norm(
-            dz_ref[...], normed, norm_ref[0, layer : layer + 1, 0:narrow], first_stat[1:2], mask_ref[:, 0:1],
-            terms[0:1], terms[1:2], count_ref[0:1, 0:1],
-        ).astype(BF16)
+        low = back_norm(dz_ref[...], first_ref[...], first_stat, terms, mask_ref[:, 0:1]).astype(BF16)
         low_ref[...] = low
-        grad = dot_nt(low, buffer[...]) + ds_ref[...]
-        inner = (h_ref[...] - stat_ref[0:1]) * stat_ref[1:2]
-        value = inner * norm_ref[0, below : below + 1, 2 * narrow :] + norm_ref[1, below : below + 1, 2 * narrow :]
-        total = grad * silu_slope(x_ref[...].astype(F32) + value)
-        out_ref[...] = total
+        grad = dot_nt(low, buffer[...]) + ds_ref[...].astype(F32)
+        hidden_here = h_ref[...].astype(F32)
+        total = grad * silu_slope(x_ref[...].astype(F32) + normed_of(hidden_here, stat_ref))
+        out_ref[...] = total.astype(BF16)
         sums[0:8] += fold_rows(total)
-        sums[8:16] += fold_rows(total * inner)
+        sums[8:16] += fold_rows(total * hidden_here)
 
         @pl.when(step == steps - 1)
         def _():
-            send_rows(send_ref, [jnp.sum(sums[i * 8 : i * 8 + 8], axis=0, keepdims=True) for i in range(2)])
+            send_back_sums(send_ref, sums, stat_ref)
 
     send = (devices, 2 * wide // LANES, LANES)
     return launch(
@@ -817,35 +853,34 @@
             whole(norms.shape), strip(strip_rows, 2), strip(strip_rows, wide), strip(strip_rows, wide), strip(strip_rows, wide),
             whole(stat_wide.shape), ANYWHERE,
         ],
-        (out_of((rows, narrow), BF16), out_of((rows, wide), F32), out_of(send, F32)),
+        (out_of((rows, narrow), BF16), out_of((rows, wide), BF16), out_of(send, F32)),
         (strip(strip_rows, narrow), strip(strip_rows, wide), whole(send)),
         weights.scratch() + [pltpu.VMEM((16, wide), F32), pltpu.VMEM((8, narrow), F32)],
         2 * rows * wide * narrow,
     )
 
 
-def last_back(dz, first_hidden, parts, stat_one, counts, norms, masks, layer):
+def last_back(dz, first_hidden, parts, stat_one, counts, masks):
     rows, narrow = dz.shape
     strip_rows = block_rows(rows, 3)
 
-    def kernel(dz_ref, first_ref, parts_ref, first_stat, count_ref, norm_ref, mask_ref, low_ref):
-        table = total_of(parts_ref)
-        normed = (first_ref[...] - first_stat[0:1]) * first_stat[1:2]
-        low_ref[...] = back_norm(
-            dz_ref[...], normed, norm_ref[0, layer : layer + 1, 0:narrow], first_stat[1:2], mask_ref[:, 0:1],
-            row_of(table, 0, narrow), row_of(table, narrow // LANES, narrow), count_ref[0:1, 0:1],
-        ).astype(BF16)
+    def kernel(dz_ref, first_ref, parts_ref, first_stat, count_ref, mask_ref, low_ref, terms):
+        @pl.when(pl.program_id(0) == 0)
+        def _():
+            back_terms(terms, total_of(parts_ref), first_stat, count_ref[0:1, 0:1], narrow)
+
+        low_ref[...] = back_norm(dz_ref[...], first_ref[...], first_stat, terms, mask_ref[:, 0:1]).astype(BF16)
 
     return launch(
         kernel, "last_back", (rows // strip_rows,),
-        (dz, first_hidden, parts, stat_one, counts, norms, masks),
+        (dz, first_hidden, parts, stat_one, counts, masks),
         [
             strip(strip_rows, narrow), strip(strip_rows, narrow), whole(parts.shape), whole(stat_one.shape), whole(counts.shape),
-            whole(norms.shape), strip(strip_rows, 2),
+            strip(strip_rows, 2),
         ],
         out_of((rows, narrow), BF16),
         strip(strip_rows, narrow),
-        [],
+        [pltpu.VMEM((8, narrow), F32)],
         rows * narrow,
     )
 
@@ -911,14 +946,88 @@
     )
 
 
-def padded(values):
-    return jnp.pad(values, ((0, -values.shape[0] % 16), (0, 0)))
-
-
-def gather_rows(moments_t):
-    low = [padded(moment.astype(BF16)) for moment in moments_t]
-    starts = [sum(part.shape[0] for part in low[:i]) for i in range(len(low))]
-    return lax.all_gather(jnp.concatenate(low, axis=0), "owner"), starts
+def gather_rows(items, olds, flipped):
+    sizes = [total.shape[0] for _, _, total in items]
+    heights = [size + -size % 16 for size in sizes]
+    starts = [sum(heights[:i]) for i in range(len(heights))]
+    kinds = sorted({kind for _, kind, _ in items})
+
+    def kernel(*refs):
+        grads, sources, out_ref = refs[: len(items)], refs[len(items) : -1], refs[-1]
+        for (layer, kind, _), grad, size, height, start in zip(items, grads, sizes, heights, starts):
+            old = sources[kinds.index(kind)][layer]
+            value = MOMENTUM * (old if flipped[kind] else old.T) + grad[...].astype(F32)
+            if height > size:
+                value = jnp.concatenate([value, jnp.zeros((height - size, LANES), F32)], axis=0)
+            out_ref[start : start + height] = value.astype(BF16)
+
+    operands = [total for _, _, total in items] + [olds[kind] for kind in kinds]
+    shape = (sum(heights), LANES)
+    low = launch(
+        kernel, "momenta_low", (1,), operands, [whole(a.shape) for a in operands], out_of(shape, BF16), whole(shape), [],
+        2**20,
+    )
+    return lax.all_gather(low, "owner"), starts
+
+
+def new_momenta(items, olds, flipped):
+    kinds = len(olds)
+
+    def kernel(*refs):
+        grads, sources, outs = refs[: len(items)], refs[len(items) : len(items) + kinds], refs[len(items) + kinds :]
+        for (layer, kind, _), grad in zip(items, grads):
+            value = grad[...].astype(F32)
+            outs[kind][layer] = MOMENTUM * sources[kind][layer] + (value if flipped[kind] else value.T)
+
+    operands = [total for _, _, total in items] + list(olds)
+    return launch(
+        kernel, "new_momenta", (1,), operands, [whole(a.shape) for a in operands],
+        tuple(out_of(old.shape, F32) for old in olds), tuple(whole(old.shape) for old in olds), [], 2**20,
+    )
+
+
+def head_update(total, head, head_m, head_v, slots):
+    classes, width = head.shape
+
+    def kernel(total_ref, *refs):
+        tiles = total_ref.shape[0] // slots
+        grad = jnp.concatenate(
+            [total_ref[i * slots : i * slots + slots, :].astype(F32)[:classes] for i in range(tiles)], axis=1
+        )[:, :width]
+        for out_ref, value in zip(refs[3:], adamw(refs[0][...], grad, refs[1][...], refs[2][...], LR_HEAD, DECAY_HEAD)):
+            out_ref[...] = value
+
+    operands = [total, head, head_m, head_v]
+    return launch(
+        kernel, "head_update", (1,), operands, [whole(a.shape) for a in operands],
+        (out_of(head.shape, F32),) * 3, (whole(head.shape),) * 3, [], 2**20,
+    )
+
+
+def norm_update(parts, norms, norm_m, norm_v):
+    layers, count = len(parts), len(parts[0])
+    narrow = parts[0][0].shape[1] * LANES // 2
+    widths = [narrow] * (count - 1) + [norms.shape[2] - narrow * (count - 1)]
+
+    def kernel(*refs):
+        tables, (p_ref, m_ref, v_ref), outs = refs[: layers * count], refs[layers * count : -3], refs[-3:]
+        for layer in range(layers):
+            begin = 0
+            for number, width in enumerate(widths):
+                table = total_of(tables[layer * count + number])
+                span = slice(begin, begin + width)
+                begin += width
+                for row in range(2):
+                    grad = row_of(table, (1 - row) * (width // LANES), width)
+                    here = (row, slice(layer, layer + 1), span)
+                    for out_ref, value in zip(outs, adamw(p_ref[here], grad, m_ref[here], v_ref[here], LR_VECTOR, 0.0)):
+                        out_ref[here] = value
+
+    operands = [part for group in parts for part in group] + [norms, norm_m, norm_v]
+    return launch(
+        kernel, "norm_update", (1,), operands, [whole(a.shape) for a in operands],
+        (out_of(norms.shape, F32),) * 3, (whole(norms.shape),) * 3, [], 2**20,
+    )
 
 
 def upper_pairs(owners):
@@ -953,15 +1062,6 @@
 
 def bit_of(bit):
     return (my_index() >> bit) & 1
-
-
-def keep_half(values, bit):
-    own = bit_of(bit)
-    half = values.shape[0] // 2
-    values = values.reshape((2, half) + values.shape[1:])
-    kept = lax.dynamic_index_in_dim(values, own, 0, keepdims=False)
-    sent = lax.dynamic_index_in_dim(values, 1 - own, 0, keepdims=False)
-    return kept + swap(sent, bit)
 
 
 def split_two(values):
@@ -1018,7 +1118,7 @@
     )
 
 
-def apply_polynomials(early, late, gathered, starts, products, masters):
+def apply_polynomials(early, late, gathered, starts, products, masters, flipped):
     owners = gathered[0].shape[0]
     y_bit, z_bit = dp_bits()[:2]
     shift = lax.axis_size("owner").bit_length() - 1
@@ -1032,19 +1132,20 @@
         my_z = (place >> (z_bit - shift)) & 1
 
         def finish(layer, kind, poly, all_ref, start):
-            size = sources[kind].shape[2]
+            size = sources[kind].shape[1 if flipped[kind] else 2]
             total = None
             for o in range(owners):
-                part = dot_nt(poly[:, o * LANES : (o + 1) * LANES], all_ref[o, start : start + size, :])
+                left, right = poly[:, o * LANES : (o + 1) * LANES], all_ref[o, start : start + size, :]
+                part = dot_nt(right, left) if flipped[kind] else dot_nt(left, right)
                 total = part if total is None else total + part
             outs[kind][layer] = sources[kind][layer] * (1.0 - LR_MATRIX * DECAY_MATRIX) - LR_MATRIX * total
 
-        for number, (layer, kind) in enumerate(early):
+        for number, (layer, kind, _) in enumerate(early):
             y, z = number // 2, number % 2
             turn = y ^ my_y
             poly = jnp.where(my_z == z, own_ref[turn].astype(F32), other_ref[turn].astype(F32)).astype(BF16)
             finish(layer, kind, poly, early_all, starts[0][number])
-        for number, (layer, kind) in enumerate(late):
+        for number, (layer, kind, _) in enumerate(late):
             finish(layer, kind, late_ref[number ^ my_y], late_all, starts[1][number])
 
     operands = (q_own, q_other, q_late, gathered[0], gathered[1]) + masters
@@ -1055,22 +1156,36 @@
     )
 
 
-def newton_schulz(early, late, moments_t, masters):
+def newton_schulz(early, late, olds, masters, flipped):
     y_bit, z_bit, turn_bit = dp_bits()[:3]
     gathered, starts, grams = [], [], []
-    for names in (early, late):
-        both, begin = gather_rows([moments_t[name] for name in names])
+    for items in (early, late):
+        both, begin = gather_rows(items, olds, flipped)
+        both, grams = lax.optimization_barrier((both, grams))
         gathered.append(both)
         starts.append(begin)
-        values = own_grams(both, begin, [moments_t[name].shape[0] for name in names])
-        for bit in dp_bits():
-            if values.shape[0] > 1:
-                values = keep_half(values, bit)
+        grams.append(own_grams(both, begin, [total.shape[0] for _, _, total in items]))
+    on_late, moments = bit_of(turn_bit) == 1, None
+    for bit in dp_bits():
+        if bit == turn_bit:
+            continue
+        kept, sent = [], []
+        for values in grams:
+            whole_count = values.shape[0]
+            if whole_count > 1:
+                halves = values.reshape((2, whole_count // 2) + values.shape[1:])
+                kept.append(lax.dynamic_index_in_dim(halves, bit_of(bit), 0, keepdims=False))
+                sent.append(lax.dynamic_index_in_dim(halves, 1 - bit_of(bit), 0, keepdims=False))
             else:
-                values = values + swap(values, bit)
-        grams.append(values[0])
-    on_late = bit_of(turn_bit) == 1
-    mine = jnp.where(on_late, grams[1], grams[0])
+                kept.append(values)
+                sent.append(values)
+        got = swap(jnp.concatenate(sent, axis=0), bit)
+        if moments is None:
+            moments = new_momenta(early + late, olds, flipped)
+            got, moments = lax.optimization_barrier((got, moments))
+        grams = [kept[0] + got[: kept[0].shape[0]], kept[1] + got[kept[0].shape[0] :]]
+    got = swap(jnp.where(on_late, grams[0][0], grams[1][0]), turn_bit)
+    mine = jnp.where(on_late, grams[1][0], grams[0][0]) + got
     packed = lax.all_gather(mine, "owner", tiled=True)
     own = polynomial(packed, gathered[0].shape[0])
     other = swap(own, turn_bit)
@@ -1080,7 +1195,7 @@
     pair = jnp.stack([both, swap(both, y_bit)])
     q_own, q_late = pair[:, 0], pair[:, 1]
     q_other = swap(q_own, z_bit)
-    return apply_polynomials(early, late, gathered, starts, (q_own, q_other, q_late), masters)
+    return apply_polynomials(early, late, gathered, starts, (q_own, q_other, q_late), masters, flipped), moments
 
 
 def adamw(weight, grad, first, second, rate, decay):
@@ -1108,12 +1223,12 @@
     weight_img = valid * loss_weight
     tallies = jnp.stack([valid_count[0] * pixels, jnp.sum(weight_img)]).astype(F32)
     tallies = jnp.pad(tallies, (0, 6))[:, None]
-    counts = jnp.sum(exchange(jnp.broadcast_to(tallies[None], (devices, 8, LANES))), axis=0)
+    tallies = jnp.broadcast_to(tallies, (8, LANES))
 
     in_map = (jnp.arange(SLOT) < side).astype(F32)
     pad_mask = jnp.broadcast_to(in_map, (side, count_img, SLOT))
     masks = jnp.stack([pad_mask * valid.astype(F32)[:, None], pad_mask], axis=-1).reshape(rows, 2)
-    pixels_in = jnp.pad(images, ((0, 0), (0, 0), (0, SLOT - side), (0, 0))).transpose(1, 0, 2, 3).reshape(rows, wide)
+    arrange = lambda maps: jnp.pad(maps, ((0, 0), (0, 0), (0, SLOT - side), (0, 0))).transpose(1, 0, 2, 3).reshape(rows, wide)
 
     rows_of = (w_reduce.shape[2], w_spatial.shape[2], w_expand.shape[2])
     starts = (0, rows_of[0], rows_of[0] + rows_of[1])
@@ -1121,14 +1236,17 @@
         [part.T.astype(BF16) for part in (w_reduce[layer], w_spatial[layer], w_expand[layer])] for layer in range(LAYERS)
     ]
     mats = []
-    if dp_size == 8 and owner_size == 4:
+    if dp_size == 8 and owner_size == 4 and LAYERS == 2:
         first = Gather(packs[0][0], (4, 3, 2, 1, 0))
         first.send()
         first.join()
         first.send()
-        halves = [[part[: part.shape[0] // 2], part[part.shape[0] // 2 :]] for part in packs[0][1:]]
-        sets = [jnp.concatenate([part[i] for part in halves], axis=0) for i in range(2)]
-        first.got, sets = lax.optimization_barrier((first.got, sets))
+        half = rows_of[1] // 2
+        sets = [packs[0][1][:half], packs[0][1][half:]]
+        packed = jnp.concatenate([packs[0][2], packs[1][0]], axis=0)
+        third = lax.all_gather(packed, AXES).reshape(dp_size, owner_size, packed.shape[0], LANES)
+        first.got, sets, images = lax.optimization_barrier((first.got, sets, images))
+        pixels_in = arrange(images)
         others = [Gather(sets[0], (4, 3, 1, 2, 0)), Gather(sets[1], (4, 2, 3, 1, 0))]
         first.join()
         first.send()
@@ -1139,38 +1257,41 @@
         for flow in others:
             flow.send()
         meet([first] + others)
-        first.values, pixels_in, masks, counts, packs[1] = lax.optimization_barrier(
-            (first.values, pixels_in, masks, counts, packs[1])
-        )
+        first.values, pixels_in, masks, tallies = lax.optimization_barrier((first.values, pixels_in, masks, tallies))
         first.send()
         for flow in others:
             flow.send()
         first.join()
         mats.append(relative_weights([(first.values, first.masks, 0, rows_of[0], 0)], rows_of[0], dp_size, owner_size))
-        h1_first, sums = first_reduce(pixels_in, masks, mats[0], devices)
-        got, h1_first = lax.optimization_barrier(([flow.got for flow in others], h1_first))
+        h1_first, sums = first_reduce(pixels_in, masks, tallies, mats[0], devices)
+        got, h1_first, packs[1] = lax.optimization_barrier(([flow.got for flow in others], h1_first, packs[1]))
         for flow, values in zip(others, got):
             flow.got = values
             flow.join()
-        for _ in range(2):
-            for flow in others:
-                flow.send()
-            meet(others)
-        tops = (rows_of[1] // 2, rows_of[2] // 2)
-        for kind in (1, 2):
-            pieces = [
-                (others[i].values, others[i].masks, 0 if kind == 1 else tops[0], tops[kind - 1], i * tops[kind - 1])
-                for i in range(2)
-            ]
-            mats.append(relative_weights(pieces, rows_of[kind], dp_size, owner_size))
+        for flow in others:
+            flow.send()
+        first_parts = exchange(sums)
+        got, first_parts = lax.optimization_barrier(([flow.got for flow in others], first_parts))
+        for flow, values in zip(others, got):
+            flow.got = values
+            flow.join()
+            flow.send()
+        meet(others)
+        pieces = [(others[i].values, others[i].masks, 0, half, i * half) for i in range(2)]
+        mats.append(relative_weights(pieces, rows_of[1], dp_size, owner_size))
+        mats.append(gathered_weights(third, 0, rows_of[2]))
     layers_done = len(mats) // 3
-    for layer in range(layers_done, LAYERS):
-        packed = jnp.concatenate(packs[layer], axis=0)
+    if layers_done:
+        packed = jnp.concatenate(packs[1][1:], axis=0)
         gathered = lax.all_gather(packed, AXES).reshape(dp_size, owner_size, packed.shape[0], LANES)
-        for kind in range(3):
-            if dp_size <= 8:
-                mats.append(gathered_weights(gathered, starts[kind], rows_of[kind]))
-            else:
+        mats.append(gathered_weights(third, rows_of[2], rows_of[0]))
+        mats.append(gathered_weights(gathered, 0, rows_of[1]))
+        mats.append(gathered_weights(gathered, rows_of[1], rows_of[2]))
+    else:
+        for layer in range(LAYERS):
+            packed = jnp.concatenate(packs[layer], axis=0)
+            gathered = lax.all_gather(packed, AXES).reshape(dp_size, owner_size, packed.shape[0], LANES)
+            for kind in range(3):
                 piece = gathered[:, :, starts[kind] : starts[kind] + rows_of[kind]]
                 piece = piece.transpose(1, 0, 2, 3).reshape(1, owner_size, -1, LANES)
                 mats.append(gathered_weights(piece, 0, piece.shape[2]))
@@ -1187,23 +1308,28 @@
     slot_labels = (labels // classes) * slots + labels % classes
     image_cols = jnp.stack([slot_labels, weight_img], axis=1)
 
-    weight_total = counts[1, 0]
     norms = norm_params
     h1, h2, h3, a1, a2, stat1, stat2, stat3 = ([None] * LAYERS for _ in range(8))
-    inputs, inputs_low = [pixels_in] + [None] * (LAYERS - 1), [pixels_in] + [None] * (LAYERS - 1)
+    if not layers_done:
+        pixels_in = arrange(images)
+    inputs = [pixels_in] + [None] * (LAYERS - 1)
     if layers_done:
         h1[0] = h1_first
     else:
-        h1[0], sums = first_reduce(pixels_in, masks, mats[0], devices)
+        h1[0], sums = first_reduce(pixels_in, masks, tallies, mats[0], devices)
     for layer in range(LAYERS):
+        parts = first_parts if layer == 0 and layers_done else exchange(sums)
+        if layer == 0:
+            counts = jnp.sum(parts[:, parts.shape[1] - 8 :], axis=0)
+            weight_total = counts[1, 0]
         a1[layer], h2[layer], stat1[layer], sums = spatial_conv(
-            h1[layer], exchange(sums), counts, norms, masks, mats[3 * layer + 1], layer, zone, devices
+            h1[layer], parts, counts, norms, masks, mats[3 * layer + 1], layer, zone, devices
         )
         a2[layer], h3[layer], stat2[layer], sums = expand(
             h2[layer], exchange(sums), counts, norms, masks, mats[3 * layer + 2], layer, devices
         )
         if layer < LAYERS - 1:
-            inputs[layer + 1], inputs_low[layer + 1], h1[layer + 1], stat3[layer], sums = close_and_reduce(
+            inputs[layer + 1], h1[layer + 1], stat3[layer], sums = close_and_reduce(
                 h3[layer], inputs[layer], exchange(sums), counts, norms, masks, mats[3 * layer + 3], layer, devices
             )
     last = LAYERS - 1
@@ -1225,7 +1351,7 @@
     blocked = lambda halves: tuple(half.reshape(devices // 2, -1, LANES) for half in halves)
     head_flow = Flow([blocked(head_halves)], left, turned[0])
     flows = [head_flow]
-    norm_sums = []
+    norm_sums, three_flow, two_flow = [], {}, {}
     wide_rows = 2 * wide // LANES
     for layer in reversed(range(LAYERS)):
         parts3 = exchange(sums)
@@ -1235,22 +1361,19 @@
         dh3, dz2, sums = back_expand(
             ds, h3[layer], parts3, stat3[layer], counts, norms, masks, h2[layer], stat2[layer], mats[3 * layer + 2], layer, devices
         )
+        sums = advance(sums, flows)
         grad_three = blocked(weight_grad(dh3, a2[layer], owner_size))
-        if layer == 0:
-            three_flow = Flow([grad_three], left, turned[0])
-            flows.append(three_flow)
+        three_flow[layer] = Flow([grad_three], left, turned[2] if layer > 0 else turned[0])
+        flows.append(three_flow[layer])
         parts2 = exchange(sums)
         parts2 = advance(parts2, flows)
         dh2, dz1, sums = back_conv(
             dz2, h2[layer], parts2, stat2[layer], counts, norms, masks, h1[layer], stat1[layer], mats[3 * layer + 1], layer, zone, devices
         )
+        sums = advance(sums, flows)
         grad_two = blocked(spatial_grad(a1[layer], dh2, owner_size, zone))
-        if layer > 0:
-            high_flow = Flow([grad_three, grad_two], left, turned[1])
-            flows.append(high_flow)
-        else:
-            two_flow = Flow([grad_two], left, [0])
-            flows.append(two_flow)
+        two_flow[layer] = Fork(grad_two, left, 0, [turned[0 if layer > 0 else 2][1:], turned[1][1:]])
+        flows.append(two_flow[layer])
         parts1 = exchange(sums)
         parts1 = advance(parts1, flows)
         if layer > 0:
@@ -1258,53 +1381,48 @@
                 dz1, h1[layer], parts1, stat1[layer], counts, norms, masks, ds, h3[layer - 1], inputs[layer - 1], stat3[layer - 1],
                 mats[3 * layer], layer, devices,
             )
+            sums = advance(sums, flows)
         else:
-            dh1 = last_back(dz1, h1[layer], parts1, stat1[layer], counts, norms, masks, layer)
-        grad_one = blocked(weight_grad(inputs_low[layer], dh1, owner_size))
+            dh1 = last_back(dz1, h1[layer], parts1, stat1[layer], counts, masks)
+            dh1 = advance(dh1, [two_flow[0]])
+        grad_one = blocked(weight_grad(inputs[layer], dh1, owner_size))
         if layer > 0:
-            one_flow = Flow([grad_one], left, turned[2])
+            one_flow = Flow([grad_one], left, turned[0])
             flows.append(one_flow)
-        norm_sums.insert(0, [jnp.sum(part, axis=0).reshape(2, -1) for part in (parts1, parts2, parts3[:, :wide_rows])])
-    norm_grad = jnp.stack(
-        [jnp.stack([jnp.concatenate([part[kind] for part in norm_sums[layer]]) for layer in range(LAYERS)]) for kind in (1, 0)]
-    )
+        norm_sums.insert(0, (parts1, parts2, parts3))
     extra = jnp.sum(extra[:, wide_rows:], axis=0)
     class_rows = owner_size * slots // LANES
     bias_raw = extra[:class_rows].reshape(owner_size, slots)[:, :classes].reshape(-1)
     loss_sum = extra[class_rows, 0]
     grad_bias = bias_raw / weight_total
-    last_flow = Flow([grad_one], left, [0])
-    low_sums = jnp.concatenate([two_flow.result(), last_flow.result()], axis=1)
-    remaining = [bit for bit in left if bit != 0]
-    height = low_sums.shape[1]
-    third = height // 3 // 16 * 16
-    cuts = [0, third, 2 * third, height]
-    thirds = []
-    for i in range(3):
-        order = turned[i][1:]
-        piece = low_sums[:, cuts[i] : cuts[i + 1]]
-        place = remaining.index(order[0])
-        own = (my_index() >> order[0]) & 1
-        thirds.append(Flow([(half_of(piece, place, own), half_of(piece, place, 1 - own))], remaining, order))
+    last_flow = Flow([grad_one], left, turned[0])
+    last_flow.sent = advance(last_flow.sent, flows, True)
+    last_flow.send()
+    flows.append(last_flow)
+    rest_updates = [
+        lambda: norm_update(norm_sums, norm_params, norm_m, norm_v),
+        lambda: head_update(head_flow.result(), head, head_m, head_v, slots),
+    ]
+    updates = []
+    while rest_updates or any(flow.got is not None for flow in flows):
+        if rest_updates:
+            updates.append(rest_updates.pop(0)())
+        updates = advance(updates, flows, True)
     high, low = LAYERS - 1, 0
-    low_sums = jnp.concatenate([flow.result() for flow in thirds], axis=0)
-    two_low, one_low = low_sums[: rows_of[1]], low_sums[rows_of[1] :]
-    three_low, one_high = three_flow.result(), one_flow.result()
-    three_high, two_high = jnp.split(high_flow.result(), [rows_of[2]])
-    head_sum = head_flow.result().astype(F32).reshape(-1, slots, LANES)[:, :classes]
-    head_sum = head_sum.transpose(1, 0, 2).reshape(classes, -1)[:, : head.shape[1]]
-
-    olds = (mom_reduce, mom_spatial, mom_expand)
-    moment = lambda layer, kind, total: MOMENTUM * olds[kind][layer].T + total.astype(F32)
+    one_low, one_high = last_flow.result(), one_flow.result()
+    three_low, three_high = three_flow[low].result(), three_flow[high].result()
+    two_low, two_high = two_flow[low].result(), two_flow[high].result()
     early = [(high, 2, three_high), (high, 1, two_high), (high, 0, one_high), (low, 2, three_low)]
     late = [(low, 1, two_low), (low, 0, one_low)]
-    moments_t = {(layer, kind): moment(layer, kind, total) for layer, kind, total in early + late}
-    updated = newton_schulz(
-        [item[:2] for item in early], [item[:2] for item in late], moments_t, (w_reduce, w_spatial, w_expand)
-    )
-    moments = [jnp.stack([moments_t[layer, kind].T for layer in range(LAYERS)]) for kind in range(3)]
-    new_head, new_head_m, new_head_v = adamw(head, head_sum, head_m, head_v, LR_HEAD, DECAY_HEAD)
-    new_norm, new_norm_m, new_norm_v = adamw(norm_params, norm_grad, norm_m, norm_v, LR_VECTOR, 0.0)
+    stored = lambda arrays: tuple(a if a.shape[2] % LANES == 0 else jnp.swapaxes(a, 1, 2) for a in arrays)
+    results = newton_schulz(
+        early, late, stored((mom_reduce, mom_spatial, mom_expand)), stored((w_reduce, w_spatial, w_expand)),
+        [size % LANES != 0 for size in rows_of],
+    )
+    updated, moments = (
+        [jnp.swapaxes(a, 1, 2) if size % LANES else a for a, size in zip(arrays, rows_of)] for arrays in results
+    )
+    (new_norm, new_norm_m, new_norm_v), (new_head, new_head_m, new_head_v) = updates
     new_bias, new_bias_m, new_bias_v = adamw(head_bias, grad_bias, bias_m, bias_v, LR_VECTOR, 0.0)
     return (
         loss_sum,

time: 805 us -> 746 us (0.927)
  waiting for transfers between devices: 178 us -> 153 us
  local copies, waits for them, and re-layouts: 69.8 us -> 46.5 us
  blocking collectives: 102 us -> 112 us
  other arithmetic: 43.6 us -> 35.3 us
    ppermute x59 -> x64, waiting for transfers between devices: 151 us -> 126 us  [swap(): lax.ppermute(values, AXES, [(src, src ^ 1 << bit) for src in range(count)])]
    unnamed x168 -> x121, local copies, waits for them, and re-layouts: 34.4 us -> 17.7 us
    all_to_all x8 -> x7, starting transfers between devices: 37.7 us -> 25.9 us  [exchange(): return lax.all_to_all(copies, AXES, 0, 0, tiled=True)]
    all_to_all x5, blocking collectives: 84.5 us -> 94.8 us  [exchange(): return lax.all_to_all(copies, AXES, 0, 0, tiled=True)]
    pallas_call x23 -> x28, Pallas kernels: 283 us -> 275 us  [launch(): pl.pallas_call(grouped, name=name, grid=grid, in_specs=flat_specs, out_sp...]
    ppermute x59 -> x64, starting transfers between devices: 62.5 us -> 69.7 us  [swap(): lax.ppermute(values, AXES, [(src, src ^ 1 << bit) for src in range(count)])]
    all_to_all x8 -> x7, waiting for transfers between devices: 23.8 us -> 19 us  [exchange(): return lax.all_to_all(copies, AXES, 0, 0, tiled=True)]
  transfers between devices with their start and end apart: 70 -> 75, of which waited for: 38 -> 32; matrix products, arithmetic and copies ran while one was open for 9% -> 5% of each run, Pallas kernels for 28% -> 29%
where the time goes in v4:
time: 746 us; the launch traced here: 734 us
  Pallas kernels  275 us (37%)
  waiting for transfers between devices  153 us (21%)
  blocking collectives  112 us (15%)
  starting transfers between devices  95.9 us (13%)
  local copies, waits for them, and re-layouts  46.5 us (6%)
  other arithmetic  35.3 us (5%)
  between operations  16.1 us (2%)
    pallas_call x28, Pallas kernels, launch(): pl.pallas_call(grouped, name=name, grid=grid, in_specs=flat_specs, out_sp...  275 us
    ppermute x64, waiting for transfers between devices, swap(): lax.ppermute(values, AXES, [(src, src ^ 1 << bit) for src in range(count)])  126 us
    all_to_all x5, blocking collectives, exchange(): return lax.all_to_all(copies, AXES, 0, 0, tiled=True)  94.8 us
    ppermute x64, starting transfers between devices, swap(): lax.ppermute(values, AXES, [(src, src ^ 1 << bit) for src in range(count)])  69.7 us
    all_to_all x7, starting transfers between devices, exchange(): return lax.all_to_all(copies, AXES, 0, 0, tiled=True)  25.9 us
    all_to_all x7, waiting for transfers between devices, exchange(): return lax.all_to_all(copies, AXES, 0, 0, tiled=True)  19 us
    unnamed x121, local copies, waits for them, and re-layouts  17.7 us
  transfers between devices with their start and end apart: 75, of which 32 were waited for; matrix products, arithmetic and copies ran while one was open for 5% of the time, Pallas kernels for 29%

profile of v4, /device:TPU:0, one launch (start us, length us, event | category | flops | bytes accessed | tf_op | source)
XLA Modules:
  0.0 733.5 jit_solution(15357577416663575465)
XLA Ops:
  56.6 8.9 %reduce_first.1 = (f32[1344,512]{1,0:T(8,128)}, f32[32,16,128]{2,1,0:T(8,128)}) custom-call(bf16[1344,2048]{1,0:T(8,128)(2,1)} %bitcast.260, f32[1344,2]{1,0:T(8,128)} %copy.74.refs_1_.refs_4_.refs_5_.refs_6_, f32[8,128]{1,0:T(8,128)} %broadcast_in_dim.36.refs_2_, bf16[16,256,128]{2,1,0:T(8,128)(2,1)} %copy-done.47, ...), custom_call_target="tpu_custom_call" | custom-call | flops 2818572288 | bytes 10631680 | tf_op jit(solution)/shard_map/reduce_first/pallas_call | solution.py:345
  78.9 8.8 %all-to-all-done.refs_1_ = f32[32,16,128]{2,1,0:T(8,128)} async-done(((f32[32,16,128]{2,1,0:T(8,128)}), f32[32,16,128]{2,1,0:T(8,128)}, u32[]{:S(2)}, u32[]{:S(2)}) %all-to-all-start) | async-done | bytes 262176 | tf_op jit(solution)/shard_map/all_to_all | solution.py:45
  94.3 13.7 %spatial_conv.2 = (bf16[1344,512]{1,0:T(8,128)(2,1)}, f32[1344,512]{1,0:T(8,128)}, f32[8,512]{1,0:T(8,128)}, f32[32,8,128]{2,1,0:T(8,128)}) custom-call(f32[1344,512]{1,0:T(8,128)} %get-tuple-element.291.refs_0_.refs_7_.refs_1_, f32[32,16,128]{2,1,0:T(8,128)} %all-to-all-done.refs_1_, f32[8,128]{1,0:T(8,128)} %slice_reduce_fusion.1.refs_2_.refs_3_.refs_4_, ...), custom_call_target="tpu_custom_call" | custom-call | flops 6341787648 | bytes 12073472 | tf_op jit(solution)/shard_map/spatial_conv/pallas_call | solution.py:345
  108.0 13.7 %all_to_all.60.refs_1_ = f32[32,8,128]{2,1,0:T(8,128)} all-to-all(f32[32,8,128]{2,1,0:T(8,128)} %get-tuple-element.301), channel_id=1, replica_groups=mesh['dp'=8,'owner'=4] {'dp','owner'}, dimensions={0} | all-to-all | bytes 262144 | tf_op jit(solution)/shard_map/all_to_all | solution.py:45
  121.7 9.6 %expand.2 = (bf16[1344,512]{1,0:T(8,128)(2,1)}, bf16[1344,2048]{1,0:T(8,128)(2,1)}, f32[8,512]{1,0:T(8,128)}, f32[32,32,128]{2,1,0:T(8,128)}) custom-call(f32[1344,512]{1,0:T(8,128)} %get-tuple-element.300.refs_0_.refs_7_.refs_1_, f32[32,8,128]{2,1,0:T(8,128)} %all_to_all.60.refs_1_, f32[8,128]{1,0:T(8,128)} %slice_reduce_fusion.1.refs_2_.refs_3_.refs_4_, ...), custom_call_target="tpu_custom_call" | custom-call | flops 2818572288 | bytes 14563840 | tf_op jit(solution)/shard_map/expand/pallas_call | solution.py:345
  131.3 33.4 %all_to_all.61.refs_2_ = f32[32,32,128]{2,1,0:T(8,128)} all-to-all(f32[32,32,128]{2,1,0:T(8,128)} %get-tuple-element.303), channel_id=1, replica_groups=mesh['dp'=8,'owner'=4] {'dp','owner'}, dimensions={0} | all-to-all | bytes 1048576 | tf_op jit(solution)/shard_map/all_to_all | solution.py:45
  164.7 13.4 %close_and_reduce.1 = (bf16[1344,2048]{1,0:T(8,128)(2,1)}, f32[1344,512]{1,0:T(8,128)}, f32[8,2048]{1,0:T(8,128)}, f32[32,8,128]{2,1,0:T(8,128)}) custom-call(bf16[1344,2048]{1,0:T(8,128)(2,1)} %get-tuple-element.302.refs_0_.refs_8_.refs_1_, bf16[1344,2048]{1,0:T(8,128)(2,1)} %bitcast.261, f32[32,32,128]{2,1,0:T(8,128)} %all_to_all.61.refs_2_, ...), custom_call_target="tpu_custom_call" | custom-call | flops 2818572288 | bytes 24246784 | tf_op jit(solution)/shard_map/close_and_reduce/pallas_call | solution.py:345
  178.1 12.3 %all_to_all.62.refs_1_ = f32[32,8,128]{2,1,0:T(8,128)} all-to-all(f32[32,8,128]{2,1,0:T(8,128)} %get-tuple-element.305), channel_id=1, replica_groups=mesh['dp'=8,'owner'=4] {'dp','owner'}, dimensions={0} | all-to-all | bytes 262144 | tf_op jit(solution)/shard_map/all_to_all | solution.py:45
  190.3 13.2 %spatial_conv.3 = (bf16[1344,512]{1,0:T(8,128)(2,1)}, f32[1344,512]{1,0:T(8,128)}, f32[8,512]{1,0:T(8,128)}, f32[32,8,128]{2,1,0:T(8,128)}) custom-call(f32[1344,512]{1,0:T(8,128)} %get-tuple-element.304.refs_0_.refs_7_.refs_1_, f32[32,8,128]{2,1,0:T(8,128)} %all_to_all.62.refs_1_, f32[8,128]{1,0:T(8,128)} %slice_reduce_fusion.1.refs_2_.refs_3_.refs_4_, ...), custom_call_target="tpu_custom_call" | custom-call | flops 6341787648 | bytes 14039552 | tf_op jit(solution)/shard_map/spatial_conv/pallas_call | solution.py:345
  203.6 11.5 %all_to_all.63.refs_1_ = f32[32,8,128]{2,1,0:T(8,128)} all-to-all(f32[32,8,128]{2,1,0:T(8,128)} %get-tuple-element.309), channel_id=1, replica_groups=mesh['dp'=8,'owner'=4] {'dp','owner'}, dimensions={0} | all-to-all | bytes 262144 | tf_op jit(solution)/shard_map/all_to_all | solution.py:45
  215.1 9.8 %expand.3 = (bf16[1344,512]{1,0:T(8,128)(2,1)}, bf16[1344,2048]{1,0:T(8,128)(2,1)}, f32[8,512]{1,0:T(8,128)}, f32[32,32,128]{2,1,0:T(8,128)}) custom-call(f32[1344,512]{1,0:T(8,128)} %get-tuple-element.308.refs_0_.refs_7_.refs_1_, f32[32,8,128]{2,1,0:T(8,128)} %all_to_all.63.refs_1_, f32[8,128]{1,0:T(8,128)} %slice_reduce_fusion.1.refs_2_.refs_3_.refs_4_, ...), custom_call_target="tpu_custom_call" | custom-call | flops 2818572288 | bytes 17185280 | tf_op jit(solution)/shard_map/expand/pallas_call | solution.py:345
  228.3 7.3 all-gather.14.cloned.1.call-done
  235.6 8.4 %all-to-all-done.5.refs_2_ = f32[32,32,128]{2,1,0:T(8,128)S(1)} async-done(((f32[32,32,128]{2,1,0:T(8,128)}), f32[32,32,128]{2,1,0:T(8,128)S(1)}, u32[]{:S(2)}, u32[]{:S(2)}) %all-to-all-start.5) | async-done | bytes 524320 | tf_op jit(solution)/shard_map/all_to_all | solution.py:45
  244.9 32.4 %head_step.1 = (bf16[1344,2048]{1,0:T(8,128)(2,1)}, f32[8,2048]{1,0:T(8,128)}, f32[32,48,128]{2,1,0:T(8,128)}, bf16[2,8,2,256,128]{4,3,2,1,0:T(8,128)(2,1)}, bf16[2,8,2,256,128]{4,3,2,1,0:T(8,128)(2,1)}) custom-call(bf16[1344,2048]{1,0:T(8,128)(2,1)} %get-tuple-element.310.refs_0_.refs_1_, bf16[1344,2048]{1,0:T(8,128)(2,1)} %get-tuple-element.311.refs_1_.refs_0_, ...), custom_call_target="tpu_custom_call" | custom-call | flops 301989888 | bytes 26376896 | tf_op jit(solution)/shard_map/head_step/pallas_call | solution.py:345
  277.3 24.0 %all_to_all.64.refs_2_.refs_5_ = f32[32,48,128]{2,1,0:T(8,128)} all-to-all(f32[32,48,128]{2,1,0:T(8,128)} %get-tuple-element.313), channel_id=1, replica_groups=mesh['dp'=8,'owner'=4] {'dp','owner'}, dimensions={0} | all-to-all | bytes 1572864 | tf_op jit(solution)/shard_map/all_to_all | solution.py:45
  301.2 13.0 %back_expand.2 = (bf16[1344,2048]{1,0:T(8,128)(2,1)}, f32[1344,512]{1,0:T(8,128)}, f32[32,8,128]{2,1,0:T(8,128)}) custom-call(bf16[1344,2048]{1,0:T(8,128)(2,1)} %get-tuple-element.315.refs_0_.refs_7_, bf16[1344,2048]{1,0:T(8,128)(2,1)} %get-tuple-element.310.refs_0_.refs_1_, f32[32,48,128]{2,1,0:T(8,128)} %all_to_all.64.refs_2_.refs_5_, ...), custom_call_target="tpu_custom_call" | custom-call | flops 2818572288 | bytes 29899264 | tf_op jit(solution)/shard_map/back_expand/pallas_call | solution.py:345
  323.2 7.3 weight_grad.4
  333.1 15.2 %back_conv.2 = (bf16[1344,512]{1,0:T(8,128)(2,1)}, f32[1344,512]{1,0:T(8,128)}, f32[32,8,128]{2,1,0:T(8,128)}) custom-call(f32[1344,512]{1,0:T(8,128)} %get-tuple-element.320.refs_0_, f32[1344,512]{1,0:T(8,128)} %get-tuple-element.308.refs_0_.refs_7_.refs_1_, f32[32,8,128]{2,1,0:T(8,128)} %copy-done.27, f32[8,512]{1,0:T(8,128)} %get-tuple-element.319.refs_8_.refs_3_, ...), custom_call_target="tpu_custom_call" | custom-call | flops 6341787648 | bytes 19560960 | tf_op jit(solution)/shard_map/back_conv/pallas_call | solution.py:345
  348.3 8.0 %collective-permute-done.16 = bf16[8,512,128]{2,1,0:T(8,128)(2,1)} collective-permute-done((bf16[8,512,128]{2,1,0:T(8,128)(2,1)}, bf16[8,512,128]{2,1,0:T(8,128)(2,1)}, u32[]{:S(2)}, u32[]{:S(2)}) %collective-permute-start.16) | collective-permute-done | bytes 1048608 | tf_op jit(solution)/shard_map/ppermute | solution.py:50
  367.7 11.7 %spatial_grad.2 = (bf16[2,4608,128]{2,1,0:T(8,128)(2,1)}, bf16[2,4608,128]{2,1,0:T(8,128)(2,1)}) custom-call(bf16[1344,512]{1,0:T(8,128)(2,1)} %get-tuple-element.346.refs_0_, bf16[1344,512]{1,0:T(8,128)(2,1)} %get-tuple-element.347.refs_1_), custom_call_target="tpu_custom_call" | custom-call | flops 6341787648 | bytes 7471104 | tf_op jit(solution)/shard_map/spatial_grad/pallas_call | solution.py:345
  386.7 18.2 %back_reduce.1 = (bf16[1344,512]{1,0:T(8,128)(2,1)}, bf16[1344,2048]{1,0:T(8,128)(2,1)}, f32[32,32,128]{2,1,0:T(8,128)}) custom-call(f32[1344,512]{1,0:T(8,128)} %get-tuple-element.332.refs_0_, f32[1344,512]{1,0:T(8,128)} %get-tuple-element.304.refs_0_.refs_7_.refs_1_, f32[32,8,128]{2,1,0:T(8,128)} %copy-done.9, ...), custom_call_target="tpu_custom_call" | custom-call | flops 2818572288 | bytes 33554432 | tf_op jit(solution)/shard_map/back_reduce/pallas_call | solution.py:345
  446.0 12.9 %back_expand.3 = (bf16[1344,2048]{1,0:T(8,128)(2,1)}, f32[1344,512]{1,0:T(8,128)}, f32[32,8,128]{2,1,0:T(8,128)}) custom-call(bf16[1344,2048]{1,0:T(8,128)(2,1)} %get-tuple-element.351.refs_0_, bf16[1344,2048]{1,0:T(8,128)(2,1)} %get-tuple-element.302.refs_0_.refs_8_.refs_1_, f32[32,32,128]{2,1,0:T(8,128)} %copy-done, ...), custom_call_target="tpu_custom_call" | custom-call | flops 2818572288 | bytes 27015680 | tf_op jit(solution)/shard_map/back_expand/pallas_call | solution.py:345
  484.0 15.6 %back_conv.3 = (bf16[1344,512]{1,0:T(8,128)(2,1)}, f32[1344,512]{1,0:T(8,128)}, f32[32,8,128]{2,1,0:T(8,128)}) custom-call(f32[1344,512]{1,0:T(8,128)} %get-tuple-element.374.refs_0_, f32[1344,512]{1,0:T(8,128)} %get-tuple-element.300.refs_0_.refs_7_.refs_1_, f32[32,8,128]{2,1,0:T(8,128)} %copy-done.28, f32[8,512]{1,0:T(8,128)} %get-tuple-element.373.refs_8_.refs_3_, ...), custom_call_target="tpu_custom_call" | custom-call | flops 6341787648 | bytes 17463808 | tf_op jit(solution)/shard_map/back_conv/pallas_call | solution.py:345
  506.4 11.7 %spatial_grad.3 = (bf16[2,4608,128]{2,1,0:T(8,128)(2,1)}, bf16[2,4608,128]{2,1,0:T(8,128)(2,1)}) custom-call(bf16[1344,512]{1,0:T(8,128)(2,1)} %get-tuple-element.314.refs_0_, bf16[1344,512]{1,0:T(8,128)(2,1)} %get-tuple-element.398.refs_1_), custom_call_target="tpu_custom_call" | custom-call | flops 6341787648 | bytes 7471104 | tf_op jit(solution)/shard_map/spatial_grad/pallas_call | solution.py:345
  566.6 12.5 %collective-permute-done.45 = bf16[2,256,128]{2,1,0:T(8,128)(2,1)S(1)} collective-permute-done((bf16[2,256,128]{2,1,0:T(8,128)(2,1)}, bf16[2,256,128]{2,1,0:T(8,128)(2,1)S(1)}, u32[]{:S(2)}, u32[]{:S(2)}) %collective-permute-start.45) | collective-permute-done | bytes 131104 | tf_op jit(solution)/shard_map/ppermute | solution.py:50
  619.8 9.6 %all-gather.3 = bf16[3328,128]{1,0:T(8,128)(2,1)} all-gather(bf16[832,128]{1,0:T(8,128)(2,1)} %momenta_low.2), channel_id=5, replica_groups=mesh['dp'=8,'owner'=4] {'owner'}, dimensions={0}, use_global_device_ids=true | all-gather | bytes 1064960 | tf_op jit(solution)/shard_map/all_gather | solution.py:970
  642.2 9.2 %collective-permute-done.58 = f32[3,320,128]{2,1,0:T(8,128)S(1)} collective-permute-done((f32[3,320,128]{2,1,0:T(8,128)S(1)}, f32[3,320,128]{2,1,0:T(8,128)S(1)}, u32[]{:S(2)}, u32[]{:S(2)}) %collective-permute-start.58) | collective-permute-done | bytes 491552 | tf_op jit(solution)/shard_map/ppermute | solution.py:50
  652.1 8.9 %collective-permute-done.59 = f32[2,320,128]{2,1,0:T(8,128)S(1)} collective-permute-done((f32[2,320,128]{2,1,0:T(8,128)S(1)}, f32[2,320,128]{2,1,0:T(8,128)S(1)}, u32[]{:S(2)}, u32[]{:S(2)}) %collective-permute-start.59) | collective-permute-done | bytes 327712 | tf_op jit(solution)/shard_map/ppermute | solution.py:50
  661.1 8.9 %collective-permute-done.60 = f32[320,128]{1,0:T(8,128)S(1)} collective-permute-done((f32[320,128]{1,0:T(8,128)S(1)}, f32[320,128]{1,0:T(8,128)S(1)}, u32[]{:S(2)}, u32[]{:S(2)}) %collective-permute-start.60) | collective-permute-done | bytes 163872 | tf_op jit(solution)/shard_map/ppermute | solution.py:50
  670.0 7.9 %all_gather.43.refs_0_ = f32[1280,128]{1,0:T(8,128)} all-gather(f32[320,128]{1,0:T(8,128)S(1)} %bitcast_add_fusion.20), channel_id=1, replica_groups=mesh['dp'=8,'owner'=4] {'owner'}, dimensions={0}, use_global_device_ids=true | all-gather | bytes 819200 | tf_op jit(solution)/shard_map/all_gather | solution.py:1189
  677.9 19.3 %polynomial.1 = bf16[128,512]{1,0:T(8,128)(2,1)} custom-call(f32[1280,128]{1,0:T(8,128)} %all_gather.43.refs_0_), custom_call_target="tpu_custom_call" | custom-call | flops 16106127360 | bytes 786432 | tf_op jit(solution)/shard_map/polynomial/pallas_call | solution.py:345
  697.2 7.5 %collective-permute-done.61 = bf16[128,512]{1,0:T(8,128)(2,1)S(1)} collective-permute-done((bf16[128,512]{1,0:T(8,128)(2,1)}, bf16[128,512]{1,0:T(8,128)(2,1)S(1)}, u32[]{:S(2)}, u32[]{:S(2)}) %collective-permute-start.61) | collective-permute-done | bytes 131104 | tf_op jit(solution)/shard_map/ppermute | solution.py:50
  (423 shorter events, 300.0 us)
Async XLA Ops:
  7.2 114.5 %all-gather.10.cloned.1.call-start = ((), (), s32[]{:S(2)}) async-start(), calls=%async_computation.12 | async-start | bytes 4325376 | tf_op jit(solution)/shard_map/all_gather | solution.py:1247
  10.2 180.2 %all-gather.12.cloned.1.call-start = ((), (), s32[]{:S(2)}) async-start(), calls=%async_computation.13 | async-start | bytes 7028736 | tf_op jit(solution)/shard_map/all_gather | solution.py:1286
  66.2 169.4 %all-gather.14.cloned.1.call-start = ((), (), s32[]{:S(2)}) async-start(), calls=%async_computation.14 | async-start | bytes 4325376 | tf_op jit(solution)/shard_map/all_gather | solution.py:1302
  67.7 19.9 %collective-permute-start.12 = (bf16[8,288,128]{2,1,0:T(8,128)(2,1)S(1)}, bf16[8,288,128]{2,1,0:T(8,128)(2,1)S(1)}, u32[]{:S(2)}, u32[]{:S(2)}) collective-permute-start(bf16[8,288,128]{2,1,0:T(8,128)(2,1)S(1)} %pad_maximum_fusion.1), channel_id=1, source_target_pairs={{0,2},{1,3},{2,0},{3,1},{4,6},{5,7},{6,4},{7,5},{8,10},{9,11},{10,... | collective-permute-start | bytes 1769480 | tf_op jit(solution)/shard_map/ppermute | solution.py:50
  68.2 19.4 %collective-permute-start.11 = (bf16[8,288,128]{2,1,0:T(8,128)(2,1)S(1)}, bf16[8,288,128]{2,1,0:T(8,128)(2,1)S(1)}, u32[]{:S(2)}, u32[]{:S(2)}) collective-permute-start(bf16[8,288,128]{2,1,0:T(8,128)(2,1)S(1)} %pad_maximum_fusion), channel_id=1, source_target_pairs={{0,4},{1,5},{2,6},{3,7},{4,0},{5,1},{6,2},{7,3},{8,12},{9,13},{10,... | collective-permute-start | bytes 1769480 | tf_op jit(solution)/shard_map/ppermute | solution.py:50
  69.2 18.4 %all-to-all-start = ((f32[32,16,128]{2,1,0:T(8,128)}), f32[32,16,128]{2,1,0:T(8,128)}, u32[]{:S(2)}, u32[]{:S(2)}) async-start(f32[32,16,128]{2,1,0:T(8,128)} %get-tuple-element.294), calls=%async_computation | async-start | bytes 524288 | tf_op jit(solution)/shard_map/all_to_all | solution.py:45
  224.9 19.2 %all-to-all-start.5 = ((f32[32,32,128]{2,1,0:T(8,128)}), f32[32,32,128]{2,1,0:T(8,128)S(1)}, u32[]{:S(2)}, u32[]{:S(2)}) async-start(f32[32,32,128]{2,1,0:T(8,128)} %get-tuple-element.312), calls=%async_computation.5 | async-start | bytes 1048576 | tf_op jit(solution)/shard_map/all_to_all | solution.py:45
  330.5 25.7 %collective-permute-start.16 = (bf16[8,512,128]{2,1,0:T(8,128)(2,1)}, bf16[8,512,128]{2,1,0:T(8,128)(2,1)}, u32[]{:S(2)}, u32[]{:S(2)}) collective-permute-start(bf16[8,512,128]{2,1,0:T(8,128)(2,1)} %dynamic-slice_bitcast_fusion), channel_id=1, source_target_pairs={{0,2},{1,3},{2,0},{3,1},{4,6},{5,7},{6,4},{7,5},{8,10},{9,11},{10,... | collective-permute-start | bytes 3145736 | tf_op jit(solution)/shard_map/ppermute | solution.py:50
  332.4 23.9 %collective-permute-start.17 = (bf16[16,256,128]{2,1,0:T(8,128)(2,1)}, bf16[16,256,128]{2,1,0:T(8,128)(2,1)}, u32[]{:S(2)}, u32[]{:S(2)}) collective-permute-start(bf16[16,256,128]{2,1,0:T(8,128)(2,1)} %bitcast.353), channel_id=1, source_target_pairs={{0,1},{1,0},{2,3},{3,2},{4,5},{5,4},{6,7},{7,6},{8,9},{9,8},{10,11... | collective-permute-start | bytes 3145736 | tf_op jit(solution)/shard_map/ppermute | solution.py:50
  360.8 19.1 %collective-permute-start.18 = (bf16[4,512,128]{2,1,0:T(8,128)(2,1)}, bf16[4,512,128]{2,1,0:T(8,128)(2,1)S(1)}, u32[]{:S(2)}, u32[]{:S(2)}) collective-permute-start(bf16[4,512,128]{2,1,0:T(8,128)(2,1)} %dynamic-slice_bitcast_fusion.7), channel_id=1, source_target_pairs={{0,4},{1,5},{2,6},{3,7},{4,0},{5,1},{6,2},{7,3},{8,12},{9,13},{10,... | collective-permute-start | bytes 1572872 | tf_op jit(solution)/shard_map/ppermute | solution.py:50
  362.5 18.3 %collective-permute-start.19 = (bf16[8,256,128]{2,1,0:T(8,128)(2,1)}, bf16[8,256,128]{2,1,0:T(8,128)(2,1)S(1)}, u32[]{:S(2)}, u32[]{:S(2)}) collective-permute-start(bf16[8,256,128]{2,1,0:T(8,128)(2,1)} %bitcast.41), channel_id=1, source_target_pairs={{0,8},{1,9},{2,10},{3,11},{4,12},{5,13},{6,14},{7,15},{8,0},{9,1},... | collective-permute-start | bytes 1572872 | tf_op jit(solution)/shard_map/ppermute | solution.py:50
  382.8 22.1 %collective-permute-start.22 = (bf16[16,576,128]{2,1,0:T(8,128)(2,1)}, bf16[16,576,128]{2,1,0:T(8,128)(2,1)}, u32[]{:S(2)}, u32[]{:S(2)}) collective-permute-start(bf16[16,576,128]{2,1,0:T(8,128)(2,1)} %bitcast.48), channel_id=1, source_target_pairs={{0,1},{1,0},{2,3},{3,2},{4,5},{5,4},{6,7},{7,6},{8,9},{9,8},{10,11... | collective-permute-start | bytes 7077896 | tf_op jit(solution)/shard_map/ppermute | solution.py:50
  383.1 21.8 %collective-permute-start.20 = (bf16[2,512,128]{2,1,0:T(8,128)(2,1)S(1)}, bf16[2,512,128]{2,1,0:T(8,128)(2,1)S(1)}, u32[]{:S(2)}, u32[]{:S(2)}) collective-permute-start(bf16[2,512,128]{2,1,0:T(8,128)(2,1)S(1)} %dynamic-slice_bitcast_fusion.15), channel_id=1, source_target_pairs={{0,8},{1,9},{2,10},{3,11},{4,12},{5,13},{6,14},{7,15},{8,0},{9,1},... | collective-permute-start | bytes 786440 | tf_op jit(solution)/shard_map/ppermute | solution.py:50
  384.3 20.6 %collective-permute-start.21 = (bf16[4,256,128]{2,1,0:T(8,128)(2,1)S(1)}, bf16[4,256,128]{2,1,0:T(8,128)(2,1)S(1)}, u32[]{:S(2)}, u32[]{:S(2)}) collective-permute-start(bf16[4,256,128]{2,1,0:T(8,128)(2,1)S(1)} %bitcast.349), channel_id=1, source_target_pairs={{0,16},{1,17},{2,18},{3,19},{4,20},{5,21},{6,22},{7,23},{8,24},{9,... | collective-permute-start | bytes 786440 | tf_op jit(solution)/shard_map/ppermute | solution.py:50
  411.3 27.8 %all-to-all-start.9 = ((f32[32,32,128]{2,1,0:T(8,128)}), f32[32,32,128]{2,1,0:T(8,128)S(1)}, u32[]{:S(2)}, u32[]{:S(2)}) async-start(f32[32,32,128]{2,1,0:T(8,128)} %get-tuple-element.361), calls=%async_computation.9 | async-start | bytes 1048576 | tf_op jit(solution)/shard_map/all_to_all | solution.py:45
  414.5 23.9 %collective-permute-start.25 = (bf16[8,288,128]{2,1,0:T(8,128)(2,1)}, bf16[8,288,128]{2,1,0:T(8,128)(2,1)}, u32[]{:S(2)}, u32[]{:S(2)}) collective-permute-start(bf16[8,288,128]{2,1,0:T(8,128)(2,1)} %dynamic-slice_bitcast_fusion.3), channel_id=1, source_target_pairs={{0,2},{1,3},{2,0},{3,1},{4,6},{5,7},{6,4},{7,5},{8,10},{9,11},{10,... | collective-permute-start | bytes 1769480 | tf_op jit(solution)/shard_map/ppermute | solution.py:50
  416.4 22.6 %collective-permute-start.26 = (bf16[8,288,128]{2,1,0:T(8,128)(2,1)S(1)}, bf16[8,288,128]{2,1,0:T(8,128)(2,1)}, u32[]{:S(2)}, u32[]{:S(2)}) collective-permute-start(bf16[8,288,128]{2,1,0:T(8,128)(2,1)S(1)} %copy-done.21), channel_id=1, source_target_pairs={{0,4},{1,5},{2,6},{3,7},{4,0},{5,1},{6,2},{7,3},{8,12},{9,13},{10,... | collective-permute-start | bytes 1769480 | tf_op jit(solution)/shard_map/ppermute | solution.py:50
  417.9 17.2 %collective-permute-start.23 = (bf16[1,512,128]{2,1,0:T(8,128)(2,1)}, bf16[1,512,128]{2,1,0:T(8,128)(2,1)S(1)}, u32[]{:S(2)}, u32[]{:S(2)}) collective-permute-start(bf16[1,512,128]{2,1,0:T(8,128)(2,1)} %constant_dynamic-slice_fusion.15), channel_id=1, source_target_pairs={{0,16},{1,17},{2,18},{3,19},{4,20},{5,21},{6,22},{7,23},{8,24},{9,... | collective-permute-start | bytes 393224 | tf_op jit(solution)/shard_map/ppermute | solution.py:50
  420.3 18.1 %collective-permute-start.24 = (bf16[2,256,128]{2,1,0:T(8,128)(2,1)}, bf16[2,256,128]{2,1,0:T(8,128)(2,1)S(1)}, u32[]{:S(2)}, u32[]{:S(2)}) collective-permute-start(bf16[2,256,128]{2,1,0:T(8,128)(2,1)} %dynamic-slice_bitcast_fusion.23), channel_id=1, source_target_pairs={{0,2},{1,3},{2,0},{3,1},{4,6},{5,7},{6,4},{7,5},{8,10},{9,11},{10,... | collective-permute-start | bytes 393224 | tf_op jit(solution)/shard_map/ppermute | solution.py:50
  479.5 20.3 %collective-permute-start.37 = (bf16[16,256,128]{2,1,0:T(8,128)(2,1)}, bf16[16,256,128]{2,1,0:T(8,128)(2,1)S(1)}, u32[]{:S(2)}, u32[]{:S(2)}) collective-permute-start(bf16[16,256,128]{2,1,0:T(8,128)(2,1)} %bitcast.80), channel_id=1, source_target_pairs={{0,1},{1,0},{2,3},{3,2},{4,5},{5,4},{6,7},{7,6},{8,9},{9,8},{10,11... | collective-permute-start | bytes 3145736 | tf_op jit(solution)/shard_map/ppermute | solution.py:50
  479.5 20.3 %collective-permute-start.36 = (bf16[4,256,128]{2,1,0:T(8,128)(2,1)S(1)}, bf16[4,256,128]{2,1,0:T(8,128)(2,1)S(1)}, u32[]{:S(2)}, u32[]{:S(2)}) collective-permute-start(bf16[4,256,128]{2,1,0:T(8,128)(2,1)S(1)} %dynamic-slice_bitcast_fusion.14), channel_id=1, source_target_pairs={{0,4},{1,5},{2,6},{3,7},{4,0},{5,1},{6,2},{7,3},{8,12},{9,13},{10,... | collective-permute-start | bytes 786440 | tf_op jit(solution)/shard_map/ppermute | solution.py:50
  480.2 19.5 %collective-permute-start.34 = (bf16[1,288,128]{2,1,0:T(8,128)(2,1)S(1)}, bf16[1,288,128]{2,1,0:T(8,128)(2,1)S(1)}, u32[]{:S(2)}, u32[]{:S(2)}) collective-permute-start(bf16[1,288,128]{2,1,0:T(8,128)(2,1)S(1)} %constant_dynamic-slice_fusion.12), channel_id=1, source_target_pairs={{0,16},{1,17},{2,18},{3,19},{4,20},{5,21},{6,22},{7,23},{8,24},{9,... | collective-permute-start | bytes 221192 | tf_op jit(solution)/shard_map/ppermute | solution.py:50
  482.6 17.1 %collective-permute-start.35 = (bf16[1,288,128]{2,1,0:T(8,128)(2,1)S(1)}, bf16[1,288,128]{2,1,0:T(8,128)(2,1)S(1)}, u32[]{:S(2)}, u32[]{:S(2)}) collective-permute-start(bf16[1,288,128]{2,1,0:T(8,128)(2,1)S(1)} %constant_dynamic-slice_fusion.11), channel_id=1, source_target_pairs={{0,2},{1,3},{2,0},{3,1},{4,6},{5,7},{6,4},{7,5},{8,10},{9,11},{10,... | collective-permute-start | bytes 221192 | tf_op jit(solution)/shard_map/ppermute | solution.py:50
  501.5 16.7 %collective-permute-start.39 = (bf16[8,256,128]{2,1,0:T(8,128)(2,1)S(1)}, bf16[8,256,128]{2,1,0:T(8,128)(2,1)S(1)}, u32[]{:S(2)}, u32[]{:S(2)}) collective-permute-start(bf16[8,256,128]{2,1,0:T(8,128)(2,1)S(1)} %dynamic-slice_bitcast_fusion.5), channel_id=1, source_target_pairs={{0,2},{1,3},{2,0},{3,1},{4,6},{5,7},{6,4},{7,5},{8,10},{9,11},{10,... | collective-permute-start | bytes 1572872 | tf_op jit(solution)/shard_map/ppermute | solution.py:50
  506.2 123.2 %all-gather.16.cloned.1.call-start = ((), (), s32[]{:S(2)}) async-start(), calls=%async_computation.15 | async-start | bytes 1720320 | tf_op jit(solution)/shard_map/all_gather | solution.py:970
  528.0 22.8 %collective-permute-start.43 = (bf16[8,288,128]{2,1,0:T(8,128)(2,1)}, bf16[8,288,128]{2,1,0:T(8,128)(2,1)S(1)}, u32[]{:S(2)}, u32[]{:S(2)}) collective-permute-start(bf16[8,288,128]{2,1,0:T(8,128)(2,1)} %bitcast.95), channel_id=1, source_target_pairs={{0,8},{1,9},{2,10},{3,11},{4,12},{5,13},{6,14},{7,15},{8,0},{9,1},... | collective-permute-start | bytes 1769480 | tf_op jit(solution)/shard_map/ppermute | solution.py:50
  529.8 21.0 %collective-permute-start.44 = (bf16[8,288,128]{2,1,0:T(8,128)(2,1)S(1)}, bf16[8,288,128]{2,1,0:T(8,128)(2,1)}, u32[]{:S(2)}, u32[]{:S(2)}) collective-permute-start(bf16[8,288,128]{2,1,0:T(8,128)(2,1)S(1)} %dynamic-slice_bitcast_fusion.1), channel_id=1, source_target_pairs={{0,4},{1,5},{2,6},{3,7},{4,0},{5,1},{6,2},{7,3},{8,12},{9,13},{10,... | collective-permute-start | bytes 1769480 | tf_op jit(solution)/shard_map/ppermute | solution.py:50
  531.3 19.5 %collective-permute-start.42 = (bf16[4,256,128]{2,1,0:T(8,128)(2,1)S(1)}, bf16[4,256,128]{2,1,0:T(8,128)(2,1)}, u32[]{:S(2)}, u32[]{:S(2)}) collective-permute-start(bf16[4,256,128]{2,1,0:T(8,128)(2,1)S(1)} %dynamic-slice_bitcast_fusion.13), channel_id=1, source_target_pairs={{0,4},{1,5},{2,6},{3,7},{4,0},{5,1},{6,2},{7,3},{8,12},{9,13},{10,... | collective-permute-start | bytes 786440 | tf_op jit(solution)/shard_map/ppermute | solution.py:50
  555.2 23.8 %collective-permute-start.48 = (bf16[16,256,128]{2,1,0:T(8,128)(2,1)}, bf16[16,256,128]{2,1,0:T(8,128)(2,1)S(1)}, u32[]{:S(2)}, u32[]{:S(2)}) collective-permute-start(bf16[16,256,128]{2,1,0:T(8,128)(2,1)} %bitcast.98), channel_id=1, source_target_pairs={{0,1},{1,0},{2,3},{3,2},{4,5},{5,4},{6,7},{7,6},{8,9},{9,8},{10,11... | collective-permute-start | bytes 3145736 | tf_op jit(solution)/shard_map/ppermute | solution.py:50
  558.1 20.9 %collective-permute-start.46 = (bf16[4,288,128]{2,1,0:T(8,128)(2,1)}, bf16[4,288,128]{2,1,0:T(8,128)(2,1)S(1)}, u32[]{:S(2)}, u32[]{:S(2)}) collective-permute-start(bf16[4,288,128]{2,1,0:T(8,128)(2,1)} %bitcast.348), channel_id=1, source_target_pairs={{0,16},{1,17},{2,18},{3,19},{4,20},{5,21},{6,22},{7,23},{8,24},{9,... | collective-permute-start | bytes 884744 | tf_op jit(solution)/shard_map/ppermute | solution.py:50
  560.6 18.4 %collective-permute-start.47 = (bf16[4,288,128]{2,1,0:T(8,128)(2,1)}, bf16[4,288,128]{2,1,0:T(8,128)(2,1)}, u32[]{:S(2)}, u32[]{:S(2)}) collective-permute-start(bf16[4,288,128]{2,1,0:T(8,128)(2,1)} %dynamic-slice_bitcast_fusion.9), channel_id=1, source_target_pairs={{0,8},{1,9},{2,10},{3,11},{4,12},{5,13},{6,14},{7,15},{8,0},{9,1},... | collective-permute-start | bytes 884744 | tf_op jit(solution)/shard_map/ppermute | solution.py:50
  561.8 17.2 %collective-permute-start.45 = (bf16[2,256,128]{2,1,0:T(8,128)(2,1)}, bf16[2,256,128]{2,1,0:T(8,128)(2,1)S(1)}, u32[]{:S(2)}, u32[]{:S(2)}) collective-permute-start(bf16[2,256,128]{2,1,0:T(8,128)(2,1)} %dynamic-slice_bitcast_fusion.21), channel_id=1, source_target_pairs={{0,8},{1,9},{2,10},{3,11},{4,12},{5,13},{6,14},{7,15},{8,0},{9,1},... | collective-permute-start | bytes 393224 | tf_op jit(solution)/shard_map/ppermute | solution.py:50
  (96 other events, 760.8 us)
Sparse Core Ops, SparseCore 0:
  11.5 70.2 all-gather.9
  85.2 83.4 all-gather.11
  172.1 63.4 all-gather.13
  601.9 15.9 all-gather.15

commit v5 on v4

--- a/solution.py
+++ b/solution.py
@@ -190,7 +190,7 @@
 
 
 def total_of(parts_ref):
-    return jnp.sum(parts_ref[...], axis=0)
+    return jnp.sum(parts_ref[...].astype(F32), axis=0)
 
 
 def row_of(table, start, width):
@@ -198,12 +198,10 @@
     return jnp.concatenate([table[start + i : start + i + 1, :] for i in range(count)], axis=1)
 
 
-def send_rows(out_ref, rows, place=0):
-    for row in rows:
-        for i in range(row.shape[1] // LANES):
-            piece = row[:, i * LANES : (i + 1) * LANES]
-            out_ref[:, place, :] = jnp.broadcast_to(piece, (out_ref.shape[0], LANES))
-            place += 1
+def send_rows(out_ref, rows):
+    pieces = [row[:, i * LANES : (i + 1) * LANES] for row in rows for i in range(row.shape[1] // LANES)]
+    block = jnp.concatenate(pieces, axis=0).astype(out_ref.dtype)
+    out_ref[...] = jnp.broadcast_to(block[None], (out_ref.shape[0],) + block.shape)
 
 
 def fold_rows(values):
@@ -238,10 +236,10 @@
     return grad * stat_ref[2:3] - mask * (terms[0:1] + hidden * terms[1:2])
 
 
-def send_back_sums(send_ref, sums, stat_ref):
+def send_back_sums(send_ref, sums, stat_ref, more=()):
     bias_sum = jnp.sum(sums[0:8], axis=0, keepdims=True)
     cross = jnp.sum(sums[8:16], axis=0, keepdims=True)
-    send_rows(send_ref, [bias_sum, (cross - stat_ref[0:1] * bias_sum) * stat_ref[1:2]])
+    send_rows(send_ref, [bias_sum, (cross - stat_ref[0:1] * bias_sum) * stat_ref[1:2], *more])
 
 
 class Weights:
@@ -272,6 +270,23 @@
         return out
 
 
+class HeadWeights(Weights):
+    def __init__(self, array, pieces, dp_size, owners, slots, cols):
+        self.operands, self.pieces = [array], pieces
+        self.shape, self.owners, self.slots = (dp_size, owners * slots, cols), owners, slots
+
+    def scratch(self):
+        return [pltpu.VMEM(self.shape, BF16), pltpu.SemaphoreType.DMA((len(self.pieces),))]
+
+    def copies(self, refs, buffer, sems):
+        return [
+            pltpu.make_async_copy(
+                refs[0].at[source], buffer.at[d, pl.ds(first, self.slots), pl.ds(column, width)], sems.at[number]
+            )
+            for number, (source, d, first, column, width) in enumerate(self.pieces)
+        ]
+
+
 def gathered_weights(array, start, rows):
     dp_size, owners = array.shape[:2]
     blocks = [(0, (d, o), start, rows, d * owners + o, 0) for d in range(dp_size) for o in range(owners)]
@@ -414,8 +429,8 @@
 
         @pl.when(step == steps - 1)
         def _():
-            send_rows(send_ref, [jnp.sum(sums[i * 8 : i * 8 + 8], axis=0, keepdims=True) for i in range(2)])
-            send_ref[:, send_ref.shape[1] - 8 :, :] = jnp.broadcast_to(tally_ref[...][None], (devices, 8, LANES))
+            rows_here = [jnp.sum(sums[i * 8 : i * 8 + 8], axis=0, keepdims=True) for i in range(2)]
+            send_rows(send_ref, rows_here + [tally_ref[i : i + 1] for i in range(8)])
 
     send = (devices, 2 * narrow // LANES + 8, LANES)
     return launch(
@@ -598,22 +613,25 @@
     )
 
 
-def head_step(hidden, inputs, parts, counts, norms, masks, head_all, slot_bias, image_cols, layer, pixels, zone, devices):
+def head_step(hidden, inputs, parts, counts, norms, masks, head_weights, slot_bias, image_cols, layer, pixels, zone, devices):
     rows, wide = hidden.shape
     images = zone // SLOT
-    dp_size, owners, slots, cols = head_all.shape
-    classes = owners * slots
+    dp_size, classes, cols = head_weights.shape
+    owners, slots = head_weights.owners, head_weights.slots
     steps = rows // zone
     count_rows = classes // LANES + 8
     tile = LANES
 
     def kernel(
         h_ref, x_ref, parts_ref, count_ref, norm_ref, mask_ref, head_ref, bias_ref, image_ref,
-        ds_ref, stat_ref, send_ref, kept_ref, sent_ref, summed, kept, piled, pooled, sums,
+        ds_ref, stat_ref, send_ref, kept_ref, sent_ref, head_buffer, sems, slopes, kept, piled, pooled, sums, extras,
     ):
         step = pl.program_id(0)
+
         @pl.when(step == 0)
         def _():
+            for copy in head_weights.copies(head_ref, head_buffer, sems):
+                copy.start()
             sums[...] = jnp.zeros_like(sums)
             piled[...] = jnp.zeros_like(piled)
             centre, inverse = norm_of(parts_ref, count_ref[0:1, 0:1], wide)
@@ -626,16 +644,19 @@
             hidden_here = h_ref[...]
             kept[place, :] = hidden_here
             value = x_ref[...].astype(F32) + normed_of(hidden_here.astype(F32), stat_ref)
-            summed[place, :] = value
-            out = silu(value) * mask_ref[:, 1:2]
-            piled[...] += out
+            half = 0.5 * value
+            bend = jnp.tanh(half)
+            piled[...] += (half * bend + half) * mask_ref[:, 1:2]
+            slopes[place, :] = (0.5 * (1.0 + bend + half * (1.0 - bend * bend)) * mask_ref[:, 1:2]).astype(BF16)
 
         @pl.when(step == steps - 1)
         def _():
+            for copy in head_weights.copies(head_ref, head_buffer, sems):
+                copy.wait()
             low = (jnp.sum(piled[...].reshape(images, SLOT, wide), axis=1) * (1.0 / pixels)).astype(BF16)
             flipped = None
             for d in range(dp_size):
-                part = dot_nt(head_ref[d].reshape(classes, cols), low[:, d * cols : (d + 1) * cols])
+                part = dot_nt(head_buffer[d], low[:, d * cols : (d + 1) * cols])
                 flipped = part if flipped is None else flipped + part
             logits = flipped.T + bias_ref[0:1, :]
             top = jnp.max(logits, axis=1, keepdims=True)
@@ -648,15 +669,17 @@
             picked = jnp.sum(logits * onehot, axis=1, keepdims=True)
             loss = jnp.sum(weight * (log_total - picked), axis=0, keepdims=True)
             residue = weight * (jnp.exp(logits - log_total) - onehot)
-            send_rows(
-                send_ref,
-                [jnp.sum(residue, axis=0, keepdims=True), jnp.broadcast_to(loss, (1, 8 * LANES))],
-                2 * wide // LANES,
-            )
+            loss = jnp.broadcast_to(loss, (1, LANES))
+            loss_high = loss.astype(BF16).astype(F32)
+            loss_middle = (loss - loss_high).astype(BF16).astype(F32)
+            extras[0:1] = jnp.sum(residue, axis=0, keepdims=True)
+            extras[1:2, 0:LANES] = loss_high
+            extras[2:3, 0:LANES] = loss_middle
+            extras[3:4, 0:LANES] = loss - loss_high - loss_middle
             exact = residue / count_ref[1:2, 0:1]
             grad, grad_flipped = exact.astype(BF16), exact.T.astype(BF16)
             for d in range(dp_size):
-                back = dot_nn(grad, head_ref[d].reshape(classes, cols))
+                back = dot_nn(grad, head_buffer[d])
                 weight_part = dot_nn(grad_flipped, low[:, d * cols : (d + 1) * cols])
                 for i in range(kept_ref.shape[2]):
                     parts = [weight_part[o * slots : (o + 1) * slots, i * tile : (i + 1) * tile] for o in range(owners)]
@@ -667,14 +690,15 @@
         def _():
             place = pl.ds(pl.multiple_of((step - steps) * zone, zone), zone)
             spread = jnp.broadcast_to(pooled[...][:, None, :], (images, SLOT, wide)).reshape(zone, wide)
-            ds = spread * silu_slope(summed[place, :]) * mask_ref[:, 1:2]
+            ds = spread * slopes[place, :].astype(F32)
             ds_ref[...] = ds.astype(BF16)
             sums[0:8] += fold_rows(ds)
             sums[8:16] += fold_rows(ds * kept[place, :].astype(F32))
 
         @pl.when(step == 2 * steps - 1)
         def _():
-            send_back_sums(send_ref, sums, stat_ref)
+            more = [extras[0:1]] + [extras[i : i + 1, 0:LANES] for i in range(1, 4)] + [jnp.zeros((1, (count_rows - 3) * LANES - classes), F32)]
+            send_back_sums(send_ref, sums, stat_ref, more)
 
     send = (devices, 2 * wide // LANES + count_rows, LANES)
     grads = (owners // 2, dp_size, cols // tile, slots, tile)
@@ -682,15 +706,16 @@
     later = pl.BlockSpec((zone, wide), lambda i: (jnp.maximum(i - steps, 0), 0))
     return launch(
         kernel, "head_step", (2 * steps,),
-        (hidden, inputs, parts, counts, norms, masks, head_all, slot_bias, image_cols),
+        (hidden, inputs, parts, counts, norms, masks, head_weights, slot_bias, image_cols),
         [
             once, once, whole(parts.shape), whole(counts.shape), whole(norms.shape),
             pl.BlockSpec((zone, 2), lambda i: (lax.rem(i, steps), 0)),
-            whole(head_all.shape), whole(slot_bias.shape), whole(image_cols.shape),
+            ANYWHERE, whole(slot_bias.shape), whole(image_cols.shape),
         ],
-        (out_of((rows, wide), BF16), out_of((8, wide), F32), out_of(send, F32), out_of(grads, BF16), out_of(grads, BF16)),
+        (out_of((rows, wide), BF16), out_of((8, wide), F32), out_of(send, BF16), out_of(grads, BF16), out_of(grads, BF16)),
         (later, whole((8, wide)), whole(send), whole(grads), whole(grads)),
-        [pltpu.VMEM((rows, wide), F32), pltpu.VMEM((rows, wide), BF16), pltpu.VMEM((zone, wide), F32), pltpu.VMEM((images, wide), F32), pltpu.VMEM((16, wide), F32)],
+        head_weights.scratch()
+        + [pltpu.VMEM((rows, wide), BF16), pltpu.VMEM((rows, wide), BF16), pltpu.VMEM((zone, wide), F32), pltpu.VMEM((images, wide), F32), pltpu.VMEM((16, wide), F32), pltpu.VMEM((8, classes), F32)],
         6 * images * classes * wide,
     )
 
@@ -853,35 +878,45 @@
             whole(norms.shape), strip(strip_rows, 2), strip(strip_rows, wide), strip(strip_rows, wide), strip(strip_rows, wide),
             whole(stat_wide.shape), ANYWHERE,
         ],
-        (out_of((rows, narrow), BF16), out_of((rows, wide), BF16), out_of(send, F32)),
+        (out_of((rows, narrow), BF16), out_of((rows, wide), BF16), out_of(send, BF16)),
         (strip(strip_rows, narrow), strip(strip_rows, wide), whole(send)),
         weights.scratch() + [pltpu.VMEM((16, wide), F32), pltpu.VMEM((8, narrow), F32)],
         2 * rows * wide * narrow,
     )
 
 
-def last_back(dz, first_hidden, parts, stat_one, counts, masks):
-    rows, narrow = dz.shape
-    strip_rows = block_rows(rows, 3)
-
-    def kernel(dz_ref, first_ref, parts_ref, first_stat, count_ref, mask_ref, low_ref, terms):
+def last_grad(inputs, dz, first_hidden, parts, stat_one, counts, masks, owners, zone):
+    rows, depth = inputs.shape
+    narrow = dz.shape[1]
+    tile = min(depth, 512)
+
+    def kernel(x_ref, dz_ref, h_ref, parts_ref, stat_ref, count_ref, mask_ref, kept_ref, sent_ref, terms, low):
         @pl.when(pl.program_id(0) == 0)
         def _():
-            back_terms(terms, total_of(parts_ref), first_stat, count_ref[0:1, 0:1], narrow)
-
-        low_ref[...] = back_norm(dz_ref[...], first_ref[...], first_stat, terms, mask_ref[:, 0:1]).astype(BF16)
-
-    return launch(
-        kernel, "last_back", (rows // strip_rows,),
-        (dz, first_hidden, parts, stat_one, counts, masks),
-        [
-            strip(strip_rows, narrow), strip(strip_rows, narrow), whole(parts.shape), whole(stat_one.shape), whole(counts.shape),
-            strip(strip_rows, 2),
-        ],
-        out_of((rows, narrow), BF16),
-        strip(strip_rows, narrow),
-        [pltpu.VMEM((8, narrow), F32)],
-        rows * narrow,
+            back_terms(terms, total_of(parts_ref), stat_ref, count_ref[0:1, 0:1], narrow)
+
+            def body(index, carry):
+                place = pl.ds(pl.multiple_of(index * zone, zone), zone)
+                value = back_norm(dz_ref[place, :], h_ref[place, :], stat_ref, terms, mask_ref[place, 0:1])
+                low[place, :] = value.astype(BF16)
+                return carry
+
+            lax.fori_loop(0, rows // zone, body, 0)
+
+        total = dot_tn(x_ref[...], low[...])
+        store_halves(kept_ref, sent_ref, (), [total[:, o * LANES : (o + 1) * LANES] for o in range(owners)])
+
+    half = out_of((owners // 2, depth, LANES), BF16)
+    half_spec = pl.BlockSpec((owners // 2, tile, LANES), lambda i: (0, i, 0))
+    operands = (inputs, dz, first_hidden, parts, stat_one, counts, masks)
+    return launch(
+        kernel, "last_grad", (depth // tile,),
+        operands,
+        [pl.BlockSpec((rows, tile), lambda i: (0, i))] + [whole(a.shape) for a in operands[1:]],
+        (half, half),
+        (half_spec, half_spec),
+        [pltpu.VMEM((8, narrow), F32), pltpu.VMEM((rows, narrow), BF16)],
+        2 * rows * depth * narrow,
     )
 
 
@@ -946,16 +981,19 @@
     )
 
 
-def gather_rows(items, olds, flipped):
-    sizes = [total.shape[0] for _, _, total in items]
-    heights = [size + -size % 16 for size in sizes]
-    starts = [sum(heights[:i]) for i in range(len(heights))]
+def places_of(items):
+    heights = [total.shape[0] + -total.shape[0] % 16 for _, _, total in items]
+    return heights, [sum(heights[:i]) for i in range(len(heights))]
+
+
+def low_momenta(items, olds, flipped):
+    heights, starts = places_of(items)
     kinds = sorted({kind for _, kind, _ in items})
 
     def kernel(*refs):
         grads, sources, out_ref = refs[: len(items)], refs[len(items) : -1], refs[-1]
-        for (layer, kind, _), grad, size, height, start in zip(items, grads, sizes, heights, starts):
-            old = sources[kinds.index(kind)][layer]
+        for (layer, kind, total), grad, height, start in zip(items, grads, heights, starts):
+            old, size = sources[kinds.index(kind)][layer], total.shape[0]
             value = MOMENTUM * (old if flipped[kind] else old.T) + grad[...].astype(F32)
             if height > size:
                 value = jnp.concatenate([value, jnp.zeros((height - size, LANES), F32)], axis=0)
@@ -963,11 +1001,10 @@
 
     operands = [total for _, _, total in items] + [olds[kind] for kind in kinds]
     shape = (sum(heights), LANES)
-    low = launch(
+    return launch(
         kernel, "momenta_low", (1,), operands, [whole(a.shape) for a in operands], out_of(shape, BF16), whole(shape), [],
         2**20,
     )
-    return lax.all_gather(low, "owner"), starts
 
 
 def new_momenta(items, olds, flipped):
@@ -1034,24 +1071,31 @@
     return [(i, j) for i in range(owners) for j in range(i, owners)]
 
 
-def own_grams(gathered, starts, sizes):
-    owners = gathered.shape[0]
+def own_grams(gathered, items):
+    gathered, relative = zip(*gathered)
+    owners = gathered[0].shape[0]
     pairs = upper_pairs(owners)
     share = len(pairs) * LANES // owners
 
-    def kernel(all_ref, out_ref, packed):
-        for number, (start, size) in enumerate(zip(starts, sizes)):
+    def kernel(*refs):
+        sources, out_ref, packed = refs[: len(gathered)], refs[-2], refs[-1]
+        me = lax.axis_index("owner")
+        own = pl.multiple_of(me * share, 8)
+        for number, (operand, start, size) in enumerate(items):
             for place, (i, j) in enumerate(pairs):
+                if relative[operand]:
+                    i, j = i ^ me, j ^ me
                 packed[place * LANES : (place + 1) * LANES] = dot_tn(
-                    all_ref[i, start : start + size, :], all_ref[j, start : start + size, :]
+                    sources[operand][i, start : start + size, :], sources[operand][j, start : start + size, :]
                 )
-            own = pl.multiple_of(lax.axis_index("owner") * share, 8)
             out_ref[number] = packed[pl.ds(own, share), :]
-
-    shape = (len(sizes), share, LANES)
-    return launch(
-        kernel, "own_grams", (1,), (gathered,), [whole(gathered.shape)], out_of(shape, F32), whole(shape),
-        [pltpu.VMEM((len(pairs) * LANES, LANES), F32)], 2 * sum(sizes) * len(pairs) * LANES * LANES,
+        for number in range(len(items), 4):
+            out_ref[number] = jnp.zeros((share, LANES), F32)
+
+    shape = (4, share, LANES)
+    return launch(
+        kernel, "own_grams", (1,), list(gathered), [whole(a.shape) for a in gathered], out_of(shape, F32), whole(shape),
+        [pltpu.VMEM((len(pairs) * LANES, LANES), F32)], 2**27,
     )
 
 
@@ -1118,37 +1162,35 @@
     )
 
 
-def apply_polynomials(early, late, gathered, starts, products, masters, flipped):
-    owners = gathered[0].shape[0]
-    y_bit, z_bit = dp_bits()[:2]
+def apply_polynomials(early, late, products, masters, flipped):
+    sets = [list(zip(*arrays)) for arrays, _ in (early, late)]
+    owners = sets[0][0][0].shape[0]
+    y_bit, z_bit, turn_bit = dp_bits()[:3]
     shift = lax.axis_size("owner").bit_length() - 1
-    q_own, q_other, q_late = products
     kinds = len(masters)
-
-    def kernel(own_ref, other_ref, late_ref, early_all, late_all, *refs):
-        sources, outs = refs[:kinds], refs[kinds:]
+    counts = [len(arrays) for arrays, _ in sets]
+
+    def kernel(pair_ref, beside_ref, far_ref, *refs):
+        arrays = [refs[: counts[0]], refs[counts[0] : sum(counts)]]
+        sources, outs = refs[sum(counts) : sum(counts) + kinds], refs[sum(counts) + kinds :]
         place = lax.axis_index("dp")
-        my_y = (place >> (y_bit - shift)) & 1
-        my_z = (place >> (z_bit - shift)) & 1
-
-        def finish(layer, kind, poly, all_ref, start):
-            size = sources[kind].shape[1 if flipped[kind] else 2]
-            total = None
-            for o in range(owners):
-                left, right = poly[:, o * LANES : (o + 1) * LANES], all_ref[o, start : start + size, :]
-                part = dot_nt(right, left) if flipped[kind] else dot_nt(left, right)
-                total = part if total is None else total + part
-            outs[kind][layer] = sources[kind][layer] * (1.0 - LR_MATRIX * DECAY_MATRIX) - LR_MATRIX * total
-
-        for number, (layer, kind, _) in enumerate(early):
-            y, z = number // 2, number % 2
-            turn = y ^ my_y
-            poly = jnp.where(my_z == z, own_ref[turn].astype(F32), other_ref[turn].astype(F32)).astype(BF16)
-            finish(layer, kind, poly, early_all, starts[0][number])
-        for number, (layer, kind, _) in enumerate(late):
-            finish(layer, kind, late_ref[number ^ my_y], late_all, starts[1][number])
-
-    operands = (q_own, q_other, q_late, gathered[0], gathered[1]) + masters
+        my_y, my_z, on_late = ((place >> (bit - shift)) & 1 for bit in (y_bit, z_bit, turn_bit))
+        for turn, (_, items) in enumerate((early, late)):
+            here = on_late ^ turn
+            for number, (layer, kind, operand, start) in enumerate(items):
+                y, z = number // 2, number % 2
+                near = jnp.where(my_y == y, pair_ref[here].astype(F32), beside_ref[here].astype(F32))
+                poly = jnp.where(my_z == z, near, far_ref[turn, y ^ my_y].astype(F32)).astype(BF16)
+                size = sources[kind].shape[1 if flipped[kind] else 2]
+                total = None
+                me = lax.axis_index("owner") if sets[turn][1][operand] else 0
+                for o in range(owners):
+                    left, right = poly[:, o * LANES : (o + 1) * LANES], arrays[turn][operand][o ^ me, start : start + size, :]
+                    part = dot_nt(right, left) if flipped[kind] else dot_nt(left, right)
+                    total = part if total is None else total + part
+                outs[kind][layer] = sources[kind][layer] * (1.0 - LR_MATRIX * DECAY_MATRIX) - LR_MATRIX * total
+
+    operands = list(products) + list(sets[0][0]) + list(sets[1][0]) + list(masters)
     outs = tuple(out_of(master.shape, F32) for master in masters)
     return launch(
         kernel, "apply_polynomials", (1,), operands, [whole(a.shape) for a in operands], outs,
@@ -1156,46 +1198,47 @@
     )
 
 
-def newton_schulz(early, late, olds, masters, flipped):
+def newton_schulz(early, late, olds, masters, flipped, early_low, late_low):
     y_bit, z_bit, turn_bit = dp_bits()[:3]
-    gathered, starts, grams = [], [], []
-    for items in (early, late):
-        both, begin = gather_rows(items, olds, flipped)
-        both, grams = lax.optimization_barrier((both, grams))
-        gathered.append(both)
-        starts.append(begin)
-        grams.append(own_grams(both, begin, [total.shape[0] for _, _, total in items]))
-    on_late, moments = bit_of(turn_bit) == 1, None
-    for bit in dp_bits():
-        if bit == turn_bit:
-            continue
-        kept, sent = [], []
-        for values in grams:
-            whole_count = values.shape[0]
-            if whole_count > 1:
-                halves = values.reshape((2, whole_count // 2) + values.shape[1:])
-                kept.append(lax.dynamic_index_in_dim(halves, bit_of(bit), 0, keepdims=False))
-                sent.append(lax.dynamic_index_in_dim(halves, 1 - bit_of(bit), 0, keepdims=False))
+    sets, grams, moments, first_got = [], [], None, None
+    for groups, lows in ((early, early_low), (late, late_low)):
+        arrays, items = [], []
+        for group, low in zip(groups, lows):
+            items += [(layer, kind, len(arrays), start) for (layer, kind, _), start in zip(group, places_of(group)[1])]
+            if low is None:
+                values, _ = lax.optimization_barrier((low_momenta(group, olds, flipped), first_got))
+                low = lax.all_gather(values, "owner"), False
+            arrays.append(low)
+        sizes = [total.shape[0] for group in groups for _, _, total in group]
+        sets.append((arrays, items))
+        values = own_grams(arrays, [item[2:] + (size,) for item, size in zip(items, sizes)])
+        for bit in dp_bits():
+            if bit == turn_bit:
+                continue
+            if values.shape[0] > 1:
+                halves = values.reshape((2, values.shape[0] // 2) + values.shape[1:])
+                kept = lax.dynamic_index_in_dim(halves, bit_of(bit), 0, keepdims=False)
+                sent = lax.dynamic_index_in_dim(halves, 1 - bit_of(bit), 0, keepdims=False)
             else:
-                kept.append(values)
-                sent.append(values)
-        got = swap(jnp.concatenate(sent, axis=0), bit)
-        if moments is None:
-            moments = new_momenta(early + late, olds, flipped)
-            got, moments = lax.optimization_barrier((got, moments))
-        grams = [kept[0] + got[: kept[0].shape[0]], kept[1] + got[kept[0].shape[0] :]]
-    got = swap(jnp.where(on_late, grams[0][0], grams[1][0]), turn_bit)
-    mine = jnp.where(on_late, grams[1][0], grams[0][0]) + got
+                kept = sent = values
+            sent = lax.optimization_barrier(sent)
+            first_got = sent if first_got is None else first_got
+            got = swap(sent, bit)
+            if groups is late and moments is None:
+                moments = new_momenta([item for group in early + late for item in group], olds, flipped)
+                got, moments = lax.optimization_barrier((got, moments))
+            values = kept + got
+        grams.append(values[0])
+    on_late = bit_of(turn_bit) == 1
+    got = swap(jnp.where(on_late, grams[0], grams[1]), turn_bit)
+    mine = jnp.where(on_late, grams[1], grams[0]) + got
     packed = lax.all_gather(mine, "owner", tiled=True)
-    own = polynomial(packed, gathered[0].shape[0])
-    other = swap(own, turn_bit)
-    q_early = jnp.where(on_late, other, own)
-    q_late = jnp.where(on_late, own, other)
-    both = jnp.stack([q_early, q_late])
-    pair = jnp.stack([both, swap(both, y_bit)])
-    q_own, q_late = pair[:, 0], pair[:, 1]
-    q_other = swap(q_own, z_bit)
-    return apply_polynomials(early, late, gathered, starts, (q_own, q_other, q_late), masters, flipped), moments
+    own = polynomial(packed, sets[0][0][0][0].shape[0])
+    pair = jnp.stack([own, swap(own, turn_bit)])
+    beside = swap(pair, y_bit)
+    far = jnp.stack([pair, beside], axis=1)
+    far = jnp.where(on_late, far[::-1], far)
+    return apply_polynomials(sets[0], sets[1], (pair, beside, swap(far, z_bit)), masters, flipped), moments
 
 
 def adamw(weight, grad, first, second, rate, decay):
@@ -1281,12 +1324,27 @@
         mats.append(relative_weights(pieces, rows_of[1], dp_size, owner_size))
         mats.append(gathered_weights(third, 0, rows_of[2]))
     layers_done = len(mats) // 3
+    classes = head.shape[0]
+    slots = -(-classes // LANES) * LANES
+    slack = slots - classes
+    head_low = jnp.pad(head.astype(BF16), ((0, slack), (0, 0)))
+    aligned = head.shape[1] % LANES == 0
     if layers_done:
-        packed = jnp.concatenate(packs[1][1:], axis=0)
+        tiles = head.shape[1] // LANES
+        head_tiles = [head_low[:, i * LANES : (i + 1) * LANES] for i in range(tiles)]
+        packed = jnp.concatenate(packs[1][1:] + head_tiles, axis=0)
         gathered = lax.all_gather(packed, AXES).reshape(dp_size, owner_size, packed.shape[0], LANES)
         mats.append(gathered_weights(third, rows_of[2], rows_of[0]))
         mats.append(gathered_weights(gathered, 0, rows_of[1]))
         mats.append(gathered_weights(gathered, rows_of[1], rows_of[2]))
+        begin = rows_of[1] + rows_of[2]
+        pieces = [
+            ((d, o, pl.ds(begin + i * slots, slots)), d, o * slots, i * LANES, LANES)
+            for d in range(dp_size)
+            for o in range(owner_size)
+            for i in range(tiles)
+        ]
+        head_weights = HeadWeights(gathered, pieces, dp_size, owner_size, slots, head.shape[1])
     else:
         for layer in range(LAYERS):
             packed = jnp.concatenate(packs[layer], axis=0)
@@ -1295,14 +1353,10 @@
                 piece = gathered[:, :, starts[kind] : starts[kind] + rows_of[kind]]
                 piece = piece.transpose(1, 0, 2, 3).reshape(1, owner_size, -1, LANES)
                 mats.append(gathered_weights(piece, 0, piece.shape[2]))
-    classes = head.shape[0]
-    slots = -(-classes // LANES) * LANES
-    slack = slots - classes
-    head_low = jnp.pad(head.astype(BF16), ((0, slack), (0, 0)))
-    head_all = lax.all_gather(head_low, AXES).reshape(dp_size, owner_size, slots, head.shape[1])
-    aligned = head.shape[1] % LANES == 0
-    if not aligned:
-        head_all = head_all.transpose(1, 2, 0, 3).reshape(1, owner_size, slots, wide)
+        head_all = lax.all_gather(head_low, AXES).reshape(dp_size, owner_size, slots, head.shape[1])
+        head_all = head_all.transpose(1, 2, 0, 3).reshape(owner_size, slots, wide)
+        pieces = [((o,), 0, o * slots, 0, wide) for o in range(owner_size)]
+        head_weights = HeadWeights(head_all, pieces, 1, owner_size, slots, wide)
     slot_bias = jnp.pad(head_bias.reshape(owner_size, classes), ((0, 0), (0, slack)), constant_values=-1e30)
     slot_bias = jnp.broadcast_to(slot_bias.reshape(1, -1), (8, owner_size * slots))
     slot_labels = (labels // classes) * slots + labels % classes
@@ -1334,12 +1388,12 @@
             )
     last = LAYERS - 1
     ds, stat3[last], sums, *head_halves = head_step(
-        h3[last], inputs[last], exchange(sums), counts, norms, masks, head_all, slot_bias, image_cols, last, pixels, zone, devices
+        h3[last], inputs[last], exchange(sums), counts, norms, masks, head_weights, slot_bias, image_cols, last, pixels, zone, devices
     )
     left = bits_of(dp_size, owner_size)
     rest = list(range(1, len(left)))
     turned = [[0] + rest[turn:] + rest[:turn] for turn in range(3)]
-    if not aligned:
+    if not layers_done:
         width = head.shape[1]
         head_halves = [
             jnp.pad(
@@ -1383,46 +1437,62 @@
             )
             sums = advance(sums, flows)
         else:
-            dh1 = last_back(dz1, h1[layer], parts1, stat1[layer], counts, masks)
-            dh1 = advance(dh1, [two_flow[0]])
-        grad_one = blocked(weight_grad(inputs[layer], dh1, owner_size))
+            grad_one = blocked(
+                last_grad(inputs[layer], dz1, h1[layer], parts1, stat1[layer], counts, masks, owner_size, zone)
+            )
+        if layer > 0:
+            grad_one = blocked(weight_grad(inputs[layer], dh1, owner_size))
         if layer > 0:
             one_flow = Flow([grad_one], left, turned[0])
             flows.append(one_flow)
         norm_sums.insert(0, (parts1, parts2, parts3))
-    extra = jnp.sum(extra[:, wide_rows:], axis=0)
+    extra = jnp.sum(extra[:, wide_rows:].astype(F32), axis=0)
     class_rows = owner_size * slots // LANES
     bias_raw = extra[:class_rows].reshape(owner_size, slots)[:, :classes].reshape(-1)
-    loss_sum = extra[class_rows, 0]
+    loss_sum = extra[class_rows, 0] + (extra[class_rows + 1, 0] + extra[class_rows + 2, 0])
     grad_bias = bias_raw / weight_total
     last_flow = Flow([grad_one], left, turned[0])
-    last_flow.sent = advance(last_flow.sent, flows, True)
+    last_flow.sent = advance(last_flow.sent, [two_flow[0]], True)
     last_flow.send()
+    advance([], [last_flow], True)
     flows.append(last_flow)
-    rest_updates = [
-        lambda: norm_update(norm_sums, norm_params, norm_m, norm_v),
-        lambda: head_update(head_flow.result(), head, head_m, head_v, slots),
-    ]
-    updates = []
-    while rest_updates or any(flow.got is not None for flow in flows):
-        if rest_updates:
-            updates.append(rest_updates.pop(0)())
-        updates = advance(updates, flows, True)
     high, low = LAYERS - 1, 0
-    one_low, one_high = last_flow.result(), one_flow.result()
-    three_low, three_high = three_flow[low].result(), three_flow[high].result()
-    two_low, two_high = two_flow[low].result(), two_flow[high].result()
-    early = [(high, 2, three_high), (high, 1, two_high), (high, 0, one_high), (low, 2, three_low)]
-    late = [(low, 1, two_low), (low, 0, one_low)]
     stored = lambda arrays: tuple(a if a.shape[2] % LANES == 0 else jnp.swapaxes(a, 1, 2) for a in arrays)
-    results = newton_schulz(
-        early, late, stored((mom_reduce, mom_spatial, mom_expand)), stored((w_reduce, w_spatial, w_expand)),
-        [size % LANES != 0 for size in rows_of],
+    flipped = [size % LANES != 0 for size in rows_of]
+    olds = stored((mom_reduce, mom_spatial, mom_expand))
+    results = {}
+    turns = 0
+    while turns < 4 or any(flow.got is not None for flow in flows):
+        turns += 1
+        if turns == 1:
+            results["norm"] = norm_update(norm_sums, norm_params, norm_m, norm_v)
+        if turns == 2:
+            three_high, two_high, one_high = (flow.result() for flow in (three_flow[high], two_flow[high], one_flow))
+            early = [[(high, 2, three_high), (high, 1, two_high), (high, 0, one_high)]]
+            rows_all = Gather(low_momenta(early[0], olds, flipped), (0, 1))
+            rows_all.send()
+            results["early"] = rows_all.got
+        if turns == 3:
+            results["head"] = head_update(head_flow.result(), head, head_m, head_v, slots)
+            rows_all.got = results["early"]
+            rows_all.join()
+            rows_all.send()
+        if turns == 4:
+            three_low = three_flow[low].result()
+            results["third"] = lax.all_gather(low_momenta([(low, 2, three_low)], olds, flipped), "owner")
+        if turns == 3:
+            results.pop("early")
+        results = advance(results, flows, True)
+    rows_all = jnp.concatenate([rows_all.values, rows_all.got], axis=0)
+    one_low, two_low = last_flow.result(), two_flow[low].result()
+    late = [[(low, 2, three_low)], [(low, 1, two_low), (low, 0, one_low)]]
+    outcomes = newton_schulz(
+        early, late, olds, stored((w_reduce, w_spatial, w_expand)), flipped, [(rows_all, True)], [(results["third"], False), None]
     )
     updated, moments = (
-        [jnp.swapaxes(a, 1, 2) if size % LANES else a for a, size in zip(arrays, rows_of)] for arrays in results
-    )
-    (new_norm, new_norm_m, new_norm_v), (new_head, new_head_m, new_head_v) = updates
+        [jnp.swapaxes(a, 1, 2) if size % LANES else a for a, size in zip(arrays, rows_of)] for arrays in outcomes
+    )
+    (new_norm, new_norm_m, new_norm_v), (new_head, new_head_m, new_head_v) = results["norm"], results["head"]
     new_bias, new_bias_m, new_bias_v = adamw(head_bias, grad_bias, bias_m, bias_v, LR_VECTOR, 0.0)
     return (
         loss_sum,

time: 746 us -> 713 us (0.956)
  waiting for transfers between devices: 153 us -> 129 us
  blocking collectives: 112 us -> 104 us
    ppermute x64 -> x68, waiting for transfers between devices: 126 us -> 98.3 us  [swap(): lax.ppermute(values, AXES, [(src, src ^ 1 << bit) for src in range(count)])]
    all_to_all x5, blocking collectives: 94.8 us -> 79.5 us  [exchange(): return lax.all_to_all(copies, AXES, 0, 0, tiled=True)]
    ppermute x64 -> x68, starting transfers between devices: 69.7 us -> 76.7 us  [swap(): lax.ppermute(values, AXES, [(src, src ^ 1 << bit) for src in range(count)])]
    all_gather x1 -> x2, blocking collectives: 9.59 us -> 15.7 us  [the longest x1 9.23 us: newton_schulz(): low = (lax.all_gather(values, 'owner'), False)]
    unnamed x121 -> x139, local copies, waits for them, and re-layouts: 17.7 us -> 17 us
  transfers between devices with their start and end apart: 75 -> 77, of which waited for: 32 -> 27; matrix products, arithmetic and copies ran while one was open for 5% -> 5% of each run, Pallas kernels for 29% -> 27%
where the time goes in v5:
time: 713 us; the launch traced here: 701 us
  Pallas kernels  269 us (38%)
  waiting for transfers between devices  129 us (18%)
  blocking collectives  104 us (15%)
  starting transfers between devices  101 us (14%)
  local copies, waits for them, and re-layouts  45.6 us (6%)
  other arithmetic  33.8 us (5%)
  between operations  19.5 us (3%)
    pallas_call x28, Pallas kernels, launch(): pl.pallas_call(grouped, name=name, grid=grid, in_specs=flat_specs, out_sp...  269 us
    ppermute x68, waiting for transfers between devices, swap(): lax.ppermute(values, AXES, [(src, src ^ 1 << bit) for src in range(count)])  98.3 us
    all_to_all x5, blocking collectives, exchange(): return lax.all_to_all(copies, AXES, 0, 0, tiled=True)  79.5 us
    ppermute x68, starting transfers between devices, swap(): lax.ppermute(values, AXES, [(src, src ^ 1 << bit) for src in range(count)])  76.7 us
    all_to_all x7, waiting for transfers between devices, exchange(): return lax.all_to_all(copies, AXES, 0, 0, tiled=True)  26 us
    all_to_all x7, starting transfers between devices, exchange(): return lax.all_to_all(copies, AXES, 0, 0, tiled=True)  24.4 us
    unnamed x139, local copies, waits for them, and re-layouts  17 us
    add x11, other arithmetic, add(): parts = [kept + got for kept, got in zip(self.kept, self.got)]  14.8 us
  transfers between devices with their start and end apart: 77, of which 27 were waited for; matrix products, arithmetic and copies ran while one was open for 5% of the time, Pallas kernels for 27%

profile of v5, /device:TPU:0, one launch (start us, length us, event | category | flops | bytes accessed | tf_op | source)
XLA Modules:
  0.0 701.4 jit_solution(6282105410976138438)
XLA Ops:
  56.6 9.0 %reduce_first.1 = (f32[1344,512]{1,0:T(8,128)}, f32[32,16,128]{2,1,0:T(8,128)}) custom-call(bf16[1344,2048]{1,0:T(8,128)(2,1)} %bitcast.264, f32[1344,2]{1,0:T(8,128)} %copy.74.refs_1_.refs_4_.refs_5_.refs_6_, f32[8,128]{1,0:T(8,128)} %broadcast_in_dim.39.refs_2_, bf16[16,256,128]{2,1,0:T(8,128)(2,1)} %copy-done.56, ...), custom_call_target="tpu_custom_call" | custom-call | flops 2818572288 | bytes 10631680 | tf_op jit(solution)/shard_map/reduce_first/pallas_call | solution.py:360
  78.0 9.7 %all-to-all-done.refs_1_ = f32[32,16,128]{2,1,0:T(8,128)} async-done(((f32[32,16,128]{2,1,0:T(8,128)}), f32[32,16,128]{2,1,0:T(8,128)}, u32[]{:S(2)}, u32[]{:S(2)}) %all-to-all-start) | async-done | bytes 262176 | tf_op jit(solution)/shard_map/all_to_all | solution.py:45
  93.2 13.6 %spatial_conv.2 = (bf16[1344,512]{1,0:T(8,128)(2,1)}, f32[1344,512]{1,0:T(8,128)}, f32[8,512]{1,0:T(8,128)}, f32[32,8,128]{2,1,0:T(8,128)}) custom-call(f32[1344,512]{1,0:T(8,128)} %get-tuple-element.272.refs_0_.refs_7_.refs_2_, f32[32,16,128]{2,1,0:T(8,128)} %all-to-all-done.refs_1_, f32[8,128]{1,0:T(8,128)} %slice_reduce_fusion.refs_2_.refs_3_.refs_4_.refs_5_, ...), custom_call_target="tpu_custom_call" | custom-call | flops 6341787648 | bytes 12073472 | tf_op jit(solution)/shard_map/spatial_conv/pallas_call | solution.py:360
  106.9 12.4 %all_to_all.60.refs_1_ = f32[32,8,128]{2,1,0:T(8,128)} all-to-all(f32[32,8,128]{2,1,0:T(8,128)} %get-tuple-element.282), channel_id=1, replica_groups=mesh['dp'=8,'owner'=4] {'dp','owner'}, dimensions={0} | all-to-all | bytes 262144 | tf_op jit(solution)/shard_map/all_to_all | solution.py:45
  119.2 9.2 %expand.2 = (bf16[1344,512]{1,0:T(8,128)(2,1)}, bf16[1344,2048]{1,0:T(8,128)(2,1)}, f32[8,512]{1,0:T(8,128)}, f32[32,32,128]{2,1,0:T(8,128)}) custom-call(f32[1344,512]{1,0:T(8,128)} %get-tuple-element.281.refs_0_.refs_7_.refs_1_, f32[32,8,128]{2,1,0:T(8,128)} %all_to_all.60.refs_1_, f32[8,128]{1,0:T(8,128)} %slice_reduce_fusion.refs_2_.refs_3_.refs_4_.refs_5_, ...), custom_call_target="tpu_custom_call" | custom-call | flops 2818572288 | bytes 14563840 | tf_op jit(solution)/shard_map/expand/pallas_call | solution.py:360
  128.5 24.6 %all_to_all.61.refs_2_ = f32[32,32,128]{2,1,0:T(8,128)} all-to-all(f32[32,32,128]{2,1,0:T(8,128)} %get-tuple-element.284), channel_id=1, replica_groups=mesh['dp'=8,'owner'=4] {'dp','owner'}, dimensions={0} | all-to-all | bytes 1048576 | tf_op jit(solution)/shard_map/all_to_all | solution.py:45
  153.1 13.1 %close_and_reduce.1 = (bf16[1344,2048]{1,0:T(8,128)(2,1)}, f32[1344,512]{1,0:T(8,128)}, f32[8,2048]{1,0:T(8,128)}, f32[32,8,128]{2,1,0:T(8,128)}) custom-call(bf16[1344,2048]{1,0:T(8,128)(2,1)} %get-tuple-element.283.refs_0_.refs_8_.refs_1_, bf16[1344,2048]{1,0:T(8,128)(2,1)} %bitcast.265, f32[32,32,128]{2,1,0:T(8,128)} %all_to_all.61.refs_2_, ...), custom_call_target="tpu_custom_call" | custom-call | flops 2818572288 | bytes 24246784 | tf_op jit(solution)/shard_map/close_and_reduce/pallas_call | solution.py:360
  166.2 14.4 %all_to_all.62.refs_1_ = f32[32,8,128]{2,1,0:T(8,128)} all-to-all(f32[32,8,128]{2,1,0:T(8,128)} %get-tuple-element.286), channel_id=1, replica_groups=mesh['dp'=8,'owner'=4] {'dp','owner'}, dimensions={0} | all-to-all | bytes 262144 | tf_op jit(solution)/shard_map/all_to_all | solution.py:45
  184.7 13.1 %spatial_conv.3 = (bf16[1344,512]{1,0:T(8,128)(2,1)}, f32[1344,512]{1,0:T(8,128)}, f32[8,512]{1,0:T(8,128)}, f32[32,8,128]{2,1,0:T(8,128)}) custom-call(f32[1344,512]{1,0:T(8,128)} %get-tuple-element.285.refs_0_.refs_7_.refs_1_, f32[32,8,128]{2,1,0:T(8,128)} %all_to_all.62.refs_1_, f32[8,128]{1,0:T(8,128)} %slice_reduce_fusion.refs_2_.refs_3_.refs_4_.refs_5_, ...), custom_call_target="tpu_custom_call" | custom-call | flops 6341787648 | bytes 18233856 | tf_op jit(solution)/shard_map/spatial_conv/pallas_call | solution.py:360
  197.9 11.5 %all_to_all.63.refs_1_ = f32[32,8,128]{2,1,0:T(8,128)} all-to-all(f32[32,8,128]{2,1,0:T(8,128)} %get-tuple-element.290), channel_id=1, replica_groups=mesh['dp'=8,'owner'=4] {'dp','owner'}, dimensions={0} | all-to-all | bytes 262144 | tf_op jit(solution)/shard_map/all_to_all | solution.py:45
  209.4 9.2 %expand.3 = (bf16[1344,512]{1,0:T(8,128)(2,1)}, bf16[1344,2048]{1,0:T(8,128)(2,1)}, f32[8,512]{1,0:T(8,128)}, f32[32,32,128]{2,1,0:T(8,128)}) custom-call(f32[1344,512]{1,0:T(8,128)} %get-tuple-element.289.refs_0_.refs_7_.refs_1_, f32[32,8,128]{2,1,0:T(8,128)} %all_to_all.63.refs_1_, f32[8,128]{1,0:T(8,128)} %slice_reduce_fusion.refs_2_.refs_3_.refs_4_.refs_5_, ...), custom_call_target="tpu_custom_call" | custom-call | flops 2818572288 | bytes 21379584 | tf_op jit(solution)/shard_map/expand/pallas_call | solution.py:360
  222.1 14.7 %all-to-all-done.5.refs_2_ = f32[32,32,128]{2,1,0:T(8,128)S(1)} async-done(((f32[32,32,128]{2,1,0:T(8,128)}), f32[32,32,128]{2,1,0:T(8,128)S(1)}, u32[]{:S(2)}, u32[]{:S(2)}) %all-to-all-start.5) | async-done | bytes 524320 | tf_op jit(solution)/shard_map/all_to_all | solution.py:45
  237.6 30.2 %head_step.1 = (bf16[1344,2048]{1,0:T(8,128)(2,1)}, f32[8,2048]{1,0:T(8,128)}, bf16[32,48,128]{2,1,0:T(8,128)(2,1)}, bf16[2,8,2,256,128]{4,3,2,1,0:T(8,128)(2,1)}, bf16[2,8,2,256,128]{4,3,2,1,0:T(8,128)(2,1)}) custom-call(bf16[1344,2048]{1,0:T(8,128)(2,1)} %get-tuple-element.291.refs_0_.refs_1_, bf16[1344,2048]{1,0:T(8,128)(2,1)} %get-tuple-element.292.refs_1_.refs_0_, ...), custom_call_target="tpu_custom_call" | custom-call | flops 301989888 | bytes 32799424 | tf_op jit(solution)/shard_map/head_step/pallas_call | solution.py:360
  267.8 16.7 %all_to_all.64.refs_2_.refs_5_ = bf16[32,48,128]{2,1,0:T(8,128)(2,1)} all-to-all(bf16[32,48,128]{2,1,0:T(8,128)(2,1)} %get-tuple-element.294), channel_id=1, replica_groups=mesh['dp'=8,'owner'=4] {'dp','owner'}, dimensions={0} | all-to-all | bytes 786432 | tf_op jit(solution)/shard_map/all_to_all | solution.py:45
  284.4 12.8 %back_expand.2 = (bf16[1344,2048]{1,0:T(8,128)(2,1)}, f32[1344,512]{1,0:T(8,128)}, f32[32,8,128]{2,1,0:T(8,128)}) custom-call(bf16[1344,2048]{1,0:T(8,128)(2,1)} %get-tuple-element.296.refs_0_.refs_7_, bf16[1344,2048]{1,0:T(8,128)(2,1)} %get-tuple-element.291.refs_0_.refs_1_, bf16[32,48,128]{2,1,0:T(8,128)(2,1)} %all_to_all.64.refs_2_.refs_5_, ...), custom_call_target="tpu_custom_call" | custom-call | flops 2818572288 | bytes 33554432 | tf_op jit(solution)/shard_map/back_expand/pallas_call | solution.py:360
  305.1 7.3 %weight_grad.3 = (bf16[2,2048,128]{2,1,0:T(8,128)(2,1)}, bf16[2,2048,128]{2,1,0:T(8,128)(2,1)}) custom-call(bf16[1344,2048]{1,0:T(8,128)(2,1)} %get-tuple-element.307.refs_0_, bf16[1344,512]{1,0:T(8,128)(2,1)} %get-tuple-element.308.refs_1_), custom_call_target="tpu_custom_call" | custom-call | flops 2818572288 | bytes 8978432 | tf_op jit(solution)/shard_map/weight_grad/pallas_call | solution.py:360
  314.8 15.2 %back_conv.2 = (bf16[1344,512]{1,0:T(8,128)(2,1)}, f32[1344,512]{1,0:T(8,128)}, f32[32,8,128]{2,1,0:T(8,128)}) custom-call(f32[1344,512]{1,0:T(8,128)} %get-tuple-element.304.refs_0_, f32[1344,512]{1,0:T(8,128)} %get-tuple-element.289.refs_0_.refs_7_.refs_1_, f32[32,8,128]{2,1,0:T(8,128)} %copy-done.29, f32[8,512]{1,0:T(8,128)} %get-tuple-element.300.refs_8_.refs_3_, ...), custom_call_target="tpu_custom_call" | custom-call | flops 6341787648 | bytes 23755264 | tf_op jit(solution)/shard_map/back_conv/pallas_call | solution.py:360
  330.0 8.0 %collective-permute-done.16 = bf16[8,512,128]{2,1,0:T(8,128)(2,1)} collective-permute-done((bf16[8,512,128]{2,1,0:T(8,128)(2,1)}, bf16[8,512,128]{2,1,0:T(8,128)(2,1)}, u32[]{:S(2)}, u32[]{:S(2)}) %collective-permute-start.16) | collective-permute-done | bytes 1048608 | tf_op jit(solution)/shard_map/ppermute | solution.py:50
  348.7 11.7 %spatial_grad.2 = (bf16[2,4608,128]{2,1,0:T(8,128)(2,1)}, bf16[2,4608,128]{2,1,0:T(8,128)(2,1)}) custom-call(bf16[1344,512]{1,0:T(8,128)(2,1)} %get-tuple-element.326.refs_0_, bf16[1344,512]{1,0:T(8,128)(2,1)} %get-tuple-element.327.refs_1_), custom_call_target="tpu_custom_call" | custom-call | flops 6341787648 | bytes 7471104 | tf_op jit(solution)/shard_map/spatial_grad/pallas_call | solution.py:360
  365.9 17.7 %back_reduce.1 = (bf16[1344,512]{1,0:T(8,128)(2,1)}, bf16[1344,2048]{1,0:T(8,128)(2,1)}, bf16[32,32,128]{2,1,0:T(8,128)(2,1)}) custom-call(f32[1344,512]{1,0:T(8,128)} %get-tuple-element.323.refs_0_, f32[1344,512]{1,0:T(8,128)} %get-tuple-element.285.refs_0_.refs_7_.refs_1_, f32[32,8,128]{2,1,0:T(8,128)} %copy-done.10, ...), custom_call_target="tpu_custom_call" | custom-call | flops 2818572288 | bytes 33554432 | tf_op jit(solution)/shard_map/back_reduce/pallas_call | solution.py:360
  416.6 12.7 %back_expand.3 = (bf16[1344,2048]{1,0:T(8,128)(2,1)}, f32[1344,512]{1,0:T(8,128)}, f32[32,8,128]{2,1,0:T(8,128)}) custom-call(bf16[1344,2048]{1,0:T(8,128)(2,1)} %get-tuple-element.350.refs_0_, bf16[1344,2048]{1,0:T(8,128)(2,1)} %get-tuple-element.283.refs_0_.refs_8_.refs_1_, bf16[32,32,128]{2,1,0:T(8,128)(2,1)} %copy-done.5, ...), custom_call_target="tpu_custom_call" | custom-call | flops 2818572288 | bytes 26753536 | tf_op jit(solution)/shard_map/back_expand/pallas_call | solution.py:360
  440.7 7.3 %weight_grad.5 = (bf16[2,2048,128]{2,1,0:T(8,128)(2,1)}, bf16[2,2048,128]{2,1,0:T(8,128)(2,1)}) custom-call(bf16[1344,2048]{1,0:T(8,128)(2,1)} %get-tuple-element.378.refs_0_, bf16[1344,512]{1,0:T(8,128)(2,1)} %get-tuple-element.379.refs_1_), custom_call_target="tpu_custom_call" | custom-call | flops 2818572288 | bytes 8978432 | tf_op jit(solution)/shard_map/weight_grad/pallas_call | solution.py:360
  455.2 15.5 %back_conv.3 = (bf16[1344,512]{1,0:T(8,128)(2,1)}, f32[1344,512]{1,0:T(8,128)}, f32[32,8,128]{2,1,0:T(8,128)}) custom-call(f32[1344,512]{1,0:T(8,128)} %get-tuple-element.374.refs_0_, f32[1344,512]{1,0:T(8,128)} %get-tuple-element.281.refs_0_.refs_7_.refs_1_, f32[32,8,128]{2,1,0:T(8,128)} %copy-done.30, f32[8,512]{1,0:T(8,128)} %get-tuple-element.357.refs_8_.refs_3_, ...), custom_call_target="tpu_custom_call" | custom-call | flops 6341787648 | bytes 17463808 | tf_op jit(solution)/shard_map/back_conv/pallas_call | solution.py:360
  477.9 11.7 %spatial_grad.3 = (bf16[2,4608,128]{2,1,0:T(8,128)(2,1)}, bf16[2,4608,128]{2,1,0:T(8,128)(2,1)}) custom-call(bf16[1344,512]{1,0:T(8,128)(2,1)} %get-tuple-element.400.refs_0_, bf16[1344,512]{1,0:T(8,128)(2,1)} %get-tuple-element.401.refs_1_), custom_call_target="tpu_custom_call" | custom-call | flops 6341787648 | bytes 7471104 | tf_op jit(solution)/shard_map/spatial_grad/pallas_call | solution.py:360
  491.5 9.8 %last_grad.1 = (bf16[2,2048,128]{2,1,0:T(8,128)(2,1)}, bf16[2,2048,128]{2,1,0:T(8,128)(2,1)}) custom-call(bf16[1344,2048]{1,0:T(8,128)(2,1)} %bitcast.267, f32[1344,512]{1,0:T(8,128)} %get-tuple-element.409.refs_1_, f32[1344,512]{1,0:T(8,128)} %get-tuple-element.272.refs_0_.refs_7_.refs_2_, f32[32,8,128]{2,1,0:T(8,128)} %copy-done.11, ...), custom_call_target="tpu_custom_call" | custom-call | flops 2818572288 | bytes 13269504 | tf_op jit(solution)/shard_map/last_grad/pallas_call | solution.py:360
  546.0 7.5 %collective-permute-done.48 = bf16[2,256,128]{2,1,0:T(8,128)(2,1)} collective-permute-done((bf16[2,256,128]{2,1,0:T(8,128)(2,1)}, bf16[2,256,128]{2,1,0:T(8,128)(2,1)}, u32[]{:S(2)}, u32[]{:S(2)}) %collective-permute-start.48) | collective-permute-done | bytes 131104 | tf_op jit(solution)/shard_map/ppermute | solution.py:50
  589.6 9.2 %all-gather.3 = bf16[3328,128]{1,0:T(8,128)(2,1)} all-gather(bf16[832,128]{1,0:T(8,128)(2,1)S(1)} %copy-done.19), channel_id=5, replica_groups=mesh['dp'=8,'owner'=4] {'owner'}, dimensions={0}, use_global_device_ids=true | all-gather | bytes 1064960 | tf_op jit(solution)/shard_map/all_gather | solution.py:1210
  622.0 7.4 %collective-permute-done.64 = f32[320,128]{1,0:T(8,128)S(1)} collective-permute-done((f32[320,128]{1,0:T(8,128)S(1)}, f32[320,128]{1,0:T(8,128)S(1)}, u32[]{:S(2)}, u32[]{:S(2)}) %collective-permute-start.64) | collective-permute-done | bytes 163872 | tf_op jit(solution)/shard_map/ppermute | solution.py:50
  629.4 8.4 %all_gather.35.refs_0_ = f32[1280,128]{1,0:T(8,128)} all-gather(f32[320,128]{1,0:T(8,128)S(1)} %bitcast_add_fusion.21), channel_id=1, replica_groups=mesh['dp'=8,'owner'=4] {'owner'}, dimensions={0}, use_global_device_ids=true | all-gather | bytes 819200 | tf_op jit(solution)/shard_map/all_gather | solution.py:1235
  637.8 19.3 %polynomial.1 = bf16[128,512]{1,0:T(8,128)(2,1)} custom-call(f32[1280,128]{1,0:T(8,128)} %all_gather.35.refs_0_), custom_call_target="tpu_custom_call" | custom-call | flops 16106127360 | bytes 786432 | tf_op jit(solution)/shard_map/polynomial/pallas_call | solution.py:360
  657.1 8.8 %collective-permute-done.65 = bf16[128,512]{1,0:T(8,128)(2,1)S(1)} collective-permute-done((bf16[128,512]{1,0:T(8,128)(2,1)}, bf16[128,512]{1,0:T(8,128)(2,1)S(1)}, u32[]{:S(2)}, u32[]{:S(2)}) %collective-permute-start.65) | collective-permute-done | bytes 131104 | tf_op jit(solution)/shard_map/ppermute | solution.py:50
  679.3 9.2 %collective-permute-done.67.refs_2_ = bf16[2,2,128,512]{3,2,1,0:T(8,128)(2,1)S(1)} collective-permute-done((bf16[2,2,128,512]{3,2,1,0:T(8,128)(2,1)S(1)}, bf16[2,2,128,512]{3,2,1,0:T(8,128)(2,1)S(1)}, u32[]{:S(2)}, u32[]{:S(2)}) %collective-permute-start.67) | collective-permute-done | bytes 524320 | tf_op jit(solution)/shard_map/ppermute | solution.py:50
  (445 shorter events, 281.1 us)
Async XLA Ops:
  7.2 112.0 %all-gather.7.cloned.1.call-start = ((), (), s32[]{:S(2)}) async-start(), calls=%async_computation.12 | async-start | bytes 4325376 | tf_op jit(solution)/shard_map/all_gather | solution.py:1290
  10.2 174.5 %all-gather.9.cloned.1.call-start = ((), (), s32[]{:S(2)}) async-start(), calls=%async_computation.13 | async-start | bytes 11354112 | tf_op jit(solution)/shard_map/all_gather | solution.py:1336
  35.6 16.5 %collective-permute-start.5 = (bf16[8,256,128]{2,1,0:T(8,128)(2,1)S(1)}, bf16[8,256,128]{2,1,0:T(8,128)(2,1)S(1)}, u32[]{:S(2)}, u32[]{:S(2)}) collective-permute-start(bf16[8,256,128]{2,1,0:T(8,128)(2,1)S(1)} %pad_maximum_fusion.4), channel_id=1, source_target_pairs={{0,2},{1,3},{2,0},{3,1},{4,6},{5,7},{6,4},{7,5},{8,10},{9,11},{10,... | collective-permute-start | bytes 1572872 | tf_op jit(solution)/shard_map/ppermute | solution.py:50
  67.1 20.5 %collective-permute-start.12 = (bf16[8,288,128]{2,1,0:T(8,128)(2,1)S(1)}, bf16[8,288,128]{2,1,0:T(8,128)(2,1)S(1)}, u32[]{:S(2)}, u32[]{:S(2)}) collective-permute-start(bf16[8,288,128]{2,1,0:T(8,128)(2,1)S(1)} %pad_maximum_fusion.2), channel_id=1, source_target_pairs={{0,2},{1,3},{2,0},{3,1},{4,6},{5,7},{6,4},{7,5},{8,10},{9,11},{10,... | collective-permute-start | bytes 1769480 | tf_op jit(solution)/shard_map/ppermute | solution.py:50
  67.4 20.2 %collective-permute-start.11 = (bf16[8,288,128]{2,1,0:T(8,128)(2,1)S(1)}, bf16[8,288,128]{2,1,0:T(8,128)(2,1)S(1)}, u32[]{:S(2)}, u32[]{:S(2)}) collective-permute-start(bf16[8,288,128]{2,1,0:T(8,128)(2,1)S(1)} %pad_maximum_fusion.1), channel_id=1, source_target_pairs={{0,4},{1,5},{2,6},{3,7},{4,0},{5,1},{6,2},{7,3},{8,12},{9,13},{10,... | collective-permute-start | bytes 1769480 | tf_op jit(solution)/shard_map/ppermute | solution.py:50
  68.4 19.2 %all-to-all-start = ((f32[32,16,128]{2,1,0:T(8,128)}), f32[32,16,128]{2,1,0:T(8,128)}, u32[]{:S(2)}, u32[]{:S(2)}) async-start(f32[32,16,128]{2,1,0:T(8,128)} %get-tuple-element.275), calls=%async_computation | async-start | bytes 524288 | tf_op jit(solution)/shard_map/all_to_all | solution.py:45
  218.6 18.2 %all-to-all-start.5 = ((f32[32,32,128]{2,1,0:T(8,128)}), f32[32,32,128]{2,1,0:T(8,128)S(1)}, u32[]{:S(2)}, u32[]{:S(2)}) async-start(f32[32,32,128]{2,1,0:T(8,128)} %get-tuple-element.293), calls=%async_computation.5 | async-start | bytes 1048576 | tf_op jit(solution)/shard_map/all_to_all | solution.py:45
  312.4 25.6 %collective-permute-start.16 = (bf16[8,512,128]{2,1,0:T(8,128)(2,1)}, bf16[8,512,128]{2,1,0:T(8,128)(2,1)}, u32[]{:S(2)}, u32[]{:S(2)}) collective-permute-start(bf16[8,512,128]{2,1,0:T(8,128)(2,1)} %dynamic-slice_bitcast_fusion), channel_id=1, source_target_pairs={{0,2},{1,3},{2,0},{3,1},{4,6},{5,7},{6,4},{7,5},{8,10},{9,11},{10,... | collective-permute-start | bytes 3145736 | tf_op jit(solution)/shard_map/ppermute | solution.py:50
  314.1 23.9 %collective-permute-start.17 = (bf16[16,256,128]{2,1,0:T(8,128)(2,1)}, bf16[16,256,128]{2,1,0:T(8,128)(2,1)}, u32[]{:S(2)}, u32[]{:S(2)}) collective-permute-start(bf16[16,256,128]{2,1,0:T(8,128)(2,1)} %bitcast.359), channel_id=1, source_target_pairs={{0,1},{1,0},{2,3},{3,2},{4,5},{5,4},{6,7},{7,6},{8,9},{9,8},{10,11... | collective-permute-start | bytes 3145736 | tf_op jit(solution)/shard_map/ppermute | solution.py:50
  341.8 19.1 %collective-permute-start.18 = (bf16[4,512,128]{2,1,0:T(8,128)(2,1)S(1)}, bf16[4,512,128]{2,1,0:T(8,128)(2,1)S(1)}, u32[]{:S(2)}, u32[]{:S(2)}) collective-permute-start(bf16[4,512,128]{2,1,0:T(8,128)(2,1)S(1)} %dynamic-slice_bitcast_fusion.7), channel_id=1, source_target_pairs={{0,4},{1,5},{2,6},{3,7},{4,0},{5,1},{6,2},{7,3},{8,12},{9,13},{10,... | collective-permute-start | bytes 1572872 | tf_op jit(solution)/shard_map/ppermute | solution.py:50
  343.5 17.5 %collective-permute-start.19 = (bf16[8,256,128]{2,1,0:T(8,128)(2,1)}, bf16[8,256,128]{2,1,0:T(8,128)(2,1)S(1)}, u32[]{:S(2)}, u32[]{:S(2)}) collective-permute-start(bf16[8,256,128]{2,1,0:T(8,128)(2,1)} %bitcast.41), channel_id=1, source_target_pairs={{0,8},{1,9},{2,10},{3,11},{4,12},{5,13},{6,14},{7,15},{8,0},{9,1},... | collective-permute-start | bytes 1572872 | tf_op jit(solution)/shard_map/ppermute | solution.py:50
  344.9 16.0 %all-to-all-start.8 = ((f32[32,8,128]{2,1,0:T(8,128)}), f32[32,8,128]{2,1,0:T(8,128)S(1)}, u32[]{:S(2)}, u32[]{:S(2)}) async-start(f32[32,8,128]{2,1,0:T(8,128)} %get-tuple-element.319), calls=%async_computation.8 | async-start | bytes 262144 | tf_op jit(solution)/shard_map/all_to_all | solution.py:45
  362.0 21.6 %collective-permute-start.22 = (bf16[16,576,128]{2,1,0:T(8,128)(2,1)}, bf16[16,576,128]{2,1,0:T(8,128)(2,1)}, u32[]{:S(2)}, u32[]{:S(2)}) collective-permute-start(bf16[16,576,128]{2,1,0:T(8,128)(2,1)} %bitcast.48), channel_id=1, source_target_pairs={{0,1},{1,0},{2,3},{3,2},{4,5},{5,4},{6,7},{7,6},{8,9},{9,8},{10,11... | collective-permute-start | bytes 7077896 | tf_op jit(solution)/shard_map/ppermute | solution.py:50
  362.3 21.3 %collective-permute-start.20 = (bf16[2,512,128]{2,1,0:T(8,128)(2,1)S(1)}, bf16[2,512,128]{2,1,0:T(8,128)(2,1)S(1)}, u32[]{:S(2)}, u32[]{:S(2)}) collective-permute-start(bf16[2,512,128]{2,1,0:T(8,128)(2,1)S(1)} %dynamic-slice_bitcast_fusion.16), channel_id=1, source_target_pairs={{0,8},{1,9},{2,10},{3,11},{4,12},{5,13},{6,14},{7,15},{8,0},{9,1},... | collective-permute-start | bytes 786440 | tf_op jit(solution)/shard_map/ppermute | solution.py:50
  363.5 20.1 %collective-permute-start.21 = (bf16[4,256,128]{2,1,0:T(8,128)(2,1)S(1)}, bf16[4,256,128]{2,1,0:T(8,128)(2,1)S(1)}, u32[]{:S(2)}, u32[]{:S(2)}) collective-permute-start(bf16[4,256,128]{2,1,0:T(8,128)(2,1)S(1)} %bitcast.353), channel_id=1, source_target_pairs={{0,16},{1,17},{2,18},{3,19},{4,20},{5,21},{6,22},{7,23},{8,24},{9,... | collective-permute-start | bytes 786440 | tf_op jit(solution)/shard_map/ppermute | solution.py:50
  389.3 20.9 %collective-permute-start.25 = (bf16[8,288,128]{2,1,0:T(8,128)(2,1)}, bf16[8,288,128]{2,1,0:T(8,128)(2,1)}, u32[]{:S(2)}, u32[]{:S(2)}) collective-permute-start(bf16[8,288,128]{2,1,0:T(8,128)(2,1)} %dynamic-slice_bitcast_fusion.3), channel_id=1, source_target_pairs={{0,2},{1,3},{2,0},{3,1},{4,6},{5,7},{6,4},{7,5},{8,10},{9,11},{10,... | collective-permute-start | bytes 1769480 | tf_op jit(solution)/shard_map/ppermute | solution.py:50
  390.8 20.0 %collective-permute-start.26 = (bf16[8,288,128]{2,1,0:T(8,128)(2,1)}, bf16[8,288,128]{2,1,0:T(8,128)(2,1)}, u32[]{:S(2)}, u32[]{:S(2)}) collective-permute-start(bf16[8,288,128]{2,1,0:T(8,128)(2,1)} %dynamic-slice_bitcast_fusion.2), channel_id=1, source_target_pairs={{0,4},{1,5},{2,6},{3,7},{4,0},{5,1},{6,2},{7,3},{8,12},{9,13},{10,... | collective-permute-start | bytes 1769480 | tf_op jit(solution)/shard_map/ppermute | solution.py:50
  392.3 17.9 %all-to-all-start.9 = ((bf16[32,32,128]{2,1,0:T(8,128)(2,1)}), bf16[32,32,128]{2,1,0:T(8,128)(2,1)S(1)}, u32[]{:S(2)}, u32[]{:S(2)}) async-start(bf16[32,32,128]{2,1,0:T(8,128)(2,1)} %get-tuple-element.340), calls=%async_computation.9 | async-start | bytes 524288 | tf_op jit(solution)/shard_map/all_to_all | solution.py:45
  433.4 15.8 %collective-permute-start.33 = (bf16[8,256,128]{2,1,0:T(8,128)(2,1)S(1)}, bf16[8,256,128]{2,1,0:T(8,128)(2,1)S(1)}, u32[]{:S(2)}, u32[]{:S(2)}) collective-permute-start(bf16[8,256,128]{2,1,0:T(8,128)(2,1)S(1)} %dynamic-slice_bitcast_fusion.6), channel_id=1, source_target_pairs={{0,2},{1,3},{2,0},{3,1},{4,6},{5,7},{6,4},{7,5},{8,10},{9,11},{10,... | collective-permute-start | bytes 1572872 | tf_op jit(solution)/shard_map/ppermute | solution.py:50
  450.5 20.3 %collective-permute-start.37 = (bf16[16,256,128]{2,1,0:T(8,128)(2,1)}, bf16[16,256,128]{2,1,0:T(8,128)(2,1)S(1)}, u32[]{:S(2)}, u32[]{:S(2)}) collective-permute-start(bf16[16,256,128]{2,1,0:T(8,128)(2,1)} %bitcast.81), channel_id=1, source_target_pairs={{0,1},{1,0},{2,3},{3,2},{4,5},{5,4},{6,7},{7,6},{8,9},{9,8},{10,11... | collective-permute-start | bytes 3145736 | tf_op jit(solution)/shard_map/ppermute | solution.py:50
  450.5 20.2 %collective-permute-start.36 = (bf16[4,256,128]{2,1,0:T(8,128)(2,1)S(1)}, bf16[4,256,128]{2,1,0:T(8,128)(2,1)S(1)}, u32[]{:S(2)}, u32[]{:S(2)}) collective-permute-start(bf16[4,256,128]{2,1,0:T(8,128)(2,1)S(1)} %dynamic-slice_bitcast_fusion.15), channel_id=1, source_target_pairs={{0,4},{1,5},{2,6},{3,7},{4,0},{5,1},{6,2},{7,3},{8,12},{9,13},{10,... | collective-permute-start | bytes 786440 | tf_op jit(solution)/shard_map/ppermute | solution.py:50
  451.3 19.4 %collective-permute-start.34 = (bf16[1,288,128]{2,1,0:T(8,128)(2,1)S(1)}, bf16[1,288,128]{2,1,0:T(8,128)(2,1)S(1)}, u32[]{:S(2)}, u32[]{:S(2)}) collective-permute-start(bf16[1,288,128]{2,1,0:T(8,128)(2,1)S(1)} %constant_dynamic-slice_fusion.12), channel_id=1, source_target_pairs={{0,16},{1,17},{2,18},{3,19},{4,20},{5,21},{6,22},{7,23},{8,24},{9,... | collective-permute-start | bytes 221192 | tf_op jit(solution)/shard_map/ppermute | solution.py:50
  453.7 17.0 %collective-permute-start.35 = (bf16[1,288,128]{2,1,0:T(8,128)(2,1)S(1)}, bf16[1,288,128]{2,1,0:T(8,128)(2,1)S(1)}, u32[]{:S(2)}, u32[]{:S(2)}) collective-permute-start(bf16[1,288,128]{2,1,0:T(8,128)(2,1)S(1)} %constant_dynamic-slice_fusion.11), channel_id=1, source_target_pairs={{0,2},{1,3},{2,0},{3,1},{4,6},{5,7},{6,4},{7,5},{8,10},{9,11},{10,... | collective-permute-start | bytes 221192 | tf_op jit(solution)/shard_map/ppermute | solution.py:50
  472.8 16.9 %collective-permute-start.39 = (bf16[8,256,128]{2,1,0:T(8,128)(2,1)S(1)}, bf16[8,256,128]{2,1,0:T(8,128)(2,1)S(1)}, u32[]{:S(2)}, u32[]{:S(2)}) collective-permute-start(bf16[8,256,128]{2,1,0:T(8,128)(2,1)S(1)} %dynamic-slice_bitcast_fusion.5), channel_id=1, source_target_pairs={{0,2},{1,3},{2,0},{3,1},{4,6},{5,7},{6,4},{7,5},{8,10},{9,11},{10,... | collective-permute-start | bytes 1572872 | tf_op jit(solution)/shard_map/ppermute | solution.py:50
  473.4 16.2 %collective-permute-start.38 = (bf16[2,256,128]{2,1,0:T(8,128)(2,1)S(1)}, bf16[2,256,128]{2,1,0:T(8,128)(2,1)S(1)}, u32[]{:S(2)}, u32[]{:S(2)}) collective-permute-start(bf16[2,256,128]{2,1,0:T(8,128)(2,1)S(1)} %dynamic-slice_bitcast_fusion.23), channel_id=1, source_target_pairs={{0,8},{1,9},{2,10},{3,11},{4,12},{5,13},{6,14},{7,15},{8,0},{9,1},... | collective-permute-start | bytes 393224 | tf_op jit(solution)/shard_map/ppermute | solution.py:50
  506.3 22.9 %collective-permute-start.43 = (bf16[8,288,128]{2,1,0:T(8,128)(2,1)}, bf16[8,288,128]{2,1,0:T(8,128)(2,1)S(1)}, u32[]{:S(2)}, u32[]{:S(2)}) collective-permute-start(bf16[8,288,128]{2,1,0:T(8,128)(2,1)} %bitcast.98), channel_id=1, source_target_pairs={{0,8},{1,9},{2,10},{3,11},{4,12},{5,13},{6,14},{7,15},{8,0},{9,1},... | collective-permute-start | bytes 1769480 | tf_op jit(solution)/shard_map/ppermute | solution.py:50
  508.2 21.0 %collective-permute-start.44 = (bf16[8,288,128]{2,1,0:T(8,128)(2,1)}, bf16[8,288,128]{2,1,0:T(8,128)(2,1)}, u32[]{:S(2)}, u32[]{:S(2)}) collective-permute-start(bf16[8,288,128]{2,1,0:T(8,128)(2,1)} %dynamic-slice_bitcast_fusion.1), channel_id=1, source_target_pairs={{0,4},{1,5},{2,6},{3,7},{4,0},{5,1},{6,2},{7,3},{8,12},{9,13},{10,... | collective-permute-start | bytes 1769480 | tf_op jit(solution)/shard_map/ppermute | solution.py:50
  510.8 18.4 %collective-permute-start.46 = (bf16[8,256,128]{2,1,0:T(8,128)(2,1)}, bf16[8,256,128]{2,1,0:T(8,128)(2,1)}, u32[]{:S(2)}, u32[]{:S(2)}) collective-permute-start(bf16[8,256,128]{2,1,0:T(8,128)(2,1)} %dynamic-slice_bitcast_fusion.4), channel_id=1, source_target_pairs={{0,2},{1,3},{2,0},{3,1},{4,6},{5,7},{6,4},{7,5},{8,10},{9,11},{10,... | collective-permute-start | bytes 1572872 | tf_op jit(solution)/shard_map/ppermute | solution.py:50
  512.2 16.9 %collective-permute-start.41 = (bf16[4,256,128]{2,1,0:T(8,128)(2,1)}, bf16[4,256,128]{2,1,0:T(8,128)(2,1)}, u32[]{:S(2)}, u32[]{:S(2)}) collective-permute-start(bf16[4,256,128]{2,1,0:T(8,128)(2,1)} %dynamic-slice_bitcast_fusion.14), channel_id=1, source_target_pairs={{0,4},{1,5},{2,6},{3,7},{4,0},{5,1},{6,2},{7,3},{8,12},{9,13},{10,... | collective-permute-start | bytes 786440 | tf_op jit(solution)/shard_map/ppermute | solution.py:50
  534.3 19.2 %collective-permute-start.49 = (bf16[4,288,128]{2,1,0:T(8,128)(2,1)S(1)}, bf16[4,288,128]{2,1,0:T(8,128)(2,1)S(1)}, u32[]{:S(2)}, u32[]{:S(2)}) collective-permute-start(bf16[4,288,128]{2,1,0:T(8,128)(2,1)S(1)} %bitcast.352), channel_id=1, source_target_pairs={{0,16},{1,17},{2,18},{3,19},{4,20},{5,21},{6,22},{7,23},{8,24},{9,... | collective-permute-start | bytes 884744 | tf_op jit(solution)/shard_map/ppermute | solution.py:50
  536.8 16.8 %collective-permute-start.50 = (bf16[4,288,128]{2,1,0:T(8,128)(2,1)S(1)}, bf16[4,288,128]{2,1,0:T(8,128)(2,1)S(1)}, u32[]{:S(2)}, u32[]{:S(2)}) collective-permute-start(bf16[4,288,128]{2,1,0:T(8,128)(2,1)S(1)} %dynamic-slice_bitcast_fusion.10), channel_id=1, source_target_pairs={{0,8},{1,9},{2,10},{3,11},{4,12},{5,13},{6,14},{7,15},{8,0},{9,1},... | collective-permute-start | bytes 884744 | tf_op jit(solution)/shard_map/ppermute | solution.py:50
  559.7 23.9 %collective-permute-start.59 = (bf16[2,1088,128]{2,1,0:T(8,128)(2,1)S(1)}, bf16[2,1088,128]{2,1,0:T(8,128)(2,1)S(1)}, u32[]{:S(2)}, u32[]{:S(2)}) collective-permute-start(bf16[2,1088,128]{2,1,0:T(8,128)(2,1)S(1)} %pad_maximum_fusion.3), channel_id=1, source_target_pairs={{0,2},{1,3},{2,0},{3,1},{4,6},{5,7},{6,4},{7,5},{8,10},{9,11},{10,... | collective-permute-start | bytes 1671176 | tf_op jit(solution)/shard_map/ppermute | solution.py:50
  (107 other events, 839.4 us)
Sparse Core Ops, SparseCore 0:
  11.5 74.6 all-gather.6
  89.7 94.9 all-gather.8

commit v6 on v5

--- a/solution.py
+++ b/solution.py
@@ -28,7 +28,7 @@
 LR_VECTOR = 0.4
 LANES = 128
 SLOT = 8
-PATIENT = 280000
+PATIENT = (2**18, 2**18 + 2**17)
 F32 = jnp.float32
 BF16 = jnp.bfloat16
 
@@ -67,7 +67,7 @@
 
     def send(self):
         self.got = [swap(sent, self.bit) for sent in self.sent]
-        self.wait = 2 if self.order is not None and self.values is not None and self.sent[0].size > PATIENT else 1
+        self.wait = 1 + sum(self.sent[0].size > most for most in PATIENT) if self.values is not None else 1
         self.sent = None
 
     def add(self):
@@ -1170,7 +1170,7 @@
     kinds = len(masters)
     counts = [len(arrays) for arrays, _ in sets]
 
-    def kernel(pair_ref, beside_ref, far_ref, *refs):
+    def kernel(upper_ref, upper_far, lower_ref, lower_far, *refs):
         arrays = [refs[: counts[0]], refs[counts[0] : sum(counts)]]
         sources, outs = refs[sum(counts) : sum(counts) + kinds], refs[sum(counts) + kinds :]
         place = lax.axis_index("dp")
@@ -1179,8 +1179,12 @@
             here = on_late ^ turn
             for number, (layer, kind, operand, start) in enumerate(items):
                 y, z = number // 2, number % 2
-                near = jnp.where(my_y == y, pair_ref[here].astype(F32), beside_ref[here].astype(F32))
-                poly = jnp.where(my_z == z, near, far_ref[turn, y ^ my_y].astype(F32)).astype(BF16)
+                turn_y, turn_z = y ^ my_y, z ^ my_z
+                halves = (
+                    jnp.where(turn_z == 0, upper_ref[turn_y, here].astype(F32), upper_far[turn_y, here].astype(F32)),
+                    jnp.where(turn_y == 0, lower_ref[turn_z, here].astype(F32), lower_far[turn_z, here].astype(F32)),
+                )
+                poly = jnp.concatenate(halves, axis=0).astype(BF16)
                 size = sources[kind].shape[1 if flipped[kind] else 2]
                 total = None
                 me = lax.axis_index("owner") if sets[turn][1][operand] else 0
@@ -1225,7 +1229,9 @@
             first_got = sent if first_got is None else first_got
             got = swap(sent, bit)
             if groups is late and moments is None:
-                moments = new_momenta([item for group in early + late for item in group], olds, flipped)
+                every = [item for group in early + late for item in group]
+                totals, _ = lax.optimization_barrier(([item[2] for item in every], sent))
+                moments = new_momenta([item[:2] + (total,) for item, total in zip(every, totals)], olds, flipped)
                 got, moments = lax.optimization_barrier((got, moments))
             values = kept + got
         grams.append(values[0])
@@ -1235,10 +1241,11 @@
     packed = lax.all_gather(mine, "owner", tiled=True)
     own = polynomial(packed, sets[0][0][0][0].shape[0])
     pair = jnp.stack([own, swap(own, turn_bit)])
-    beside = swap(pair, y_bit)
-    far = jnp.stack([pair, beside], axis=1)
-    far = jnp.where(on_late, far[::-1], far)
-    return apply_polynomials(sets[0], sets[1], (pair, beside, swap(far, z_bit)), masters, flipped), moments
+    middle = own.shape[0] // 2
+    upper, lower = pair[:, :middle], pair[:, middle:]
+    upper, lower = jnp.stack([upper, swap(upper, y_bit)]), jnp.stack([lower, swap(lower, z_bit)])
+    products = (upper, swap(upper, z_bit), lower, swap(lower, y_bit))
+    return apply_polynomials(sets[0], sets[1], products, masters, flipped), moments
 
 
 def adamw(weight, grad, first, second, rate, decay):
@@ -1452,9 +1459,8 @@
     loss_sum = extra[class_rows, 0] + (extra[class_rows + 1, 0] + extra[class_rows + 2, 0])
     grad_bias = bias_raw / weight_total
     last_flow = Flow([grad_one], left, turned[0])
-    last_flow.sent = advance(last_flow.sent, [two_flow[0]], True)
     last_flow.send()
-    advance([], [last_flow], True)
+    advance([], [two_flow[0], last_flow], True)
     flows.append(last_flow)
     high, low = LAYERS - 1, 0
     stored = lambda arrays: tuple(a if a.shape[2] % LANES == 0 else jnp.swapaxes(a, 1, 2) for a in arrays)

time: 713 us -> 703 us (0.986)
  waiting for transfers between devices: 129 us -> 116 us
    ppermute x68 -> x70, waiting for transfers between devices: 98.3 us -> 84.2 us  [swap(): lax.ppermute(values, AXES, [(src, src ^ 1 << bit) for src in range(count)])]
    ppermute x68 -> x70, starting transfers between devices: 76.7 us -> 75.4 us  [swap(): lax.ppermute(values, AXES, [(src, src ^ 1 << bit) for src in range(count)])]
    unnamed x139 -> x143, local copies, waits for them, and re-layouts: 17 us -> 17.6 us
  transfers between devices with their start and end apart: 77 -> 79, of which waited for: 27 -> 28; matrix products, arithmetic and copies ran while one was open for 5% -> 5% of each run, Pallas kernels for 27% -> 27%
where the time goes in v6:
time: 703 us; the launch traced here: 692 us
  Pallas kernels  269 us (38%)
  waiting for transfers between devices  116 us (17%)
  blocking collectives  104 us (15%)
  starting transfers between devices  98.7 us (14%)
  local copies, waits for them, and re-layouts  48.5 us (7%)
  other arithmetic  35.9 us (5%)
  between operations  19.7 us (3%)
    pallas_call x28, Pallas kernels, launch(): pl.pallas_call(grouped, name=name, grid=grid, in_specs=flat_specs, out_sp...  269 us
    ppermute x70, waiting for transfers between devices, swap(): lax.ppermute(values, AXES, [(src, src ^ 1 << bit) for src in range(count)])  84.2 us
    all_to_all x5, blocking collectives, exchange(): return lax.all_to_all(copies, AXES, 0, 0, tiled=True)  79.8 us
    ppermute x70, starting transfers between devices, swap(): lax.ppermute(values, AXES, [(src, src ^ 1 << bit) for src in range(count)])  75.4 us
    all_to_all x7, waiting for transfers between devices, exchange(): return lax.all_to_all(copies, AXES, 0, 0, tiled=True)  27.8 us
    all_to_all x7, starting transfers between devices, exchange(): return lax.all_to_all(copies, AXES, 0, 0, tiled=True)  23.3 us
    unnamed x143, local copies, waits for them, and re-layouts  17.6 us
    add x11, other arithmetic, add(): parts = [kept + got for kept, got in zip(self.kept, self.got)]  16.1 us
  transfers between devices with their start and end apart: 79, of which 28 were waited for; matrix products, arithmetic and copies ran while one was open for 5% of the time, Pallas kernels for 27%

profile of v6, /device:TPU:0, one launch (start us, length us, event | category | flops | bytes accessed | tf_op | source)
XLA Modules:
  0.0 692.1 jit_solution(4168693073691433694)
XLA Ops:
  27.9 6.7 collective-permute-done.3
  56.6 9.0 %reduce_first.1 = (f32[1344,512]{1,0:T(8,128)}, f32[32,16,128]{2,1,0:T(8,128)}) custom-call(bf16[1344,2048]{1,0:T(8,128)(2,1)} %bitcast.263, f32[1344,2]{1,0:T(8,128)} %copy.71.refs_1_.refs_4_.refs_5_.refs_6_, f32[8,128]{1,0:T(8,128)} %broadcast_in_dim.39.refs_2_, bf16[16,256,128]{2,1,0:T(8,128)(2,1)} %copy-done.58, ...), custom_call_target="tpu_custom_call" | custom-call | flops 2818572288 | bytes 10631680 | tf_op jit(solution)/shard_map/reduce_first/pallas_call | solution.py:360
  78.0 9.6 %all-to-all-done.refs_1_ = f32[32,16,128]{2,1,0:T(8,128)} async-done(((f32[32,16,128]{2,1,0:T(8,128)}), f32[32,16,128]{2,1,0:T(8,128)}, u32[]{:S(2)}, u32[]{:S(2)}) %all-to-all-start) | async-done | bytes 262176 | tf_op jit(solution)/shard_map/all_to_all | solution.py:45
  93.2 13.6 %spatial_conv.2 = (bf16[1344,512]{1,0:T(8,128)(2,1)}, f32[1344,512]{1,0:T(8,128)}, f32[8,512]{1,0:T(8,128)}, f32[32,8,128]{2,1,0:T(8,128)}) custom-call(f32[1344,512]{1,0:T(8,128)} %get-tuple-element.278.refs_0_.refs_7_.refs_2_, f32[32,16,128]{2,1,0:T(8,128)} %all-to-all-done.refs_1_, f32[8,128]{1,0:T(8,128)} %slice_reduce_fusion.refs_2_.refs_3_.refs_4_.refs_5_, ...), custom_call_target="tpu_custom_call" | custom-call | flops 6341787648 | bytes 12073472 | tf_op jit(solution)/shard_map/spatial_conv/pallas_call | solution.py:360
  106.8 12.4 %all_to_all.60.refs_1_ = f32[32,8,128]{2,1,0:T(8,128)} all-to-all(f32[32,8,128]{2,1,0:T(8,128)} %get-tuple-element.288), channel_id=1, replica_groups=mesh['dp'=8,'owner'=4] {'dp','owner'}, dimensions={0} | all-to-all | bytes 262144 | tf_op jit(solution)/shard_map/all_to_all | solution.py:45
  119.2 9.2 %expand.2 = (bf16[1344,512]{1,0:T(8,128)(2,1)}, bf16[1344,2048]{1,0:T(8,128)(2,1)}, f32[8,512]{1,0:T(8,128)}, f32[32,32,128]{2,1,0:T(8,128)}) custom-call(f32[1344,512]{1,0:T(8,128)} %get-tuple-element.287.refs_0_.refs_7_.refs_1_, f32[32,8,128]{2,1,0:T(8,128)} %all_to_all.60.refs_1_, f32[8,128]{1,0:T(8,128)} %slice_reduce_fusion.refs_2_.refs_3_.refs_4_.refs_5_, ...), custom_call_target="tpu_custom_call" | custom-call | flops 2818572288 | bytes 14563840 | tf_op jit(solution)/shard_map/expand/pallas_call | solution.py:360
  128.5 24.4 %all_to_all.61.refs_2_ = f32[32,32,128]{2,1,0:T(8,128)} all-to-all(f32[32,32,128]{2,1,0:T(8,128)} %get-tuple-element.290), channel_id=1, replica_groups=mesh['dp'=8,'owner'=4] {'dp','owner'}, dimensions={0} | all-to-all | bytes 1048576 | tf_op jit(solution)/shard_map/all_to_all | solution.py:45
  152.8 13.1 %close_and_reduce.1 = (bf16[1344,2048]{1,0:T(8,128)(2,1)}, f32[1344,512]{1,0:T(8,128)}, f32[8,2048]{1,0:T(8,128)}, f32[32,8,128]{2,1,0:T(8,128)}) custom-call(bf16[1344,2048]{1,0:T(8,128)(2,1)} %get-tuple-element.289.refs_0_.refs_8_.refs_1_, bf16[1344,2048]{1,0:T(8,128)(2,1)} %bitcast.264, f32[32,32,128]{2,1,0:T(8,128)} %all_to_all.61.refs_2_, ...), custom_call_target="tpu_custom_call" | custom-call | flops 2818572288 | bytes 24246784 | tf_op jit(solution)/shard_map/close_and_reduce/pallas_call | solution.py:360
  165.9 14.6 %all_to_all.62.refs_1_ = f32[32,8,128]{2,1,0:T(8,128)} all-to-all(f32[32,8,128]{2,1,0:T(8,128)} %get-tuple-element.292), channel_id=1, replica_groups=mesh['dp'=8,'owner'=4] {'dp','owner'}, dimensions={0} | all-to-all | bytes 262144 | tf_op jit(solution)/shard_map/all_to_all | solution.py:45
  184.8 13.1 %spatial_conv.3 = (bf16[1344,512]{1,0:T(8,128)(2,1)}, f32[1344,512]{1,0:T(8,128)}, f32[8,512]{1,0:T(8,128)}, f32[32,8,128]{2,1,0:T(8,128)}) custom-call(f32[1344,512]{1,0:T(8,128)} %get-tuple-element.291.refs_0_.refs_7_.refs_1_, f32[32,8,128]{2,1,0:T(8,128)} %all_to_all.62.refs_1_, f32[8,128]{1,0:T(8,128)} %slice_reduce_fusion.refs_2_.refs_3_.refs_4_.refs_5_, ...), custom_call_target="tpu_custom_call" | custom-call | flops 6341787648 | bytes 18233856 | tf_op jit(solution)/shard_map/spatial_conv/pallas_call | solution.py:360
  198.0 11.5 %all_to_all.63.refs_1_ = f32[32,8,128]{2,1,0:T(8,128)} all-to-all(f32[32,8,128]{2,1,0:T(8,128)} %get-tuple-element.296), channel_id=1, replica_groups=mesh['dp'=8,'owner'=4] {'dp','owner'}, dimensions={0} | all-to-all | bytes 262144 | tf_op jit(solution)/shard_map/all_to_all | solution.py:45
  209.5 9.2 %expand.3 = (bf16[1344,512]{1,0:T(8,128)(2,1)}, bf16[1344,2048]{1,0:T(8,128)(2,1)}, f32[8,512]{1,0:T(8,128)}, f32[32,32,128]{2,1,0:T(8,128)}) custom-call(f32[1344,512]{1,0:T(8,128)} %get-tuple-element.295.refs_0_.refs_7_.refs_1_, f32[32,8,128]{2,1,0:T(8,128)} %all_to_all.63.refs_1_, f32[8,128]{1,0:T(8,128)} %slice_reduce_fusion.refs_2_.refs_3_.refs_4_.refs_5_, ...), custom_call_target="tpu_custom_call" | custom-call | flops 2818572288 | bytes 21379584 | tf_op jit(solution)/shard_map/expand/pallas_call | solution.py:360
  222.2 14.7 %all-to-all-done.5.refs_2_ = f32[32,32,128]{2,1,0:T(8,128)S(1)} async-done(((f32[32,32,128]{2,1,0:T(8,128)}), f32[32,32,128]{2,1,0:T(8,128)S(1)}, u32[]{:S(2)}, u32[]{:S(2)}) %all-to-all-start.5) | async-done | bytes 524320 | tf_op jit(solution)/shard_map/all_to_all | solution.py:45
  237.7 30.0 %head_step.1 = (bf16[1344,2048]{1,0:T(8,128)(2,1)}, f32[8,2048]{1,0:T(8,128)}, bf16[32,48,128]{2,1,0:T(8,128)(2,1)}, bf16[2,8,2,256,128]{4,3,2,1,0:T(8,128)(2,1)}, bf16[2,8,2,256,128]{4,3,2,1,0:T(8,128)(2,1)}) custom-call(bf16[1344,2048]{1,0:T(8,128)(2,1)} %get-tuple-element.297.refs_0_.refs_1_, bf16[1344,2048]{1,0:T(8,128)(2,1)} %get-tuple-element.298.refs_1_.refs_0_, ...), custom_call_target="tpu_custom_call" | custom-call | flops 301989888 | bytes 32799424 | tf_op jit(solution)/shard_map/head_step/pallas_call | solution.py:360
  267.7 16.9 %all_to_all.64.refs_2_.refs_5_ = bf16[32,48,128]{2,1,0:T(8,128)(2,1)} all-to-all(bf16[32,48,128]{2,1,0:T(8,128)(2,1)} %get-tuple-element.300), channel_id=1, replica_groups=mesh['dp'=8,'owner'=4] {'dp','owner'}, dimensions={0} | all-to-all | bytes 786432 | tf_op jit(solution)/shard_map/all_to_all | solution.py:45
  284.6 12.8 %back_expand.2 = (bf16[1344,2048]{1,0:T(8,128)(2,1)}, f32[1344,512]{1,0:T(8,128)}, f32[32,8,128]{2,1,0:T(8,128)}) custom-call(bf16[1344,2048]{1,0:T(8,128)(2,1)} %get-tuple-element.302.refs_0_.refs_7_, bf16[1344,2048]{1,0:T(8,128)(2,1)} %get-tuple-element.297.refs_0_.refs_1_, bf16[32,48,128]{2,1,0:T(8,128)(2,1)} %all_to_all.64.refs_2_.refs_5_, ...), custom_call_target="tpu_custom_call" | custom-call | flops 2818572288 | bytes 33554432 | tf_op jit(solution)/shard_map/back_expand/pallas_call | solution.py:360
  303.9 7.3 %weight_grad.3 = (bf16[2,2048,128]{2,1,0:T(8,128)(2,1)}, bf16[2,2048,128]{2,1,0:T(8,128)(2,1)}) custom-call(bf16[1344,2048]{1,0:T(8,128)(2,1)} %get-tuple-element.313.refs_0_, bf16[1344,512]{1,0:T(8,128)(2,1)} %get-tuple-element.314.refs_1_), custom_call_target="tpu_custom_call" | custom-call | flops 2818572288 | bytes 8978432 | tf_op jit(solution)/shard_map/weight_grad/pallas_call | solution.py:360
  313.2 15.2 %back_conv.2 = (bf16[1344,512]{1,0:T(8,128)(2,1)}, f32[1344,512]{1,0:T(8,128)}, f32[32,8,128]{2,1,0:T(8,128)}) custom-call(f32[1344,512]{1,0:T(8,128)} %get-tuple-element.310.refs_0_, f32[1344,512]{1,0:T(8,128)} %get-tuple-element.295.refs_0_.refs_7_.refs_1_, f32[32,8,128]{2,1,0:T(8,128)} %copy-done.30, f32[8,512]{1,0:T(8,128)} %get-tuple-element.306.refs_8_.refs_3_, ...), custom_call_target="tpu_custom_call" | custom-call | flops 6341787648 | bytes 23755264 | tf_op jit(solution)/shard_map/back_conv/pallas_call | solution.py:360
  336.0 11.7 %spatial_grad.2 = (bf16[2,4608,128]{2,1,0:T(8,128)(2,1)}, bf16[2,4608,128]{2,1,0:T(8,128)(2,1)}) custom-call(bf16[1344,512]{1,0:T(8,128)(2,1)} %get-tuple-element.330.refs_0_, bf16[1344,512]{1,0:T(8,128)(2,1)} %get-tuple-element.331.refs_1_), custom_call_target="tpu_custom_call" | custom-call | flops 6341787648 | bytes 7471104 | tf_op jit(solution)/shard_map/spatial_grad/pallas_call | solution.py:360
  355.1 17.7 %back_reduce.1 = (bf16[1344,512]{1,0:T(8,128)(2,1)}, bf16[1344,2048]{1,0:T(8,128)(2,1)}, bf16[32,32,128]{2,1,0:T(8,128)(2,1)}) custom-call(f32[1344,512]{1,0:T(8,128)} %get-tuple-element.327.refs_0_, f32[1344,512]{1,0:T(8,128)} %get-tuple-element.291.refs_0_.refs_7_.refs_1_, f32[32,8,128]{2,1,0:T(8,128)} %copy-done.9, ...), custom_call_target="tpu_custom_call" | custom-call | flops 2818572288 | bytes 33554432 | tf_op jit(solution)/shard_map/back_reduce/pallas_call | solution.py:360
  389.3 7.3 %weight_grad.4 = (bf16[2,2048,128]{2,1,0:T(8,128)(2,1)}, bf16[2,2048,128]{2,1,0:T(8,128)(2,1)}) custom-call(bf16[1344,2048]{1,0:T(8,128)(2,1)} %get-tuple-element.298.refs_1_.refs_0_, bf16[1344,512]{1,0:T(8,128)(2,1)} %get-tuple-element.355.refs_1_), custom_call_target="tpu_custom_call" | custom-call | flops 2818572288 | bytes 8978432 | tf_op jit(solution)/shard_map/weight_grad/pallas_call | solution.py:360
  411.9 12.8 %back_expand.3 = (bf16[1344,2048]{1,0:T(8,128)(2,1)}, f32[1344,512]{1,0:T(8,128)}, f32[32,8,128]{2,1,0:T(8,128)}) custom-call(bf16[1344,2048]{1,0:T(8,128)(2,1)} %get-tuple-element.350.refs_0_, bf16[1344,2048]{1,0:T(8,128)(2,1)} %get-tuple-element.289.refs_0_.refs_8_.refs_1_, bf16[32,32,128]{2,1,0:T(8,128)(2,1)} %copy-done.5, ...), custom_call_target="tpu_custom_call" | custom-call | flops 2818572288 | bytes 26753536 | tf_op jit(solution)/shard_map/back_expand/pallas_call | solution.py:360
  436.6 7.3 %weight_grad.5 = (bf16[2,2048,128]{2,1,0:T(8,128)(2,1)}, bf16[2,2048,128]{2,1,0:T(8,128)(2,1)}) custom-call(bf16[1344,2048]{1,0:T(8,128)(2,1)} %get-tuple-element.384.refs_0_, bf16[1344,512]{1,0:T(8,128)(2,1)} %get-tuple-element.385.refs_1_), custom_call_target="tpu_custom_call" | custom-call | flops 2818572288 | bytes 8978432 | tf_op jit(solution)/shard_map/weight_grad/pallas_call | solution.py:360
  451.1 15.5 %back_conv.3 = (bf16[1344,512]{1,0:T(8,128)(2,1)}, f32[1344,512]{1,0:T(8,128)}, f32[32,8,128]{2,1,0:T(8,128)}) custom-call(f32[1344,512]{1,0:T(8,128)} %get-tuple-element.380.refs_0_, f32[1344,512]{1,0:T(8,128)} %get-tuple-element.287.refs_0_.refs_7_.refs_1_, f32[32,8,128]{2,1,0:T(8,128)} %copy-done.31, f32[8,512]{1,0:T(8,128)} %get-tuple-element.358.refs_8_.refs_3_, ...), custom_call_target="tpu_custom_call" | custom-call | flops 6341787648 | bytes 17463808 | tf_op jit(solution)/shard_map/back_conv/pallas_call | solution.py:360
  473.6 11.7 %spatial_grad.3 = (bf16[2,4608,128]{2,1,0:T(8,128)(2,1)}, bf16[2,4608,128]{2,1,0:T(8,128)(2,1)}) custom-call(bf16[1344,512]{1,0:T(8,128)(2,1)} %get-tuple-element.406.refs_0_, bf16[1344,512]{1,0:T(8,128)(2,1)} %get-tuple-element.407.refs_1_), custom_call_target="tpu_custom_call" | custom-call | flops 6341787648 | bytes 7471104 | tf_op jit(solution)/shard_map/spatial_grad/pallas_call | solution.py:360
  487.0 9.6 %last_grad.1 = (bf16[2,2048,128]{2,1,0:T(8,128)(2,1)}, bf16[2,2048,128]{2,1,0:T(8,128)(2,1)}) custom-call(bf16[1344,2048]{1,0:T(8,128)(2,1)} %bitcast.266, f32[1344,512]{1,0:T(8,128)} %get-tuple-element.417.refs_1_, f32[1344,512]{1,0:T(8,128)} %get-tuple-element.278.refs_0_.refs_7_.refs_2_, f32[32,8,128]{2,1,0:T(8,128)} %copy-done.10, ...), custom_call_target="tpu_custom_call" | custom-call | flops 2818572288 | bytes 13269504 | tf_op jit(solution)/shard_map/last_grad/pallas_call | solution.py:360
  547.1 7.5 %collective-permute-done.48 = bf16[2,256,128]{2,1,0:T(8,128)(2,1)S(1)} collective-permute-done((bf16[2,256,128]{2,1,0:T(8,128)(2,1)S(1)}, bf16[2,256,128]{2,1,0:T(8,128)(2,1)S(1)}, u32[]{:S(2)}, u32[]{:S(2)}) %collective-permute-start.48) | collective-permute-done | bytes 131104 | tf_op jit(solution)/shard_map/ppermute | solution.py:50
  587.9 9.2 %all-gather.3 = bf16[3328,128]{1,0:T(8,128)(2,1)} all-gather(bf16[832,128]{1,0:T(8,128)(2,1)S(1)} %copy-done.18), channel_id=5, replica_groups=mesh['dp'=8,'owner'=4] {'owner'}, dimensions={0}, use_global_device_ids=true | all-gather | bytes 1064960 | tf_op jit(solution)/shard_map/all_gather | solution.py:1214
  620.2 6.7 collective-permute-done.64
  626.9 8.6 %all_gather.35.refs_0_ = f32[1280,128]{1,0:T(8,128)} all-gather(f32[320,128]{1,0:T(8,128)S(1)} %bitcast_add_fusion.21), channel_id=1, replica_groups=mesh['dp'=8,'owner'=4] {'owner'}, dimensions={0}, use_global_device_ids=true | all-gather | bytes 819200 | tf_op jit(solution)/shard_map/all_gather | solution.py:1241
  635.5 19.3 %polynomial.1 = bf16[128,512]{1,0:T(8,128)(2,1)} custom-call(f32[1280,128]{1,0:T(8,128)} %all_gather.35.refs_0_), custom_call_target="tpu_custom_call" | custom-call | flops 16106127360 | bytes 786432 | tf_op jit(solution)/shard_map/polynomial/pallas_call | solution.py:360
  657.0 7.2 %collective-permute-done.65 = bf16[128,512]{1,0:T(8,128)(2,1)S(1)} collective-permute-done((bf16[128,512]{1,0:T(8,128)(2,1)}, bf16[128,512]{1,0:T(8,128)(2,1)S(1)}, u32[]{:S(2)}, u32[]{:S(2)}) %collective-permute-start.65) | collective-permute-done | bytes 131104 | tf_op jit(solution)/shard_map/ppermute | solution.py:50
  (453 shorter events, 276.9 us)
Async XLA Ops:
  7.2 112.0 %all-gather.7.cloned.1.call-start = ((), (), s32[]{:S(2)}) async-start(), calls=%async_computation.12 | async-start | bytes 4325376 | tf_op jit(solution)/shard_map/all_gather | solution.py:1297
  10.2 174.6 %all-gather.9.cloned.1.call-start = ((), (), s32[]{:S(2)}) async-start(), calls=%async_computation.13 | async-start | bytes 11354112 | tf_op jit(solution)/shard_map/all_gather | solution.py:1343
  35.6 16.5 %collective-permute-start.5 = (bf16[8,256,128]{2,1,0:T(8,128)(2,1)S(1)}, bf16[8,256,128]{2,1,0:T(8,128)(2,1)S(1)}, u32[]{:S(2)}, u32[]{:S(2)}) collective-permute-start(bf16[8,256,128]{2,1,0:T(8,128)(2,1)S(1)} %pad_maximum_fusion.4), channel_id=1, source_target_pairs={{0,2},{1,3},{2,0},{3,1},{4,6},{5,7},{6,4},{7,5},{8,10},{9,11},{10,... | collective-permute-start | bytes 1572872 | tf_op jit(solution)/shard_map/ppermute | solution.py:50
  67.1 20.5 %collective-permute-start.12 = (bf16[8,288,128]{2,1,0:T(8,128)(2,1)S(1)}, bf16[8,288,128]{2,1,0:T(8,128)(2,1)S(1)}, u32[]{:S(2)}, u32[]{:S(2)}) collective-permute-start(bf16[8,288,128]{2,1,0:T(8,128)(2,1)S(1)} %pad_maximum_fusion.2), channel_id=1, source_target_pairs={{0,2},{1,3},{2,0},{3,1},{4,6},{5,7},{6,4},{7,5},{8,10},{9,11},{10,... | collective-permute-start | bytes 1769480 | tf_op jit(solution)/shard_map/ppermute | solution.py:50
  67.4 20.2 %collective-permute-start.11 = (bf16[8,288,128]{2,1,0:T(8,128)(2,1)S(1)}, bf16[8,288,128]{2,1,0:T(8,128)(2,1)S(1)}, u32[]{:S(2)}, u32[]{:S(2)}) collective-permute-start(bf16[8,288,128]{2,1,0:T(8,128)(2,1)S(1)} %pad_maximum_fusion.1), channel_id=1, source_target_pairs={{0,4},{1,5},{2,6},{3,7},{4,0},{5,1},{6,2},{7,3},{8,12},{9,13},{10,... | collective-permute-start | bytes 1769480 | tf_op jit(solution)/shard_map/ppermute | solution.py:50
  68.4 19.2 %all-to-all-start = ((f32[32,16,128]{2,1,0:T(8,128)}), f32[32,16,128]{2,1,0:T(8,128)}, u32[]{:S(2)}, u32[]{:S(2)}) async-start(f32[32,16,128]{2,1,0:T(8,128)} %get-tuple-element.281), calls=%async_computation | async-start | bytes 524288 | tf_op jit(solution)/shard_map/all_to_all | solution.py:45
  218.7 18.2 %all-to-all-start.5 = ((f32[32,32,128]{2,1,0:T(8,128)}), f32[32,32,128]{2,1,0:T(8,128)S(1)}, u32[]{:S(2)}, u32[]{:S(2)}) async-start(f32[32,32,128]{2,1,0:T(8,128)} %get-tuple-element.299), calls=%async_computation.5 | async-start | bytes 1048576 | tf_op jit(solution)/shard_map/all_to_all | solution.py:45
  312.3 35.4 %collective-permute-start.17 = (bf16[8,512,128]{2,1,0:T(8,128)(2,1)}, bf16[8,512,128]{2,1,0:T(8,128)(2,1)}, u32[]{:S(2)}, u32[]{:S(2)}) collective-permute-start(bf16[8,512,128]{2,1,0:T(8,128)(2,1)} %dynamic-slice_bitcast_fusion), channel_id=1, source_target_pairs={{0,2},{1,3},{2,0},{3,1},{4,6},{5,7},{6,4},{7,5},{8,10},{9,11},{10,... | collective-permute-start | bytes 3145736 | tf_op jit(solution)/shard_map/ppermute | solution.py:50
  330.8 18.5 %collective-permute-start.18 = (bf16[8,256,128]{2,1,0:T(8,128)(2,1)}, bf16[8,256,128]{2,1,0:T(8,128)(2,1)S(1)}, u32[]{:S(2)}, u32[]{:S(2)}) collective-permute-start(bf16[8,256,128]{2,1,0:T(8,128)(2,1)} %bitcast.38), channel_id=1, source_target_pairs={{0,8},{1,9},{2,10},{3,11},{4,12},{5,13},{6,14},{7,15},{8,0},{9,1},... | collective-permute-start | bytes 1572872 | tf_op jit(solution)/shard_map/ppermute | solution.py:50
  332.3 17.0 %all-to-all-start.8 = ((f32[32,8,128]{2,1,0:T(8,128)}), f32[32,8,128]{2,1,0:T(8,128)S(1)}, u32[]{:S(2)}, u32[]{:S(2)}) async-start(f32[32,8,128]{2,1,0:T(8,128)} %get-tuple-element.323), calls=%async_computation.8 | async-start | bytes 262144 | tf_op jit(solution)/shard_map/all_to_all | solution.py:45
  352.4 20.5 %collective-permute-start.21 = (bf16[16,576,128]{2,1,0:T(8,128)(2,1)}, bf16[16,576,128]{2,1,0:T(8,128)(2,1)}, u32[]{:S(2)}, u32[]{:S(2)}) collective-permute-start(bf16[16,576,128]{2,1,0:T(8,128)(2,1)} %bitcast.45), channel_id=1, source_target_pairs={{0,1},{1,0},{2,3},{3,2},{4,5},{5,4},{6,7},{7,6},{8,9},{9,8},{10,11... | collective-permute-start | bytes 7077896 | tf_op jit(solution)/shard_map/ppermute | solution.py:50
  352.6 20.3 %collective-permute-start.19 = (bf16[4,512,128]{2,1,0:T(8,128)(2,1)}, bf16[4,512,128]{2,1,0:T(8,128)(2,1)S(1)}, u32[]{:S(2)}, u32[]{:S(2)}) collective-permute-start(bf16[4,512,128]{2,1,0:T(8,128)(2,1)} %dynamic-slice_bitcast_fusion.7), channel_id=1, source_target_pairs={{0,4},{1,5},{2,6},{3,7},{4,0},{5,1},{6,2},{7,3},{8,12},{9,13},{10,... | collective-permute-start | bytes 1572872 | tf_op jit(solution)/shard_map/ppermute | solution.py:50
  353.3 19.5 %collective-permute-start.20 = (bf16[4,256,128]{2,1,0:T(8,128)(2,1)}, bf16[4,256,128]{2,1,0:T(8,128)(2,1)}, u32[]{:S(2)}, u32[]{:S(2)}) collective-permute-start(bf16[4,256,128]{2,1,0:T(8,128)(2,1)} %bitcast.44), channel_id=1, source_target_pairs={{0,16},{1,17},{2,18},{3,19},{4,20},{5,21},{6,22},{7,23},{8,24},{9,... | collective-permute-start | bytes 786440 | tf_op jit(solution)/shard_map/ppermute | solution.py:50
  381.1 21.6 %collective-permute-start.24 = (bf16[8,288,128]{2,1,0:T(8,128)(2,1)}, bf16[8,288,128]{2,1,0:T(8,128)(2,1)S(1)}, u32[]{:S(2)}, u32[]{:S(2)}) collective-permute-start(bf16[8,288,128]{2,1,0:T(8,128)(2,1)} %dynamic-slice_bitcast_fusion.3), channel_id=1, source_target_pairs={{0,2},{1,3},{2,0},{3,1},{4,6},{5,7},{6,4},{7,5},{8,10},{9,11},{10,... | collective-permute-start | bytes 1769480 | tf_op jit(solution)/shard_map/ppermute | solution.py:50
  382.6 20.9 %collective-permute-start.25 = (bf16[8,288,128]{2,1,0:T(8,128)(2,1)}, bf16[8,288,128]{2,1,0:T(8,128)(2,1)}, u32[]{:S(2)}, u32[]{:S(2)}) collective-permute-start(bf16[8,288,128]{2,1,0:T(8,128)(2,1)} %dynamic-slice_bitcast_fusion.2), channel_id=1, source_target_pairs={{0,4},{1,5},{2,6},{3,7},{4,0},{5,1},{6,2},{7,3},{8,12},{9,13},{10,... | collective-permute-start | bytes 1769480 | tf_op jit(solution)/shard_map/ppermute | solution.py:50
  383.2 19.5 %all-to-all-start.9 = ((bf16[32,32,128]{2,1,0:T(8,128)(2,1)}), bf16[32,32,128]{2,1,0:T(8,128)(2,1)S(1)}, u32[]{:S(2)}, u32[]{:S(2)}) async-start(bf16[32,32,128]{2,1,0:T(8,128)(2,1)} %get-tuple-element.344), calls=%async_computation.9 | async-start | bytes 524288 | tf_op jit(solution)/shard_map/all_to_all | solution.py:45
  386.0 16.7 %collective-permute-start.22 = (bf16[2,512,128]{2,1,0:T(8,128)(2,1)S(1)}, bf16[2,512,128]{2,1,0:T(8,128)(2,1)}, u32[]{:S(2)}, u32[]{:S(2)}) collective-permute-start(bf16[2,512,128]{2,1,0:T(8,128)(2,1)S(1)} %dynamic-slice_bitcast_fusion.16), channel_id=1, source_target_pairs={{0,8},{1,9},{2,10},{3,11},{4,12},{5,13},{6,14},{7,15},{8,0},{9,1},... | collective-permute-start | bytes 786440 | tf_op jit(solution)/shard_map/ppermute | solution.py:50
  407.7 17.0 %collective-permute-start.30 = (bf16[16,256,128]{2,1,0:T(8,128)(2,1)}, bf16[16,256,128]{2,1,0:T(8,128)(2,1)S(1)}, u32[]{:S(2)}, u32[]{:S(2)}) collective-permute-start(bf16[16,256,128]{2,1,0:T(8,128)(2,1)} %bitcast.64), channel_id=1, source_target_pairs={{0,1},{1,0},{2,3},{3,2},{4,5},{5,4},{6,7},{7,6},{8,9},{9,8},{10,11... | collective-permute-start | bytes 3145736 | tf_op jit(solution)/shard_map/ppermute | solution.py:50
  407.8 16.9 %collective-permute-start.28 = (bf16[4,288,128]{2,1,0:T(8,128)(2,1)S(1)}, bf16[4,288,128]{2,1,0:T(8,128)(2,1)S(1)}, u32[]{:S(2)}, u32[]{:S(2)}) collective-permute-start(bf16[4,288,128]{2,1,0:T(8,128)(2,1)S(1)} %dynamic-slice_bitcast_fusion.12), channel_id=1, source_target_pairs={{0,4},{1,5},{2,6},{3,7},{4,0},{5,1},{6,2},{7,3},{8,12},{9,13},{10,... | collective-permute-start | bytes 884744 | tf_op jit(solution)/shard_map/ppermute | solution.py:50
  446.1 20.5 %collective-permute-start.37 = (bf16[16,256,128]{2,1,0:T(8,128)(2,1)}, bf16[16,256,128]{2,1,0:T(8,128)(2,1)S(1)}, u32[]{:S(2)}, u32[]{:S(2)}) collective-permute-start(bf16[16,256,128]{2,1,0:T(8,128)(2,1)} %bitcast.81), channel_id=1, source_target_pairs={{0,1},{1,0},{2,3},{3,2},{4,5},{5,4},{6,7},{7,6},{8,9},{9,8},{10,11... | collective-permute-start | bytes 3145736 | tf_op jit(solution)/shard_map/ppermute | solution.py:50
  446.4 20.3 %collective-permute-start.36 = (bf16[4,256,128]{2,1,0:T(8,128)(2,1)S(1)}, bf16[4,256,128]{2,1,0:T(8,128)(2,1)S(1)}, u32[]{:S(2)}, u32[]{:S(2)}) collective-permute-start(bf16[4,256,128]{2,1,0:T(8,128)(2,1)S(1)} %dynamic-slice_bitcast_fusion.15), channel_id=1, source_target_pairs={{0,4},{1,5},{2,6},{3,7},{4,0},{5,1},{6,2},{7,3},{8,12},{9,13},{10,... | collective-permute-start | bytes 786440 | tf_op jit(solution)/shard_map/ppermute | solution.py:50
  447.2 19.4 %collective-permute-start.34 = (bf16[1,288,128]{2,1,0:T(8,128)(2,1)S(1)}, bf16[1,288,128]{2,1,0:T(8,128)(2,1)S(1)}, u32[]{:S(2)}, u32[]{:S(2)}) collective-permute-start(bf16[1,288,128]{2,1,0:T(8,128)(2,1)S(1)} %constant_dynamic-slice_fusion.12), channel_id=1, source_target_pairs={{0,16},{1,17},{2,18},{3,19},{4,20},{5,21},{6,22},{7,23},{8,24},{9,... | collective-permute-start | bytes 221192 | tf_op jit(solution)/shard_map/ppermute | solution.py:50
  449.7 17.0 %collective-permute-start.35 = (bf16[1,288,128]{2,1,0:T(8,128)(2,1)S(1)}, bf16[1,288,128]{2,1,0:T(8,128)(2,1)S(1)}, u32[]{:S(2)}, u32[]{:S(2)}) collective-permute-start(bf16[1,288,128]{2,1,0:T(8,128)(2,1)S(1)} %constant_dynamic-slice_fusion.11), channel_id=1, source_target_pairs={{0,2},{1,3},{2,0},{3,1},{4,6},{5,7},{6,4},{7,5},{8,10},{9,11},{10,... | collective-permute-start | bytes 221192 | tf_op jit(solution)/shard_map/ppermute | solution.py:50
  468.7 16.6 %collective-permute-start.39 = (bf16[8,256,128]{2,1,0:T(8,128)(2,1)S(1)}, bf16[8,256,128]{2,1,0:T(8,128)(2,1)S(1)}, u32[]{:S(2)}, u32[]{:S(2)}) collective-permute-start(bf16[8,256,128]{2,1,0:T(8,128)(2,1)S(1)} %dynamic-slice_bitcast_fusion.5), channel_id=1, source_target_pairs={{0,2},{1,3},{2,0},{3,1},{4,6},{5,7},{6,4},{7,5},{8,10},{9,11},{10,... | collective-permute-start | bytes 1572872 | tf_op jit(solution)/shard_map/ppermute | solution.py:50
  506.3 23.0 %collective-permute-start.44 = (bf16[8,288,128]{2,1,0:T(8,128)(2,1)}, bf16[8,288,128]{2,1,0:T(8,128)(2,1)}, u32[]{:S(2)}, u32[]{:S(2)}) collective-permute-start(bf16[8,288,128]{2,1,0:T(8,128)(2,1)} %bitcast.98), channel_id=1, source_target_pairs={{0,8},{1,9},{2,10},{3,11},{4,12},{5,13},{6,14},{7,15},{8,0},{9,1},... | collective-permute-start | bytes 1769480 | tf_op jit(solution)/shard_map/ppermute | solution.py:50
  508.0 21.2 %collective-permute-start.45 = (bf16[8,288,128]{2,1,0:T(8,128)(2,1)}, bf16[8,288,128]{2,1,0:T(8,128)(2,1)}, u32[]{:S(2)}, u32[]{:S(2)}) collective-permute-start(bf16[8,288,128]{2,1,0:T(8,128)(2,1)} %dynamic-slice_bitcast_fusion.1), channel_id=1, source_target_pairs={{0,4},{1,5},{2,6},{3,7},{4,0},{5,1},{6,2},{7,3},{8,12},{9,13},{10,... | collective-permute-start | bytes 1769480 | tf_op jit(solution)/shard_map/ppermute | solution.py:50
  510.1 19.1 %collective-permute-start.46 = (bf16[8,256,128]{2,1,0:T(8,128)(2,1)}, bf16[8,256,128]{2,1,0:T(8,128)(2,1)}, u32[]{:S(2)}, u32[]{:S(2)}) collective-permute-start(bf16[8,256,128]{2,1,0:T(8,128)(2,1)} %dynamic-slice_bitcast_fusion.4), channel_id=1, source_target_pairs={{0,2},{1,3},{2,0},{3,1},{4,6},{5,7},{6,4},{7,5},{8,10},{9,11},{10,... | collective-permute-start | bytes 1572872 | tf_op jit(solution)/shard_map/ppermute | solution.py:50
  511.6 17.6 %collective-permute-start.41 = (bf16[4,256,128]{2,1,0:T(8,128)(2,1)}, bf16[4,256,128]{2,1,0:T(8,128)(2,1)}, u32[]{:S(2)}, u32[]{:S(2)}) collective-permute-start(bf16[4,256,128]{2,1,0:T(8,128)(2,1)} %dynamic-slice_bitcast_fusion.14), channel_id=1, source_target_pairs={{0,4},{1,5},{2,6},{3,7},{4,0},{5,1},{6,2},{7,3},{8,12},{9,13},{10,... | collective-permute-start | bytes 786440 | tf_op jit(solution)/shard_map/ppermute | solution.py:50
  535.2 19.5 %collective-permute-start.49 = (bf16[4,288,128]{2,1,0:T(8,128)(2,1)}, bf16[4,288,128]{2,1,0:T(8,128)(2,1)S(1)}, u32[]{:S(2)}, u32[]{:S(2)}) collective-permute-start(bf16[4,288,128]{2,1,0:T(8,128)(2,1)} %bitcast.112), channel_id=1, source_target_pairs={{0,16},{1,17},{2,18},{3,19},{4,20},{5,21},{6,22},{7,23},{8,24},{9,... | collective-permute-start | bytes 884744 | tf_op jit(solution)/shard_map/ppermute | solution.py:50
  537.8 16.9 %collective-permute-start.50 = (bf16[4,288,128]{2,1,0:T(8,128)(2,1)S(1)}, bf16[4,288,128]{2,1,0:T(8,128)(2,1)S(1)}, u32[]{:S(2)}, u32[]{:S(2)}) collective-permute-start(bf16[4,288,128]{2,1,0:T(8,128)(2,1)S(1)} %dynamic-slice_bitcast_fusion.10), channel_id=1, source_target_pairs={{0,8},{1,9},{2,10},{3,11},{4,12},{5,13},{6,14},{7,15},{8,0},{9,1},... | collective-permute-start | bytes 884744 | tf_op jit(solution)/shard_map/ppermute | solution.py:50
  560.1 21.5 %collective-permute-start.59 = (bf16[2,1088,128]{2,1,0:T(8,128)(2,1)S(1)}, bf16[2,1088,128]{2,1,0:T(8,128)(2,1)S(1)}, u32[]{:S(2)}, u32[]{:S(2)}) collective-permute-start(bf16[2,1088,128]{2,1,0:T(8,128)(2,1)S(1)} %pad_maximum_fusion.3), channel_id=1, source_target_pairs={{0,2},{1,3},{2,0},{3,1},{4,6},{5,7},{6,4},{7,5},{8,10},{9,11},{10,... | collective-permute-start | bytes 1671176 | tf_op jit(solution)/shard_map/ppermute | solution.py:50
  587.0 18.3 %collective-permute-start.62 = (f32[2,320,128]{2,1,0:T(8,128)S(1)}, f32[2,320,128]{2,1,0:T(8,128)S(1)}, u32[]{:S(2)}, u32[]{:S(2)}) collective-permute-start(f32[2,320,128]{2,1,0:T(8,128)S(1)} %dynamic-slice_bitcast_fusion.9), channel_id=1, source_target_pairs={{0,4},{1,5},{2,6},{3,7},{4,0},{5,1},{6,2},{7,3},{8,12},{9,13},{10,... | collective-permute-start | bytes 983048 | tf_op jit(solution)/shard_map/ppermute | solution.py:50
  (111 other events, 827.1 us)
Sparse Core Ops, SparseCore 0:
  11.5 75.0 all-gather.6
  90.0 94.7 all-gather.8

commit v7 on v6

--- a/solution.py
+++ b/solution.py
@@ -567,7 +567,7 @@
 def close_and_reduce(hidden, inputs, parts, counts, norms, masks, weights, layer, devices):
     rows, wide = hidden.shape
     narrow = weights.width
-    strip_rows = block_rows(rows, 6)
+    strip_rows = block_rows(rows, 4)
     steps = rows // strip_rows
 
     def kernel(
@@ -837,7 +837,7 @@
 def back_reduce(dz, first_hidden, parts, stat_one, counts, norms, masks, ds, hidden, inputs, stat_wide, weights, layer, devices):
     rows, narrow = dz.shape
     wide = ds.shape[1]
-    strip_rows = block_rows(rows, 6)
+    strip_rows = block_rows(rows, 4)
     steps = rows // strip_rows
 
     def kernel(

time: 703 us -> 703 us (level)
  no operation moved by 1% of the time
where the time goes in v7:
time: 703 us; the launch traced here: 691 us
  Pallas kernels  268 us (38%)
  waiting for transfers between devices  117 us (17%)
  blocking collectives  104 us (15%)
  starting transfers between devices  99.1 us (14%)
  local copies, waits for them, and re-layouts  48.5 us (7%)
  other arithmetic  35.9 us (5%)
  between operations  19.4 us (3%)
    pallas_call x28, Pallas kernels, launch(): pl.pallas_call(grouped, name=name, grid=grid, in_specs=flat_specs, out_sp...  268 us
    ppermute x70, waiting for transfers between devices, swap(): lax.ppermute(values, AXES, [(src, src ^ 1 << bit) for src in range(count)])  84.1 us
    all_to_all x5, blocking collectives, exchange(): return lax.all_to_all(copies, AXES, 0, 0, tiled=True)  79.6 us
    ppermute x70, starting transfers between devices, swap(): lax.ppermute(values, AXES, [(src, src ^ 1 << bit) for src in range(count)])  75.5 us
    all_to_all x7, waiting for transfers between devices, exchange(): return lax.all_to_all(copies, AXES, 0, 0, tiled=True)  27.8 us
    all_to_all x7, starting transfers between devices, exchange(): return lax.all_to_all(copies, AXES, 0, 0, tiled=True)  23.5 us
    unnamed x143, local copies, waits for them, and re-layouts  17.6 us
    add x11, other arithmetic, add(): parts = [kept + got for kept, got in zip(self.kept, self.got)]  16.1 us
  transfers between devices with their start and end apart: 79, of which 28 were waited for; matrix products, arithmetic and copies ran while one was open for 5% of the time, Pallas kernels for 27%

profile of v7, /device:TPU:0, one launch (start us, length us, event | category | flops | bytes accessed | tf_op | source)
XLA Modules:
  0.0 691.4 jit_solution(12902942299155640197)
XLA Ops:
  27.9 6.7 collective-permute-done.3
  56.6 9.0 %reduce_first.1 = (f32[1344,512]{1,0:T(8,128)}, f32[32,16,128]{2,1,0:T(8,128)}) custom-call(bf16[1344,2048]{1,0:T(8,128)(2,1)} %bitcast.263, f32[1344,2]{1,0:T(8,128)} %copy.71.refs_1_.refs_4_.refs_5_.refs_6_, f32[8,128]{1,0:T(8,128)} %broadcast_in_dim.39.refs_2_, bf16[16,256,128]{2,1,0:T(8,128)(2,1)} %copy-done.58, ...), custom_call_target="tpu_custom_call" | custom-call | flops 2818572288 | bytes 10631680 | tf_op jit(solution)/shard_map/reduce_first/pallas_call | solution.py:360
  78.0 9.6 %all-to-all-done.refs_1_ = f32[32,16,128]{2,1,0:T(8,128)} async-done(((f32[32,16,128]{2,1,0:T(8,128)}), f32[32,16,128]{2,1,0:T(8,128)}, u32[]{:S(2)}, u32[]{:S(2)}) %all-to-all-start) | async-done | bytes 262176 | tf_op jit(solution)/shard_map/all_to_all | solution.py:45
  93.2 13.6 %spatial_conv.2 = (bf16[1344,512]{1,0:T(8,128)(2,1)}, f32[1344,512]{1,0:T(8,128)}, f32[8,512]{1,0:T(8,128)}, f32[32,8,128]{2,1,0:T(8,128)}) custom-call(f32[1344,512]{1,0:T(8,128)} %get-tuple-element.278.refs_0_.refs_7_.refs_2_, f32[32,16,128]{2,1,0:T(8,128)} %all-to-all-done.refs_1_, f32[8,128]{1,0:T(8,128)} %slice_reduce_fusion.refs_2_.refs_3_.refs_4_.refs_5_, ...), custom_call_target="tpu_custom_call" | custom-call | flops 6341787648 | bytes 12073472 | tf_op jit(solution)/shard_map/spatial_conv/pallas_call | solution.py:360
  106.8 12.4 %all_to_all.60.refs_1_ = f32[32,8,128]{2,1,0:T(8,128)} all-to-all(f32[32,8,128]{2,1,0:T(8,128)} %get-tuple-element.288), channel_id=1, replica_groups=mesh['dp'=8,'owner'=4] {'dp','owner'}, dimensions={0} | all-to-all | bytes 262144 | tf_op jit(solution)/shard_map/all_to_all | solution.py:45
  119.2 9.2 %expand.2 = (bf16[1344,512]{1,0:T(8,128)(2,1)}, bf16[1344,2048]{1,0:T(8,128)(2,1)}, f32[8,512]{1,0:T(8,128)}, f32[32,32,128]{2,1,0:T(8,128)}) custom-call(f32[1344,512]{1,0:T(8,128)} %get-tuple-element.287.refs_0_.refs_7_.refs_1_, f32[32,8,128]{2,1,0:T(8,128)} %all_to_all.60.refs_1_, f32[8,128]{1,0:T(8,128)} %slice_reduce_fusion.refs_2_.refs_3_.refs_4_.refs_5_, ...), custom_call_target="tpu_custom_call" | custom-call | flops 2818572288 | bytes 14563840 | tf_op jit(solution)/shard_map/expand/pallas_call | solution.py:360
  128.5 24.6 %all_to_all.61.refs_2_ = f32[32,32,128]{2,1,0:T(8,128)} all-to-all(f32[32,32,128]{2,1,0:T(8,128)} %get-tuple-element.290), channel_id=1, replica_groups=mesh['dp'=8,'owner'=4] {'dp','owner'}, dimensions={0} | all-to-all | bytes 1048576 | tf_op jit(solution)/shard_map/all_to_all | solution.py:45
  153.1 12.2 %close_and_reduce.1 = (bf16[1344,2048]{1,0:T(8,128)(2,1)}, f32[1344,512]{1,0:T(8,128)}, f32[8,2048]{1,0:T(8,128)}, f32[32,8,128]{2,1,0:T(8,128)}) custom-call(bf16[1344,2048]{1,0:T(8,128)(2,1)} %get-tuple-element.289.refs_0_.refs_8_.refs_1_, bf16[1344,2048]{1,0:T(8,128)(2,1)} %bitcast.264, f32[32,32,128]{2,1,0:T(8,128)} %all_to_all.61.refs_2_, ...), custom_call_target="tpu_custom_call" | custom-call | flops 2818572288 | bytes 24246784 | tf_op jit(solution)/shard_map/close_and_reduce/pallas_call | solution.py:360
  165.2 14.5 %all_to_all.62.refs_1_ = f32[32,8,128]{2,1,0:T(8,128)} all-to-all(f32[32,8,128]{2,1,0:T(8,128)} %get-tuple-element.292), channel_id=1, replica_groups=mesh['dp'=8,'owner'=4] {'dp','owner'}, dimensions={0} | all-to-all | bytes 262144 | tf_op jit(solution)/shard_map/all_to_all | solution.py:45
  184.8 13.1 %spatial_conv.3 = (bf16[1344,512]{1,0:T(8,128)(2,1)}, f32[1344,512]{1,0:T(8,128)}, f32[8,512]{1,0:T(8,128)}, f32[32,8,128]{2,1,0:T(8,128)}) custom-call(f32[1344,512]{1,0:T(8,128)} %get-tuple-element.291.refs_0_.refs_7_.refs_1_, f32[32,8,128]{2,1,0:T(8,128)} %all_to_all.62.refs_1_, f32[8,128]{1,0:T(8,128)} %slice_reduce_fusion.refs_2_.refs_3_.refs_4_.refs_5_, ...), custom_call_target="tpu_custom_call" | custom-call | flops 6341787648 | bytes 18233856 | tf_op jit(solution)/shard_map/spatial_conv/pallas_call | solution.py:360
  198.0 11.5 %all_to_all.63.refs_1_ = f32[32,8,128]{2,1,0:T(8,128)} all-to-all(f32[32,8,128]{2,1,0:T(8,128)} %get-tuple-element.296), channel_id=1, replica_groups=mesh['dp'=8,'owner'=4] {'dp','owner'}, dimensions={0} | all-to-all | bytes 262144 | tf_op jit(solution)/shard_map/all_to_all | solution.py:45
  209.5 9.2 %expand.3 = (bf16[1344,512]{1,0:T(8,128)(2,1)}, bf16[1344,2048]{1,0:T(8,128)(2,1)}, f32[8,512]{1,0:T(8,128)}, f32[32,32,128]{2,1,0:T(8,128)}) custom-call(f32[1344,512]{1,0:T(8,128)} %get-tuple-element.295.refs_0_.refs_7_.refs_1_, f32[32,8,128]{2,1,0:T(8,128)} %all_to_all.63.refs_1_, f32[8,128]{1,0:T(8,128)} %slice_reduce_fusion.refs_2_.refs_3_.refs_4_.refs_5_, ...), custom_call_target="tpu_custom_call" | custom-call | flops 2818572288 | bytes 21379584 | tf_op jit(solution)/shard_map/expand/pallas_call | solution.py:360
  222.2 14.7 %all-to-all-done.5.refs_2_ = f32[32,32,128]{2,1,0:T(8,128)S(1)} async-done(((f32[32,32,128]{2,1,0:T(8,128)}), f32[32,32,128]{2,1,0:T(8,128)S(1)}, u32[]{:S(2)}, u32[]{:S(2)}) %all-to-all-start.5) | async-done | bytes 524320 | tf_op jit(solution)/shard_map/all_to_all | solution.py:45
  237.7 30.0 %head_step.1 = (bf16[1344,2048]{1,0:T(8,128)(2,1)}, f32[8,2048]{1,0:T(8,128)}, bf16[32,48,128]{2,1,0:T(8,128)(2,1)}, bf16[2,8,2,256,128]{4,3,2,1,0:T(8,128)(2,1)}, bf16[2,8,2,256,128]{4,3,2,1,0:T(8,128)(2,1)}) custom-call(bf16[1344,2048]{1,0:T(8,128)(2,1)} %get-tuple-element.297.refs_0_.refs_1_, bf16[1344,2048]{1,0:T(8,128)(2,1)} %get-tuple-element.298.refs_1_.refs_0_, ...), custom_call_target="tpu_custom_call" | custom-call | flops 301989888 | bytes 32799424 | tf_op jit(solution)/shard_map/head_step/pallas_call | solution.py:360
  267.7 16.7 %all_to_all.64.refs_2_.refs_5_ = bf16[32,48,128]{2,1,0:T(8,128)(2,1)} all-to-all(bf16[32,48,128]{2,1,0:T(8,128)(2,1)} %get-tuple-element.300), channel_id=1, replica_groups=mesh['dp'=8,'owner'=4] {'dp','owner'}, dimensions={0} | all-to-all | bytes 786432 | tf_op jit(solution)/shard_map/all_to_all | solution.py:45
  284.4 12.8 %back_expand.2 = (bf16[1344,2048]{1,0:T(8,128)(2,1)}, f32[1344,512]{1,0:T(8,128)}, f32[32,8,128]{2,1,0:T(8,128)}) custom-call(bf16[1344,2048]{1,0:T(8,128)(2,1)} %get-tuple-element.302.refs_0_.refs_7_, bf16[1344,2048]{1,0:T(8,128)(2,1)} %get-tuple-element.297.refs_0_.refs_1_, bf16[32,48,128]{2,1,0:T(8,128)(2,1)} %all_to_all.64.refs_2_.refs_5_, ...), custom_call_target="tpu_custom_call" | custom-call | flops 2818572288 | bytes 33554432 | tf_op jit(solution)/shard_map/back_expand/pallas_call | solution.py:360
  303.6 7.3 %weight_grad.3 = (bf16[2,2048,128]{2,1,0:T(8,128)(2,1)}, bf16[2,2048,128]{2,1,0:T(8,128)(2,1)}) custom-call(bf16[1344,2048]{1,0:T(8,128)(2,1)} %get-tuple-element.313.refs_0_, bf16[1344,512]{1,0:T(8,128)(2,1)} %get-tuple-element.314.refs_1_), custom_call_target="tpu_custom_call" | custom-call | flops 2818572288 | bytes 8978432 | tf_op jit(solution)/shard_map/weight_grad/pallas_call | solution.py:360
  312.9 15.2 %back_conv.2 = (bf16[1344,512]{1,0:T(8,128)(2,1)}, f32[1344,512]{1,0:T(8,128)}, f32[32,8,128]{2,1,0:T(8,128)}) custom-call(f32[1344,512]{1,0:T(8,128)} %get-tuple-element.310.refs_0_, f32[1344,512]{1,0:T(8,128)} %get-tuple-element.295.refs_0_.refs_7_.refs_1_, f32[32,8,128]{2,1,0:T(8,128)} %copy-done.30, f32[8,512]{1,0:T(8,128)} %get-tuple-element.306.refs_8_.refs_3_, ...), custom_call_target="tpu_custom_call" | custom-call | flops 6341787648 | bytes 23755264 | tf_op jit(solution)/shard_map/back_conv/pallas_call | solution.py:360
  335.8 11.7 %spatial_grad.2 = (bf16[2,4608,128]{2,1,0:T(8,128)(2,1)}, bf16[2,4608,128]{2,1,0:T(8,128)(2,1)}) custom-call(bf16[1344,512]{1,0:T(8,128)(2,1)} %get-tuple-element.330.refs_0_, bf16[1344,512]{1,0:T(8,128)(2,1)} %get-tuple-element.331.refs_1_), custom_call_target="tpu_custom_call" | custom-call | flops 6341787648 | bytes 7471104 | tf_op jit(solution)/shard_map/spatial_grad/pallas_call | solution.py:360
  354.9 17.3 %back_reduce.1 = (bf16[1344,512]{1,0:T(8,128)(2,1)}, bf16[1344,2048]{1,0:T(8,128)(2,1)}, bf16[32,32,128]{2,1,0:T(8,128)(2,1)}) custom-call(f32[1344,512]{1,0:T(8,128)} %get-tuple-element.327.refs_0_, f32[1344,512]{1,0:T(8,128)} %get-tuple-element.291.refs_0_.refs_7_.refs_1_, f32[32,8,128]{2,1,0:T(8,128)} %copy-done.9, ...), custom_call_target="tpu_custom_call" | custom-call | flops 2818572288 | bytes 33554432 | tf_op jit(solution)/shard_map/back_reduce/pallas_call | solution.py:360
  388.8 7.3 %weight_grad.4 = (bf16[2,2048,128]{2,1,0:T(8,128)(2,1)}, bf16[2,2048,128]{2,1,0:T(8,128)(2,1)}) custom-call(bf16[1344,2048]{1,0:T(8,128)(2,1)} %get-tuple-element.298.refs_1_.refs_0_, bf16[1344,512]{1,0:T(8,128)(2,1)} %get-tuple-element.355.refs_1_), custom_call_target="tpu_custom_call" | custom-call | flops 2818572288 | bytes 8978432 | tf_op jit(solution)/shard_map/weight_grad/pallas_call | solution.py:360
  411.3 12.8 %back_expand.3 = (bf16[1344,2048]{1,0:T(8,128)(2,1)}, f32[1344,512]{1,0:T(8,128)}, f32[32,8,128]{2,1,0:T(8,128)}) custom-call(bf16[1344,2048]{1,0:T(8,128)(2,1)} %get-tuple-element.350.refs_0_, bf16[1344,2048]{1,0:T(8,128)(2,1)} %get-tuple-element.289.refs_0_.refs_8_.refs_1_, bf16[32,32,128]{2,1,0:T(8,128)(2,1)} %copy-done.5, ...), custom_call_target="tpu_custom_call" | custom-call | flops 2818572288 | bytes 26753536 | tf_op jit(solution)/shard_map/back_expand/pallas_call | solution.py:360
  436.4 7.3 %weight_grad.5 = (bf16[2,2048,128]{2,1,0:T(8,128)(2,1)}, bf16[2,2048,128]{2,1,0:T(8,128)(2,1)}) custom-call(bf16[1344,2048]{1,0:T(8,128)(2,1)} %get-tuple-element.384.refs_0_, bf16[1344,512]{1,0:T(8,128)(2,1)} %get-tuple-element.385.refs_1_), custom_call_target="tpu_custom_call" | custom-call | flops 2818572288 | bytes 8978432 | tf_op jit(solution)/shard_map/weight_grad/pallas_call | solution.py:360
  451.0 15.5 %back_conv.3 = (bf16[1344,512]{1,0:T(8,128)(2,1)}, f32[1344,512]{1,0:T(8,128)}, f32[32,8,128]{2,1,0:T(8,128)}) custom-call(f32[1344,512]{1,0:T(8,128)} %get-tuple-element.380.refs_0_, f32[1344,512]{1,0:T(8,128)} %get-tuple-element.287.refs_0_.refs_7_.refs_1_, f32[32,8,128]{2,1,0:T(8,128)} %copy-done.31, f32[8,512]{1,0:T(8,128)} %get-tuple-element.358.refs_8_.refs_3_, ...), custom_call_target="tpu_custom_call" | custom-call | flops 6341787648 | bytes 17463808 | tf_op jit(solution)/shard_map/back_conv/pallas_call | solution.py:360
  473.3 11.7 %spatial_grad.3 = (bf16[2,4608,128]{2,1,0:T(8,128)(2,1)}, bf16[2,4608,128]{2,1,0:T(8,128)(2,1)}) custom-call(bf16[1344,512]{1,0:T(8,128)(2,1)} %get-tuple-element.406.refs_0_, bf16[1344,512]{1,0:T(8,128)(2,1)} %get-tuple-element.407.refs_1_), custom_call_target="tpu_custom_call" | custom-call | flops 6341787648 | bytes 7471104 | tf_op jit(solution)/shard_map/spatial_grad/pallas_call | solution.py:360
  486.7 9.6 %last_grad.1 = (bf16[2,2048,128]{2,1,0:T(8,128)(2,1)}, bf16[2,2048,128]{2,1,0:T(8,128)(2,1)}) custom-call(bf16[1344,2048]{1,0:T(8,128)(2,1)} %bitcast.266, f32[1344,512]{1,0:T(8,128)} %get-tuple-element.417.refs_1_, f32[1344,512]{1,0:T(8,128)} %get-tuple-element.278.refs_0_.refs_7_.refs_2_, f32[32,8,128]{2,1,0:T(8,128)} %copy-done.10, ...), custom_call_target="tpu_custom_call" | custom-call | flops 2818572288 | bytes 13269504 | tf_op jit(solution)/shard_map/last_grad/pallas_call | solution.py:360
  546.8 7.5 %collective-permute-done.48 = bf16[2,256,128]{2,1,0:T(8,128)(2,1)S(1)} collective-permute-done((bf16[2,256,128]{2,1,0:T(8,128)(2,1)S(1)}, bf16[2,256,128]{2,1,0:T(8,128)(2,1)S(1)}, u32[]{:S(2)}, u32[]{:S(2)}) %collective-permute-start.48) | collective-permute-done | bytes 131104 | tf_op jit(solution)/shard_map/ppermute | solution.py:50
  587.5 9.2 %all-gather.3 = bf16[3328,128]{1,0:T(8,128)(2,1)} all-gather(bf16[832,128]{1,0:T(8,128)(2,1)S(1)} %copy-done.18), channel_id=5, replica_groups=mesh['dp'=8,'owner'=4] {'owner'}, dimensions={0}, use_global_device_ids=true | all-gather | bytes 1064960 | tf_op jit(solution)/shard_map/all_gather | solution.py:1214
  619.8 6.7 collective-permute-done.64
  626.5 8.5 %all_gather.35.refs_0_ = f32[1280,128]{1,0:T(8,128)} all-gather(f32[320,128]{1,0:T(8,128)S(1)} %bitcast_add_fusion.21), channel_id=1, replica_groups=mesh['dp'=8,'owner'=4] {'owner'}, dimensions={0}, use_global_device_ids=true | all-gather | bytes 819200 | tf_op jit(solution)/shard_map/all_gather | solution.py:1241
  635.1 19.3 %polynomial.1 = bf16[128,512]{1,0:T(8,128)(2,1)} custom-call(f32[1280,128]{1,0:T(8,128)} %all_gather.35.refs_0_), custom_call_target="tpu_custom_call" | custom-call | flops 16106127360 | bytes 786432 | tf_op jit(solution)/shard_map/polynomial/pallas_call | solution.py:360
  656.5 7.2 %collective-permute-done.65 = bf16[128,512]{1,0:T(8,128)(2,1)S(1)} collective-permute-done((bf16[128,512]{1,0:T(8,128)(2,1)}, bf16[128,512]{1,0:T(8,128)(2,1)S(1)}, u32[]{:S(2)}, u32[]{:S(2)}) %collective-permute-start.65) | collective-permute-done | bytes 131104 | tf_op jit(solution)/shard_map/ppermute | solution.py:50
  (453 shorter events, 278.0 us)
Async XLA Ops:
  7.2 112.0 %all-gather.7.cloned.1.call-start = ((), (), s32[]{:S(2)}) async-start(), calls=%async_computation.12 | async-start | bytes 4325376 | tf_op jit(solution)/shard_map/all_gather | solution.py:1297
  10.2 174.6 %all-gather.9.cloned.1.call-start = ((), (), s32[]{:S(2)}) async-start(), calls=%async_computation.13 | async-start | bytes 11354112 | tf_op jit(solution)/shard_map/all_gather | solution.py:1343
  35.6 16.5 %collective-permute-start.5 = (bf16[8,256,128]{2,1,0:T(8,128)(2,1)S(1)}, bf16[8,256,128]{2,1,0:T(8,128)(2,1)S(1)}, u32[]{:S(2)}, u32[]{:S(2)}) collective-permute-start(bf16[8,256,128]{2,1,0:T(8,128)(2,1)S(1)} %pad_maximum_fusion.4), channel_id=1, source_target_pairs={{0,2},{1,3},{2,0},{3,1},{4,6},{5,7},{6,4},{7,5},{8,10},{9,11},{10,... | collective-permute-start | bytes 1572872 | tf_op jit(solution)/shard_map/ppermute | solution.py:50
  67.1 20.5 %collective-permute-start.12 = (bf16[8,288,128]{2,1,0:T(8,128)(2,1)S(1)}, bf16[8,288,128]{2,1,0:T(8,128)(2,1)S(1)}, u32[]{:S(2)}, u32[]{:S(2)}) collective-permute-start(bf16[8,288,128]{2,1,0:T(8,128)(2,1)S(1)} %pad_maximum_fusion.2), channel_id=1, source_target_pairs={{0,2},{1,3},{2,0},{3,1},{4,6},{5,7},{6,4},{7,5},{8,10},{9,11},{10,... | collective-permute-start | bytes 1769480 | tf_op jit(solution)/shard_map/ppermute | solution.py:50
  67.4 20.2 %collective-permute-start.11 = (bf16[8,288,128]{2,1,0:T(8,128)(2,1)S(1)}, bf16[8,288,128]{2,1,0:T(8,128)(2,1)S(1)}, u32[]{:S(2)}, u32[]{:S(2)}) collective-permute-start(bf16[8,288,128]{2,1,0:T(8,128)(2,1)S(1)} %pad_maximum_fusion.1), channel_id=1, source_target_pairs={{0,4},{1,5},{2,6},{3,7},{4,0},{5,1},{6,2},{7,3},{8,12},{9,13},{10,... | collective-permute-start | bytes 1769480 | tf_op jit(solution)/shard_map/ppermute | solution.py:50
  68.4 19.2 %all-to-all-start = ((f32[32,16,128]{2,1,0:T(8,128)}), f32[32,16,128]{2,1,0:T(8,128)}, u32[]{:S(2)}, u32[]{:S(2)}) async-start(f32[32,16,128]{2,1,0:T(8,128)} %get-tuple-element.281), calls=%async_computation | async-start | bytes 524288 | tf_op jit(solution)/shard_map/all_to_all | solution.py:45
  218.7 18.2 %all-to-all-start.5 = ((f32[32,32,128]{2,1,0:T(8,128)}), f32[32,32,128]{2,1,0:T(8,128)S(1)}, u32[]{:S(2)}, u32[]{:S(2)}) async-start(f32[32,32,128]{2,1,0:T(8,128)} %get-tuple-element.299), calls=%async_computation.5 | async-start | bytes 1048576 | tf_op jit(solution)/shard_map/all_to_all | solution.py:45
  312.1 35.4 %collective-permute-start.17 = (bf16[8,512,128]{2,1,0:T(8,128)(2,1)}, bf16[8,512,128]{2,1,0:T(8,128)(2,1)}, u32[]{:S(2)}, u32[]{:S(2)}) collective-permute-start(bf16[8,512,128]{2,1,0:T(8,128)(2,1)} %dynamic-slice_bitcast_fusion), channel_id=1, source_target_pairs={{0,2},{1,3},{2,0},{3,1},{4,6},{5,7},{6,4},{7,5},{8,10},{9,11},{10,... | collective-permute-start | bytes 3145736 | tf_op jit(solution)/shard_map/ppermute | solution.py:50
  330.6 18.5 %collective-permute-start.18 = (bf16[8,256,128]{2,1,0:T(8,128)(2,1)}, bf16[8,256,128]{2,1,0:T(8,128)(2,1)S(1)}, u32[]{:S(2)}, u32[]{:S(2)}) collective-permute-start(bf16[8,256,128]{2,1,0:T(8,128)(2,1)} %bitcast.38), channel_id=1, source_target_pairs={{0,8},{1,9},{2,10},{3,11},{4,12},{5,13},{6,14},{7,15},{8,0},{9,1},... | collective-permute-start | bytes 1572872 | tf_op jit(solution)/shard_map/ppermute | solution.py:50
  332.0 17.0 %all-to-all-start.8 = ((f32[32,8,128]{2,1,0:T(8,128)}), f32[32,8,128]{2,1,0:T(8,128)S(1)}, u32[]{:S(2)}, u32[]{:S(2)}) async-start(f32[32,8,128]{2,1,0:T(8,128)} %get-tuple-element.323), calls=%async_computation.8 | async-start | bytes 262144 | tf_op jit(solution)/shard_map/all_to_all | solution.py:45
  352.2 20.1 %collective-permute-start.21 = (bf16[16,576,128]{2,1,0:T(8,128)(2,1)}, bf16[16,576,128]{2,1,0:T(8,128)(2,1)}, u32[]{:S(2)}, u32[]{:S(2)}) collective-permute-start(bf16[16,576,128]{2,1,0:T(8,128)(2,1)} %bitcast.45), channel_id=1, source_target_pairs={{0,1},{1,0},{2,3},{3,2},{4,5},{5,4},{6,7},{7,6},{8,9},{9,8},{10,11... | collective-permute-start | bytes 7077896 | tf_op jit(solution)/shard_map/ppermute | solution.py:50
  352.4 19.9 %collective-permute-start.19 = (bf16[4,512,128]{2,1,0:T(8,128)(2,1)}, bf16[4,512,128]{2,1,0:T(8,128)(2,1)S(1)}, u32[]{:S(2)}, u32[]{:S(2)}) collective-permute-start(bf16[4,512,128]{2,1,0:T(8,128)(2,1)} %dynamic-slice_bitcast_fusion.7), channel_id=1, source_target_pairs={{0,4},{1,5},{2,6},{3,7},{4,0},{5,1},{6,2},{7,3},{8,12},{9,13},{10,... | collective-permute-start | bytes 1572872 | tf_op jit(solution)/shard_map/ppermute | solution.py:50
  353.1 19.2 %collective-permute-start.20 = (bf16[4,256,128]{2,1,0:T(8,128)(2,1)}, bf16[4,256,128]{2,1,0:T(8,128)(2,1)}, u32[]{:S(2)}, u32[]{:S(2)}) collective-permute-start(bf16[4,256,128]{2,1,0:T(8,128)(2,1)} %bitcast.44), channel_id=1, source_target_pairs={{0,16},{1,17},{2,18},{3,19},{4,20},{5,21},{6,22},{7,23},{8,24},{9,... | collective-permute-start | bytes 786440 | tf_op jit(solution)/shard_map/ppermute | solution.py:50
  380.5 21.6 %collective-permute-start.24 = (bf16[8,288,128]{2,1,0:T(8,128)(2,1)}, bf16[8,288,128]{2,1,0:T(8,128)(2,1)S(1)}, u32[]{:S(2)}, u32[]{:S(2)}) collective-permute-start(bf16[8,288,128]{2,1,0:T(8,128)(2,1)} %dynamic-slice_bitcast_fusion.3), channel_id=1, source_target_pairs={{0,2},{1,3},{2,0},{3,1},{4,6},{5,7},{6,4},{7,5},{8,10},{9,11},{10,... | collective-permute-start | bytes 1769480 | tf_op jit(solution)/shard_map/ppermute | solution.py:50
  382.1 20.9 %collective-permute-start.25 = (bf16[8,288,128]{2,1,0:T(8,128)(2,1)}, bf16[8,288,128]{2,1,0:T(8,128)(2,1)}, u32[]{:S(2)}, u32[]{:S(2)}) collective-permute-start(bf16[8,288,128]{2,1,0:T(8,128)(2,1)} %dynamic-slice_bitcast_fusion.2), channel_id=1, source_target_pairs={{0,4},{1,5},{2,6},{3,7},{4,0},{5,1},{6,2},{7,3},{8,12},{9,13},{10,... | collective-permute-start | bytes 1769480 | tf_op jit(solution)/shard_map/ppermute | solution.py:50
  382.6 19.5 %all-to-all-start.9 = ((bf16[32,32,128]{2,1,0:T(8,128)(2,1)}), bf16[32,32,128]{2,1,0:T(8,128)(2,1)S(1)}, u32[]{:S(2)}, u32[]{:S(2)}) async-start(bf16[32,32,128]{2,1,0:T(8,128)(2,1)} %get-tuple-element.344), calls=%async_computation.9 | async-start | bytes 524288 | tf_op jit(solution)/shard_map/all_to_all | solution.py:45
  385.5 16.7 %collective-permute-start.22 = (bf16[2,512,128]{2,1,0:T(8,128)(2,1)S(1)}, bf16[2,512,128]{2,1,0:T(8,128)(2,1)}, u32[]{:S(2)}, u32[]{:S(2)}) collective-permute-start(bf16[2,512,128]{2,1,0:T(8,128)(2,1)S(1)} %dynamic-slice_bitcast_fusion.16), channel_id=1, source_target_pairs={{0,8},{1,9},{2,10},{3,11},{4,12},{5,13},{6,14},{7,15},{8,0},{9,1},... | collective-permute-start | bytes 786440 | tf_op jit(solution)/shard_map/ppermute | solution.py:50
  407.1 17.0 %collective-permute-start.30 = (bf16[16,256,128]{2,1,0:T(8,128)(2,1)}, bf16[16,256,128]{2,1,0:T(8,128)(2,1)S(1)}, u32[]{:S(2)}, u32[]{:S(2)}) collective-permute-start(bf16[16,256,128]{2,1,0:T(8,128)(2,1)} %bitcast.64), channel_id=1, source_target_pairs={{0,1},{1,0},{2,3},{3,2},{4,5},{5,4},{6,7},{7,6},{8,9},{9,8},{10,11... | collective-permute-start | bytes 3145736 | tf_op jit(solution)/shard_map/ppermute | solution.py:50
  407.2 16.9 %collective-permute-start.28 = (bf16[4,288,128]{2,1,0:T(8,128)(2,1)S(1)}, bf16[4,288,128]{2,1,0:T(8,128)(2,1)S(1)}, u32[]{:S(2)}, u32[]{:S(2)}) collective-permute-start(bf16[4,288,128]{2,1,0:T(8,128)(2,1)S(1)} %dynamic-slice_bitcast_fusion.12), channel_id=1, source_target_pairs={{0,4},{1,5},{2,6},{3,7},{4,0},{5,1},{6,2},{7,3},{8,12},{9,13},{10,... | collective-permute-start | bytes 884744 | tf_op jit(solution)/shard_map/ppermute | solution.py:50
  446.0 20.6 %collective-permute-start.37 = (bf16[16,256,128]{2,1,0:T(8,128)(2,1)}, bf16[16,256,128]{2,1,0:T(8,128)(2,1)S(1)}, u32[]{:S(2)}, u32[]{:S(2)}) collective-permute-start(bf16[16,256,128]{2,1,0:T(8,128)(2,1)} %bitcast.81), channel_id=1, source_target_pairs={{0,1},{1,0},{2,3},{3,2},{4,5},{5,4},{6,7},{7,6},{8,9},{9,8},{10,11... | collective-permute-start | bytes 3145736 | tf_op jit(solution)/shard_map/ppermute | solution.py:50
  446.2 20.4 %collective-permute-start.36 = (bf16[4,256,128]{2,1,0:T(8,128)(2,1)S(1)}, bf16[4,256,128]{2,1,0:T(8,128)(2,1)S(1)}, u32[]{:S(2)}, u32[]{:S(2)}) collective-permute-start(bf16[4,256,128]{2,1,0:T(8,128)(2,1)S(1)} %dynamic-slice_bitcast_fusion.15), channel_id=1, source_target_pairs={{0,4},{1,5},{2,6},{3,7},{4,0},{5,1},{6,2},{7,3},{8,12},{9,13},{10,... | collective-permute-start | bytes 786440 | tf_op jit(solution)/shard_map/ppermute | solution.py:50
  447.0 19.5 %collective-permute-start.34 = (bf16[1,288,128]{2,1,0:T(8,128)(2,1)S(1)}, bf16[1,288,128]{2,1,0:T(8,128)(2,1)S(1)}, u32[]{:S(2)}, u32[]{:S(2)}) collective-permute-start(bf16[1,288,128]{2,1,0:T(8,128)(2,1)S(1)} %constant_dynamic-slice_fusion.12), channel_id=1, source_target_pairs={{0,16},{1,17},{2,18},{3,19},{4,20},{5,21},{6,22},{7,23},{8,24},{9,... | collective-permute-start | bytes 221192 | tf_op jit(solution)/shard_map/ppermute | solution.py:50
  449.5 17.0 %collective-permute-start.35 = (bf16[1,288,128]{2,1,0:T(8,128)(2,1)S(1)}, bf16[1,288,128]{2,1,0:T(8,128)(2,1)S(1)}, u32[]{:S(2)}, u32[]{:S(2)}) collective-permute-start(bf16[1,288,128]{2,1,0:T(8,128)(2,1)S(1)} %constant_dynamic-slice_fusion.11), channel_id=1, source_target_pairs={{0,2},{1,3},{2,0},{3,1},{4,6},{5,7},{6,4},{7,5},{8,10},{9,11},{10,... | collective-permute-start | bytes 221192 | tf_op jit(solution)/shard_map/ppermute | solution.py:50
  468.6 16.5 %collective-permute-start.39 = (bf16[8,256,128]{2,1,0:T(8,128)(2,1)S(1)}, bf16[8,256,128]{2,1,0:T(8,128)(2,1)S(1)}, u32[]{:S(2)}, u32[]{:S(2)}) collective-permute-start(bf16[8,256,128]{2,1,0:T(8,128)(2,1)S(1)} %dynamic-slice_bitcast_fusion.5), channel_id=1, source_target_pairs={{0,2},{1,3},{2,0},{3,1},{4,6},{5,7},{6,4},{7,5},{8,10},{9,11},{10,... | collective-permute-start | bytes 1572872 | tf_op jit(solution)/shard_map/ppermute | solution.py:50
  505.9 23.0 %collective-permute-start.44 = (bf16[8,288,128]{2,1,0:T(8,128)(2,1)}, bf16[8,288,128]{2,1,0:T(8,128)(2,1)}, u32[]{:S(2)}, u32[]{:S(2)}) collective-permute-start(bf16[8,288,128]{2,1,0:T(8,128)(2,1)} %bitcast.98), channel_id=1, source_target_pairs={{0,8},{1,9},{2,10},{3,11},{4,12},{5,13},{6,14},{7,15},{8,0},{9,1},... | collective-permute-start | bytes 1769480 | tf_op jit(solution)/shard_map/ppermute | solution.py:50
  507.7 21.2 %collective-permute-start.45 = (bf16[8,288,128]{2,1,0:T(8,128)(2,1)}, bf16[8,288,128]{2,1,0:T(8,128)(2,1)}, u32[]{:S(2)}, u32[]{:S(2)}) collective-permute-start(bf16[8,288,128]{2,1,0:T(8,128)(2,1)} %dynamic-slice_bitcast_fusion.1), channel_id=1, source_target_pairs={{0,4},{1,5},{2,6},{3,7},{4,0},{5,1},{6,2},{7,3},{8,12},{9,13},{10,... | collective-permute-start | bytes 1769480 | tf_op jit(solution)/shard_map/ppermute | solution.py:50
  509.8 19.1 %collective-permute-start.46 = (bf16[8,256,128]{2,1,0:T(8,128)(2,1)}, bf16[8,256,128]{2,1,0:T(8,128)(2,1)}, u32[]{:S(2)}, u32[]{:S(2)}) collective-permute-start(bf16[8,256,128]{2,1,0:T(8,128)(2,1)} %dynamic-slice_bitcast_fusion.4), channel_id=1, source_target_pairs={{0,2},{1,3},{2,0},{3,1},{4,6},{5,7},{6,4},{7,5},{8,10},{9,11},{10,... | collective-permute-start | bytes 1572872 | tf_op jit(solution)/shard_map/ppermute | solution.py:50
  511.3 17.6 %collective-permute-start.41 = (bf16[4,256,128]{2,1,0:T(8,128)(2,1)}, bf16[4,256,128]{2,1,0:T(8,128)(2,1)}, u32[]{:S(2)}, u32[]{:S(2)}) collective-permute-start(bf16[4,256,128]{2,1,0:T(8,128)(2,1)} %dynamic-slice_bitcast_fusion.14), channel_id=1, source_target_pairs={{0,4},{1,5},{2,6},{3,7},{4,0},{5,1},{6,2},{7,3},{8,12},{9,13},{10,... | collective-permute-start | bytes 786440 | tf_op jit(solution)/shard_map/ppermute | solution.py:50
  534.9 19.5 %collective-permute-start.49 = (bf16[4,288,128]{2,1,0:T(8,128)(2,1)}, bf16[4,288,128]{2,1,0:T(8,128)(2,1)S(1)}, u32[]{:S(2)}, u32[]{:S(2)}) collective-permute-start(bf16[4,288,128]{2,1,0:T(8,128)(2,1)} %bitcast.112), channel_id=1, source_target_pairs={{0,16},{1,17},{2,18},{3,19},{4,20},{5,21},{6,22},{7,23},{8,24},{9,... | collective-permute-start | bytes 884744 | tf_op jit(solution)/shard_map/ppermute | solution.py:50
  537.4 16.9 %collective-permute-start.50 = (bf16[4,288,128]{2,1,0:T(8,128)(2,1)S(1)}, bf16[4,288,128]{2,1,0:T(8,128)(2,1)S(1)}, u32[]{:S(2)}, u32[]{:S(2)}) collective-permute-start(bf16[4,288,128]{2,1,0:T(8,128)(2,1)S(1)} %dynamic-slice_bitcast_fusion.10), channel_id=1, source_target_pairs={{0,8},{1,9},{2,10},{3,11},{4,12},{5,13},{6,14},{7,15},{8,0},{9,1},... | collective-permute-start | bytes 884744 | tf_op jit(solution)/shard_map/ppermute | solution.py:50
  559.8 21.5 %collective-permute-start.59 = (bf16[2,1088,128]{2,1,0:T(8,128)(2,1)S(1)}, bf16[2,1088,128]{2,1,0:T(8,128)(2,1)S(1)}, u32[]{:S(2)}, u32[]{:S(2)}) collective-permute-start(bf16[2,1088,128]{2,1,0:T(8,128)(2,1)S(1)} %pad_maximum_fusion.3), channel_id=1, source_target_pairs={{0,2},{1,3},{2,0},{3,1},{4,6},{5,7},{6,4},{7,5},{8,10},{9,11},{10,... | collective-permute-start | bytes 1671176 | tf_op jit(solution)/shard_map/ppermute | solution.py:50
  586.7 18.3 %collective-permute-start.62 = (f32[2,320,128]{2,1,0:T(8,128)S(1)}, f32[2,320,128]{2,1,0:T(8,128)S(1)}, u32[]{:S(2)}, u32[]{:S(2)}) collective-permute-start(f32[2,320,128]{2,1,0:T(8,128)S(1)} %dynamic-slice_bitcast_fusion.9), channel_id=1, source_target_pairs={{0,4},{1,5},{2,6},{3,7},{4,0},{5,1},{6,2},{7,3},{8,12},{9,13},{10,... | collective-permute-start | bytes 983048 | tf_op jit(solution)/shard_map/ppermute | solution.py:50
  (111 other events, 828.8 us)
Sparse Core Ops, SparseCore 0:
  11.5 75.0 all-gather.6
  90.0 94.7 all-gather.8
